TPU v7x, 32 devices: a whole 2x2x4 slice. The times are simulated.
32 devices in a mesh: dp: 16 (over z, y, x), fsdp: 2 (over core).
Axes of the slice: x: 2, y: 2, z: 4, core: 2. Of those that a mesh axis runs over, the one named last changes fastest.
Arguments:
- prompt_states: bfloat16 [32, 1024, 1024], P('dp', 'fsdp'), may hold values from -6 to 6
- branch_states: bfloat16 [32, 2, 128, 1024], P('dp', 'fsdp'), may hold values from -6 to 6
- encoder_states: bfloat16 [32, 256, 1024], P('dp', 'fsdp'), may hold values from -6 to 6
- branch_start: int32 [32, 2], P('dp', 'fsdp'), may hold values from 512 to 1024, as said below
- bucket_table: int32 [1152], replicated, may hold values from 0 to 31, as said below
- prompt_cotangent: bfloat16 [32, 1024, 1024], P('dp', 'fsdp'), may hold values from -6 to 6
- branch_cotangent: bfloat16 [32, 2, 128, 1024], P('dp', 'fsdp'), may hold values from -6 to 6
- projections: float32 [6, 1024, 1024], P(None, ('dp', 'fsdp')), may hold values from -0.1875 to 0.1875
- projections_first: float32 [6, 1024, 1024], P(None, ('dp', 'fsdp')), may hold values from -0.00015258789 to 0.00015258789
- projections_second: float32 [6, 1024, 1024], P(None, ('dp', 'fsdp')), may hold values from 5.868765e-11 to 2.347506e-10
- combiners: float32 [2, 1024, 1024], P(None, ('dp', 'fsdp')), may hold values from -1 to 1
- combiners_first: float32 [2, 1024, 1024], P(None, ('dp', 'fsdp')), may hold values from -7.6293945e-05 to 7.6293945e-05
- combiners_second: float32 [2, 1024, 1024], P(None, ('dp', 'fsdp')), may hold values from 1.173753e-11 to 4.695012e-11
- expansion: float32 [2, 1024, 2816], P(None, ('dp', 'fsdp')), may hold values from -0.1875 to 0.1875
- expansion_first: float32 [2, 1024, 2816], P(None, ('dp', 'fsdp')), may hold values from -0.00015258789 to 0.00015258789
- expansion_second: float32 [2, 1024, 2816], P(None, ('dp', 'fsdp')), may hold values from 5.868765e-11 to 2.347506e-10
- contraction: float32 [2816, 1024], P(('dp', 'fsdp')), may hold values from -0.109375 to 0.109375
- contraction_first: float32 [2816, 1024], P(('dp', 'fsdp')), may hold values from -0.00015258789 to 0.00015258789
- contraction_second: float32 [2816, 1024], P(('dp', 'fsdp')), may hold values from 5.868765e-11 to 2.347506e-10
- norm_gains: float32 [3, 1024], replicated
- gains_first: float32 [3, 1024], replicated, may hold values from -0.00061035156 to 0.00061035156
- gains_second: float32 [3, 1024], replicated, may hold values from 9.390024e-10 to 3.7560097e-09
- position_bias: float32 [32, 16], replicated, may hold values from -4 to 4
- bias_first: float32 [32, 16], replicated, may hold values from -0.0004272461 to 0.0004272461
- bias_second: float32 [32, 16], replicated, may hold values from 2.9343825e-10 to 1.173753e-09
Outputs:
- prompt_output: bfloat16 [32, 1024, 1024], P('dp', 'fsdp')
- branch_output: bfloat16 [32, 2, 128, 1024], P('dp', 'fsdp')
- prompt_grad: float32 [32, 1024, 1024], P('dp', 'fsdp')
- branch_grad: float32 [32, 2, 128, 1024], P('dp', 'fsdp')
- encoder_grad: float32 [32, 256, 1024], P('dp', 'fsdp')
- grad_norm: float32 [], replicated
- projections_new: float32 [6, 1024, 1024], P(None, ('dp', 'fsdp'))
- projections_first_new: float32 [6, 1024, 1024], P(None, ('dp', 'fsdp'))
- projections_second_new: float32 [6, 1024, 1024], P(None, ('dp', 'fsdp'))
- combiners_new: float32 [2, 1024, 1024], P(None, ('dp', 'fsdp'))
- combiners_first_new: float32 [2, 1024, 1024], P(None, ('dp', 'fsdp'))
- combiners_second_new: float32 [2, 1024, 1024], P(None, ('dp', 'fsdp'))
- expansion_new: float32 [2, 1024, 2816], P(None, ('dp', 'fsdp'))
- expansion_first_new: float32 [2, 1024, 2816], P(None, ('dp', 'fsdp'))
- expansion_second_new: float32 [2, 1024, 2816], P(None, ('dp', 'fsdp'))
- contraction_new: float32 [2816, 1024], P(('dp', 'fsdp'))
- contraction_first_new: float32 [2816, 1024], P(('dp', 'fsdp'))
- contraction_second_new: float32 [2816, 1024], P(('dp', 'fsdp'))
- gains_new: float32 [3, 1024], replicated
- gains_first_new: float32 [3, 1024], replicated
- gains_second_new: float32 [3, 1024], replicated
- bias_new: float32 [32, 16], replicated
- bias_first_new: float32 [32, 16], replicated
- bias_second_new: float32 [32, 16], replicated
- projections_copy: bfloat16 [6, 1024, 1024], P(None, ('dp', 'fsdp'))
- combiners_copy: bfloat16 [2, 1024, 1024], P(None, ('dp', 'fsdp'))
- expansion_copy: bfloat16 [2, 1024, 2816], P(None, ('dp', 'fsdp'))
- contraction_copy: bfloat16 [2816, 1024], P(('dp', 'fsdp'))
Inputs may be any that keep to these rules, and one draw needn't show every extreme that they name: `bucket_table`: nondecreasing in the distance, 0 at distance 0 and 31 at the largest distance. `branch_start`: in every group one branch continues the whole prompt.
All inputs are finite; a program needn't handle non-finite values.
Results may differ from a plain program's by a relative error of at most 0.022.
The roundings to bfloat16 on the way count: a program that leaves them out, or rounds other values in their place, can miss the bound.
Values may be sent and summed in bfloat16 or wider, within the bound.
No kernel may reach another device: no remote copies, remote signals or barrier semaphores. Data moves between devices by JAX's collectives and lax.ppermute only.
A program may use at most 576 MiB of HBM per device.

v0:
```python
import functools

import jax
import jax.numpy as jnp
from jax import lax
from jax.experimental import pallas as pl
from jax.experimental.pallas import tpu as pltpu
from jax.sharding import PartitionSpec as P

D = 1024
FF = 2816
HEADS = 16
HD = 64
BUCKETS = 32
PROMPT = 1024
STEP = 10


EPS = 1e-06
CLIP = 1.0
BETA_ONE = 0.9
BETA_TWO = 0.999
ADAM_EPS = 1e-08
DECAY = 0.01
RATES = (0.05, 0.3, 0.05, 0.03, 1.0, 1.0)
MASKED = -1e30


def rms_forward(stream, gain):
    scale = lax.rsqrt(jnp.mean(stream * stream, axis=-1, keepdims=True) + EPS)
    return (stream * scale * gain, scale)


def rms_backward(stream, scale, gain, upstream):
    weighted = upstream * gain
    grad_in = scale * weighted - stream * scale**3 * jnp.mean(
        weighted * stream, axis=-1, keepdims=True
    )
    return (grad_in, jnp.sum(upstream * stream * scale, axis=0))


def gelu_mix(gate, up_value):
    inner = 0.7978845608028654 * (gate + 0.044715 * gate * gate * gate)
    return 0.5 * gate * (1.0 + jnp.tanh(inner)) * up_value


def raw_scores(queries, key_rows):
    qh = queries.reshape(queries.shape[0], HEADS, HD)
    kh = key_rows.reshape(key_rows.shape[0], HEADS, HD)
    return jnp.einsum("rhd,khd->hrk", qh, kh, preferred_element_type=jnp.float32) * HD ** (-0.5)


def softmax_forward(scores, value_rows):
    row_max = jnp.max(scores, axis=-1, keepdims=True)
    expo = jnp.exp(scores - row_max)
    total = jnp.sum(expo, axis=-1, keepdims=True)
    probs = (expo / total).astype(jnp.bfloat16)
    vh = value_rows.reshape(value_rows.shape[0], HEADS, HD)
    mixed = jnp.einsum("hrk,khd->rhd", probs, vh, preferred_element_type=jnp.float32)
    return (mixed.reshape(mixed.shape[0], D).astype(jnp.bfloat16), row_max + jnp.log(total))


def softmax_backward(scores, logsum, queries, key_rows, value_rows, grad_mixed):
    probs = jnp.exp(scores - logsum)
    grad_heads = grad_mixed.reshape(grad_mixed.shape[0], HEADS, HD)
    vh = value_rows.reshape(value_rows.shape[0], HEADS, HD)
    kh = key_rows.reshape(key_rows.shape[0], HEADS, HD)
    qh = queries.reshape(queries.shape[0], HEADS, HD)
    grad_values = jnp.einsum(
        "hrk,rhd->khd", probs.astype(jnp.bfloat16), grad_heads, preferred_element_type=jnp.float32
    )
    grad_probs = jnp.einsum("rhd,khd->hrk", grad_heads, vh, preferred_element_type=jnp.float32)
    grad_scores = probs * (grad_probs - jnp.sum(probs * grad_probs, axis=-1, keepdims=True))
    scaled = (grad_scores * HD ** (-0.5)).astype(jnp.bfloat16)
    grad_queries = jnp.einsum("hrk,khd->rhd", scaled, kh, preferred_element_type=jnp.float32)
    grad_keys = jnp.einsum("hrk,rhd->khd", scaled, qh, preferred_element_type=jnp.float32)
    return (
        grad_queries.reshape(-1, D),
        grad_keys.reshape(-1, D),
        grad_values.reshape(-1, D),
        grad_scores,
    )


def hankel_bias(per_distance, shift, rows, keys):
    heads = per_distance.shape[0]
    front = jnp.broadcast_to(per_distance[:, :1], (heads, keys - 1))
    padded = jnp.concatenate([front, per_distance], axis=1)
    width = rows + keys - 1
    window = lax.dynamic_slice_in_dim(padded, shift, width, 1)
    tiled = jnp.tile(window, (1, rows + 1))[:, : rows * (width + 1)]
    skewed = tiled.reshape(heads, rows, width + 1)[:, :, :keys]
    return jnp.flip(skewed, axis=2)


def distance_grads(grad_block, shift, dist_count):
    heads, rows, keys = grad_block.shape
    width = rows + keys - 1
    flipped = jnp.flip(grad_block, axis=2)
    widened = jnp.concatenate(
        [flipped, jnp.zeros((heads, rows, width + 1 - keys), jnp.float32)], axis=2
    )
    flat = jnp.concatenate(
        [widened.reshape(heads, rows * (width + 1)), jnp.zeros((heads, keys - 1), jnp.float32)],
        axis=1,
    )
    window = jnp.sum(flat.reshape(heads, rows + 1, width), axis=1)
    padded = lax.dynamic_update_slice_in_dim(
        jnp.zeros((heads, dist_count + keys - 1), jnp.float32), window, shift, 1
    )
    head_part = jnp.sum(padded[:, :keys], axis=1, keepdims=True)
    return jnp.concatenate([head_part, padded[:, keys:]], axis=1)


def adam(weight, first, second, grad, rate):
    first_new = BETA_ONE * first + (1.0 - BETA_ONE) * grad
    second_new = BETA_TWO * second + (1.0 - BETA_TWO) * grad * grad
    mean_hat = first_new / (1.0 - BETA_ONE**STEP)
    square_hat = second_new / (1.0 - BETA_TWO**STEP)
    updated = weight - rate * (mean_hat / (jnp.sqrt(square_hat) + ADAM_EPS) + DECAY * weight)
    return (updated, first_new, second_new)


def body(
    prompt_states,
    branch_states,
    encoder_states,
    branch_start,
    bucket_table,
    prompt_cotangent,
    branch_cotangent,
    projections,
    projections_first,
    projections_second,
    combiners,
    combiners_first,
    combiners_second,
    expansion,
    expansion_first,
    expansion_second,
    contraction,
    contraction_first,
    contraction_second,
    norm_gains,
    gains_first,
    gains_second,
    position_bias,
    bias_first,
    bias_second,
):
    rows_here = prompt_states.shape[1]
    branch_count = branch_states.shape[1]
    branch_size = branch_states.shape[2]
    branch_rows = branch_count * branch_size
    dist_count = bucket_table.shape[0]
    offset = lax.axis_index("fsdp") * rows_here
    local_rows = jnp.arange(rows_here, dtype=jnp.int32)
    steps_in = jnp.arange(branch_size, dtype=jnp.int32)
    bucket_ids = jnp.arange(BUCKETS, dtype=jnp.int32)
    bucket_onehot = (bucket_table[:, None] == bucket_ids[None, :]).astype(jnp.float32)
    per_distance = jnp.dot(bucket_onehot, position_bias, precision=lax.Precision.HIGHEST).T
    own_bias = hankel_bias(per_distance, 0, branch_size, branch_size)
    shards = (
        projections.astype(jnp.bfloat16),
        combiners.astype(jnp.bfloat16),
        expansion.astype(jnp.bfloat16),
        contraction.astype(jnp.bfloat16),
    )

    def layout(starts):
        branch_pos = (starts[:, None] + steps_in[None, :]).reshape(-1)
        branch_seg = jnp.arange(branch_rows, dtype=jnp.int32) // branch_size
        query_pos = jnp.concatenate([offset + local_rows, branch_pos])
        query_seg = jnp.concatenate([jnp.full((rows_here,), -1, jnp.int32), branch_seg])
        query_limit = jnp.concatenate(
            [
                jnp.zeros((rows_here,), jnp.int32),
                jnp.broadcast_to(starts[:, None], (branch_count, branch_size)).reshape(-1),
            ]
        )
        key_pos = jnp.concatenate([jnp.arange(PROMPT, dtype=jnp.int32), branch_pos])
        key_seg = jnp.concatenate([jnp.full((PROMPT,), -1, jnp.int32), branch_seg])
        same_seg = (key_seg[None, :] == query_seg[:, None]) & (
            key_pos[None, :] <= query_pos[:, None]
        )
        from_prompt = (key_seg[None, :] == -1) & (key_pos[None, :] < query_limit[:, None])
        return same_seg | from_prompt

    def build_bias(starts):
        prompt_block = hankel_bias(per_distance, offset, rows_here, PROMPT)
        upper = jnp.concatenate(
            [prompt_block, jnp.zeros((HEADS, rows_here, branch_rows), jnp.float32)], axis=2
        )

        def branch_block(start):
            return hankel_bias(per_distance, start, branch_size, PROMPT)

        cross_blocks = lax.map(branch_block, starts)
        cross_blocks = jnp.transpose(cross_blocks, (1, 0, 2, 3)).reshape(HEADS, branch_rows, PROMPT)
        lower = jnp.concatenate(
            [cross_blocks, jnp.tile(own_bias, (1, branch_count, branch_count))], axis=2
        )
        return jnp.concatenate([upper, lower], axis=1)

    def bias_gradient(grad_scores, starts):
        total = distance_grads(grad_scores[:, :rows_here, :PROMPT], offset, dist_count)

        def add_branch(index, running):
            begin = rows_here + index * branch_size
            rows_block = lax.dynamic_slice_in_dim(grad_scores, begin, branch_size, 1)
            running = running + distance_grads(rows_block[:, :, :PROMPT], starts[index], dist_count)
            own_block = lax.dynamic_slice_in_dim(
                rows_block, PROMPT + index * branch_size, branch_size, 2
            )
            return running + distance_grads(own_block, 0, dist_count)

        total = lax.fori_loop(0, branch_count, add_branch, total)
        return jnp.dot(total, bucket_onehot, precision=lax.Precision.HIGHEST).T

    def group_step(running, item):
        big_sum, gain_sum, bias_sum = running
        prompt, branches, encoder, starts, prompt_cot, branch_cot = item
        weights = (
            lax.all_gather(shards[0], ("dp", "fsdp"), axis=1, tiled=True),
            lax.all_gather(shards[1], ("dp", "fsdp"), axis=1, tiled=True),
            lax.all_gather(shards[2], ("dp", "fsdp"), axis=1, tiled=True),
            lax.all_gather(shards[3], ("dp", "fsdp"), axis=0, tiled=True),
        )
        w_proj, w_comb, w_exp, w_con = weights
        pair_mask = layout(starts)
        stream = jnp.concatenate(
            [prompt.astype(jnp.float32), branches.reshape(-1, D).astype(jnp.float32)], axis=0
        )
        normed_one, scale_one = rms_forward(stream, norm_gains[0])
        input_one = normed_one.astype(jnp.bfloat16)
        self_rows = jnp.einsum(
            "td,kde->kte", input_one, w_proj[:3], preferred_element_type=jnp.float32
        ).astype(jnp.bfloat16)
        prompt_keys, prompt_values = (
            lax.all_gather(self_rows[1, :rows_here], "fsdp", axis=0, tiled=True),
            lax.all_gather(self_rows[2, :rows_here], "fsdp", axis=0, tiled=True),
        )
        encoder_rows = jnp.einsum(
            "td,kde->kte", encoder, w_proj[4:], preferred_element_type=jnp.float32
        ).astype(jnp.bfloat16)
        cross_keys, cross_values = (
            lax.all_gather(encoder_rows[0], "fsdp", axis=0, tiled=True),
            lax.all_gather(encoder_rows[1], "fsdp", axis=0, tiled=True),
        )
        key_rows = jnp.concatenate([prompt_keys, self_rows[1, rows_here:]], axis=0)
        value_rows = jnp.concatenate([prompt_values, self_rows[2, rows_here:]], axis=0)
        pair_bias = build_bias(starts)
        scores_one = jnp.where(
            pair_mask[None], raw_scores(self_rows[0], key_rows) + pair_bias, MASKED
        )
        mixed_one, logsum_one = softmax_forward(scores_one, value_rows)
        after_one = stream + jnp.dot(mixed_one, w_comb[0], preferred_element_type=jnp.float32)
        normed_two, scale_two = rms_forward(after_one, norm_gains[1])
        input_two = normed_two.astype(jnp.bfloat16)
        query_two = jnp.dot(input_two, w_proj[3], preferred_element_type=jnp.float32).astype(
            jnp.bfloat16
        )
        scores_two = raw_scores(query_two, cross_keys)
        mixed_two, logsum_two = softmax_forward(scores_two, cross_values)
        after_two = after_one + jnp.dot(mixed_two, w_comb[1], preferred_element_type=jnp.float32)
        normed_three, scale_three = rms_forward(after_two, norm_gains[2])
        input_three = normed_three.astype(jnp.bfloat16)
        gate_up = jnp.einsum("td,kdf->ktf", input_three, w_exp, preferred_element_type=jnp.float32)
        hidden, mix_pull = jax.vjp(gelu_mix, gate_up[0], gate_up[1])
        hidden_low = hidden.astype(jnp.bfloat16)
        output = after_two + jnp.dot(hidden_low, w_con, preferred_element_type=jnp.float32)
        again = (
            lax.all_gather(shards[0], ("dp", "fsdp"), axis=1, tiled=True),
            lax.all_gather(shards[1], ("dp", "fsdp"), axis=1, tiled=True),
            lax.all_gather(shards[2], ("dp", "fsdp"), axis=1, tiled=True),
            lax.all_gather(shards[3], ("dp", "fsdp"), axis=0, tiled=True),
        )
        b_proj, b_comb, b_exp, b_con = again
        upstream = jnp.concatenate(
            [prompt_cot.astype(jnp.float32), branch_cot.reshape(-1, D).astype(jnp.float32)], axis=0
        )
        upstream_low = upstream.astype(jnp.bfloat16)
        grad_con = jnp.einsum(
            "tf,td->fd", hidden_low, upstream_low, preferred_element_type=jnp.float32
        )
        grad_hidden = jnp.einsum(
            "td,fd->tf", upstream_low, b_con, preferred_element_type=jnp.float32
        )
        grad_gate, grad_up = mix_pull(grad_hidden)
        gate_low = jnp.stack([grad_gate, grad_up]).astype(jnp.bfloat16)
        grad_exp = jnp.einsum(
            "td,ktf->kdf", input_three, gate_low, preferred_element_type=jnp.float32
        )
        grad_three = jnp.einsum("ktf,kdf->td", gate_low, b_exp, preferred_element_type=jnp.float32)
        back_three, gain_three = rms_backward(after_two, scale_three, norm_gains[2], grad_three)
        grad_after_two = upstream + back_three
        cross_low = grad_after_two.astype(jnp.bfloat16)
        grad_comb_two = jnp.einsum(
            "te,td->ed", mixed_two, cross_low, preferred_element_type=jnp.float32
        )
        grad_mixed_two = jnp.einsum(
            "td,ed->te", cross_low, b_comb[1], preferred_element_type=jnp.float32
        ).astype(jnp.bfloat16)
        grad_query_two, grad_keys_two, grad_values_two, unused_scores = softmax_backward(
            scores_two, logsum_two, query_two, cross_keys, cross_values, grad_mixed_two
        )
        own_keys, own_values = (
            lax.psum_scatter(
                grad_keys_two.astype(jnp.bfloat16), "fsdp", scatter_dimension=0, tiled=True
            ).astype(jnp.float32),
            lax.psum_scatter(
                grad_values_two.astype(jnp.bfloat16), "fsdp", scatter_dimension=0, tiled=True
            ).astype(jnp.float32),
        )
        encoder_low = jnp.stack([own_keys, own_values]).astype(jnp.bfloat16)
        grad_cross_proj = jnp.einsum(
            "td,kte->kde", encoder, encoder_low, preferred_element_type=jnp.float32
        )
        encoder_grad = jnp.einsum(
            "kte,kde->td", encoder_low, b_proj[4:], preferred_element_type=jnp.float32
        )
        query_two_low = grad_query_two.astype(jnp.bfloat16)
        grad_query_proj = jnp.einsum(
            "td,te->de", input_two, query_two_low, preferred_element_type=jnp.float32
        )
        grad_two = jnp.einsum(
            "te,de->td", query_two_low, b_proj[3], preferred_element_type=jnp.float32
        )
        back_two, gain_two = rms_backward(after_one, scale_two, norm_gains[1], grad_two)
        grad_after_one = grad_after_two + back_two
        self_low = grad_after_one.astype(jnp.bfloat16)
        grad_comb_one = jnp.einsum(
            "te,td->ed", mixed_one, self_low, preferred_element_type=jnp.float32
        )
        grad_mixed_one = jnp.einsum(
            "td,ed->te", self_low, b_comb[0], preferred_element_type=jnp.float32
        ).astype(jnp.bfloat16)
        grad_query, grad_keys, grad_values, grad_scores = softmax_backward(
            scores_one, logsum_one, self_rows[0], key_rows, value_rows, grad_mixed_one
        )
        prompt_key_grad, prompt_value_grad = (
            lax.psum_scatter(
                grad_keys[:PROMPT].astype(jnp.bfloat16), "fsdp", scatter_dimension=0, tiled=True
            ).astype(jnp.float32),
            lax.psum_scatter(
                grad_values[:PROMPT].astype(jnp.bfloat16), "fsdp", scatter_dimension=0, tiled=True
            ).astype(jnp.float32),
        )
        self_grad_low = jnp.stack(
            [
                grad_query,
                jnp.concatenate([prompt_key_grad, grad_keys[PROMPT:]], axis=0),
                jnp.concatenate([prompt_value_grad, grad_values[PROMPT:]], axis=0),
            ]
        ).astype(jnp.bfloat16)
        grad_self_proj = jnp.einsum(
            "td,kte->kde", input_one, self_grad_low, preferred_element_type=jnp.float32
        )
        grad_one = jnp.einsum(
            "kte,kde->td", self_grad_low, b_proj[:3], preferred_element_type=jnp.float32
        )
        back_one, gain_one = rms_backward(stream, scale_one, norm_gains[0], grad_one)
        stream_grad = grad_after_one + back_one
        grad_bias = bias_gradient(grad_scores, starts)
        group_big = (
            jnp.concatenate([grad_self_proj, grad_query_proj[None], grad_cross_proj], axis=0),
            jnp.stack([grad_comb_one, grad_comb_two]),
            grad_exp,
            grad_con,
        )
        big_sum = jax.tree.map(jnp.add, big_sum, group_big)
        gain_sum = gain_sum + jnp.stack([gain_one, gain_two, gain_three])
        bias_sum = bias_sum + grad_bias
        results = (
            output[:rows_here].astype(jnp.bfloat16),
            output[rows_here:].reshape(branch_count, branch_size, D).astype(jnp.bfloat16),
            stream_grad[:rows_here],
            stream_grad[rows_here:].reshape(branch_count, branch_size, D),
            encoder_grad,
        )
        return ((big_sum, gain_sum, bias_sum), results)

    big_start = (
        jnp.zeros((6, D, D), jnp.float32),
        jnp.zeros((2, D, D), jnp.float32),
        jnp.zeros((2, D, FF), jnp.float32),
        jnp.zeros((FF, D), jnp.float32),
    )
    start_state = (
        big_start,
        jnp.zeros(norm_gains.shape, jnp.float32),
        jnp.zeros(position_bias.shape, jnp.float32),
    )
    final_state, results = lax.scan(
        group_step,
        start_state,
        (
            prompt_states,
            branch_states,
            encoder_states,
            branch_start,
            prompt_cotangent,
            branch_cotangent,
        ),
    )
    big_sum, gain_sum, bias_sum = final_state
    owned = (
        lax.psum_scatter(big_sum[0], ("dp", "fsdp"), scatter_dimension=1, tiled=True),
        lax.psum_scatter(big_sum[1], ("dp", "fsdp"), scatter_dimension=1, tiled=True),
        lax.psum_scatter(big_sum[2], ("dp", "fsdp"), scatter_dimension=1, tiled=True),
        lax.psum_scatter(big_sum[3], ("dp", "fsdp"), scatter_dimension=0, tiled=True),
    )
    squares = sum((jnp.sum(grad * grad) for grad in owned))
    gain_total, bias_total, square_total = lax.psum((gain_sum, bias_sum, squares), ("dp", "fsdp"))
    grad_norm = jnp.sqrt(
        square_total + jnp.sum(gain_total * gain_total) + jnp.sum(bias_total * bias_total)
    )
    factor = jnp.minimum(1.0, CLIP / (grad_norm + 1e-06))
    params = (projections, combiners, expansion, contraction, norm_gains, position_bias)
    firsts = (
        projections_first,
        combiners_first,
        expansion_first,
        contraction_first,
        gains_first,
        bias_first,
    )
    seconds = (
        projections_second,
        combiners_second,
        expansion_second,
        contraction_second,
        gains_second,
        bias_second,
    )
    grads = (owned[0], owned[1], owned[2], owned[3], gain_total, bias_total)
    states = [
        adam(params[index], firsts[index], seconds[index], grads[index] * factor, RATES[index])
        for index in range(6)
    ]
    return (
        results[0],
        results[1],
        results[2],
        results[3],
        results[4],
        grad_norm,
        states[0][0],
        states[0][1],
        states[0][2],
        states[1][0],
        states[1][1],
        states[1][2],
        states[2][0],
        states[2][1],
        states[2][2],
        states[3][0],
        states[3][1],
        states[3][2],
        states[4][0],
        states[4][1],
        states[4][2],
        states[5][0],
        states[5][1],
        states[5][2],
        states[0][0].astype(jnp.bfloat16),
        states[1][0].astype(jnp.bfloat16),
        states[2][0].astype(jnp.bfloat16),
        states[3][0].astype(jnp.bfloat16),
    )


BF = jnp.bfloat16
F32 = jnp.float32
PAIR = 2 * HD
PAIRS = HEADS // 2
TILE = 256


def params(limit=60):
    return pltpu.CompilerParams(vmem_limit_bytes=limit * 1024 * 1024)


def cost(microseconds):
    return pl.CostEstimate(flops=int(microseconds), bytes_accessed=1, transcendentals=0)


def dot(left, right, contract):
    return lax.dot_general(
        left, right, ((contract[:1], contract[1:]), ((), ())), preferred_element_type=F32
    )


def bias_rows(flipped, starts, prompt, size):
    base = jnp.pad(flipped[:, size - 1:], ((0, 0), (0, TILE - 1)), constant_values=MASKED)
    padded = jnp.pad(flipped, ((0, 0), (1, prompt)))
    rows = [
        lax.dynamic_slice_in_dim(padded, prompt - starts[index], prompt + size, 1) for index in range(2)
    ]
    return base[:, None], jnp.stack(rows, axis=1)[:, :, None]


def fill_bias(prompt, size, starts_ref, base, branches, strip_ref, cross_ref):
    wide = jnp.broadcast_to(base, (TILE, prompt + TILE))
    strip_ref[...] = pltpu.roll(wide, 0, 1, stride=1, stride_axis=0)[:, TILE:]
    place = lax.broadcasted_iota(jnp.int32, (size, prompt), 1)
    for index, branch in enumerate(branches):
        row = jnp.broadcast_to(branch, (size, prompt + size))
        skewed = pltpu.roll(row, 0, 1, stride=1, stride_axis=0)[:, size:]
        cross_ref[index * size:(index + 1) * size] = jnp.where(place < starts_ref[index], skewed, MASKED)


def lanes_of(value, half):
    lane = lax.broadcasted_iota(jnp.int32, value.shape, 1)
    return jnp.where((lane >= HD) if half else (lane < HD), value, jnp.zeros_like(value))


def probs_width(prompt, size):
    blocks = prompt // TILE
    return TILE * blocks * (blocks + 1) // 2 + prompt + size


def fold(grid):
    rows, width = grid.shape
    while rows > 1:
        rows //= 2
        grid = grid[:rows] + pltpu.roll(grid[rows:], width - rows, 1)
    return grid


def self_kernel(prompt, size, more, starts_ref, q_ref, k_ref, v_ref, base_ref, branch_ref, *refs):
    o_ref, e_ref, inv_ref, s_ref, strips_ref, crosses_ref = refs[more:]
    blocks = prompt // TILE
    begins = [TILE * i * (i + 1) // 2 for i in range(blocks + 1)]
    lane = lax.broadcasted_iota(jnp.int32, (TILE, PAIR), 1)
    for half in range(2):
        strip_ref, cross_ref = strips_ref.at[half], crosses_ref.at[half]
        branches = [branch_ref[half, index] for index in range(2)]
        fill_bias(prompt, size, starts_ref, base_ref[half], branches, strip_ref, cross_ref)
        for i in range(blocks + 1):
            rows = slice(i * TILE, (i + 1) * TILE)
            q = lanes_of(q_ref[rows] * BF(HD ** -0.5), half)
            tiles = []
            for j in range(min(i + 1, blocks)):
                keys = slice(j * TILE, (j + 1) * TILE)
                begin = prompt - (i + 1 - j) * TILE
                bias = strip_ref.at[:, begin:begin + TILE] if i < blocks else cross_ref.at[:, keys]
                tiles.append((keys, bias))
            top = None
            for j, (keys, bias) in enumerate(tiles):
                s = dot(q, k_ref[keys], (1, 1)) + bias[...]
                s_ref[:, j * TILE:(j + 1) * TILE] = s
                high = jnp.maximum(s[:, :PAIR], s[:, PAIR:])
                top = high if top is None else jnp.maximum(top, high)
            if i == blocks:
                near = strip_ref[:size, prompt - TILE:prompt - TILE + size]
                own = jnp.concatenate(
                    [
                        dot(q[b * size:(b + 1) * size], k_ref[prompt + b * size:prompt + (b + 1) * size], (1, 1)) + near
                        for b in range(2)
                    ],
                    axis=0,
                )
                top = jnp.maximum(top, own)
            top = jnp.max(top, axis=1, keepdims=True)
            total = None
            out = None
            for j, (keys, _) in enumerate(tiles):
                e = jnp.exp(s_ref[:, j * TILE:(j + 1) * TILE] - top)
                part = e[:, :PAIR] + e[:, PAIR:]
                total = part if total is None else total + part
                low = e.astype(BF)
                e_ref[half, :, begins[i] + j * TILE:begins[i] + (j + 1) * TILE] = low
                part = dot(low, v_ref[keys], (1, 0))
                out = part if out is None else out + part
            if i == blocks:
                e = jnp.exp(own - top)
                total = total + e
                low = e.astype(BF)
                e_ref[half, :, begins[i] + prompt:] = low
                out = out + jnp.concatenate(
                    [
                        dot(low[b * size:(b + 1) * size], v_ref[prompt + b * size:prompt + (b + 1) * size], (1, 0))
                        for b in range(2)
                    ],
                    axis=0,
                )
            inverse = 1.0 / jnp.sum(total, axis=1, keepdims=True)
            out = out * inverse
            if half == 0:
                o_ref[rows] = out.astype(BF)
                inv_ref[rows] = jnp.broadcast_to(inverse, (TILE, PAIR))
            else:
                o_ref[rows] = jnp.where(lane >= HD, out.astype(BF), o_ref[rows])
                inv_ref[rows] = jnp.where(lane >= HD, inverse, inv_ref[rows])


def self_forward(qkv, base, branch, starts, prompt, size, first, pairs, before=None):
    count = prompt + 2 * size
    width = probs_width(prompt, size)
    column = lambda part: pl.BlockSpec((None, count, PAIR), lambda j, s, part=part: (part, 0, first + j))
    flat = pl.BlockSpec((count, PAIR), lambda j, s: (0, first + j))
    bias = pltpu.VMEM((2, TILE, prompt), F32)
    more = [] if before is None else list(before)
    return pl.pallas_call(
        functools.partial(self_kernel, prompt, size, len(more)),
        grid_spec=pltpu.PrefetchScalarGridSpec(
            num_scalar_prefetch=1,
            grid=(pairs,),
            in_specs=[
                column(0),
                column(1),
                column(2),
                pl.BlockSpec((2, 1, prompt + TILE), lambda j, s: (first + j, 0, 0)),
                pl.BlockSpec((2, 2, 1, prompt + size), lambda j, s: (first + j, 0, 0, 0)),
            ]
            + [pl.BlockSpec(memory_space=pl.ANY)] * len(more),
            out_specs=[flat, pl.BlockSpec((2, TILE, width), lambda j, s: (first + j, 0, 0)), flat],
            scratch_shapes=[pltpu.VMEM((TILE, prompt), F32), bias, bias],
        ),
        out_shape=[
            jax.ShapeDtypeStruct((count, D), BF),
            jax.ShapeDtypeStruct((HEADS, TILE, width), BF),
            jax.ShapeDtypeStruct((count, D), F32),
        ],
        input_output_aliases={6 + index: index for index in range(len(more))},
        compiler_params=params(),
        cost_estimate=cost(6 * pairs),
        name="self_forward",
    )(starts, qkv, qkv, qkv, base, branch, *more)


def self_back_kernel(prompt, size, q_ref, k_ref, v_ref, do_ref, o_ref, e_ref, inv_ref, dq_ref, dk_ref, dv_ref,
                     strip_ref, cross_ref, sums, far_sums, dk_acc, dv_acc):
    blocks = prompt // TILE
    begins = [TILE * i * (i + 1) // 2 for i in range(blocks + 1)]
    scale = BF(HD ** -0.5)
    lane = lax.broadcasted_iota(jnp.int32, (TILE, PAIR), 1)
    dk_acc[...] = jnp.zeros_like(dk_acc)
    dv_acc[...] = jnp.zeros_like(dv_acc)
    for half in range(2):
        sums[...] = jnp.zeros_like(sums)

        def gather(left, grads, keys, acc):
            acc[half * HD:(half + 1) * HD, keys] += dot(grads[half * HD:(half + 1) * HD], left, (1, 0))

        for i in range(blocks + 1):
            rows = slice(i * TILE, (i + 1) * TILE)
            scaled = do_ref[rows].astype(F32) * inv_ref[rows]
            do = lanes_of(scaled.astype(BF), half)
            part = lanes_of(do.astype(F32) * o_ref[rows].astype(F32), half)
            drop = jnp.sum(part, axis=1, keepdims=True)
            do_left, q_left = do.T, (q_ref[rows] * scale).T
            dq = None
            for j in range(min(i + 1, blocks)):
                keys = slice(j * TILE, (j + 1) * TILE)
                low = e_ref[half, :, begins[i] + j * TILE:begins[i] + (j + 1) * TILE]
                ds = low.astype(F32) * (dot(do, v_ref[keys], (1, 1)) - drop)
                if i < blocks:
                    begin = TILE + prompt - (i + 1 - j) * TILE
                    sums[:, begin:begin + TILE] += ds
                else:
                    far_sums[:, size + j * TILE:size + (j + 1) * TILE] = ds
                down = ds.astype(BF)
                part = dot(down, k_ref[keys], (1, 0))
                dq = part if dq is None else dq + part
                gather(down, q_left, keys, dk_acc)
                gather(low, do_left, keys, dv_acc)
            if i == blocks:
                low = e_ref[half, :, begins[i] + prompt:]
                parts = [slice(b * size, (b + 1) * size) for b in range(2)]
                keys = [slice(prompt + b * size, prompt + (b + 1) * size) for b in range(2)]
                own = jnp.concatenate([dot(do[parts[b]], v_ref[keys[b]], (1, 1)) for b in range(2)], axis=0)
                ds = low.astype(F32) * (own - drop)
                sums[:size, prompt:prompt + size] += ds[:size] + ds[size:]
                down = ds.astype(BF)
                dq = dq + jnp.concatenate(
                    [dot(down[parts[b]], k_ref[keys[b]], (1, 0)) for b in range(2)], axis=0
                )
                for b in range(2):
                    gather(down[parts[b]], q_left[:, parts[b]], keys[b], dk_acc)
                    gather(low[parts[b]], do_left[:, parts[b]], keys[b], dv_acc)
            dq = (dq * (HD ** -0.5)).astype(BF)
            dq_ref[rows] = dq if half == 0 else jnp.where(lane >= HD, dq, dq_ref[rows])
        strip_ref[half] = fold(sums[...])
        for b in range(2):
            wide = far_sums[b * size:(b + 1) * size]
            place = lax.broadcasted_iota(jnp.int32, wide.shape, 1)
            cross_ref[half, b] = fold(jnp.where(place < size, 0.0, wide))
    dk_ref[...] = dk_acc[...].T.astype(BF)
    dv_ref[...] = dv_acc[...].T.astype(BF)


def self_backward(qkv, do, mixed, expos, inverse, prompt, size, first, pairs):
    count = prompt + 2 * size
    width = probs_width(prompt, size)
    column = lambda part: pl.BlockSpec((None, count, PAIR), lambda j, part=part: (part, 0, first + j))
    flat = pl.BlockSpec((count, PAIR), lambda j: (0, j))
    given = pl.BlockSpec((count, PAIR), lambda j: (0, first + j))
    acc = pltpu.VMEM((PAIR, count), F32)
    return pl.pallas_call(
        functools.partial(self_back_kernel, prompt, size),
        grid=(pairs,),
        in_specs=[
            column(0),
            column(1),
            column(2),
            given,
            given,
            pl.BlockSpec((2, TILE, width), lambda j: (first + j, 0, 0)),
            given,
        ],
        out_specs=[
            flat,
            flat,
            flat,
            pl.BlockSpec((2, 1, prompt + TILE), lambda j: (j, 0, 0)),
            pl.BlockSpec((2, 2, 1, prompt + size), lambda j: (j, 0, 0, 0)),
        ],
        out_shape=[
            jax.ShapeDtypeStruct((count, pairs * PAIR), BF),
            jax.ShapeDtypeStruct((count, pairs * PAIR), BF),
            jax.ShapeDtypeStruct((count, pairs * PAIR), BF),
            jax.ShapeDtypeStruct((2 * pairs, 1, prompt + TILE), F32),
            jax.ShapeDtypeStruct((2 * pairs, 2, 1, prompt + size), F32),
        ],
        scratch_shapes=[pltpu.VMEM((TILE, prompt + TILE), F32), pltpu.VMEM((2 * size, prompt + size), F32), acc, acc],
        compiler_params=params(),
        cost_estimate=cost(8 * pairs),
        name="self_backward",
    )(qkv, qkv, qkv, do, mixed, expos, inverse)


def distance_buckets(flipped, starts, prompt, size):
    bucket_ids = jnp.arange(BUCKETS, dtype=jnp.int32)
    whole = jnp.pad(flipped[size - 1:], (0, TILE - 1), constant_values=-1)
    padded = jnp.pad(flipped, (1, prompt), constant_values=-1)
    rows = [lax.dynamic_slice_in_dim(padded, prompt - starts[index], prompt + size, 0) for index in range(2)]
    order = jnp.concatenate([whole] + rows)
    return (order[:, None] == bucket_ids[None, :]).astype(F32)


def bias_gradient(strip, cross, buckets):
    sums = jnp.concatenate([strip[:, 0], cross[:, 0, 0], cross[:, 1, 0]], axis=1)
    return jnp.dot(sums, buckets, precision=lax.Precision.HIGHEST).T


def mlp_kernel(core_ref, x_ref, a_ref, a_t, dy_ref, wg_ref, wu_ref, wd_ref, out_ref, da_ref, away_ref, keep_ref,
               away_con_ref, keep_con_ref, y_ref, hid, dgate, dup, dwd, sem):
    count = a_ref.shape[0]
    step = pl.program_id(0)

    @pl.when(step == 0)
    def _():
        copy = pltpu.make_async_copy(x_ref, y_ref, sem)
        copy.start()
        da_ref[...] = jnp.zeros_like(da_ref)
        copy.wait()

    slope = 0.7978845608028654
    for i in range(0, count, TILE):
        rows = slice(i, i + TILE)
        g = dot(a_ref[rows], wg_ref[...], (1, 0))
        u = dot(a_ref[rows], wu_ref[...], (1, 0))
        dh = dot(dy_ref[rows], wd_ref[...], (1, 1))
        square = g * g
        th = jnp.tanh(slope * g * (1.0 + 0.044715 * square))
        half = 0.5 + 0.5 * th
        gelu = g * half
        slant = half + (0.5 * slope) * g * (1.0 - th * th) * (1.0 + 0.134145 * square)
        low = (gelu * u).astype(BF)
        dg = (dh * u * slant).astype(BF)
        du = (dh * gelu).astype(BF)
        hid[rows] = low
        dgate[rows] = dg
        dup[rows] = du
        y_ref[rows] += dot(low, wd_ref[...], (1, 0))
        da_ref[rows] += dot(dg, wg_ref[...], (1, 1)) + dot(du, wu_ref[...], (1, 1))
    dwd[pl.ds(pl.multiple_of(step * TILE, TILE), TILE)] = dot(hid[...], dy_ref[...], (0, 0))
    core = core_ref[0]
    for index, grad in enumerate((dgate, dup)):
        blocks = dot(a_t[...], grad[...], (1, 0)).astype(BF).reshape(D // 64, 2, 32, TILE)
        away_ref[index] = jnp.where(core == 0, blocks[:, 1], blocks[:, 0])
        keep_ref[index] = jnp.where(core == 0, blocks[:, 0], blocks[:, 1])

    @pl.when(step == pl.num_programs(0) - 1)
    def _():
        for i in range(0, count, TILE):
            out_ref[i:i + TILE] = y_ref[i:i + TILE].astype(BF)
        pairs, m, _ = keep_con_ref.shape
        for index in range(pairs):
            even = dwd[2 * index * m:(2 * index + 1) * m].astype(BF)
            odd = dwd[(2 * index + 1) * m:(2 * index + 2) * m].astype(BF)
            away_con_ref[index] = jnp.where(core == 0, odd, even)
            keep_con_ref[index] = jnp.where(core == 0, even, odd)


def mlp(core, after_two, inputs, turned, low_up, w_gate, w_up, w_con, owners):
    count = inputs.shape[0]
    hidden = w_gate.shape[1]
    m = hidden // owners
    once = pl.Buffered(1)
    flat = pl.BlockSpec((count, D), lambda t, c: (0, 0), pipeline_mode=once)
    column = pl.BlockSpec((D, TILE), lambda t, c: (0, t))
    row = pl.BlockSpec((TILE, D), lambda t, c: (t, 0))
    shared = pl.BlockSpec((2, D // 64, 32, TILE), lambda t, c: (0, 0, 0, t))
    part = jax.ShapeDtypeStruct((2, D // 64, 32, hidden), BF)
    con = pl.BlockSpec((owners // 2, m, D), lambda t, c: (0, 0, 0), pipeline_mode=once)
    con_part = jax.ShapeDtypeStruct((owners // 2, m, D), BF)
    tile = pltpu.VMEM((count, TILE), BF)
    return pl.pallas_call(
        mlp_kernel,
        grid_spec=pltpu.PrefetchScalarGridSpec(
            num_scalar_prefetch=1,
            grid=(hidden // TILE,),
            in_specs=[pl.BlockSpec(memory_space=pl.ANY), flat, whole_block(turned), flat, column, column, row],
            out_specs=[flat, flat, shared, shared, con, con],
            scratch_shapes=[
                pltpu.VMEM((count, D), F32),
                tile,
                tile,
                tile,
                pltpu.VMEM((hidden, D), F32),
                pltpu.SemaphoreType.DMA,
            ],
        ),
        out_shape=[
            jax.ShapeDtypeStruct((count, D), BF),
            jax.ShapeDtypeStruct((count, D), F32),
            part,
            part,
            con_part,
            con_part,
        ],
        compiler_params=params(),
        cost_estimate=cost(85),
        name="mlp",
    )(core, after_two, inputs, turned, low_up, w_gate, w_up, w_con)


def part_kernel(jobs, counts, plan_ref, *refs):
    lefts = refs[:1 + max(jobs)]
    rights = refs[len(lefts):len(lefts) + sum(counts)]
    rest = refs[len(lefts) + len(rights):]

    def finish(index, value):
        if len(rest) == 1:
            rest[0][index] = value.astype(BF).reshape(rest[0].shape[1:])
        else:
            got, away, stay, held = rest
            held[...] = (value + got[index].astype(F32).reshape(value.shape)).astype(BF).reshape(held.shape)
            for slot in range(2):
                away[slot, :, index] = held[:, plan_ref[1 + slot]]
                stay[slot, :, index] = held[:, plan_ref[3 + slot]]

    first = 0
    for index, left in enumerate(jobs):
        if counts[index] == 1:
            finish(index, dot(lefts[left][...], rights[first][...], (1, 0)))
        else:
            for tile in range(counts[index]):
                @pl.when(pl.program_id(0) == tile)
                def _(index=index, left=left, right=rights[first + tile]):
                    finish(index, dot(lefts[left][...], right[...], (1, 0)))
        first += counts[index]


def weight_part(plan, lefts, jobs, got=None):
    rights = [right if isinstance(right, list) else [right] for _, right in jobs]
    columns = sum(right.shape[1] for right in rights[0])
    counts = [len(right) for right in rights]
    m = 32

    def side(left):
        return pl.BlockSpec((None,) + left.shape[1:], lambda t, p: (p[0], 0, 0), pipeline_mode=pl.Buffered(1))

    def tile(right):
        return pl.BlockSpec((right.shape[0], TILE), lambda t, p: (0, t) if right.shape[1] > TILE else (0, 0))

    shared = pl.BlockSpec((len(jobs), D // 64, m, TILE), lambda t, p: (0, 0, 0, t))
    part = jax.ShapeDtypeStruct((len(jobs), D // 64, m, columns), BF)
    split = pl.BlockSpec((2, LINE, len(jobs), m, TILE), lambda t, p: (0, 0, 0, 0, t))
    half = jax.ShapeDtypeStruct((2, LINE, len(jobs), m, columns), BF)
    return pl.pallas_call(
        functools.partial(part_kernel, [left for left, _ in jobs], counts),
        grid_spec=pltpu.PrefetchScalarGridSpec(
            num_scalar_prefetch=1,
            grid=(columns // TILE,),
            in_specs=[side(left) for left in lefts]
            + [tile(value) for right in rights for value in right]
            + ([] if got is None else [shared]),
            out_specs=shared if got is None else [split, split],
            scratch_shapes=[] if got is None else [pltpu.VMEM((LINE, SIDE * SIDE, m, TILE), BF)],
        ),
        out_shape=part if got is None else [half, half],
        compiler_params=params(),
        cost_estimate=cost(2),
        name="weight_part",
    )(plan, *lefts, *(value for right in rights for value in right), *([] if got is None else [got]))


def root(value):
    return lax.rsqrt(jnp.mean(value * value, axis=1, keepdims=True) + EPS)


def normed(value, gain):
    return (value * root(value) * gain).astype(BF)


def norm_back(value, gain, upstream):
    scale = root(value)
    weighted = upstream * gain
    grad = scale * weighted - value * (scale * scale * scale) * jnp.mean(weighted * value, axis=1, keepdims=True)
    terms = upstream * value * scale
    return grad, jnp.sum(terms.reshape(-1, 8, D), axis=0)


def whole_block(value):
    zeros = (0,) * len(value.shape)
    return pl.BlockSpec(value.shape, lambda *index: zeros, pipeline_mode=pl.Buffered(1))


def row_block(columns=D):
    return pl.BlockSpec((TILE, columns), lambda i: (i, 0))


def turned_block():
    return pl.BlockSpec((D, TILE), lambda i: (0, i))


def sided_block():
    return pl.BlockSpec((2, D // 2, TILE), lambda i: (0, 0, i))


def put_sides(ref, value):
    columns = value.T.reshape(D // 64, 2, 32, value.shape[0])
    for side in range(2):
        ref[side] = columns[:, side].reshape(D // 2, value.shape[0])


def fetch(slots_ref, sources, held, sems, index):
    copies = []
    for number, source in enumerate(sources):
        for half in range(2):
            spot = slots_ref[2 * number + half, 0]
            side = slots_ref[2 * number + half, 1]
            copies.append(
                pltpu.make_async_copy(
                    source.at[half, index], held.at[index, :, spot, side], sems.at[index, 2 * number + half]
                )
            )
    return copies


def held_weight(held, index):
    return held[index].reshape(D, D)


def arrive(slots_ref, sources, held, in_sems, count):
    @pl.when(pl.program_id(0) == 0)
    def _():
        for index in range(count):
            for copy in fetch(slots_ref, sources, held, in_sems, index):
                copy.start()


def ready(slots_ref, sources, held, outs, in_sems, out_sems, index):
    @pl.when(pl.program_id(0) == 0)
    def _():
        for copy in fetch(slots_ref, sources, held, in_sems, index):
            copy.wait()
        pltpu.make_async_copy(held.at[index], outs[index], out_sems.at[index]).start()


def settle(held, outs, out_sems):
    @pl.when(pl.program_id(0) == pl.num_programs(0) - 1)
    def _():
        for index, out in enumerate(outs):
            pltpu.make_async_copy(held.at[index], out, out_sems.at[index]).wait()


def weight_specs(sources):
    _, count, line, rows, columns = sources[0].shape
    shape = (line, SIDE * SIDE, 2, rows, columns)
    anywhere = pl.BlockSpec(memory_space=pl.ANY)
    return (
        [pl.BlockSpec(memory_space=pltpu.SMEM)] + [anywhere] * 4,
        [anywhere] * count,
        [jax.ShapeDtypeStruct(shape, BF)] * count,
        [
            pltpu.VMEM((count,) + shape, BF),
            pltpu.SemaphoreType.DMA((count, 8)),
            pltpu.SemaphoreType.DMA((count,)),
        ],
    )


def enter_kernel(slots_ref, *refs):
    sources = refs[:4]
    x_ref, gain_ref, a_ref, qkv_ref = refs[4:8]
    outs = refs[8:11]
    held, in_sems, out_sems = refs[11:]
    arrive(slots_ref, sources, held, in_sems, 3)
    a = normed(x_ref[...].astype(F32), gain_ref[...])
    put_sides(a_ref, a)
    for index in range(3):
        ready(slots_ref, sources, held, outs, in_sems, out_sems, index)
        qkv_ref[index] = dot(a, held_weight(held, index), (1, 0)).astype(BF)
    settle(held, outs, out_sems)


def enter(stream_low, gain, slots, sources):
    count = stream_low.shape[0]
    weight_ins, weight_outs, weight_shapes, scratch = weight_specs(sources)
    turned, qkv, *weights = pl.pallas_call(
        enter_kernel,
        grid=(count // TILE,),
        in_specs=weight_ins + [row_block(), whole_block(gain)],
        out_specs=[sided_block(), pl.BlockSpec((3, TILE, D), lambda i: (0, i, 0))] + weight_outs,
        out_shape=[jax.ShapeDtypeStruct((2, D // 2, count), BF), jax.ShapeDtypeStruct((3, count, D), BF)] + weight_shapes,
        scratch_shapes=scratch,
        compiler_params=params(),
        cost_estimate=cost(12),
        name="enter",
    )(slots, *sources, stream_low, gain)
    return turned, qkv, [weight.reshape(D, D) for weight in weights]


def middle_kernel(parts, slots_ref, *refs):
    sources = refs[:4]
    x_ref, *mixed_refs = refs[4:5 + parts]
    (gain_two_ref, gain_three_ref, e_ref, x1_ref, x2_ref, a2_ref, a3_ref, q_ref, o_ref, p_ref, kv_ref, a3_t_ref,
     mixed_t_ref, e_t_ref, *outs) = refs[5 + parts:24 + parts]
    held, in_sems, out_sems, o_scr = refs[24 + parts:]
    arrive(slots_ref, sources, held, in_sems, 5)

    def weight(index):
        ready(slots_ref, sources, held, outs, in_sems, out_sems, index)
        return held_weight(held, index)

    for index in range(2):
        w = weight(2 + index)

        @pl.when(pl.program_id(0) == 0)
        def _(index=index, w=w):
            kv_ref[index] = dot(e_ref[...], w, (1, 0)).astype(BF)

    @pl.when(pl.program_id(0) == 0)
    def _():
        put_sides(e_t_ref, e_ref[...])

    w_first = weight(0)
    (mixed_ref,) = mixed_refs
    x1 = x_ref[...].astype(F32) + dot(mixed_ref[...], w_first, (1, 0))
    x1_ref[...] = x1
    a2 = normed(x1, gain_two_ref[...])
    put_sides(mixed_t_ref, mixed_ref[...])
    put_sides(a2_ref, a2)
    q_ref[...] = dot(a2, weight(1), (1, 0)).astype(BF)
    for pair in range(PAIRS):
        columns = slice(pair * PAIR, (pair + 1) * PAIR)
        k = kv_ref[0, :, columns]
        v = kv_ref[1, :, columns]
        mixed = []
        for half in range(2):
            q = lanes_of(q_ref[:, columns] * BF(HD ** -0.5), half)
            s = dot(q, k, (1, 1))
            e = jnp.exp(s - jnp.max(s, axis=1, keepdims=True))
            p = (e * (1.0 / jnp.sum(e, axis=1, keepdims=True))).astype(BF)
            p_ref[2 * pair + half] = p
            mixed.append(dot(p, v, (1, 0)))
        lane = lax.broadcasted_iota(jnp.int32, mixed[0].shape, 1)
        o_scr[:, columns] = jnp.where(lane < HD, mixed[0], mixed[1]).astype(BF)
    put_sides(o_ref, o_scr[...])
    x2 = x1_ref[...] + dot(o_scr[...], weight(4), (1, 0))
    x2_ref[...] = x2
    a3 = normed(x2, gain_three_ref[...])
    a3_ref[...] = a3
    a3_t_ref[...] = a3.T
    settle(held, outs, out_sems)


def middle(stream_low, mixed, gain_two, gain_three, encoder, slots, sources):
    count = stream_low.shape[0]
    enc = encoder.shape[0]
    low = jax.ShapeDtypeStruct((count, D), BF)
    wide = jax.ShapeDtypeStruct((count, D), F32)
    turned = jax.ShapeDtypeStruct((D, count), BF)
    sided = jax.ShapeDtypeStruct((2, D // 2, count), BF)
    weight_ins, weight_outs, weight_shapes, scratch = weight_specs(sources)
    *results, w1, w2, w3, w4, w5 = pl.pallas_call(
        functools.partial(middle_kernel, len(mixed)),
        grid=(count // TILE,),
        in_specs=weight_ins
        + [row_block()]
        + [row_block(part.shape[1]) for part in mixed]
        + [whole_block(value) for value in (gain_two, gain_three, encoder)],
        out_specs=[row_block(), row_block(), sided_block(), row_block(), row_block(), sided_block()]
        + [
            pl.BlockSpec((HEADS, TILE, enc), lambda i: (0, i, 0)),
            pl.BlockSpec((2, enc, D), lambda i: (0, 0, 0)),
            turned_block(),
            sided_block(),
            pl.BlockSpec((2, D // 2, enc), lambda i: (0, 0, 0)),
        ]
        + weight_outs,
        out_shape=[
            wide,
            wide,
            sided,
            low,
            low,
            sided,
            jax.ShapeDtypeStruct((HEADS, count, enc), BF),
            jax.ShapeDtypeStruct((2, enc, D), BF),
            turned,
            sided,
            jax.ShapeDtypeStruct((2, D // 2, enc), BF),
        ]
        + weight_shapes,
        scratch_shapes=scratch + [pltpu.VMEM((TILE, D), BF)],
        compiler_params=params(),
        cost_estimate=cost(30),
        name="middle",
    )(slots, *sources, stream_low, *mixed, gain_two, gain_three, encoder)
    return results + [[weight.reshape(D, D) for weight in (w1, w2, w3, w4, w5)]]


def middle_back_kernel(dy_ref, da3_ref, x2_ref, x1_ref, q_ref, p_ref, kv_ref, gain_two_ref, gain_three_ref, wc_ref, wq_ref,
                       wo_ref, *refs):
    before = refs[:-9]
    low2_ref, dq_ref, dx1_ref, low1_ref, do1_ref, dkv_ref, sums_ref, gains_ref, do_ref = refs[-9:]
    dk_acc, dv_acc = sums_ref.at[0], sums_ref.at[1]
    step = pl.program_id(0)

    @pl.when(step == 0)
    def _():
        sums_ref[...] = before[-2][...] if before else jnp.zeros_like(sums_ref)
        gains_ref[...] = before[-1][...] if before else jnp.zeros_like(gains_ref)

    back, terms = norm_back(x2_ref[...], gain_three_ref[...], da3_ref[...])
    gains_ref[1] += terms
    dx2 = dy_ref[...].astype(F32) + back
    dx1_ref[...] = dx2
    low2 = dx2.astype(BF)
    low2_ref[...] = low2
    do_ref[...] = dot(low2, wo_ref[...], (1, 1)).astype(BF)
    scale = BF(HD ** -0.5)
    for pair in range(PAIRS):
        columns = slice(pair * PAIR, (pair + 1) * PAIR)
        k = kv_ref[0, :, columns] * scale
        v = kv_ref[1, :, columns]
        dq = None
        for half in range(2):
            do = lanes_of(do_ref[:, columns], half)
            q = lanes_of(q_ref[:, columns] * scale, half)
            low = p_ref[2 * pair + half]
            p = low.astype(F32)
            pull = p * dot(do, v, (1, 1))
            down = (pull - p * jnp.sum(pull, axis=1, keepdims=True)).astype(BF)
            part = dot(down, lanes_of(k, half), (1, 0))
            dq = part if dq is None else dq + part
            dk_acc[:, columns] += dot(down, q, (0, 0))
            dv_acc[:, columns] += dot(low, do, (0, 0))
        dq_ref[:, columns] = dq.astype(BF)
    da2 = dot(dq_ref[...], wq_ref[...], (1, 1))
    back, terms = norm_back(x1_ref[...], gain_two_ref[...], da2)
    gains_ref[0] += terms
    dx1 = dx1_ref[...] + back
    dx1_ref[...] = dx1
    low1 = dx1.astype(BF)
    low1_ref[...] = low1
    do1_ref[...] = dot(low1, wc_ref[...], (1, 1)).astype(BF)

    @pl.when(step == pl.num_programs(0) - 1)
    def _():
        dkv_ref[0] = dk_acc[...].astype(BF)
        dkv_ref[1] = dv_acc[...].astype(BF)


def middle_back(first, blocks, low_up, grad_three, after_two, after_one, query_two, probs_two, kv_two, gain_two, gain_three,
                w_comb_one, w_query_two, w_comb_two, before=None):
    count = low_up.shape[0]
    enc = kv_two.shape[1]
    low = jax.ShapeDtypeStruct((count, D), BF)
    wide = jax.ShapeDtypeStruct((count, D), F32)
    rows = pl.BlockSpec((TILE, D), lambda i: (first + i, 0))
    sums = jax.ShapeDtypeStruct((2, enc, D), F32)
    gains = jax.ShapeDtypeStruct((2, 8, D), F32)
    whole = (kv_two, gain_two, gain_three, w_comb_one, w_query_two, w_comb_two)
    operands = (low_up, grad_three, after_two, after_one, query_two, probs_two) + whole
    more = [] if before is None else list(before[:5]) + list(before[6:])
    aliases = {} if before is None else {len(operands) + index: index for index in range(5)}
    return pl.pallas_call(
        middle_back_kernel,
        grid=(blocks,),
        in_specs=[rows] * 5
        + [pl.BlockSpec((HEADS, TILE, enc), lambda i: (0, first + i, 0))]
        + [whole_block(value) for value in whole]
        + ([] if before is None else [pl.BlockSpec(memory_space=pl.ANY)] * 5 + [whole_block(sums), whole_block(gains)]),
        out_specs=[rows] * 5
        + [
            pl.BlockSpec((2, enc, D), lambda i: (0, 0, 0)),
            pl.BlockSpec((2, enc, D), lambda i: (0, 0, 0)),
            pl.BlockSpec((2, 8, D), lambda i: (0, 0, 0)),
        ],
        out_shape=[low, low, wide, low, low, jax.ShapeDtypeStruct((2, enc, D), BF), sums, gains],
        scratch_shapes=[pltpu.VMEM((TILE, D), BF)],
        input_output_aliases=aliases,
        compiler_params=params(),
        cost_estimate=cost(45),
        name="middle_back",
    )(*operands, *more)


def leave_kernel(parts, plan_ref, x_ref, dx1_ref, *refs):
    grads = refs[:3 * parts]
    gain_ref, wq_ref, wk_ref, wv_ref, out_ref, gains_ref = refs[3 * parts:]
    width = D // parts

    @pl.when(pl.program_id(0) == 0)
    def _():
        gains_ref[...] = jnp.zeros_like(gains_ref)

    da = None
    for index in range(parts):
        columns = slice(index * width, (index + 1) * width)
        for which, w_ref in enumerate((wq_ref, wk_ref, wv_ref)):
            part = dot(grads[3 * index + which][...], w_ref[:, columns], (1, 1))
            da = part if da is None else da + part
    back, terms = norm_back(x_ref[...].astype(F32), gain_ref[...], da)
    gains_ref[...] += terms
    out_ref[...] = dx1_ref[...] + back


def leave(plan, blocks, stream_low, grad_after_one, parts, gain, w_query, w_key, w_value):
    weights = (w_query, w_key, w_value)
    flat = [value for part in parts for value in part]

    def rows(value):
        return pl.BlockSpec((TILE, value.shape[1]), lambda i, p: (p[i], 0))

    return pl.pallas_call(
        functools.partial(leave_kernel, len(parts)),
        grid_spec=pltpu.PrefetchScalarGridSpec(
            num_scalar_prefetch=1,
            grid=(blocks,),
            in_specs=[rows(stream_low), rows(grad_after_one)]
            + [rows(value) for value in flat]
            + [whole_block(value) for value in (gain,) + weights],
            out_specs=[pl.BlockSpec((TILE, D), lambda i, p: (i, 0)), pl.BlockSpec((8, D), lambda i, p: (0, 0))],
        ),
        out_shape=[jax.ShapeDtypeStruct((blocks * TILE, D), F32), jax.ShapeDtypeStruct((8, D), F32)],
        compiler_params=params(),
        cost_estimate=cost(2),
        name="leave",
    )(plan, stream_low, grad_after_one, *flat, gain, *weights)


SIDE = 2
LINE = 4
AXES = ("dp", "fsdp")


def place_of(z, y, x, core):
    return ((z * SIDE + y) * SIDE + x) * 2 + core


def moves(rule):
    every = [(z, y, x, c) for z in range(LINE) for y in range(SIDE) for x in range(SIDE) for c in range(2)]
    return [(place_of(*here), place_of(*rule(*here))) for here in every]


def send(value, rule):
    return lax.ppermute(value, AXES, moves(rule))


def along_line(shift):
    return lambda z, y, x, c: ((z + shift) % LINE, y, x, c)


def line_far(z, y, x, c):
    return (z ^ 2, y, x, c)


def line_near(z, y, x, c):
    return (z ^ 1, y, x, c)


def first_flip(z, y, x, c):
    return (z, y, 1 - x, c) if c == 0 else (z, 1 - y, x, c)


def second_flip(z, y, x, c):
    return (z, 1 - y, x, c) if c == 0 else (z, y, 1 - x, c)


def core_flip(z, y, x, c):
    return (z, y, x, 1 - c)


def spots(y, x, core):
    here = y * SIDE + x
    along_x = y * SIDE + 1 - x
    along_y = (1 - y) * SIDE + x
    across = (1 - y) * SIDE + 1 - x
    near = jnp.where(core == 0, along_x, along_y)
    far = jnp.where(core == 0, along_y, along_x)
    return here, near, far, across


def put_kernel(z_ref, shard, far, near, out, sems):
    z = z_ref[0]
    sources = [(shard, z), (far, z ^ 2), (near.at[0], z ^ 1), (near.at[1], z ^ 3)]
    copies = [
        pltpu.make_async_copy(source, out.at[:, slot], sems.at[index])
        for index, (source, slot) in enumerate(sources)
    ]
    for copy in copies:
        copy.start()
    for copy in copies:
        copy.wait()


def put_in_line(shard, far, near, z):
    count, rows, columns = shard.shape
    return pl.pallas_call(
        put_kernel,
        in_specs=[pl.BlockSpec(memory_space=pltpu.SMEM)] + [pl.BlockSpec(memory_space=pl.ANY)] * 3,
        out_specs=pl.BlockSpec(memory_space=pltpu.VMEM),
        out_shape=jax.ShapeDtypeStruct((count, LINE, rows, columns), shard.dtype),
        scratch_shapes=[pltpu.SemaphoreType.DMA((LINE,))],
        compiler_params=params(40),
        cost_estimate=cost(1),
        name="put_in_line",
    )(z[None], shard, far, near)


def assemble_kernel(slots_ref, *refs):
    sources = refs[:4]
    outs, sems = refs[4:-1], refs[-1]
    copies = []
    for index, source in enumerate(sources):
        for half in range(2):
            spot = slots_ref[2 * index + half, 0]
            side = slots_ref[2 * index + half, 1]
            for k, out in enumerate(outs):
                copies.append(
                    pltpu.make_async_copy(source.at[half, k], out.at[:, spot, side], sems.at[len(copies)])
                )
    for copy in copies:
        copy.start()
    for copy in copies:
        copy.wait()


def assemble(sources, slots):
    _, count, line, rows, columns = sources[0].shape
    shape = (line, SIDE * SIDE, 2, rows, columns)
    outs = pl.pallas_call(
        assemble_kernel,
        in_specs=[pl.BlockSpec(memory_space=pltpu.SMEM)] + [pl.BlockSpec(memory_space=pl.ANY)] * 4,
        out_specs=[pl.BlockSpec(memory_space=pltpu.VMEM)] * count,
        out_shape=[jax.ShapeDtypeStruct(shape, sources[0].dtype)] * count,
        scratch_shapes=[pltpu.SemaphoreType.DMA((8 * count,))],
        compiler_params=params(40),
        cost_estimate=cost(2 * count),
        name="assemble",
    )(slots, *sources)
    return [out.reshape(line * SIDE * SIDE * 2 * rows, columns) for out in outs]


def tie(*values):
    return lax.optimization_barrier(values)


def line_stage(shard):
    return [send(shard, along_line(shift)) for shift in range(1, LINE)]


def piece_slots(place):
    _, y, x, core = place
    mine = spots(y, x, core)
    theirs = spots(y, x, 1 - core)
    order = [(mine[0], core), (mine[1], core), (theirs[0], 1 - core), (theirs[1], 1 - core)]
    order += [(mine[2], core), (mine[3], core), (theirs[2], 1 - core), (theirs[3], 1 - core)]
    return jnp.stack([jnp.stack(pair) for pair in order])


def add_split_kernel(spots_ref, one_ref, two_ref, away_ref, stay_ref):
    slot = pl.program_id(0)
    value = one_ref[...] + two_ref[...]

    for out_ref, here in ((away_ref, slot < 2), (stay_ref, slot >= 2)):
        @pl.when(here)
        def _(out_ref=out_ref):
            for index in range(value.shape[0]):
                out_ref[0, :, index] = value[index, :, 0]


def add_split(keep, received, place):
    _, y, x, core = place
    here, near, far, across = spots(y, x, core)
    count, _, rows, columns = keep.shape
    grid = (count, LINE, SIDE * SIDE, rows, columns)
    wide = columns // 2
    source = pl.BlockSpec((count, LINE, 1, rows, wide), lambda j, t, s: (0, 0, s[j], 0, t))
    out = jax.ShapeDtypeStruct((2, LINE, count, rows, columns), BF)
    block = (1, LINE, count, rows, wide)
    return pl.pallas_call(
        add_split_kernel,
        grid_spec=pltpu.PrefetchScalarGridSpec(
            num_scalar_prefetch=1,
            grid=(4, 2),
            in_specs=[source, source],
            out_specs=[
                pl.BlockSpec(block, lambda j, t, s: (jnp.minimum(j, 1), 0, 0, 0, jnp.where(j < 2, t, 1))),
                pl.BlockSpec(block, lambda j, t, s: (jnp.maximum(j - 2, 0), 0, 0, 0, jnp.where(j < 2, 0, t))),
            ],
        ),
        out_shape=[out, out],
        compiler_params=params(),
        cost_estimate=cost(1),
        name="add_split",
    )(jnp.stack([far, across, here, near]), keep.reshape(grid), received.reshape(grid))


def plus(one, two):
    return (one.astype(F32) + two.astype(F32)).astype(BF)


def line_split(line, place):
    z = place[0]

    def at(index):
        return lax.dynamic_index_in_dim(line, index, 0, keepdims=False)

    return (at(z), at(z ^ 2)), jnp.stack([at(z ^ 1), at(z ^ 3)])


def add_in_order(value, received, own, owners):
    total = None
    for index in range(4):
        term = jnp.where(own == index, value, 0.0)
        for part, owner in zip(received, owners):
            term = term + jnp.where(owner == index, part, 0.0)
        total = term if total is None else total + term
    return total


def sum_everywhere(value, place):
    z, y, x, core = place
    parts = [send(value, along_line(shift)) for shift in range(1, LINE)]
    value = add_in_order(value, parts, z, [(z - shift) % LINE for shift in range(1, LINE)])
    flips = [(0, 1), (1, 0), (1, 1)]
    parts = [send(value, lambda z, y, x, c, dy=dy, dx=dx: (z, y ^ dy, x ^ dx, c)) for dy, dx in flips]
    value = add_in_order(
        value, parts, y * SIDE + x, [jnp.bitwise_xor(y, dy) * SIDE + jnp.bitwise_xor(x, dx) for dy, dx in flips]
    )
    return value + send(value, core_flip)


def swap_halves(parts, core):
    def block(index):
        return jnp.concatenate(
            [lax.dynamic_index_in_dim(part, index, 0, keepdims=False).reshape(-1, D) for part in parts], axis=0
        )

    mine = block(core)
    theirs = send(block(1 - core), core_flip)
    first = jnp.where(core == 0, mine, theirs)
    second = jnp.where(core == 0, theirs, mine)
    whole, begin = [], 0
    for part in parts:
        end = begin + part.size // 2 // D
        whole.append(jnp.concatenate([first[begin:end], second[begin:end]], axis=0))
        begin = end
    return whole


def hand_over(parts, core):
    halves = [part.reshape((2, -1, D)) for part in parts]

    def block(index):
        return jnp.concatenate([lax.dynamic_index_in_dim(part, index, 0, keepdims=False) for part in halves], axis=0)

    return block(core), send(block(1 - core), core_flip)


def both_groups(mine, other, core):
    return jnp.stack([jnp.where(core == 0, mine, other), jnp.where(core == 0, other, mine)])


def matmul(left, right):
    return jnp.dot(left, right, preferred_element_type=F32)


def matmul_t(left, right):
    return lax.dot_general(left, right, (((1,), (1,)), ((), ())), preferred_element_type=F32)


def paired_body(
    prompt_states,
    branch_states,
    encoder_states,
    branch_start,
    bucket_table,
    prompt_cotangent,
    branch_cotangent,
    projections,
    projections_first,
    projections_second,
    combiners,
    combiners_first,
    combiners_second,
    expansion,
    expansion_first,
    expansion_second,
    contraction,
    contraction_first,
    contraction_second,
    norm_gains,
    gains_first,
    gains_second,
    position_bias,
    bias_first,
    bias_second,
):
    rows_here = prompt_states.shape[1]
    prompt = 2 * rows_here
    size = branch_states.shape[2]
    place_index = lax.axis_index("dp")
    core = lax.axis_index("fsdp")
    place = (place_index // (SIDE * SIDE), place_index // SIDE % SIDE, place_index % SIDE, core)

    z = place[0]
    core_ref = core[None]

    shard_qkv = projections[:3].astype(BF)
    shard_mid = jnp.concatenate([combiners[:1], projections[3:], combiners[1:]], axis=0).astype(BF)
    shard_exp = expansion.astype(BF)
    shard_con = contraction[None].astype(BF)
    far_line_qkv = send(shard_qkv, line_far)

    other_start = send(lax.dynamic_index_in_dim(branch_start, 1 - core, 0, keepdims=False), core_flip)
    own_start = lax.dynamic_index_in_dim(branch_start, core, 0, keepdims=False)
    starts = jnp.concatenate(
        [jnp.where(core == 0, own_start, other_start), jnp.where(core == 0, other_start, own_start)]
    )
    gain_rows = [norm_gains[index:index + 1] for index in range(3)]

    bucket_ids = jnp.arange(BUCKETS, dtype=jnp.int32)
    flipped_table = jnp.flip(bucket_table)
    flipped_onehot = (flipped_table[:, None] == bucket_ids[None, :]).astype(F32)
    flipped_bias = jnp.dot(flipped_onehot, position_bias, precision=lax.Precision.HIGHEST).T
    buckets = distance_buckets(flipped_table, starts, prompt, size)
    slots = piece_slots(place)

    shard_mid, far_line_qkv, prompt_states, starts = tie(shard_mid, far_line_qkv, prompt_states, starts)
    near_line_qkv = send(jnp.stack([shard_qkv, far_line_qkv]), line_near)
    far_line_mid = send(shard_mid, line_far)
    prompt_rows, branch_rows, prompt_up, branch_up, encoder = swap_halves(
        [prompt_states, branch_states, prompt_cotangent, branch_cotangent, encoder_states], core
    )
    own_qkv = put_in_line(shard_qkv, far_line_qkv, near_line_qkv, z)
    near_qkv = send(own_qkv, first_flip)
    near_qkv, own_qkv, far_line_mid = tie(near_qkv, own_qkv, far_line_mid)
    close_qkv = jnp.stack([own_qkv, near_qkv])
    far_qkv = send(close_qkv, second_flip)
    near_line_mid = send(jnp.stack([shard_mid, far_line_mid]), line_near)
    close_qkv_two = send(close_qkv, core_flip)
    base, branch = bias_rows(flipped_bias, starts, prompt, size)
    stream_low = jnp.concatenate([prompt_rows, branch_rows], axis=0)
    low_up = jnp.concatenate([prompt_up, branch_up], axis=0)
    far_qkv, near_line_mid, close_qkv_two, stream_low, low_up, encoder, base, branch, shard_exp, shard_con = tie(
        far_qkv, near_line_mid, close_qkv_two, stream_low, low_up, encoder, base, branch, shard_exp, shard_con
    )
    far_qkv_two = send(far_qkv, core_flip)
    own_mid = put_in_line(shard_mid, far_line_mid, near_line_mid, z)
    near_mid = send(own_mid, first_flip)
    far_line_exp = send(shard_exp, line_far)
    stream_low, own_mid, far_qkv_two = tie(stream_low, own_mid, far_qkv_two)

    turned_one, qkv, (w_query, w_key, w_value) = enter(
        stream_low, gain_rows[0], slots, [close_qkv, close_qkv_two, far_qkv, far_qkv_two]
    )
    qkv, near_mid, far_line_exp, shard_con = tie(qkv, near_mid, far_line_exp, shard_con)
    close_mid = jnp.stack([own_mid, near_mid])
    far_mid = send(close_mid, second_flip)
    near_line_exp = send(jnp.stack([shard_exp, far_line_exp]), line_near)
    far_line_con = send(shard_con, line_far)
    close_mid_two = send(close_mid, core_flip)
    qkv, close_mid = tie(qkv, close_mid)
    most = 5 * PAIRS // 8
    heads = self_forward(qkv, base, branch, starts, prompt, size, 0, most)
    *heads, qkv, far_mid, close_mid_two, near_line_exp, far_line_con = tie(
        *heads, qkv, far_mid, close_mid_two, near_line_exp, far_line_con
    )
    own_exp = put_in_line(shard_exp, far_line_exp, near_line_exp, z)
    near_exp = send(own_exp, first_flip)
    far_mid_two = send(far_mid, core_flip)
    near_line_con = send(jnp.stack([shard_con, far_line_con]), line_near)
    qkv, own_exp, far_mid = tie(qkv, own_exp, far_mid)
    heads = self_forward(qkv, base, branch, starts, prompt, size, most, PAIRS - most, heads)
    *heads, far_mid_two, near_exp, near_line_con = tie(*heads, far_mid_two, near_exp, near_line_con)
    mixed_one, expos, inverse = heads
    close_exp = jnp.stack([own_exp, near_exp])
    far_exp = send(close_exp, second_flip)
    close_exp_two = send(close_exp, core_flip)
    own_con = put_in_line(shard_con, far_line_con, near_line_con, z)
    near_con = send(own_con, first_flip)
    mixed_one, close_exp, own_con = tie(mixed_one, close_exp, own_con)
    (after_one, after_two, turned_two, input_three, query_two, turned_mixed_two, probs_two, kv_two, turned_three,
     turned_mixed_one, turned_encoder, weights_mid) = middle(
        stream_low,
        [mixed_one],
        gain_rows[1],
        gain_rows[2],
        encoder,
        slots,
        [close_mid, close_mid_two, far_mid, far_mid_two],
    )
    w_comb_one, w_query_two, w_key_two, w_value_two, w_comb_two = weights_mid
    input_three, far_exp, near_con, close_exp_two = tie(input_three, far_exp, near_con, close_exp_two)
    far_exp_two = send(far_exp, core_flip)
    close_con = jnp.stack([own_con, near_con])
    far_con = send(close_con, second_flip)
    close_con_two = send(close_con, core_flip)
    w_gate, w_up = assemble([close_exp, close_exp_two, far_exp, far_exp_two], slots)
    w_gate, w_up, far_con, close_con_two = tie(w_gate, w_up, far_con, close_con_two)
    far_con_two = send(far_con, core_flip)
    w_con = assemble([close_con, close_con_two, far_con, far_con_two], slots)[0]

    owners = LINE * SIDE * SIDE * 2
    output, grad_three, away_exp, keep_exp, away_con, keep_con = mlp(
        core_ref, after_two, input_three, turned_three, low_up, w_gate, w_up, w_con, owners
    )
    got_exp = send(away_exp, core_flip)
    got_con = send(away_con[None], core_flip)
    low_up, away_exp, away_con, grad_three, output = tie(low_up, away_exp, away_con, grad_three, output)
    own_output, other_output = hand_over([output[:prompt], output[prompt:]], core)
    low_up, own_output = tie(low_up, own_output)

    def middle_part(first, blocks, before=None):
        return middle_back(
            first,
            blocks,
            low_up,
            grad_three,
            after_two,
            after_one,
            query_two,
            probs_two,
            kv_two,
            gain_rows[1],
            gain_rows[2],
            w_comb_one,
            w_query_two,
            w_comb_two,
            before,
        )

    before = middle_part(0, 1)
    *before, got_exp, got_con = tie(*before, got_exp, got_con)
    away_con, stay_con = add_split(keep_con[None], got_con, place)
    got_con = send(away_con, second_flip)
    away_exp, stay_exp = add_split(keep_exp, got_exp, place)
    got_exp = send(away_exp, second_flip)
    *before, away_exp, away_con = tie(*before, away_exp, away_con)
    (cross_low, query_two_low, grad_after_one, self_low, grad_mixed_one, kv_two_low, _, gain_back) = middle_part(
        1, prompt // TILE + 2 * size // TILE - 1, before
    )
    _, y, x, _ = place
    here, near, far, across = spots(y, x, core)
    keep_plan = jnp.stack([core, far, across, here, near])
    away_plan = jnp.stack([1 - core, far, across, here, near])
    lefts_mid = [turned_mixed_one, turned_two, turned_encoder, turned_mixed_two]
    jobs_mid = [(0, self_low), (1, query_two_low), (2, kv_two_low[0]), (2, kv_two_low[1]), (3, cross_low)]
    away_mid = weight_part(away_plan, lefts_mid, jobs_mid)
    encoder_grad = matmul_t(kv_two_low[0], w_key_two) + matmul_t(kv_two_low[1], w_value_two)
    away_mid, encoder_grad, other_output, got_exp, got_con = tie(away_mid, encoder_grad, other_output, got_exp, got_con)
    got_mid = send(away_mid, core_flip)
    near_con = plus(stay_con[1], got_con[1])
    got_near_con = send(near_con, first_flip)
    near_exp = plus(stay_exp[1], got_exp[1])
    got_near_exp = send(near_exp, first_flip)
    own_encoder, other_encoder = hand_over([encoder_grad], core)
    grad_mixed_one, away_mid, near_exp, near_con, own_encoder = tie(
        grad_mixed_one, away_mid, near_exp, near_con, own_encoder
    )

    half = PAIRS // 2

    def attend_back(index, *values):
        part = self_backward(
            qkv, grad_mixed_one, mixed_one, expos, inverse, prompt, size, index * half, half
        )
        first, *rest = tie(part[0], grad_mixed_one, *values)
        return ((first,) + tuple(part[1:]), *rest)

    def jobs_of(part):
        return [(0, part[i]) for i in range(3)]

    part_one, grad_mixed_one, got_mid, other_encoder, got_near_con, got_near_exp = attend_back(
        0, got_mid, other_encoder, got_near_con, got_near_exp
    )
    line_exp, away_exp = line_split(plus(plus(stay_exp[0], got_exp[0]), got_near_exp), place)
    got_line_exp = send(away_exp, line_near)
    away_mid, stay_mid = weight_part(keep_plan, lefts_mid, jobs_mid, got_mid)
    got_mid = send(away_mid, second_flip)
    line_con, away_con = line_split(plus(plus(stay_con[0], got_con[0]), got_near_con), place)
    got_line_con = send(away_con, line_near)
    away_plan, away_exp, away_con, away_mid = tie(away_plan, away_exp, away_con, away_mid)
    away_one = weight_part(away_plan, [turned_one], jobs_of(part_one))
    got_one = send(away_one, core_flip)
    grad_mixed_one, away_one = tie(grad_mixed_one, away_one)

    part_two, grad_mixed_one, got_one, got_mid, got_line_exp, got_line_con, away_plan = attend_back(
        1, got_one, got_mid, got_line_exp, got_line_con, away_plan
    )
    away_two = weight_part(away_plan, [turned_one], jobs_of(part_two))
    got_two = send(away_two, core_flip)
    near_mid = plus(stay_mid[1], got_mid[1])
    got_near_mid = send(near_mid, first_flip)
    last_exp = plus(line_exp[1], got_line_exp[1])
    got_last_exp = send(last_exp, line_far)
    keep_plan, away_two, near_mid, last_exp = tie(keep_plan, away_two, near_mid, last_exp)
    away_one, stay_one = weight_part(keep_plan, [turned_one], jobs_of(part_one), got_one)
    got_one = send(away_one, second_flip)
    leave_values = (
        stream_low,
        grad_after_one,
        [part_one[:3], part_two[:3]],
        gain_rows[0],
        w_query,
        w_key,
        w_value,
    )
    blocks = prompt // TILE // 2
    steps = jnp.arange(blocks, dtype=jnp.int32)
    theirs_plan = jnp.concatenate([(1 - core) * blocks + steps, jnp.full((1,), 2 * blocks, jnp.int32)])
    ours_plan = core * blocks + steps

    theirs_plan, away_one, got_two = tie(theirs_plan, away_one, got_two)
    theirs_grad, gain_one = leave(theirs_plan, blocks + 1, *leave_values)
    theirs_grad, got_one, got_near_mid, got_last_exp, keep_plan = tie(
        theirs_grad, got_one, got_near_mid, got_last_exp, keep_plan
    )
    near_one = plus(stay_one[1], got_one[1])
    got_near_one = send(near_one, first_flip)
    line_mid, away_mid = line_split(plus(plus(stay_mid[0], got_mid[0]), got_near_mid), place)
    got_line_mid = send(away_mid, line_near)
    last_con = plus(line_con[1], got_line_con[1])
    got_last_con = send(last_con, line_far)
    keep_plan, near_one, away_mid, last_con = tie(keep_plan, near_one, away_mid, last_con)
    away_two, stay_two = weight_part(keep_plan, [turned_one], jobs_of(part_two), got_two)
    got_two = send(away_two, second_flip)
    got_grad = send(theirs_grad, core_flip)
    ours_plan, away_two, got_near_one, got_line_mid, got_last_con = tie(
        ours_plan, away_two, got_near_one, got_line_mid, got_last_con
    )
    line_one, away_one = line_split(plus(plus(stay_one[0], got_one[0]), got_near_one), place)
    got_line_one = send(away_one, line_near)
    last_mid = plus(line_mid[1], got_line_mid[1])
    got_last_mid = send(last_mid, line_far)
    ours_plan, away_one, last_mid = tie(ours_plan, away_one, last_mid)
    ours_grad, gain_more = leave(ours_plan, blocks, *leave_values)
    ours_grad, got_two, got_line_one, got_grad = tie(ours_grad, got_two, got_line_one, got_grad)
    near_two = plus(stay_two[1], got_two[1])
    got_near_two = send(near_two, first_flip)
    last_one = plus(line_one[1], got_line_one[1])
    got_last_one = send(last_one, line_far)

    def owned_part(line, got_line, got_last):
        return line[0].astype(F32) + got_line[0].astype(F32) + got_last.astype(F32)

    def square(value):
        return jnp.sum(value * value)

    owned_exp = owned_part(line_exp, got_line_exp, got_last_exp)
    owned_con = owned_part(line_con, got_line_con, got_last_con)[0]
    squares = square(owned_exp) + square(owned_con)
    half_rows = prompt // 2
    prompt_grad = both_groups(ours_grad, got_grad[:half_rows], core)
    own_branch = lax.dynamic_slice_in_dim(theirs_grad, half_rows + core * size, size, 0)
    other_branch = lax.dynamic_slice_in_dim(got_grad, half_rows + core * size, size, 0)
    branch_grad = both_groups(own_branch, other_branch, core)
    squares, got_near_two, prompt_grad, branch_grad = tie(squares, got_near_two, prompt_grad, branch_grad)
    line_two, away_two = line_split(plus(plus(stay_two[0], got_two[0]), got_near_two), place)
    got_line_two = send(away_two, line_near)
    whole_output = both_groups(own_output, other_output, core)
    prompt_output, branch_output = whole_output[:, :half_rows], whole_output[:, half_rows:]
    encoder_out = both_groups(own_encoder, other_encoder, core)
    owned_mid = owned_part(line_mid, got_line_mid, got_last_mid)
    squares = squares + square(owned_mid)
    squares, got_line_two, prompt_output, branch_output, encoder_out = tie(
        squares, got_line_two, prompt_output, branch_output, encoder_out
    )
    got_last_two = send(plus(line_two[1], got_line_two[1]), line_far)
    grad_bias = bias_gradient(
        jnp.concatenate([part_one[3], part_two[3]]), jnp.concatenate([part_one[4], part_two[4]]), buckets
    )
    owned_one = owned_part(line_one, got_line_one, got_last_one)
    squares = squares + square(owned_one)
    squares, grad_bias, got_last_two = tie(squares, grad_bias, got_last_two)
    owned_two = owned_part(line_two, got_line_two, got_last_two)
    squares = squares + square(owned_two)
    owned_self = jnp.concatenate([owned_one, owned_two], axis=2)

    owned = (
        jnp.concatenate([owned_self, owned_mid[1:4]], axis=0),
        jnp.stack([owned_mid[0], owned_mid[4]]),
        owned_exp,
        owned_con,
    )
    gain_back = jnp.sum(jnp.concatenate([(gain_one + gain_more)[None], gain_back]), axis=1)
    rest = jnp.concatenate([grad_bias.reshape(-1), squares[None]])
    shared = sum_everywhere(
        jnp.concatenate([gain_back, jnp.pad(rest, (0, D - rest.size))[None]]), place
    )
    gain_total = shared[:3]
    bias_total = shared[3, :grad_bias.size].reshape(grad_bias.shape)
    square_total = shared[3, grad_bias.size]
    grad_norm = jnp.sqrt(
        square_total + jnp.sum(gain_total * gain_total) + jnp.sum(bias_total * bias_total)
    )
    factor = jnp.minimum(1.0, CLIP / (grad_norm + 1e-06))
    weights = (projections, combiners, expansion, contraction, norm_gains, position_bias)
    firsts = (projections_first, combiners_first, expansion_first, contraction_first, gains_first, bias_first)
    seconds = (
        projections_second,
        combiners_second,
        expansion_second,
        contraction_second,
        gains_second,
        bias_second,
    )
    grads = owned + (gain_total, bias_total)
    states = [
        adam(weights[index], firsts[index], seconds[index], grads[index] * factor, RATES[index])
        for index in range(6)
    ]
    branch_shape = (2, 1, size, D)
    return (
        prompt_output,
        branch_output.reshape(branch_shape),
        prompt_grad,
        branch_grad.reshape(branch_shape),
        encoder_out,
        grad_norm,
        *states[0],
        *states[1],
        *states[2],
        *states[3],
        *states[4],
        *states[5],
        states[0][0].astype(BF),
        states[1][0].astype(BF),
        states[2][0].astype(BF),
        states[3][0].astype(BF),
    )


def solution(mesh):
    paired = mesh.shape["dp"] == 4 * SIDE * SIDE and mesh.shape["fsdp"] == 2
    return jax.shard_map(
        paired_body if paired else body,
        mesh=mesh,
        in_specs=(
            P("dp", "fsdp", None),
            P("dp", "fsdp", None, None),
            P("dp", "fsdp", None),
            P("dp", "fsdp"),
            P(),
            P("dp", "fsdp", None),
            P("dp", "fsdp", None, None),
            P(None, ("dp", "fsdp"), None),
            P(None, ("dp", "fsdp"), None),
            P(None, ("dp", "fsdp"), None),
            P(None, ("dp", "fsdp"), None),
            P(None, ("dp", "fsdp"), None),
            P(None, ("dp", "fsdp"), None),
            P(None, ("dp", "fsdp"), None),
            P(None, ("dp", "fsdp"), None),
            P(None, ("dp", "fsdp"), None),
            P(("dp", "fsdp"), None),
            P(("dp", "fsdp"), None),
            P(("dp", "fsdp"), None),
            P(),
            P(),
            P(),
            P(),
            P(),
            P(),
        ),
        out_specs=(
            P("dp", "fsdp", None),
            P("dp", "fsdp", None, None),
            P("dp", "fsdp", None),
            P("dp", "fsdp", None, None),
            P("dp", "fsdp", None),
            P(),
            P(None, ("dp", "fsdp"), None),
            P(None, ("dp", "fsdp"), None),
            P(None, ("dp", "fsdp"), None),
            P(None, ("dp", "fsdp"), None),
            P(None, ("dp", "fsdp"), None),
            P(None, ("dp", "fsdp"), None),
            P(None, ("dp", "fsdp"), None),
            P(None, ("dp", "fsdp"), None),
            P(None, ("dp", "fsdp"), None),
            P(("dp", "fsdp"), None),
            P(("dp", "fsdp"), None),
            P(("dp", "fsdp"), None),
            P(),
            P(),
            P(),
            P(),
            P(),
            P(),
            P(None, ("dp", "fsdp"), None),
            P(None, ("dp", "fsdp"), None),
            P(None, ("dp", "fsdp"), None),
            P(("dp", "fsdp"), None),
        ),
        check_vma=False,
    )
```

profile of v0, /device:TPU:0, one launch (start us, length us, event | category | flops | bytes accessed | tf_op | source)
XLA Modules:
  0.0 692.3 jit_solution(3397341107321329680)
XLA Ops:
  3.7 3.7 collective-permute-start
  11.0 6.2 collective-permute-done.far
  17.1 2.7 bitcast_dynamic-update-slice_fusion.3
  27.1 8.7 %collective-permute-done.2.near = bf16[2,3,32,1024]{3,2,1,0:T(8,128)(2,1)S(1)} collective-permute-done((bf16[2,3,32,1024]{3,2,1,0:T(8,128)(2,1)S(1)}, bf16[2,3,32,1024]{3,2,1,0:T(8,128)(2,1)S(1)}, u32[]{:S(2)}, u32[]{:S(2)}) %collective-permute-start.2) | collective-permute-done | bytes 393248 | tf_op jit(solution)/shard_map/ppermute | solution.py:1275
  40.8 2.7 collective-permute-start.4
  44.7 13.0 %collective-permute-done.4.far = bf16[5,32,1024]{2,1,0:T(8,128)(2,1)S(1)} collective-permute-done((bf16[5,32,1024]{2,1,0:T(8,128)(2,1)S(1)}, bf16[5,32,1024]{2,1,0:T(8,128)(2,1)S(1)}, u32[]{:S(2)}, u32[]{:S(2)}) %collective-permute-start.4) | collective-permute-done | bytes 327712 | tf_op jit(solution)/shard_map/ppermute | solution.py:1275
  61.1 2.2 broadcast_select_fusion.1
  68.1 8.8 %collective-permute-done.6.near = bf16[2,5,32,1024]{3,2,1,0:T(8,128)(2,1)S(1)} collective-permute-done((bf16[2,5,32,1024]{3,2,1,0:T(8,128)(2,1)S(1)}, bf16[2,5,32,1024]{3,2,1,0:T(8,128)(2,1)S(1)}, u32[]{:S(2)}, u32[]{:S(2)}) %collective-permute-start.6) | collective-permute-done | bytes 655392 | tf_op jit(solution)/shard_map/ppermute | solution.py:1275
  76.9 2.7 collective-permute-done.5.refs_2_
  83.8 17.0 %enter.1 = (bf16[2,512,1280]{2,1,0:T(8,128)(2,1)}, bf16[3,1280,1024]{2,1,0:T(8,128)(2,1)}, bf16[4,4,2,32,1024]{4,3,2,1,0:T(8,128)(2,1)}, bf16[4,4,2,32,1024]{4,3...) custom-call(s32[8,2]{1,0:T(8,128)} %stack.278.slots_ref, bf16[2,3,4,32,1024]{4,3,2,1,0:T(8,128)(2,1)} %copy-done.5, ...), custom_call_target="tpu_custom_call" | custom-call | flops 12 | bytes 1 | tf_op jit(solution)/shard_map/enter/pallas_call | solution.py:1015
  100.9 3.0 pad_maximum_fusion.4.refs_0_
  105.1 3.5 collective-permute-start.14
  109.0 30.2 %self_forward.2 = (bf16[1280,1024]{1,0:T(8,128)(2,1)}, bf16[16,256,3712]{2,1,0:T(8,128)(2,1)}, f32[1280,1024]{1,0:T(8,128)}) custom-call(s32[2]{0:T(128)} %copy-done.57, bf16[3,1280,1024]{2,1,0:T(8,128)(2,1)} %get-tuple-element.260.q_ref.k_ref.v_ref, bf16[3,1280,1024]{2,1,0:T(8,128)(2,1)} %get-tuple-element.260.q_ref.k_ref.v_ref, ...), custom_call_target="tpu_custom_call" | custom-call | flops 30 | bytes 1 | tf_op jit(solution)/shard_map/self_forward/pallas_call | solution.py:605
  141.0 28.4 %self_forward.3 = (bf16[1280,1024]{1,0:T(8,128)(2,1)}, bf16[16,256,3712]{2,1,0:T(8,128)(2,1)}, f32[1280,1024]{1,0:T(8,128)}) custom-call(s32[2]{0:T(128)} %copy-done.57, bf16[3,1280,1024]{2,1,0:T(8,128)(2,1)} %get-tuple-element.260.q_ref.k_ref.v_ref, ...), custom_call_target="tpu_custom_call", output_to_operand_aliasing={{0}: (6, {}), {1}: (7, {}), {2}: (8, {})} | custom-call | flops 18 | bytes 1 | tf_op jit(solution)/shard_map/self_forward/pallas_call | solution.py:605
  171.3 2.1 pad_maximum_fusion.1.refs_0_
  177.4 35.6 %middle.1 = (f32[1280,1024]{1,0:T(8,128)}, f32[1280,1024]{1,0:T(8,128)}, bf16[2,512,1280]{2,1,0:T(8,128)(2,1)}, bf16[1280,1024]{1,0:T(8,128)(2,1)}, bf16[1280,10...) custom-call(s32[8,2]{1,0:T(8,128)} %stack.278.slots_ref, ...), custom_call_target="tpu_custom_call" | custom-call | flops 30 | bytes 1 | tf_op jit(solution)/shard_map/middle/pallas_call | solution.py:1091
  213.0 2.7 collective-permute-done.19.refs_2_
  218.8 2.5 collective-permute-done.22.refs_3_
  221.3 8.0 %assemble.2 = (bf16[4,4,2,32,2816]{4,3,2,1,0:T(8,128)(2,1)}, bf16[4,4,2,32,2816]{4,3,2,1,0:T(8,128)(2,1)}) custom-call(s32[8,2]{1,0:T(8,128)S(1)} %copy-done.4, bf16[2,2,4,32,2816]{4,3,2,1,0:T(8,128)(2,1)S(1)} %pad_maximum_fusion.1.refs_0_, bf16[2,2,4,32,2816]{4,3,2,1,0:T(8,128)(2,1)} %collective-permute-done.21.refs_1_, ...), custom_call_target="tpu_custom_call" | custom-call | flops 4 | bytes 1 | tf_op jit(solution)/shard_map/assemble/pallas_call | solution.py:1360
  229.3 6.8 collective-permute-done.23.refs_2_
  236.1 3.2 collective-permute-done.25.refs_3_
  241.1 2.5 copy-done
  243.6 91.1 %mlp.1 = (bf16[1280,1024]{1,0:T(8,128)(2,1)}, f32[1280,1024]{1,0:T(8,128)}, bf16[2,16,32,2816]{3,2,1,0:T(8,128)(2,1)}, bf16[2,16,32,2816]{3,2,1,0:T(8,128)(2,1)}...) custom-call(s32[1]{0:T(128)} %bitcast.4.core_ref, f32[1280,1024]{1,0:T(8,128)} %get-tuple-element.275.x_ref.x2_ref, ...), custom_call_target="tpu_custom_call" | custom-call | flops 85 | bytes 1 | tf_op jit(solution)/shard_map/mlp/pallas_call | solution.py:811
  339.0 14.7 %middle_back.2 = (bf16[1280,1024]{1,0:T(8,128)(2,1)}, bf16[1280,1024]{1,0:T(8,128)(2,1)}, f32[1280,1024]{1,0:T(8,128)}, bf16[1280,1024]{1,0:T(8,128)(2,1)}, bf16...) custom-call(bf16[1280,1024]{1,0:T(8,128)(2,1)} %pad_maximum_fusion.3.dy, ...), custom_call_target="tpu_custom_call" | custom-call | flops 45 | bytes 1 | tf_op jit(solution)/shard_map/middle_back/pallas_call | solution.py:1194
  353.7 9.7 %add_split.2 = (bf16[2,4,2,32,2816]{4,3,2,1,0:T(8,128)(2,1)}, bf16[2,4,2,32,2816]{4,3,2,1,0:T(8,128)(2,1)}) custom-call(s32[4]{0:T(128)} %pad_add_fusion.spots_ref, bf16[2,4,4,32,2816]{4,3,2,1,0:T(8,128)(2,1)} %bitcast.270, bf16[2,4,4,32,2816]{4,3,2,1,0:T(8,128)(2,1)} %bitcast.64.two_ref), custom_call_target="tpu_custom_call" | custom-call | flops 1 | bytes 1 | tf_op jit(solution)/shard_map/add_split/pallas_call | solution.py:1410
  364.8 7.6 %add_split.3 = (bf16[2,4,1,88,1024]{4,3,2,1,0:T(8,128)(2,1)}, bf16[2,4,1,88,1024]{4,3,2,1,0:T(8,128)(2,1)}) custom-call(s32[4]{0:T(128)} %pad_add_fusion.spots_ref, bf16[1,4,4,88,1024]{4,3,2,1,0:T(8,128)(2,1)} %bitcast.277, bf16[1,4,4,88,1024]{4,3,2,1,0:T(8,128)(2,1)} %bitcast.66.two_ref), custom_call_target="tpu_custom_call" | custom-call | flops 1 | bytes 1 | tf_op jit(solution)/shard_map/add_split/pallas_call | solution.py:1410
  374.9 43.1 %middle_back.3 = (bf16[1280,1024]{1,0:T(8,128)(2,1)}, bf16[1280,1024]{1,0:T(8,128)(2,1)}, f32[1280,1024]{1,0:T(8,128)}, bf16[1280,1024]{1,0:T(8,128)(2,1)}, bf16...) custom-call(bf16[1280,1024]{1,0:T(8,128)(2,1)} %pad_maximum_fusion.3, ...), custom_call_target="tpu_custom_call", output_to_operand_aliasing={{0}: (12, {}), {1}: (13, {}), {2}: (14, {}), {3}: (15, {}),... | custom-call | flops 45 | bytes 1 | tf_op jit(solution)/shard_map/middle_back/pallas_call | solution.py:1194
  418.1 2.2 slice_bitcast_fusion
  420.3 11.3 %weight_part.6 = bf16[5,16,32,1024]{3,2,1,0:T(8,128)(2,1)} custom-call(s32[5]{0:T(128)} %stack.306.plan_ref, bf16[2,512,1280]{2,1,0:T(8,128)(2,1)} %get-tuple-element.316.refs_0_, bf16[2,512,1280]{2,1,0:T(8,128)(2,1)} %get-tuple-element.317.refs_1_, bf16[2,512,256]{2,1,0:T(8,128)(2,1)} %get-tuple-element.318.refs_2_, ...), custom_call_target="tpu_custom_call" | custom-call | flops 2 | bytes 1 | tf_op jit(solution)/shard_map/weight_part/pallas_call | solution.py:884
  431.6 2.5 fusion.40
  442.8 30.5 %self_backward.2 = (bf16[1280,512]{1,0:T(8,128)(2,1)}, bf16[1280,512]{1,0:T(8,128)(2,1)}, bf16[1280,512]{1,0:T(8,128)(2,1)}, f32[8,1,1280]{2,1,0:T(1,128)}, f32[8,2,1,1152]{3,2,1,0:T(1,128)}) custom-call(bf16[3,1280,1024]{2,1,0:T(8,128)(2,1)} %get-tuple-element.260.q_ref.k_ref.v_ref, bf16[3,1280,1024]{2,1,0:T(8,128)(2,1)} %get-tuple-element.260.q_ref.k_ref.v_ref, ...), custom_call_target="tpu_custom_call" | custom-call | flops 32 | bytes 1 | tf_op jit(solution)/shard_map/self_backward/pallas_call | solution.py:701
  473.4 2.7 fusion
  476.1 12.4 %weight_part.7 = (bf16[2,4,5,32,1024]{4,3,2,1,0:T(8,128)(2,1)}, bf16[2,4,5,32,1024]{4,3,2,1,0:T(8,128)(2,1)}) custom-call(s32[5]{0:T(128)} %stack.309.plan_ref, bf16[2,512,1280]{2,1,0:T(8,128)(2,1)} %get-tuple-element.316.refs_0_, bf16[2,512,1280]{2,1,0:T(8,128)(2,1)} %get-tuple-element.317.refs_1_, bf16[2,512,256]{2,1,0:T(8,128)(2,1)} %get-tuple-element.318.refs_2_, ...), custom_call_target="tpu_custom_call" | custom-call | flops 2 | bytes 1 | tf_op jit(solution)/shard_map/weight_part/pallas_call | solution.py:884
  489.9 1.9 fusion.5
  493.7 6.1 weight_part.8
  507.5 30.7 %self_backward.3 = (bf16[1280,512]{1,0:T(8,128)(2,1)}, bf16[1280,512]{1,0:T(8,128)(2,1)}, bf16[1280,512]{1,0:T(8,128)(2,1)}, f32[8,1,1280]{2,1,0:T(1,128)}, f32[8,2,1,1152]{3,2,1,0:T(1,128)}) custom-call(bf16[3,1280,1024]{2,1,0:T(8,128)(2,1)} %get-tuple-element.260.q_ref.k_ref.v_ref, bf16[3,1280,1024]{2,1,0:T(8,128)(2,1)} %get-tuple-element.260.q_ref.k_ref.v_ref, ...), custom_call_target="tpu_custom_call" | custom-call | flops 32 | bytes 1 | tf_op jit(solution)/shard_map/self_backward/pallas_call | solution.py:701
  538.3 6.1 weight_part.9
  544.4 3.4 fusion.7
  548.9 1.8 fusion.21
  550.7 6.6 weight_part.10
  558.2 2.4 collective-permute-start.42
  560.7 12.8 %leave.2 = (f32[768,1024]{1,0:T(8,128)}, f32[8,1024]{1,0:T(8,128)}) custom-call(s32[3]{0:T(128)} %pad_add_fusion.2.plan_ref, bf16[1280,1024]{1,0:T(8,128)(2,1)} %pad_maximum_fusion.2.refs_4_.x_ref, f32[1280,1024]{1,0:T(8,128)} %get-tuple-element.377.dx1_ref, bf16[1280,512]{1,0:T(8,128)(2,1)} %get-tuple-element.361.refs_1_.refs_0_, ...), custom_call_target="tpu_custom_call" | custom-call | flops 2 | bytes 1 | tf_op jit(solution)/shard_map/leave/pallas_call | solution.py:1243
  573.4 3.9 collective-permute-done.42
  579.5 3.0 fusion.1
  587.2 3.2 collective-permute-start.45
  591.4 6.6 weight_part.11
  600.3 2.5 collective-permute-done.45
  602.9 2.0 collective-permute-done.44
  607.7 2.0 collective-permute-start.47
  609.7 1.8 fusion.24
  613.3 10.3 %leave.3 = (f32[512,1024]{1,0:T(8,128)}, f32[8,1024]{1,0:T(8,128)}) custom-call(s32[2]{0:T(128)} %iota_add_fusion.plan_ref, bf16[1280,1024]{1,0:T(8,128)(2,1)} %pad_maximum_fusion.2.refs_4_.x_ref, f32[1280,1024]{1,0:T(8,128)} %get-tuple-element.377.dx1_ref, bf16[1280,512]{1,0:T(8,128)(2,1)} %get-tuple-element.361.refs_1_.refs_0_, ...), custom_call_target="tpu_custom_call" | custom-call | flops 2 | bytes 1 | tf_op jit(solution)/shard_map/leave/pallas_call | solution.py:1243
  626.6 2.5 collective-permute-done.50
  629.0 2.7 multiply_reduce_fusion.1
  634.5 2.2 select_bitcast_fusion.1
  639.0 2.3 pad_maximum_fusion
  643.6 1.9 collective-permute-start.52
  646.2 4.2 collective-permute-done.51
  654.2 2.7 collective-permute-done.53
  657.0 2.3 multiply_reduce_fusion.3
  660.1 2.4 collective-permute-start.55
  670.9 2.2 collective-permute-done.59
  681.4 2.6 fusion.41
  684.2 3.1 fusion.44
  689.0 2.0 fusion.48
  (344 shorter events, 114.4 us)
Async XLA Ops:
  2.0 6.4 collective-permute-start.1
  3.7 13.4 %collective-permute-start = (bf16[3,32,1024]{2,1,0:T(8,128)(2,1)S(1)}, bf16[3,32,1024]{2,1,0:T(8,128)(2,1)S(1)}, u32[]{:S(2)}, u32[]{:S(2)}) collective-permute-start(bf16[3,32,1024]{2,1,0:T(8,128)(2,1)S(1)} %get-tuple-element.646.shard), channel_id=1, source_target_pairs={{0,16},{1,17},{2,18},{3,19},{4,20},{5,21},{6,22},{7,23},{8,24},{9,... | collective-permute-start | bytes 589832 | tf_op jit(solution)/shard_map/ppermute | solution.py:1275
  23.2 37.9 %collective-permute-start.8 = (bf16[1408,1024]{1,0:T(8,128)(2,1)}, bf16[1408,1024]{1,0:T(8,128)(2,1)}, u32[]{:S(2)}, u32[]{:S(2)}) collective-permute-start(bf16[1408,1024]{1,0:T(8,128)(2,1)} %get-tuple-element.635), channel_id=1, source_target_pairs={{0,1},{1,0},{2,3},{3,2},{4,5},{5,4},{6,7},{7,6},{8,9},{9,8},{10,11... | collective-permute-start | bytes 8650760 | tf_op jit(solution)/shard_map/ppermute | solution.py:1275
  24.8 11.0 %collective-permute-start.2 = (bf16[2,3,32,1024]{3,2,1,0:T(8,128)(2,1)S(1)}, bf16[2,3,32,1024]{3,2,1,0:T(8,128)(2,1)S(1)}, u32[]{:S(2)}, u32[]{:S(2)}) collective-permute-start(bf16[2,3,32,1024]{3,2,1,0:T(8,128)(2,1)S(1)} %pad_maximum_fusion.17), channel_id=1, source_target_pairs={{0,8},{1,9},{2,10},{3,11},{4,12},{5,13},{6,14},{7,15},{8,0},{9,1},... | collective-permute-start | bytes 1179656 | tf_op jit(solution)/shard_map/ppermute | solution.py:1275
  36.2 21.5 %collective-permute-start.3 = (bf16[3,4,32,1024]{3,2,1,0:T(8,128)(2,1)S(1)}, bf16[3,4,32,1024]{3,2,1,0:T(8,128)(2,1)}, u32[]{:S(2)}, u32[]{:S(2)}) collective-permute-start(bf16[3,4,32,1024]{3,2,1,0:T(8,128)(2,1)S(1)} %put_in_line.4), channel_id=1, source_target_pairs={{0,2},{1,5},{2,0},{3,7},{4,6},{5,1},{6,4},{7,3},{8,10},{9,13},{10,... | collective-permute-start | bytes 2359304 | tf_op jit(solution)/shard_map/ppermute | solution.py:1275
  40.8 16.9 %collective-permute-start.4 = (bf16[5,32,1024]{2,1,0:T(8,128)(2,1)S(1)}, bf16[5,32,1024]{2,1,0:T(8,128)(2,1)S(1)}, u32[]{:S(2)}, u32[]{:S(2)}) collective-permute-start(bf16[5,32,1024]{2,1,0:T(8,128)(2,1)S(1)} %pad_maximum_fusion.20.shard), channel_id=1, source_target_pairs={{0,16},{1,17},{2,18},{3,19},{4,20},{5,21},{6,22},{7,23},{8,24},{9,... | collective-permute-start | bytes 983048 | tf_op jit(solution)/shard_map/ppermute | solution.py:1275
  59.1 20.6 %collective-permute-start.5 = (bf16[2,3,4,32,1024]{4,3,2,1,0:T(8,128)(2,1)S(1)}, bf16[2,3,4,32,1024]{4,3,2,1,0:T(8,128)(2,1)}, u32[]{:S(2)}, u32[]{:S(2)}) collective-permute-start(bf16[2,3,4,32,1024]{4,3,2,1,0:T(8,128)(2,1)S(1)} %pad_maximum_fusion.5.refs_0_), channel_id=1, source_target_pairs={{0,4},{1,3},{2,6},{3,1},{4,0},{5,7},{6,2},{7,5},{8,12},{9,11},{10,... | collective-permute-start | bytes 4718600 | tf_op jit(solution)/shard_map/ppermute | solution.py:1275
  59.6 20.0 %collective-permute-start.7 = (bf16[2,3,4,32,1024]{4,3,2,1,0:T(8,128)(2,1)S(1)}, bf16[2,3,4,32,1024]{4,3,2,1,0:T(8,128)(2,1)S(1)}, u32[]{:S(2)}, u32[]{:S(2)}) collective-permute-start(bf16[2,3,4,32,1024]{4,3,2,1,0:T(8,128)(2,1)S(1)} %pad_maximum_fusion.5.refs_0_), channel_id=1, source_target_pairs={{0,1},{1,0},{2,3},{3,2},{4,5},{5,4},{6,7},{7,6},{8,9},{9,8},{10,11... | collective-permute-start | bytes 4718600 | tf_op jit(solution)/shard_map/ppermute | solution.py:1275
  59.7 17.2 %collective-permute-start.6 = (bf16[2,5,32,1024]{3,2,1,0:T(8,128)(2,1)S(1)}, bf16[2,5,32,1024]{3,2,1,0:T(8,128)(2,1)S(1)}, u32[]{:S(2)}, u32[]{:S(2)}) collective-permute-start(bf16[2,5,32,1024]{3,2,1,0:T(8,128)(2,1)S(1)} %pad_maximum_fusion.13), channel_id=1, source_target_pairs={{0,8},{1,9},{2,10},{3,11},{4,12},{5,13},{6,14},{7,15},{8,0},{9,1},... | collective-permute-start | bytes 1966088 | tf_op jit(solution)/shard_map/ppermute | solution.py:1275
  79.7 4.2 collective-permute-start.9
  80.8 20.1 %collective-permute-start.10 = (bf16[5,4,32,1024]{3,2,1,0:T(8,128)(2,1)S(1)}, bf16[5,4,32,1024]{3,2,1,0:T(8,128)(2,1)}, u32[]{:S(2)}, u32[]{:S(2)}) collective-permute-start(bf16[5,4,32,1024]{3,2,1,0:T(8,128)(2,1)S(1)} %put_in_line.5), channel_id=1, source_target_pairs={{0,2},{1,5},{2,0},{3,7},{4,6},{5,1},{6,4},{7,3},{8,10},{9,13},{10,... | collective-permute-start | bytes 3932168 | tf_op jit(solution)/shard_map/ppermute | solution.py:1275
  82.4 18.4 %collective-permute-start.11 = (bf16[2,32,2816]{2,1,0:T(8,128)(2,1)S(1)}, bf16[2,32,2816]{2,1,0:T(8,128)(2,1)S(1)}, u32[]{:S(2)}, u32[]{:S(2)}) collective-permute-start(bf16[2,32,2816]{2,1,0:T(8,128)(2,1)S(1)} %convert_element_type.440.shard), channel_id=1, source_target_pairs={{0,16},{1,17},{2,18},{3,19},{4,20},{5,21},{6,22},{7,23},{8,24},{9,... | collective-permute-start | bytes 1081352 | tf_op jit(solution)/shard_map/ppermute | solution.py:1275
  103.9 35.3 %collective-permute-start.12 = (bf16[2,5,4,32,1024]{4,3,2,1,0:T(8,128)(2,1)}, bf16[2,5,4,32,1024]{4,3,2,1,0:T(8,128)(2,1)}, u32[]{:S(2)}, u32[]{:S(2)}) collective-permute-start(bf16[2,5,4,32,1024]{4,3,2,1,0:T(8,128)(2,1)} %pad_maximum_fusion.4.refs_0_), channel_id=1, source_target_pairs={{0,4},{1,3},{2,6},{3,1},{4,0},{5,7},{6,2},{7,5},{8,12},{9,11},{10,... | collective-permute-start | bytes 7864328 | tf_op jit(solution)/shard_map/ppermute | solution.py:1275
  105.0 34.2 %collective-permute-start.13 = (bf16[2,5,4,32,1024]{4,3,2,1,0:T(8,128)(2,1)}, bf16[2,5,4,32,1024]{4,3,2,1,0:T(8,128)(2,1)}, u32[]{:S(2)}, u32[]{:S(2)}) collective-permute-start(bf16[2,5,4,32,1024]{4,3,2,1,0:T(8,128)(2,1)} %pad_maximum_fusion.4.refs_0_), channel_id=1, source_target_pairs={{0,1},{1,0},{2,3},{3,2},{4,5},{5,4},{6,7},{7,6},{8,9},{9,8},{10,11... | collective-permute-start | bytes 7864328 | tf_op jit(solution)/shard_map/ppermute | solution.py:1275
  105.1 34.1 %collective-permute-start.14 = (bf16[2,2,32,2816]{3,2,1,0:T(8,128)(2,1)S(1)}, bf16[2,2,32,2816]{3,2,1,0:T(8,128)(2,1)S(1)}, u32[]{:S(2)}, u32[]{:S(2)}) collective-permute-start(bf16[2,2,32,2816]{3,2,1,0:T(8,128)(2,1)S(1)} %pad_maximum_fusion.11), channel_id=1, source_target_pairs={{0,8},{1,9},{2,10},{3,11},{4,12},{5,13},{6,14},{7,15},{8,0},{9,1},... | collective-permute-start | bytes 2162696 | tf_op jit(solution)/shard_map/ppermute | solution.py:1275
  108.6 30.6 %collective-permute-start.15 = (bf16[1,88,1024]{2,1,0:T(8,128)(2,1)S(1)}, bf16[1,88,1024]{2,1,0:T(8,128)(2,1)S(1)}, u32[]{:S(2)}, u32[]{:S(2)}) collective-permute-start(bf16[1,88,1024]{2,1,0:T(8,128)(2,1)S(1)} %convert_bitcast_fusion.shard), channel_id=1, source_target_pairs={{0,16},{1,17},{2,18},{3,19},{4,20},{5,21},{6,22},{7,23},{8,24},{9,... | collective-permute-start | bytes 540680 | tf_op jit(solution)/shard_map/ppermute | solution.py:1275
  139.2 31.0 %collective-permute-start.16 = (bf16[2,5,4,32,1024]{4,3,2,1,0:T(8,128)(2,1)}, bf16[2,5,4,32,1024]{4,3,2,1,0:T(8,128)(2,1)}, u32[]{:S(2)}, u32[]{:S(2)}) collective-permute-start(bf16[2,5,4,32,1024]{4,3,2,1,0:T(8,128)(2,1)} %collective-permute-done.12.refs_2_), channel_id=1, source_target_pairs={{0,1},{1,0},{2,3},{3,2},{4,5},{5,4},{6,7},{7,6},{8,9},{9,8},{10,11... | collective-permute-start | bytes 7864328 | tf_op jit(solution)/shard_map/ppermute | solution.py:1275
  139.7 30.5 %collective-permute-start.17 = (bf16[2,4,32,2816]{3,2,1,0:T(8,128)(2,1)S(1)}, bf16[2,4,32,2816]{3,2,1,0:T(8,128)(2,1)S(1)}, u32[]{:S(2)}, u32[]{:S(2)}) collective-permute-start(bf16[2,4,32,2816]{3,2,1,0:T(8,128)(2,1)S(1)} %put_in_line.6), channel_id=1, source_target_pairs={{0,2},{1,5},{2,0},{3,7},{4,6},{5,1},{6,4},{7,3},{8,10},{9,13},{10,... | collective-permute-start | bytes 4325384 | tf_op jit(solution)/shard_map/ppermute | solution.py:1275
  140.5 29.0 %collective-permute-start.18 = (bf16[2,1,88,1024]{3,2,1,0:T(8,128)(2,1)S(1)}, bf16[2,1,88,1024]{3,2,1,0:T(8,128)(2,1)S(1)}, u32[]{:S(2)}, u32[]{:S(2)}) collective-permute-start(bf16[2,1,88,1024]{3,2,1,0:T(8,128)(2,1)S(1)} %pad_maximum_fusion.18), channel_id=1, source_target_pairs={{0,8},{1,9},{2,10},{3,11},{4,12},{5,13},{6,14},{7,15},{8,0},{9,1},... | collective-permute-start | bytes 1081352 | tf_op jit(solution)/shard_map/ppermute | solution.py:1275
  173.4 42.4 %collective-permute-start.19 = (bf16[2,2,4,32,2816]{4,3,2,1,0:T(8,128)(2,1)S(1)}, bf16[2,2,4,32,2816]{4,3,2,1,0:T(8,128)(2,1)}, u32[]{:S(2)}, u32[]{:S(2)}) collective-permute-start(bf16[2,2,4,32,2816]{4,3,2,1,0:T(8,128)(2,1)S(1)} %pad_maximum_fusion.1.refs_0_), channel_id=1, source_target_pairs={{0,4},{1,3},{2,6},{3,1},{4,0},{5,7},{6,2},{7,5},{8,12},{9,11},{10,... | collective-permute-start | bytes 8650760 | tf_op jit(solution)/shard_map/ppermute | solution.py:1275
  174.9 40.9 %collective-permute-start.21 = (bf16[2,2,4,32,2816]{4,3,2,1,0:T(8,128)(2,1)S(1)}, bf16[2,2,4,32,2816]{4,3,2,1,0:T(8,128)(2,1)}, u32[]{:S(2)}, u32[]{:S(2)}) collective-permute-start(bf16[2,2,4,32,2816]{4,3,2,1,0:T(8,128)(2,1)S(1)} %pad_maximum_fusion.1.refs_0_), channel_id=1, source_target_pairs={{0,1},{1,0},{2,3},{3,2},{4,5},{5,4},{6,7},{7,6},{8,9},{9,8},{10,11... | collective-permute-start | bytes 8650760 | tf_op jit(solution)/shard_map/ppermute | solution.py:1275
  175.8 37.2 %collective-permute-start.20 = (bf16[1,4,88,1024]{3,2,1,0:T(8,128)(2,1)S(1)}, bf16[1,4,88,1024]{3,2,1,0:T(8,128)(2,1)}, u32[]{:S(2)}, u32[]{:S(2)}) collective-permute-start(bf16[1,4,88,1024]{3,2,1,0:T(8,128)(2,1)S(1)} %put_in_line.7), channel_id=1, source_target_pairs={{0,2},{1,5},{2,0},{3,7},{4,6},{5,1},{6,4},{7,3},{8,10},{9,13},{10,... | collective-permute-start | bytes 2162696 | tf_op jit(solution)/shard_map/ppermute | solution.py:1275
  215.8 5.5 collective-permute-start.22
  217.0 19.1 %collective-permute-start.23 = (bf16[2,1,4,88,1024]{4,3,2,1,0:T(8,128)(2,1)S(1)}, bf16[2,1,4,88,1024]{4,3,2,1,0:T(8,128)(2,1)S(1)}, u32[]{:S(2)}, u32[]{:S(2)}) collective-permute-start(bf16[2,1,4,88,1024]{4,3,2,1,0:T(8,128)(2,1)S(1)} %pad_maximum_fusion.6.refs_0_), channel_id=1, source_target_pairs={{0,4},{1,3},{2,6},{3,1},{4,0},{5,7},{6,2},{7,5},{8,12},{9,11},{10,... | collective-permute-start | bytes 4325384 | tf_op jit(solution)/shard_map/ppermute | solution.py:1275
  218.5 17.6 %collective-permute-start.24 = (bf16[2,1,4,88,1024]{4,3,2,1,0:T(8,128)(2,1)S(1)}, bf16[2,1,4,88,1024]{4,3,2,1,0:T(8,128)(2,1)S(1)}, u32[]{:S(2)}, u32[]{:S(2)}) collective-permute-start(bf16[2,1,4,88,1024]{4,3,2,1,0:T(8,128)(2,1)S(1)} %pad_maximum_fusion.6.refs_0_), channel_id=1, source_target_pairs={{0,1},{1,0},{2,3},{3,2},{4,5},{5,4},{6,7},{7,6},{8,9},{9,8},{10,11... | collective-permute-start | bytes 4325384 | tf_op jit(solution)/shard_map/ppermute | solution.py:1275
  236.1 3.2 collective-permute-start.25
  334.7 19.0 %collective-permute-start.26 = (bf16[2,16,32,2816]{3,2,1,0:T(8,128)(2,1)}, bf16[2,16,32,2816]{3,2,1,0:T(8,128)(2,1)}, u32[]{:S(2)}, u32[]{:S(2)}) collective-permute-start(bf16[2,16,32,2816]{3,2,1,0:T(8,128)(2,1)} %get-tuple-element.292), channel_id=1, source_target_pairs={{0,1},{1,0},{2,3},{3,2},{4,5},{5,4},{6,7},{7,6},{8,9},{9,8},{10,11... | collective-permute-start | bytes 17301512 | tf_op jit(solution)/shard_map/ppermute | solution.py:1275
  334.9 18.8 %collective-permute-start.27 = (bf16[1,16,88,1024]{3,2,1,0:T(8,128)(2,1)}, bf16[1,16,88,1024]{3,2,1,0:T(8,128)(2,1)}, u32[]{:S(2)}, u32[]{:S(2)}) collective-permute-start(bf16[1,16,88,1024]{3,2,1,0:T(8,128)(2,1)} %bitcast.290), channel_id=1, source_target_pairs={{0,1},{1,0},{2,3},{3,2},{4,5},{5,4},{6,7},{7,6},{8,9},{9,8},{10,11... | collective-permute-start | bytes 8650760 | tf_op jit(solution)/shard_map/ppermute | solution.py:1275
  363.5 71.5 %collective-permute-start.29 = (bf16[2,4,2,32,2816]{4,3,2,1,0:T(8,128)(2,1)}, bf16[2,4,2,32,2816]{4,3,2,1,0:T(8,128)(2,1)}, u32[]{:S(2)}, u32[]{:S(2)}) collective-permute-start(bf16[2,4,2,32,2816]{4,3,2,1,0:T(8,128)(2,1)} %get-tuple-element.327), channel_id=1, source_target_pairs={{0,4},{1,3},{2,6},{3,1},{4,0},{5,7},{6,2},{7,5},{8,12},{9,11},{10,... | collective-permute-start | bytes 8650760 | tf_op jit(solution)/shard_map/ppermute | solution.py:1275
  372.4 62.6 %collective-permute-start.30 = (bf16[2,4,1,88,1024]{4,3,1,2,0:T(8,128)(2,1)}, bf16[2,4,1,88,1024]{4,3,1,2,0:T(8,128)(2,1)}, u32[]{:S(2)}, u32[]{:S(2)}) collective-permute-start(bf16[2,4,1,88,1024]{4,3,1,2,0:T(8,128)(2,1)} %bitcast.291), channel_id=1, source_target_pairs={{0,4},{1,3},{2,6},{3,1},{4,0},{5,7},{6,2},{7,5},{8,12},{9,11},{10,... | collective-permute-start | bytes 4325384 | tf_op jit(solution)/shard_map/ppermute | solution.py:1275
  374.3 60.7 %collective-permute-start.28 = (bf16[640,1024]{1,0:T(8,128)(2,1)}, bf16[640,1024]{1,0:T(8,128)(2,1)}, u32[]{:S(2)}, u32[]{:S(2)}) collective-permute-start(bf16[640,1024]{1,0:T(8,128)(2,1)} %pad_maximum_fusion.8), channel_id=1, source_target_pairs={{0,1},{1,0},{2,3},{3,2},{4,5},{5,4},{6,7},{7,6},{8,9},{9,8},{10,11... | collective-permute-start | bytes 3932168 | tf_op jit(solution)/shard_map/ppermute | solution.py:1275
  435.0 38.4 %collective-permute-start.31 = (bf16[5,16,32,1024]{3,2,1,0:T(8,128)(2,1)}, bf16[5,16,32,1024]{3,2,1,0:T(8,128)(2,1)}, u32[]{:S(2)}, u32[]{:S(2)}) collective-permute-start(bf16[5,16,32,1024]{3,2,1,0:T(8,128)(2,1)} %weight_part.6), channel_id=1, source_target_pairs={{0,1},{1,0},{2,3},{3,2},{4,5},{5,4},{6,7},{7,6},{8,9},{9,8},{10,11... | collective-permute-start | bytes 15728648 | tf_op jit(solution)/shard_map/ppermute | solution.py:1275
  437.7 35.7 %collective-permute-start.34 = (bf16[4,2,32,2816]{3,2,1,0:T(8,128)(2,1)S(1)}, bf16[4,2,32,2816]{3,2,1,0:T(8,128)(2,1)}, u32[]{:S(2)}, u32[]{:S(2)}) collective-permute-start(bf16[4,2,32,2816]{3,2,1,0:T(8,128)(2,1)S(1)} %fusion.4), channel_id=1, source_target_pairs={{0,2},{1,5},{2,0},{3,7},{4,6},{5,1},{6,4},{7,3},{8,10},{9,13},{10,... | collective-permute-start | bytes 4325384 | tf_op jit(solution)/shard_map/ppermute | solution.py:1275
  440.6 32.8 %collective-permute-start.33 = (bf16[4,1,88,1024]{3,2,0,1:T(8,128)(2,1)S(1)}, bf16[4,1,88,1024]{3,2,0,1:T(8,128)(2,1)}, u32[]{:S(2)}, u32[]{:S(2)}) collective-permute-start(bf16[4,1,88,1024]{3,2,0,1:T(8,128)(2,1)S(1)} %fusion.13), channel_id=1, source_target_pairs={{0,2},{1,5},{2,0},{3,7},{4,6},{5,1},{6,4},{7,3},{8,10},{9,13},{10,... | collective-permute-start | bytes 2162696 | tf_op jit(solution)/shard_map/ppermute | solution.py:1275
  442.2 31.1 %collective-permute-start.32 = (f32[128,1024]{1,0:T(8,128)}, f32[128,1024]{1,0:T(8,128)}, u32[]{:S(2)}, u32[]{:S(2)}) collective-permute-start(f32[128,1024]{1,0:T(8,128)} %get-tuple-element.624), channel_id=1, source_target_pairs={{0,1},{1,0},{2,3},{3,2},{4,5},{5,4},{6,7},{7,6},{8,9},{9,8},{10,11... | collective-permute-start | bytes 1572872 | tf_op jit(solution)/shard_map/ppermute | solution.py:1275
  488.6 49.7 %collective-permute-start.36 = (bf16[2,4,5,32,1024]{4,3,2,1,0:T(8,128)(2,1)}, bf16[2,4,5,32,1024]{4,3,2,1,0:T(8,128)(2,1)}, u32[]{:S(2)}, u32[]{:S(2)}) collective-permute-start(bf16[2,4,5,32,1024]{4,3,2,1,0:T(8,128)(2,1)} %get-tuple-element.358), channel_id=1, source_target_pairs={{0,4},{1,3},{2,6},{3,1},{4,0},{5,7},{6,2},{7,5},{8,12},{9,11},{10,... | collective-permute-start | bytes 7864328 | tf_op jit(solution)/shard_map/ppermute | solution.py:1275
  499.8 38.5 %collective-permute-start.35 = (bf16[3,16,32,512]{3,2,1,0:T(8,128)(2,1)}, bf16[3,16,32,512]{3,2,1,0:T(8,128)(2,1)}, u32[]{:S(2)}, u32[]{:S(2)}) collective-permute-start(bf16[3,16,32,512]{3,2,1,0:T(8,128)(2,1)} %weight_part.8), channel_id=1, source_target_pairs={{0,1},{1,0},{2,3},{3,2},{4,5},{5,4},{6,7},{7,6},{8,9},{9,8},{10,11... | collective-permute-start | bytes 4718600 | tf_op jit(solution)/shard_map/ppermute | solution.py:1275
  501.5 36.8 %collective-permute-start.37 = (bf16[2,2,32,2816]{3,2,1,0:T(8,128)(2,1)}, bf16[2,2,32,2816]{3,2,1,0:T(8,128)(2,1)}, u32[]{:S(2)}, u32[]{:S(2)}) collective-permute-start(bf16[2,2,32,2816]{3,2,1,0:T(8,128)(2,1)} %pad_maximum_fusion.12), channel_id=1, source_target_pairs={{0,8},{1,9},{2,10},{3,11},{4,12},{5,13},{6,14},{7,15},{8,0},{9,1},... | collective-permute-start | bytes 2162696 | tf_op jit(solution)/shard_map/ppermute | solution.py:1275
  504.4 33.8 %collective-permute-start.38 = (bf16[2,1,88,1024]{3,2,1,0:T(8,128)(2,1)}, bf16[2,1,88,1024]{3,2,1,0:T(8,128)(2,1)S(1)}, u32[]{:S(2)}, u32[]{:S(2)}) collective-permute-start(bf16[2,1,88,1024]{3,2,1,0:T(8,128)(2,1)} %pad_maximum_fusion.19), channel_id=1, source_target_pairs={{0,8},{1,9},{2,10},{3,11},{4,12},{5,13},{6,14},{7,15},{8,0},{9,1},... | collective-permute-start | bytes 1081352 | tf_op jit(solution)/shard_map/ppermute | solution.py:1275
  544.4 16.2 %collective-permute-start.39 = (bf16[3,16,32,512]{3,2,1,0:T(8,128)(2,1)}, bf16[3,16,32,512]{3,2,1,0:T(8,128)(2,1)}, u32[]{:S(2)}, u32[]{:S(2)}) collective-permute-start(bf16[3,16,32,512]{3,2,1,0:T(8,128)(2,1)} %weight_part.9), channel_id=1, source_target_pairs={{0,1},{1,0},{2,3},{3,2},{4,5},{5,4},{6,7},{7,6},{8,9},{9,8},{10,11... | collective-permute-start | bytes 4718600 | tf_op jit(solution)/shard_map/ppermute | solution.py:1275
  547.8 29.6 %collective-permute-start.41 = (bf16[4,5,32,1024]{3,2,1,0:T(8,128)(2,1)}, bf16[4,5,32,1024]{3,2,1,0:T(8,128)(2,1)}, u32[]{:S(2)}, u32[]{:S(2)}) collective-permute-start(bf16[4,5,32,1024]{3,2,1,0:T(8,128)(2,1)} %fusion.7), channel_id=1, source_target_pairs={{0,2},{1,5},{2,0},{3,7},{4,6},{5,1},{6,4},{7,3},{8,10},{9,13},{10,... | collective-permute-start | bytes 3932168 | tf_op jit(solution)/shard_map/ppermute | solution.py:1275
  557.3 20.1 %collective-permute-start.40 = (bf16[2,4,3,32,512]{4,3,2,1,0:T(8,128)(2,1)}, bf16[2,4,3,32,512]{4,3,2,1,0:T(8,128)(2,1)S(1)}, u32[]{:S(2)}, u32[]{:S(2)}) collective-permute-start(bf16[2,4,3,32,512]{4,3,2,1,0:T(8,128)(2,1)} %get-tuple-element.375), channel_id=1, source_target_pairs={{0,4},{1,3},{2,6},{3,1},{4,0},{5,7},{6,2},{7,5},{8,12},{9,11},{10,... | collective-permute-start | bytes 2359304 | tf_op jit(solution)/shard_map/ppermute | solution.py:1275
  558.2 19.2 %collective-permute-start.42 = (bf16[2,32,2816]{2,1,0:T(8,128)(2,1)}, bf16[2,32,2816]{2,1,0:T(8,128)(2,1)S(1)}, u32[]{:S(2)}, u32[]{:S(2)}) collective-permute-start(bf16[2,32,2816]{2,1,0:T(8,128)(2,1)} %fusion.21), channel_id=1, source_target_pairs={{0,16},{1,17},{2,18},{3,19},{4,20},{5,21},{6,22},{7,23},{8,24},{9,... | collective-permute-start | bytes 1081352 | tf_op jit(solution)/shard_map/ppermute | solution.py:1275
  577.4 54.3 %collective-permute-start.48 = (f32[768,1024]{1,0:T(8,128)}, f32[768,1024]{1,0:T(8,128)}, u32[]{:S(2)}, u32[]{:S(2)}) collective-permute-start(f32[768,1024]{1,0:T(8,128)} %get-tuple-element.398), channel_id=1, source_target_pairs={{0,1},{1,0},{2,3},{3,2},{4,5},{5,4},{6,7},{7,6},{8,9},{9,8},{10,11... | collective-permute-start | bytes 9437192 | tf_op jit(solution)/shard_map/ppermute | solution.py:1275
  583.5 21.3 %collective-permute-start.44 = (bf16[2,5,32,1024]{3,2,1,0:T(8,128)(2,1)}, bf16[2,5,32,1024]{3,2,1,0:T(8,128)(2,1)}, u32[]{:S(2)}, u32[]{:S(2)}) collective-permute-start(bf16[2,5,32,1024]{3,2,1,0:T(8,128)(2,1)} %pad_maximum_fusion.14), channel_id=1, source_target_pairs={{0,8},{1,9},{2,10},{3,11},{4,12},{5,13},{6,14},{7,15},{8,0},{9,1},... | collective-permute-start | bytes 1966088 | tf_op jit(solution)/shard_map/ppermute | solution.py:1275
  585.0 17.9 %collective-permute-start.43 = (bf16[4,3,32,512]{3,2,1,0:T(8,128)(2,1)}, bf16[4,3,32,512]{3,2,1,0:T(8,128)(2,1)}, u32[]{:S(2)}, u32[]{:S(2)}) collective-permute-start(bf16[4,3,32,512]{3,2,1,0:T(8,128)(2,1)} %fusion.16), channel_id=1, source_target_pairs={{0,2},{1,5},{2,0},{3,7},{4,6},{5,1},{6,4},{7,3},{8,10},{9,13},{10,... | collective-permute-start | bytes 1179656 | tf_op jit(solution)/shard_map/ppermute | solution.py:1275
  587.2 15.7 %collective-permute-start.45 = (bf16[1,88,1024]{2,1,0:T(8,128)(2,1)}, bf16[1,88,1024]{2,1,0:T(8,128)(2,1)S(1)}, u32[]{:S(2)}, u32[]{:S(2)}) collective-permute-start(bf16[1,88,1024]{2,1,0:T(8,128)(2,1)} %fusion.33), channel_id=1, source_target_pairs={{0,16},{1,17},{2,18},{3,19},{4,20},{5,21},{6,22},{7,23},{8,24},{9,... | collective-permute-start | bytes 540680 | tf_op jit(solution)/shard_map/ppermute | solution.py:1275
  598.0 33.6 %collective-permute-start.46 = (bf16[2,4,3,32,512]{4,3,2,1,0:T(8,128)(2,1)}, bf16[2,4,3,32,512]{4,3,2,1,0:T(8,128)(2,1)}, u32[]{:S(2)}, u32[]{:S(2)}) collective-permute-start(bf16[2,4,3,32,512]{4,3,2,1,0:T(8,128)(2,1)} %get-tuple-element.390), channel_id=1, source_target_pairs={{0,4},{1,3},{2,6},{3,1},{4,0},{5,7},{6,2},{7,5},{8,12},{9,11},{10,... | collective-permute-start | bytes 2359304 | tf_op jit(solution)/shard_map/ppermute | solution.py:1275
  607.7 24.0 %collective-permute-start.47 = (bf16[2,3,32,512]{3,2,1,0:T(8,128)(2,1)}, bf16[2,3,32,512]{3,2,1,0:T(8,128)(2,1)}, u32[]{:S(2)}, u32[]{:S(2)}) collective-permute-start(bf16[2,3,32,512]{3,2,1,0:T(8,128)(2,1)} %pad_maximum_fusion.21), channel_id=1, source_target_pairs={{0,8},{1,9},{2,10},{3,11},{4,12},{5,13},{6,14},{7,15},{8,0},{9,1},... | collective-permute-start | bytes 589832 | tf_op jit(solution)/shard_map/ppermute | solution.py:1275
  611.5 17.5 %collective-permute-start.50 = (bf16[5,32,1024]{2,1,0:T(8,128)(2,1)}, bf16[5,32,1024]{2,1,0:T(8,128)(2,1)}, u32[]{:S(2)}, u32[]{:S(2)}) collective-permute-start(bf16[5,32,1024]{2,1,0:T(8,128)(2,1)} %fusion.24), channel_id=1, source_target_pairs={{0,16},{1,17},{2,18},{3,19},{4,20},{5,21},{6,22},{7,23},{8,24},{9,... | collective-permute-start | bytes 983048 | tf_op jit(solution)/shard_map/ppermute | solution.py:1275
  632.9 8.4 %collective-permute-start.49 = (bf16[4,3,32,512]{3,2,1,0:T(8,128)(2,1)S(1)}, bf16[4,3,32,512]{3,2,1,0:T(8,128)(2,1)S(1)}, u32[]{:S(2)}, u32[]{:S(2)}) collective-permute-start(bf16[4,3,32,512]{3,2,1,0:T(8,128)(2,1)S(1)} %fusion.18), channel_id=1, source_target_pairs={{0,2},{1,5},{2,0},{3,7},{4,6},{5,1},{6,4},{7,3},{8,10},{9,13},{10,... | collective-permute-start | bytes 1179656 | tf_op jit(solution)/shard_map/ppermute | solution.py:1275
  641.3 38.6 %copy-start.52 = (f32[3,1024]{1,0:T(4,128)S(1)}, f32[3,1024]{1,0:T(4,128)}, u32[]{:S(2)}) copy-start(f32[3,1024]{1,0:T(4,128)} %param.44) | copy-start | bytes 36868
  641.3 38.6 %copy-start.56 = (f32[3,1024]{1,0:T(4,128)S(1)}, f32[3,1024]{1,0:T(4,128)}, u32[]{:S(2)}) copy-start(f32[3,1024]{1,0:T(4,128)} %param.45) | copy-start | bytes 36868
  642.6 7.8 %collective-permute-start.51 = (bf16[2,3,32,512]{3,2,1,0:T(8,128)(2,1)S(1)}, bf16[2,3,32,512]{3,2,1,0:T(8,128)(2,1)S(1)}, u32[]{:S(2)}, u32[]{:S(2)}) collective-permute-start(bf16[2,3,32,512]{3,2,1,0:T(8,128)(2,1)S(1)} %pad_maximum_fusion.22), channel_id=1, source_target_pairs={{0,8},{1,9},{2,10},{3,11},{4,12},{5,13},{6,14},{7,15},{8,0},{9,1},... | collective-permute-start | bytes 589832 | tf_op jit(solution)/shard_map/ppermute | solution.py:1275
  643.6 8.3 %collective-permute-start.52 = (bf16[3,32,512]{2,1,0:T(8,128)(2,1)S(1)}, bf16[3,32,512]{2,1,0:T(8,128)(2,1)}, u32[]{:S(2)}, u32[]{:S(2)}) collective-permute-start(bf16[3,32,512]{2,1,0:T(8,128)(2,1)S(1)} %fusion.34), channel_id=1, source_target_pairs={{0,16},{1,17},{2,18},{3,19},{4,20},{5,21},{6,22},{7,23},{8,24},{9,... | collective-permute-start | bytes 294920 | tf_op jit(solution)/shard_map/ppermute | solution.py:1275
  651.1 5.9 collective-permute-start.53
  654.2 29.8 %copy-start.11 = (f32[2,32,2816]{2,1,0:T(8,128)S(1)}, f32[2,32,2816]{2,1,0:T(8,128)}, u32[]{:S(2)}) copy-start(f32[2,32,2816]{2,1,0:T(8,128)} %param.38) | copy-start | bytes 2162692
  660.1 5.6 collective-permute-start.54
  660.1 5.5 collective-permute-start.55
  662.6 3.7 collective-permute-start.56
  666.4 3.8 collective-permute-start.57
  667.2 3.7 collective-permute-start.58
  668.5 4.6 collective-permute-start.59
  673.1 2.8 collective-permute-start.60
  (60 other events, 393.2 us)
where the time goes:
time: 699 us; the launch traced here: 692 us
  Pallas kernels  422 us (60%)
  other arithmetic  83.1 us (12%)
  waiting for transfers between devices  79 us (11%)
  starting transfers between devices  57.8 us (8%)
  local copies, waits for them, and re-layouts  31.7 us (5%)
  between operations  13.5 us (2%)
    pallas_call x1, Pallas kernels, mlp(): pl.pallas_call(mlp_kernel, grid_spec=pltpu.PrefetchScalarGridSpec(num_sca...  91.1 us
    ppermute x61, waiting for transfers between devices, send(): return lax.ppermute(value, AXES, moves(rule))  79 us
    pallas_call x2, Pallas kernels, self_backward(): pl.pallas_call(functools.partial(self_back_kernel, prompt, size), grid=(p...  61.2 us
    pallas_call x2, Pallas kernels, self_forward(): pl.pallas_call(functools.partial(self_kernel, prompt, size, len(more)), g...  58.6 us
    pallas_call x2, Pallas kernels, middle_back(): pl.pallas_call(middle_back_kernel, grid=(blocks,), in_specs=[rows] * 5 +...  57.8 us
    ppermute x61, starting transfers between devices, send(): return lax.ppermute(value, AXES, moves(rule))  57.8 us
    pallas_call x6, Pallas kernels, weight_part(): pl.pallas_call(functools.partial(part_kernel, [left for left, _ in jobs],...  49.2 us
    pallas_call x1, Pallas kernels, middle(): pl.pallas_call(functools.partial(middle_kernel, len(mixed)), grid=(count...  35.6 us
  transfers between devices with their start and end apart: 61, of which 21 were waited for; matrix products, arithmetic and copies ran while one was open for 11% of the time, Pallas kernels for 44%

commit v1 on v0

--- a/solution.py
+++ b/solution.py
@@ -1030,8 +1030,8 @@
     sources = refs[:4]
     x_ref, *mixed_refs = refs[4:5 + parts]
     (gain_two_ref, gain_three_ref, e_ref, x1_ref, x2_ref, a2_ref, a3_ref, q_ref, o_ref, p_ref, kv_ref, a3_t_ref,
-     mixed_t_ref, e_t_ref, *outs) = refs[5 + parts:24 + parts]
-    held, in_sems, out_sems, o_scr = refs[24 + parts:]
+     mixed_t_ref, e_t_ref, o_scr, inv_ref, *outs) = refs[5 + parts:26 + parts]
+    held, in_sems, out_sems = refs[26 + parts:]
     arrive(slots_ref, sources, held, in_sems, 5)
 
     def weight(index):
@@ -1057,6 +1057,8 @@
     put_sides(mixed_t_ref, mixed_ref[...])
     put_sides(a2_ref, a2)
     q_ref[...] = dot(a2, weight(1), (1, 0)).astype(BF)
+    lane = lax.broadcasted_iota(jnp.int32, (TILE, PAIR), 1)
+    inverses = jnp.zeros((TILE, PAIR), F32)
     for pair in range(PAIRS):
         columns = slice(pair * PAIR, (pair + 1) * PAIR)
         k = kv_ref[0, :, columns]
@@ -1066,11 +1068,13 @@
             q = lanes_of(q_ref[:, columns] * BF(HD ** -0.5), half)
             s = dot(q, k, (1, 1))
             e = jnp.exp(s - jnp.max(s, axis=1, keepdims=True))
-            p = (e * (1.0 / jnp.sum(e, axis=1, keepdims=True))).astype(BF)
-            p_ref[2 * pair + half] = p
-            mixed.append(dot(p, v, (1, 0)))
-        lane = lax.broadcasted_iota(jnp.int32, mixed[0].shape, 1)
+            inverse = 1.0 / jnp.sum(e, axis=1, keepdims=True)
+            low = e.astype(BF)
+            p_ref[2 * pair + half] = low
+            inverses = jnp.where(lane == 2 * pair + half, inverse, inverses)
+            mixed.append(dot(low, v, (1, 0)) * inverse)
         o_scr[:, columns] = jnp.where(lane < HD, mixed[0], mixed[1]).astype(BF)
+    inv_ref[...] = inverses
     put_sides(o_ref, o_scr[...])
     x2 = x1_ref[...] + dot(o_scr[...], weight(4), (1, 0))
     x2_ref[...] = x2
@@ -1102,6 +1106,8 @@
             turned_block(),
             sided_block(),
             pl.BlockSpec((2, D // 2, enc), lambda i: (0, 0, 0)),
+            row_block(),
+            row_block(PAIR),
         ]
         + weight_outs,
         out_shape=[
@@ -1116,9 +1122,11 @@
             turned,
             sided,
             jax.ShapeDtypeStruct((2, D // 2, enc), BF),
+            low,
+            jax.ShapeDtypeStruct((count, PAIR), F32),
         ]
         + weight_shapes,
-        scratch_shapes=scratch + [pltpu.VMEM((TILE, D), BF)],
+        scratch_shapes=scratch,
         compiler_params=params(),
         cost_estimate=cost(30),
         name="middle",
@@ -1126,7 +1134,7 @@
     return results + [[weight.reshape(D, D) for weight in (w1, w2, w3, w4, w5)]]
 
 
-def middle_back_kernel(dy_ref, da3_ref, x2_ref, x1_ref, q_ref, p_ref, kv_ref, gain_two_ref, gain_three_ref, wc_ref, wq_ref,
+def middle_back_kernel(dy_ref, da3_ref, x2_ref, x1_ref, q_ref, o_ref, inv_ref, p_ref, kv_ref, gain_two_ref, gain_three_ref, wc_ref, wq_ref,
                        wo_ref, *refs):
     before = refs[:-9]
     low2_ref, dq_ref, dx1_ref, low1_ref, do1_ref, dkv_ref, sums_ref, gains_ref, do_ref = refs[-9:]
@@ -1145,24 +1153,26 @@
     low2 = dx2.astype(BF)
     low2_ref[...] = low2
     do_ref[...] = dot(low2, wo_ref[...], (1, 1)).astype(BF)
-    scale = BF(HD ** -0.5)
+    lane = lax.broadcasted_iota(jnp.int32, (TILE, PAIR), 1)
     for pair in range(PAIRS):
         columns = slice(pair * PAIR, (pair + 1) * PAIR)
-        k = kv_ref[0, :, columns] * scale
+        k = kv_ref[0, :, columns]
         v = kv_ref[1, :, columns]
-        dq = None
+        inverse = jnp.where(lane < HD, inv_ref[:, 2 * pair:2 * pair + 1], inv_ref[:, 2 * pair + 1:2 * pair + 2])
+        do = (do_ref[:, columns].astype(F32) * inverse).astype(BF)
+        drops = do.astype(F32) * o_ref[:, columns].astype(F32)
+        q_left, do_left = (q_ref[:, columns] * BF(HD ** -0.5)).T, do.T
+        parts = []
         for half in range(2):
-            do = lanes_of(do_ref[:, columns], half)
-            q = lanes_of(q_ref[:, columns] * scale, half)
+            rows = slice(half * HD, (half + 1) * HD)
+            places = slice(pair * PAIR + half * HD, pair * PAIR + (half + 1) * HD)
             low = p_ref[2 * pair + half]
-            p = low.astype(F32)
-            pull = p * dot(do, v, (1, 1))
-            down = (pull - p * jnp.sum(pull, axis=1, keepdims=True)).astype(BF)
-            part = dot(down, lanes_of(k, half), (1, 0))
-            dq = part if dq is None else dq + part
-            dk_acc[:, columns] += dot(down, q, (0, 0))
-            dv_acc[:, columns] += dot(low, do, (0, 0))
-        dq_ref[:, columns] = dq.astype(BF)
+            drop = jnp.sum(lanes_of(drops, half), axis=1, keepdims=True)
+            down = (low.astype(F32) * (dot(lanes_of(do, half), v, (1, 1)) - drop)).astype(BF)
+            parts.append(dot(down, k, (1, 0)))
+            dk_acc[places] += dot(q_left[rows], down, (1, 0))
+            dv_acc[places] += dot(do_left[rows], low, (1, 0))
+        dq_ref[:, columns] = (jnp.where(lane < HD, parts[0], parts[1]) * (HD ** -0.5)).astype(BF)
     da2 = dot(dq_ref[...], wq_ref[...], (1, 1))
     back, terms = norm_back(x1_ref[...], gain_two_ref[...], da2)
     gains_ref[0] += terms
@@ -1174,34 +1184,37 @@
 
     @pl.when(step == pl.num_programs(0) - 1)
     def _():
-        dkv_ref[0] = dk_acc[...].astype(BF)
-        dkv_ref[1] = dv_acc[...].astype(BF)
-
-
-def middle_back(first, blocks, low_up, grad_three, after_two, after_one, query_two, probs_two, kv_two, gain_two, gain_three,
-                w_comb_one, w_query_two, w_comb_two, before=None):
+        dkv_ref[0] = dk_acc[...].T.astype(BF)
+        dkv_ref[1] = dv_acc[...].T.astype(BF)
+
+
+def middle_back(first, blocks, low_up, grad_three, after_two, after_one, query_two, mixed_two, inverse_two, expos_two,
+                kv_two, gain_two, gain_three, w_comb_one, w_query_two, w_comb_two, before=None):
     count = low_up.shape[0]
     enc = kv_two.shape[1]
     low = jax.ShapeDtypeStruct((count, D), BF)
     wide = jax.ShapeDtypeStruct((count, D), F32)
     rows = pl.BlockSpec((TILE, D), lambda i: (first + i, 0))
-    sums = jax.ShapeDtypeStruct((2, enc, D), F32)
+    sums = jax.ShapeDtypeStruct((2, D, enc), F32)
     gains = jax.ShapeDtypeStruct((2, 8, D), F32)
     whole = (kv_two, gain_two, gain_three, w_comb_one, w_query_two, w_comb_two)
-    operands = (low_up, grad_three, after_two, after_one, query_two, probs_two) + whole
+    operands = (low_up, grad_three, after_two, after_one, query_two, mixed_two, inverse_two, expos_two) + whole
     more = [] if before is None else list(before[:5]) + list(before[6:])
     aliases = {} if before is None else {len(operands) + index: index for index in range(5)}
     return pl.pallas_call(
         middle_back_kernel,
         grid=(blocks,),
-        in_specs=[rows] * 5
-        + [pl.BlockSpec((HEADS, TILE, enc), lambda i: (0, first + i, 0))]
+        in_specs=[rows] * 6
+        + [
+            pl.BlockSpec((TILE, PAIR), lambda i: (first + i, 0)),
+            pl.BlockSpec((HEADS, TILE, enc), lambda i: (0, first + i, 0)),
+        ]
         + [whole_block(value) for value in whole]
         + ([] if before is None else [pl.BlockSpec(memory_space=pl.ANY)] * 5 + [whole_block(sums), whole_block(gains)]),
         out_specs=[rows] * 5
         + [
             pl.BlockSpec((2, enc, D), lambda i: (0, 0, 0)),
-            pl.BlockSpec((2, enc, D), lambda i: (0, 0, 0)),
+            pl.BlockSpec((2, D, enc), lambda i: (0, 0, 0)),
             pl.BlockSpec((2, 8, D), lambda i: (0, 0, 0)),
         ],
         out_shape=[low, low, wide, low, low, jax.ShapeDtypeStruct((2, enc, D), BF), sums, gains],
@@ -1216,15 +1229,16 @@
 def leave_kernel(parts, plan_ref, x_ref, dx1_ref, *refs):
     grads = refs[:3 * parts]
     gain_ref, wq_ref, wk_ref, wv_ref, out_ref, gains_ref = refs[3 * parts:]
-    width = D // parts
 
     @pl.when(pl.program_id(0) == 0)
     def _():
         gains_ref[...] = jnp.zeros_like(gains_ref)
 
     da = None
+    end = 0
     for index in range(parts):
-        columns = slice(index * width, (index + 1) * width)
+        columns = slice(end, end + grads[3 * index].shape[1])
+        end = columns.stop
         for which, w_ref in enumerate((wq_ref, wk_ref, wv_ref)):
             part = dot(grads[3 * index + which][...], w_ref[:, columns], (1, 1))
             da = part if da is None else da + part
@@ -1255,6 +1269,54 @@
         cost_estimate=cost(2),
         name="leave",
     )(plan, stream_low, grad_after_one, *flat, gain, *weights)
+
+
+def update_kernel(count, lows, factor_ref, *refs):
+    ins = refs[:4 * count]
+    outs = refs[4 * count:7 * count + lows]
+    held = refs[7 * count + lows:11 * count + lows]
+    ready = refs[11 * count + lows:14 * count + 2 * lows]
+    in_sems, out_sems = refs[14 * count + 2 * lows:]
+    arrivals = [pltpu.make_async_copy(ref, kept, in_sems.at[n]) for n, (ref, kept) in enumerate(zip(ins, held))]
+    departures = [pltpu.make_async_copy(kept, ref, out_sems.at[n]) for n, (ref, kept) in enumerate(zip(outs, ready))]
+    for index in range(count):
+        for group in range(4):
+            arrivals[group * count + index].start()
+    factor = factor_ref[0]
+    for index in range(count):
+        for group in range(4):
+            arrivals[group * count + index].wait()
+        weight, first, second, grad = (held[group * count + index] for group in range(4))
+        states = adam(weight[...], first[...], second[...], grad[...] * factor, RATES[index])
+        for place, value in enumerate(states):
+            ready[3 * index + place][...] = value
+            departures[3 * index + place].start()
+        if index < lows:
+            ready[3 * count + index][...] = states[0].astype(BF)
+            departures[3 * count + index].start()
+    for copy in departures:
+        copy.wait()
+
+
+def update(factor, weights, firsts, seconds, grads, lows=4):
+    count = len(weights)
+    operands = tuple(weights) + tuple(firsts) + tuple(seconds) + tuple(grads)
+    shapes = [jax.ShapeDtypeStruct(weight.shape, F32) for weight in weights for _ in range(3)]
+    shapes += [jax.ShapeDtypeStruct(weight.shape, BF) for weight in weights[:lows]]
+    anywhere = pl.BlockSpec(memory_space=pl.ANY)
+    outs = pl.pallas_call(
+        functools.partial(update_kernel, count, lows),
+        in_specs=[pl.BlockSpec(memory_space=pltpu.SMEM)] + [anywhere] * len(operands),
+        out_specs=[anywhere] * len(shapes),
+        out_shape=shapes,
+        scratch_shapes=[pltpu.VMEM(value.shape, F32) for value in operands]
+        + [pltpu.VMEM(shape.shape, shape.dtype) for shape in shapes]
+        + [pltpu.SemaphoreType.DMA((len(operands),)), pltpu.SemaphoreType.DMA((len(shapes),))],
+        compiler_params=params(),
+        cost_estimate=cost(5),
+        name="update",
+    )(factor.reshape(1), *operands)
+    return [outs[3 * index:3 * index + 3] for index in range(count)], outs[3 * count:]
 
 
 SIDE = 2
@@ -1556,17 +1618,19 @@
     buckets = distance_buckets(flipped_table, starts, prompt, size)
     slots = piece_slots(place)
 
-    shard_mid, far_line_qkv, prompt_states, starts = tie(shard_mid, far_line_qkv, prompt_states, starts)
+    far_line_qkv, starts = tie(far_line_qkv, starts)
     near_line_qkv = send(jnp.stack([shard_qkv, far_line_qkv]), line_near)
+    near_line_qkv, prompt_states, shard_mid = tie(near_line_qkv, prompt_states, shard_mid)
     far_line_mid = send(shard_mid, line_far)
     prompt_rows, branch_rows, prompt_up, branch_up, encoder = swap_halves(
         [prompt_states, branch_states, prompt_cotangent, branch_cotangent, encoder_states], core
     )
     own_qkv = put_in_line(shard_qkv, far_line_qkv, near_line_qkv, z)
     near_qkv = send(own_qkv, first_flip)
-    near_qkv, own_qkv, far_line_mid = tie(near_qkv, own_qkv, far_line_mid)
+    near_qkv, own_qkv = tie(near_qkv, own_qkv)
     close_qkv = jnp.stack([own_qkv, near_qkv])
     far_qkv = send(close_qkv, second_flip)
+    close_qkv, far_line_mid = tie(close_qkv, far_line_mid)
     near_line_mid = send(jnp.stack([shard_mid, far_line_mid]), line_near)
     close_qkv_two = send(close_qkv, core_flip)
     base, branch = bias_rows(flipped_bias, starts, prompt, size)
@@ -1591,7 +1655,7 @@
     far_line_con = send(shard_con, line_far)
     close_mid_two = send(close_mid, core_flip)
     qkv, close_mid = tie(qkv, close_mid)
-    most = 5 * PAIRS // 8
+    most = PAIRS // 2
     heads = self_forward(qkv, base, branch, starts, prompt, size, 0, most)
     *heads, qkv, far_mid, close_mid_two, near_line_exp, far_line_con = tie(
         *heads, qkv, far_mid, close_mid_two, near_line_exp, far_line_con
@@ -1610,8 +1674,8 @@
     own_con = put_in_line(shard_con, far_line_con, near_line_con, z)
     near_con = send(own_con, first_flip)
     mixed_one, close_exp, own_con = tie(mixed_one, close_exp, own_con)
-    (after_one, after_two, turned_two, input_three, query_two, turned_mixed_two, probs_two, kv_two, turned_three,
-     turned_mixed_one, turned_encoder, weights_mid) = middle(
+    (after_one, after_two, turned_two, input_three, query_two, turned_mixed_two, expos_two, kv_two, turned_three,
+     turned_mixed_one, turned_encoder, mixed_two, inverse_two, weights_mid) = middle(
         stream_low,
         [mixed_one],
         gain_rows[1],
@@ -1650,7 +1714,9 @@
             after_two,
             after_one,
             query_two,
-            probs_two,
+            mixed_two,
+            inverse_two,
+            expos_two,
             kv_two,
             gain_rows[1],
             gain_rows[2],
@@ -1691,18 +1757,16 @@
 
     half = PAIRS // 2
 
-    def attend_back(index, *values):
-        part = self_backward(
-            qkv, grad_mixed_one, mixed_one, expos, inverse, prompt, size, index * half, half
-        )
+    def attend_back(first, pairs, *values):
+        part = self_backward(qkv, grad_mixed_one, mixed_one, expos, inverse, prompt, size, first, pairs)
         first, *rest = tie(part[0], grad_mixed_one, *values)
         return ((first,) + tuple(part[1:]), *rest)
 
-    def jobs_of(part):
-        return [(0, part[i]) for i in range(3)]
+    def jobs_of(*parts):
+        return [(0, [part[i] for part in parts] if len(parts) > 1 else parts[0][i]) for i in range(3)]
 
     part_one, grad_mixed_one, got_mid, other_encoder, got_near_con, got_near_exp = attend_back(
-        0, got_mid, other_encoder, got_near_con, got_near_exp
+        0, half, got_mid, other_encoder, got_near_con, got_near_exp
     )
     line_exp, away_exp = line_split(plus(plus(stay_exp[0], got_exp[0]), got_near_exp), place)
     got_line_exp = send(away_exp, line_near)
@@ -1715,22 +1779,29 @@
     got_one = send(away_one, core_flip)
     grad_mixed_one, away_one = tie(grad_mixed_one, away_one)
 
-    part_two, grad_mixed_one, got_one, got_mid, got_line_exp, got_line_con, away_plan = attend_back(
-        1, got_one, got_mid, got_line_exp, got_line_con, away_plan
-    )
-    away_two = weight_part(away_plan, [turned_one], jobs_of(part_two))
-    got_two = send(away_two, core_flip)
+    part_two, grad_mixed_one, got_one, got_mid, got_line_exp, got_line_con = attend_back(
+        half, half // 2, got_one, got_mid, got_line_exp, got_line_con
+    )
     near_mid = plus(stay_mid[1], got_mid[1])
     got_near_mid = send(near_mid, first_flip)
     last_exp = plus(line_exp[1], got_line_exp[1])
     got_last_exp = send(last_exp, line_far)
-    keep_plan, away_two, near_mid, last_exp = tie(keep_plan, away_two, near_mid, last_exp)
+    grad_mixed_one, near_mid, last_exp = tie(grad_mixed_one, near_mid, last_exp)
+
+    part_three, grad_mixed_one, got_near_mid, got_last_exp, away_plan = attend_back(
+        half + half // 2, half // 2, got_near_mid, got_last_exp, away_plan
+    )
+    away_two = weight_part(away_plan, [turned_one], jobs_of(part_two, part_three))
+    got_two = send(away_two, core_flip)
+    line_mid, away_mid = line_split(plus(plus(stay_mid[0], got_mid[0]), got_near_mid), place)
+    got_line_mid = send(away_mid, line_near)
+    keep_plan, away_two, away_mid = tie(keep_plan, away_two, away_mid)
     away_one, stay_one = weight_part(keep_plan, [turned_one], jobs_of(part_one), got_one)
     got_one = send(away_one, second_flip)
     leave_values = (
         stream_low,
         grad_after_one,
-        [part_one[:3], part_two[:3]],
+        [part_one[:3], part_two[:3], part_three[:3]],
         gain_rows[0],
         w_query,
         w_key,
@@ -1743,33 +1814,34 @@
 
     theirs_plan, away_one, got_two = tie(theirs_plan, away_one, got_two)
     theirs_grad, gain_one = leave(theirs_plan, blocks + 1, *leave_values)
-    theirs_grad, got_one, got_near_mid, got_last_exp, keep_plan = tie(
-        theirs_grad, got_one, got_near_mid, got_last_exp, keep_plan
-    )
+    theirs_grad, got_one, got_line_mid, keep_plan = tie(theirs_grad, got_one, got_line_mid, keep_plan)
+    away_two, stay_two = weight_part(keep_plan, [turned_one], jobs_of(part_two, part_three), got_two)
+    got_two = send(away_two, second_flip)
+    away_two, stay_one, stay_mid, theirs_grad = tie(away_two, stay_one, stay_mid, theirs_grad)
     near_one = plus(stay_one[1], got_one[1])
     got_near_one = send(near_one, first_flip)
-    line_mid, away_mid = line_split(plus(plus(stay_mid[0], got_mid[0]), got_near_mid), place)
-    got_line_mid = send(away_mid, line_near)
+    last_mid = plus(line_mid[1], got_line_mid[1])
+    got_last_mid = send(last_mid, line_far)
     last_con = plus(line_con[1], got_line_con[1])
     got_last_con = send(last_con, line_far)
-    keep_plan, near_one, away_mid, last_con = tie(keep_plan, near_one, away_mid, last_con)
-    away_two, stay_two = weight_part(keep_plan, [turned_one], jobs_of(part_two), got_two)
-    got_two = send(away_two, second_flip)
-    got_grad = send(theirs_grad, core_flip)
-    ours_plan, away_two, got_near_one, got_line_mid, got_last_con = tie(
-        ours_plan, away_two, got_near_one, got_line_mid, got_last_con
-    )
+    ours_plan, near_one, last_mid, last_con = tie(ours_plan, near_one, last_mid, last_con)
+    ours_grad, gain_more = leave(ours_plan, blocks, *leave_values)
+    ours_grad, got_two, got_near_one = tie(ours_grad, got_two, got_near_one)
+    near_two = plus(stay_two[1], got_two[1])
+    got_near_two = send(near_two, first_flip)
     line_one, away_one = line_split(plus(plus(stay_one[0], got_one[0]), got_near_one), place)
     got_line_one = send(away_one, line_near)
-    last_mid = plus(line_mid[1], got_line_mid[1])
-    got_last_mid = send(last_mid, line_far)
-    ours_plan, away_one, last_mid = tie(ours_plan, away_one, last_mid)
-    ours_grad, gain_more = leave(ours_plan, blocks, *leave_values)
-    ours_grad, got_two, got_line_one, got_grad = tie(ours_grad, got_two, got_line_one, got_grad)
-    near_two = plus(stay_two[1], got_two[1])
-    got_near_two = send(near_two, first_flip)
-    last_one = plus(line_one[1], got_line_one[1])
-    got_last_one = send(last_one, line_far)
+    got_grad = send(theirs_grad, core_flip)
+    half_rows = prompt // 2
+    whole_output = both_groups(own_output, other_output, core)
+    prompt_output, branch_output = whole_output[:, :half_rows], whole_output[:, half_rows:]
+    encoder_out = both_groups(own_encoder, other_encoder, core)
+    got_near_two, got_line_one, got_last_mid, got_last_con, prompt_output, branch_output, encoder_out = tie(
+        got_near_two, got_line_one, got_last_mid, got_last_con, prompt_output, branch_output, encoder_out
+    )
+    line_two, away_two = line_split(plus(plus(stay_two[0], got_two[0]), got_near_two), place)
+    got_line_two = send(away_two, line_near)
+    got_last_one = send(plus(line_one[1], got_line_one[1]), line_far)
 
     def owned_part(line, got_line, got_last):
         return line[0].astype(F32) + got_line[0].astype(F32) + got_last.astype(F32)
@@ -1780,29 +1852,21 @@
     owned_exp = owned_part(line_exp, got_line_exp, got_last_exp)
     owned_con = owned_part(line_con, got_line_con, got_last_con)[0]
     squares = square(owned_exp) + square(owned_con)
-    half_rows = prompt // 2
     prompt_grad = both_groups(ours_grad, got_grad[:half_rows], core)
+    squares, got_line_two, got_last_one, prompt_grad = tie(squares, got_line_two, got_last_one, prompt_grad)
+    got_last_two = send(plus(line_two[1], got_line_two[1]), line_far)
+    owned_mid = owned_part(line_mid, got_line_mid, got_last_mid)
+    owned_one = owned_part(line_one, got_line_one, got_last_one)
+    squares = squares + square(owned_mid) + square(owned_one)
+    grad_bias = bias_gradient(
+        jnp.concatenate([part_one[3], part_two[3], part_three[3]]),
+        jnp.concatenate([part_one[4], part_two[4], part_three[4]]),
+        buckets,
+    )
     own_branch = lax.dynamic_slice_in_dim(theirs_grad, half_rows + core * size, size, 0)
     other_branch = lax.dynamic_slice_in_dim(got_grad, half_rows + core * size, size, 0)
     branch_grad = both_groups(own_branch, other_branch, core)
-    squares, got_near_two, prompt_grad, branch_grad = tie(squares, got_near_two, prompt_grad, branch_grad)
-    line_two, away_two = line_split(plus(plus(stay_two[0], got_two[0]), got_near_two), place)
-    got_line_two = send(away_two, line_near)
-    whole_output = both_groups(own_output, other_output, core)
-    prompt_output, branch_output = whole_output[:, :half_rows], whole_output[:, half_rows:]
-    encoder_out = both_groups(own_encoder, other_encoder, core)
-    owned_mid = owned_part(line_mid, got_line_mid, got_last_mid)
-    squares = squares + square(owned_mid)
-    squares, got_line_two, prompt_output, branch_output, encoder_out = tie(
-        squares, got_line_two, prompt_output, branch_output, encoder_out
-    )
-    got_last_two = send(plus(line_two[1], got_line_two[1]), line_far)
-    grad_bias = bias_gradient(
-        jnp.concatenate([part_one[3], part_two[3]]), jnp.concatenate([part_one[4], part_two[4]]), buckets
-    )
-    owned_one = owned_part(line_one, got_line_one, got_last_one)
-    squares = squares + square(owned_one)
-    squares, grad_bias, got_last_two = tie(squares, grad_bias, got_last_two)
+    squares, grad_bias, got_last_two, branch_grad = tie(squares, grad_bias, got_last_two, branch_grad)
     owned_two = owned_part(line_two, got_line_two, got_last_two)
     squares = squares + square(owned_two)
     owned_self = jnp.concatenate([owned_one, owned_two], axis=2)
@@ -1835,11 +1899,8 @@
         gains_second,
         bias_second,
     )
-    grads = owned + (gain_total, bias_total)
-    states = [
-        adam(weights[index], firsts[index], seconds[index], grads[index] * factor, RATES[index])
-        for index in range(6)
-    ]
+    states, copies = update(factor, weights[:5], firsts[:5], seconds[:5], owned + (gain_total,))
+    states.append(adam(weights[5], firsts[5], seconds[5], bias_total * factor, RATES[5]))
     branch_shape = (2, 1, size, D)
     return (
         prompt_output,
@@ -1854,10 +1915,10 @@
         *states[3],
         *states[4],
         *states[5],
-        states[0][0].astype(BF),
-        states[1][0].astype(BF),
-        states[2][0].astype(BF),
-        states[3][0].astype(BF),
+        copies[0],
+        copies[1],
+        copies[2],
+        copies[3],
     )
 
 

time: 699 us -> 678 us (0.970)
  Pallas kernels: 422 us -> 414 us
    convert_element_type x4 -> x0, other arithmetic: 8.73 us -> none  [the longest x1 3.07 us: paired_body(): states[2][0].astype(BF)]
    pallas_call x2, Pallas kernels: 58.6 us -> 50 us  [self_forward(): pl.pallas_call(functools.partial(self_kernel, prompt, size, len(more)), g...]
    pallas_call x2 -> x3, Pallas kernels: 61.2 us -> 64.7 us  [self_backward(): pl.pallas_call(functools.partial(self_back_kernel, prompt, size), grid=(p...]
    pallas_call x2 -> x3, Pallas kernels: 57.8 us -> 55.1 us  [the longest x2 49.3 us: middle_back(): pl.pallas_call(middle_back_kernel, grid=(blocks,), in_specs=[rows] * 6 +...]
  transfers between devices with their start and end apart: 61 -> 61, of which waited for: 21 -> 21; matrix products, arithmetic and copies ran while one was open for 11% -> 12% of each run, Pallas kernels for 44% -> 43%
where the time goes in v1:
time: 678 us; the launch traced here: 667 us
  Pallas kernels  414 us (61%)
  other arithmetic  77.4 us (11%)
  waiting for transfers between devices  76.3 us (11%)
  starting transfers between devices  54.7 us (8%)
  local copies, waits for them, and re-layouts  25.9 us (4%)
  between operations  13.7 us (2%)
    pallas_call x1, Pallas kernels, mlp(): pl.pallas_call(mlp_kernel, grid_spec=pltpu.PrefetchScalarGridSpec(num_sca...  91.3 us
    ppermute x61, waiting for transfers between devices, send(): return lax.ppermute(value, AXES, moves(rule))  76.3 us
    pallas_call x3, Pallas kernels, self_backward(): pl.pallas_call(functools.partial(self_back_kernel, prompt, size), grid=(p...  64.7 us
    ppermute x61, starting transfers between devices, send(): return lax.ppermute(value, AXES, moves(rule))  54.7 us
    pallas_call x6, Pallas kernels, weight_part(): pl.pallas_call(functools.partial(part_kernel, [left for left, _ in jobs],...  51.5 us
    pallas_call x2, Pallas kernels, self_forward(): pl.pallas_call(functools.partial(self_kernel, prompt, size, len(more)), g...  50 us
    pallas_call x2, Pallas kernels, middle_back(): pl.pallas_call(middle_back_kernel, grid=(blocks,), in_specs=[rows] * 6 +...  49.3 us
    pallas_call x1, Pallas kernels, middle(): pl.pallas_call(functools.partial(middle_kernel, len(mixed)), grid=(count...  33.2 us
  transfers between devices with their start and end apart: 61, of which 21 were waited for; matrix products, arithmetic and copies ran while one was open for 12% of the time, Pallas kernels for 43%

profile of v1, /device:TPU:0, one launch (start us, length us, event | category | flops | bytes accessed | tf_op | source)
XLA Modules:
  0.0 666.9 jit_solution(9667432133219364489)
XLA Ops:
  2.0 4.1 collective-permute-start
  11.2 4.0 collective-permute-done.far
  16.1 9.5 %collective-permute-done.2.near = bf16[2,3,32,1024]{3,2,1,0:T(8,128)(2,1)S(1)} collective-permute-done((bf16[2,3,32,1024]{3,2,1,0:T(8,128)(2,1)S(1)}, bf16[2,3,32,1024]{3,2,1,0:T(8,128)(2,1)S(1)}, u32[]{:S(2)}, u32[]{:S(2)}) %collective-permute-start.2) | collective-permute-done | bytes 393248 | tf_op jit(solution)/shard_map/ppermute | solution.py:1337
  37.8 3.4 collective-permute-start.4
  42.1 3.1 collective-permute-done.3
  47.8 8.5 %collective-permute-done.4.far = bf16[5,32,1024]{2,1,0:T(8,128)(2,1)S(1)} collective-permute-done((bf16[5,32,1024]{2,1,0:T(8,128)(2,1)S(1)}, bf16[5,32,1024]{2,1,0:T(8,128)(2,1)S(1)}, u32[]{:S(2)}, u32[]{:S(2)}) %collective-permute-start.4) | collective-permute-done | bytes 327712 | tf_op jit(solution)/shard_map/ppermute | solution.py:1337
  57.2 3.1 broadcast_select_fusion.1
  65.1 7.8 %collective-permute-done.6.near = bf16[2,5,32,1024]{3,2,1,0:T(8,128)(2,1)S(1)} collective-permute-done((bf16[2,5,32,1024]{3,2,1,0:T(8,128)(2,1)S(1)}, bf16[2,5,32,1024]{3,2,1,0:T(8,128)(2,1)S(1)}, u32[]{:S(2)}, u32[]{:S(2)}) %collective-permute-start.6) | collective-permute-done | bytes 655392 | tf_op jit(solution)/shard_map/ppermute | solution.py:1337
  75.2 2.9 collective-permute-start.11
  79.5 17.1 %enter.1 = (bf16[2,512,1280]{2,1,0:T(8,128)(2,1)}, bf16[3,1280,1024]{2,1,0:T(8,128)(2,1)}, bf16[4,4,2,32,1024]{4,3,2,1,0:T(8,128)(2,1)}, bf16[4,4,2,32,1024]{4,3...) custom-call(s32[8,2]{1,0:T(8,128)} %stack.281.slots_ref, bf16[2,3,4,32,1024]{4,3,2,1,0:T(8,128)(2,1)} %copy-done.5, ...), custom_call_target="tpu_custom_call" | custom-call | flops 12 | bytes 1 | tf_op jit(solution)/shard_map/enter/pallas_call | solution.py:1015
  96.6 3.0 pad_maximum_fusion.4.refs_0_
  100.4 1.8 collective-permute-start.14
  102.5 24.9 %self_forward.2 = (bf16[1280,1024]{1,0:T(8,128)(2,1)}, bf16[16,256,3712]{2,1,0:T(8,128)(2,1)}, f32[1280,1024]{1,0:T(8,128)}) custom-call(s32[2]{0:T(128)} %copy-done.42, bf16[3,1280,1024]{2,1,0:T(8,128)(2,1)} %get-tuple-element.290.q_ref.k_ref.v_ref, bf16[3,1280,1024]{2,1,0:T(8,128)(2,1)} %get-tuple-element.290.q_ref.k_ref.v_ref, ...), custom_call_target="tpu_custom_call" | custom-call | flops 24 | bytes 1 | tf_op jit(solution)/shard_map/self_forward/pallas_call | solution.py:605
  127.5 4.1 collective-permute-done.12.refs_2_
  132.9 1.8 collective-permute-start.18
  134.7 25.1 %self_forward.3 = (bf16[1280,1024]{1,0:T(8,128)(2,1)}, bf16[16,256,3712]{2,1,0:T(8,128)(2,1)}, f32[1280,1024]{1,0:T(8,128)}) custom-call(s32[2]{0:T(128)} %copy-done.42, bf16[3,1280,1024]{2,1,0:T(8,128)(2,1)} %get-tuple-element.290.q_ref.k_ref.v_ref, ...), custom_call_target="tpu_custom_call", output_to_operand_aliasing={{0}: (6, {}), {1}: (7, {}), {2}: (8, {})} | custom-call | flops 24 | bytes 1 | tf_op jit(solution)/shard_map/self_forward/pallas_call | solution.py:605
  161.6 2.1 pad_maximum_fusion.1.refs_0_
  166.8 33.2 %middle.1 = (f32[1280,1024]{1,0:T(8,128)}, f32[1280,1024]{1,0:T(8,128)}, bf16[2,512,1280]{2,1,0:T(8,128)(2,1)}, bf16[1280,1024]{1,0:T(8,128)(2,1)}, bf16[1280,10...) custom-call(s32[8,2]{1,0:T(8,128)} %stack.281.slots_ref, ...), custom_call_target="tpu_custom_call" | custom-call | flops 30 | bytes 1 | tf_op jit(solution)/shard_map/middle/pallas_call | solution.py:1095
  200.0 6.1 collective-permute-done.19.refs_2_
  208.9 2.7 collective-permute-done.22.refs_3_
  211.6 8.0 %assemble.2 = (bf16[4,4,2,32,2816]{4,3,2,1,0:T(8,128)(2,1)}, bf16[4,4,2,32,2816]{4,3,2,1,0:T(8,128)(2,1)}) custom-call(s32[8,2]{1,0:T(8,128)S(1)} %copy-done.4, bf16[2,2,4,32,2816]{4,3,2,1,0:T(8,128)(2,1)S(1)} %pad_maximum_fusion.1.refs_0_, bf16[2,2,4,32,2816]{4,3,2,1,0:T(8,128)(2,1)} %collective-permute-done.21.refs_1_, ...), custom_call_target="tpu_custom_call" | custom-call | flops 4 | bytes 1 | tf_op jit(solution)/shard_map/assemble/pallas_call | solution.py:1422
  219.6 6.8 %collective-permute-done.23.refs_2_ = bf16[2,1,4,88,1024]{4,3,2,1,0:T(8,128)(2,1)S(1)} collective-permute-done((bf16[2,1,4,88,1024]{4,3,2,1,0:T(8,128)(2,1)S(1)}, bf16[2,1,4,88,1024]{4,3,2,1,0:T(8,128)(2,1)S(1)}, u32[]{:S(2)}, u32[]{:S(2)}) %collective-permute-start.23) | collective-permute-done | bytes 1441824 | tf_op jit(solution)/shard_map/ppermute | solution.py:1337
  226.4 3.2 collective-permute-done.25.refs_3_
  231.2 2.5 copy-done
  233.6 91.3 %mlp.1 = (bf16[1280,1024]{1,0:T(8,128)(2,1)}, f32[1280,1024]{1,0:T(8,128)}, bf16[2,16,32,2816]{3,2,1,0:T(8,128)(2,1)}, bf16[2,16,32,2816]{3,2,1,0:T(8,128)(2,1)}...) custom-call(s32[1]{0:T(128)} %bitcast.core_ref, f32[1280,1024]{1,0:T(8,128)} %get-tuple-element.309.x_ref.x2_ref, ...), custom_call_target="tpu_custom_call" | custom-call | flops 85 | bytes 1 | tf_op jit(solution)/shard_map/mlp/pallas_call | solution.py:811
  326.1 1.8 slice.227
  329.3 13.8 %middle_back.2 = (bf16[1280,1024]{1,0:T(8,128)(2,1)}, bf16[1280,1024]{1,0:T(8,128)(2,1)}, f32[1280,1024]{1,0:T(8,128)}, bf16[1280,1024]{1,0:T(8,128)(2,1)}, bf16...) custom-call(bf16[1280,1024]{1,0:T(8,128)(2,1)} %pad_maximum_fusion.3.dy, ...), custom_call_target="tpu_custom_call" | custom-call | flops 45 | bytes 1 | tf_op jit(solution)/shard_map/middle_back/pallas_call | solution.py:1204
  343.1 9.7 %add_split.2 = (bf16[2,4,2,32,2816]{4,3,2,1,0:T(8,128)(2,1)}, bf16[2,4,2,32,2816]{4,3,2,1,0:T(8,128)(2,1)}) custom-call(s32[4]{0:T(128)} %pad_add_fusion.2.spots_ref, bf16[2,4,4,32,2816]{4,3,2,1,0:T(8,128)(2,1)} %bitcast.250, bf16[2,4,4,32,2816]{4,3,2,1,0:T(8,128)(2,1)} %bitcast.64.two_ref), custom_call_target="tpu_custom_call" | custom-call | flops 1 | bytes 1 | tf_op jit(solution)/shard_map/add_split/pallas_call | solution.py:1472
  353.3 7.6 %add_split.3 = (bf16[2,4,1,88,1024]{4,3,2,1,0:T(8,128)(2,1)}, bf16[2,4,1,88,1024]{4,3,2,1,0:T(8,128)(2,1)}) custom-call(s32[4]{0:T(128)} %pad_add_fusion.2.spots_ref, bf16[1,4,4,88,1024]{4,3,2,1,0:T(8,128)(2,1)} %bitcast.254, bf16[1,4,4,88,1024]{4,3,2,1,0:T(8,128)(2,1)} %bitcast.66.two_ref), custom_call_target="tpu_custom_call" | custom-call | flops 1 | bytes 1 | tf_op jit(solution)/shard_map/add_split/pallas_call | solution.py:1472
  364.2 35.5 %middle_back.3 = (bf16[1280,1024]{1,0:T(8,128)(2,1)}, bf16[1280,1024]{1,0:T(8,128)(2,1)}, f32[1280,1024]{1,0:T(8,128)}, bf16[1280,1024]{1,0:T(8,128)(2,1)}, bf16...) custom-call(bf16[1280,1024]{1,0:T(8,128)(2,1)} %pad_maximum_fusion.3, ...), custom_call_target="tpu_custom_call", output_to_operand_aliasing={{0}: (14, {}), {1}: (15, {}), {2}: (16, {}), {3}: (17, {}),... | custom-call | flops 45 | bytes 1 | tf_op jit(solution)/shard_map/middle_back/pallas_call | solution.py:1204
  399.7 2.2 slice_bitcast_fusion
  401.9 11.4 %weight_part.6 = bf16[5,16,32,1024]{3,2,1,0:T(8,128)(2,1)} custom-call(s32[5]{0:T(128)} %stack.310.plan_ref, bf16[2,512,1280]{2,1,0:T(8,128)(2,1)} %get-tuple-element.369.refs_0_, bf16[2,512,1280]{2,1,0:T(8,128)(2,1)} %get-tuple-element.370.refs_1_, bf16[2,512,256]{2,1,0:T(8,128)(2,1)} %get-tuple-element.371.refs_2_, ...), custom_call_target="tpu_custom_call" | custom-call | flops 2 | bytes 1 | tf_op jit(solution)/shard_map/weight_part/pallas_call | solution.py:884
  413.3 2.5 fusion.33
  424.5 30.7 %self_backward.3 = (bf16[1280,512]{1,0:T(8,128)(2,1)}, bf16[1280,512]{1,0:T(8,128)(2,1)}, bf16[1280,512]{1,0:T(8,128)(2,1)}, f32[8,1,1280]{2,1,0:T(1,128)}, f32[8,2,1,1152]{3,2,1,0:T(1,128)}) custom-call(bf16[3,1280,1024]{2,1,0:T(8,128)(2,1)} %get-tuple-element.290.q_ref.k_ref.v_ref, bf16[3,1280,1024]{2,1,0:T(8,128)(2,1)} %get-tuple-element.290.q_ref.k_ref.v_ref, ...), custom_call_target="tpu_custom_call" | custom-call | flops 32 | bytes 1 | tf_op jit(solution)/shard_map/self_backward/pallas_call | solution.py:701
  455.2 2.7 fusion
  458.0 12.5 %weight_part.7 = (bf16[2,4,5,32,1024]{4,3,2,1,0:T(8,128)(2,1)}, bf16[2,4,5,32,1024]{4,3,2,1,0:T(8,128)(2,1)}) custom-call(s32[5]{0:T(128)} %stack.261.plan_ref, bf16[2,512,1280]{2,1,0:T(8,128)(2,1)} %get-tuple-element.369.refs_0_, bf16[2,512,1280]{2,1,0:T(8,128)(2,1)} %get-tuple-element.370.refs_1_, bf16[2,512,256]{2,1,0:T(8,128)(2,1)} %get-tuple-element.371.refs_2_, ...), custom_call_target="tpu_custom_call" | custom-call | flops 2 | bytes 1 | tf_op jit(solution)/shard_map/weight_part/pallas_call | solution.py:884
  470.9 1.9 fusion.5
  474.6 6.1 weight_part.8
  485.5 1.8 collective-permute-start.38
  489.7 17.1 %self_backward.4 = (bf16[1280,256]{1,0:T(8,128)(2,1)}, bf16[1280,256]{1,0:T(8,128)(2,1)}, bf16[1280,256]{1,0:T(8,128)(2,1)}, f32[4,1,1280]{2,1,0:T(1,128)}, f32[4,2,1,1152]{3,2,1,0:T(1,128)}) custom-call(bf16[3,1280,1024]{2,1,0:T(8,128)(2,1)} %get-tuple-element.290.q_ref.k_ref.v_ref, bf16[3,1280,1024]{2,1,0:T(8,128)(2,1)} %get-tuple-element.290.q_ref.k_ref.v_ref, ...), custom_call_target="tpu_custom_call" | custom-call | flops 16 | bytes 1 | tf_op jit(solution)/shard_map/self_backward/pallas_call | solution.py:701
  506.8 2.9 collective-permute-done.38
  509.8 3.5 fusion.6
  515.3 1.8 fusion.17
  518.4 17.0 %self_backward.5 = (bf16[1280,256]{1,0:T(8,128)(2,1)}, bf16[1280,256]{1,0:T(8,128)(2,1)}, bf16[1280,256]{1,0:T(8,128)(2,1)}, f32[4,1,1280]{2,1,0:T(1,128)}, f32[4,2,1,1152]{3,2,1,0:T(1,128)}) custom-call(bf16[3,1280,1024]{2,1,0:T(8,128)(2,1)} %get-tuple-element.290.q_ref.k_ref.v_ref, bf16[3,1280,1024]{2,1,0:T(8,128)(2,1)} %get-tuple-element.290.q_ref.k_ref.v_ref, ...), custom_call_target="tpu_custom_call" | custom-call | flops 16 | bytes 1 | tf_op jit(solution)/shard_map/self_backward/pallas_call | solution.py:701
  535.4 7.4 %weight_part.9 = bf16[3,16,32,512]{3,2,1,0:T(8,128)(2,1)} custom-call(s32[5]{0:T(128)} %stack.310.plan_ref, bf16[2,512,1280]{2,1,0:T(8,128)(2,1)} %get-tuple-element.395.refs_0_, bf16[1280,256]{1,0:T(8,128)(2,1)} %get-tuple-element.408.refs_1_.refs_3_, bf16[1280,256]{1,0:T(8,128)(2,1)} %get-tuple-element.409.refs_2_.refs_6_, ...), custom_call_target="tpu_custom_call" | custom-call | flops 2 | bytes 1 | tf_op jit(solution)/shard_map/weight_part/pallas_call | solution.py:884
  543.5 2.7 collective-permute-start.49
  546.2 3.0 fusion.1
  550.2 6.6 weight_part.10
  558.7 12.3 %leave.2 = (f32[768,1024]{1,0:T(8,128)}, f32[8,1024]{1,0:T(8,128)}) custom-call(s32[3]{0:T(128)} %pad_add_fusion.plan_ref, bf16[1280,1024]{1,0:T(8,128)(2,1)} %pad_maximum_fusion.2.refs_4_.x_ref, f32[1280,1024]{1,0:T(8,128)} %get-tuple-element.419.dx1_ref, bf16[1280,512]{1,0:T(8,128)(2,1)} %get-tuple-element.396.refs_1_.refs_0_, ...), custom_call_target="tpu_custom_call" | custom-call | flops 2 | bytes 1 | tf_op jit(solution)/shard_map/leave/pallas_call | solution.py:1257
  571.0 3.9 collective-permute-done.43
  574.9 7.6 %weight_part.11 = (bf16[2,4,3,32,512]{4,3,2,1,0:T(8,128)(2,1)}, bf16[2,4,3,32,512]{4,3,2,1,0:T(8,128)(2,1)}) custom-call(s32[5]{0:T(128)} %stack.261.plan_ref, bf16[2,512,1280]{2,1,0:T(8,128)(2,1)} %get-tuple-element.395.refs_0_, bf16[1280,256]{1,0:T(8,128)(2,1)} %get-tuple-element.408.refs_1_.refs_3_, bf16[1280,256]{1,0:T(8,128)(2,1)} %get-tuple-element.409.refs_2_.refs_6_, ...), custom_call_target="tpu_custom_call" | custom-call | flops 2 | bytes 1 | tf_op jit(solution)/shard_map/weight_part/pallas_call | solution.py:884
  584.5 2.0 fusion.13
  587.8 2.6 multiply_reduce_fusion
  590.4 1.8 fusion.19
  592.5 10.4 %leave.3 = (f32[512,1024]{1,0:T(8,128)}, f32[8,1024]{1,0:T(8,128)}) custom-call(s32[2]{0:T(128)} %iota_add_fusion.plan_ref, bf16[1280,1024]{1,0:T(8,128)(2,1)} %pad_maximum_fusion.2.refs_4_.x_ref, f32[1280,1024]{1,0:T(8,128)} %get-tuple-element.419.dx1_ref, bf16[1280,512]{1,0:T(8,128)(2,1)} %get-tuple-element.396.refs_1_.refs_0_, ...), custom_call_target="tpu_custom_call" | custom-call | flops 2 | bytes 1 | tf_op jit(solution)/shard_map/leave/pallas_call | solution.py:1257
  606.8 3.0 collective-permute-done.48
  609.8 4.0 collective-permute-done.47
  618.2 2.3 multiply_reduce_fusion.2
  621.8 1.9 multiply_reduce_fusion.1
  623.7 2.7 select_bitcast_fusion.1
  626.4 2.3 pad_maximum_fusion
  638.6 2.1 collective-permute-start.54
  651.0 2.0 collective-permute-done.59
  659.5 5.8 update.1
  (314 shorter events, 104.6 us)
Async XLA Ops:
  2.0 13.2 %collective-permute-start = (bf16[3,32,1024]{2,1,0:T(8,128)(2,1)S(1)}, bf16[3,32,1024]{2,1,0:T(8,128)(2,1)S(1)}, u32[]{:S(2)}, u32[]{:S(2)}) collective-permute-start(bf16[3,32,1024]{2,1,0:T(8,128)(2,1)S(1)} %get-tuple-element.693.shard), channel_id=1, source_target_pairs={{0,16},{1,17},{2,18},{3,19},{4,20},{5,21},{6,22},{7,23},{8,24},{9,... | collective-permute-start | bytes 589832 | tf_op jit(solution)/shard_map/ppermute | solution.py:1337
  7.4 1.2 collective-permute-start.1
  11.2 23.2 %copy-start.42 = (s32[2]{0:T(128)}, s32[2]{0:T(128)S(1)}, u32[]{:S(2)}) copy-start(s32[2]{0:T(128)S(1)} %pad_add_fusion.1.starts_ref) | copy-start | bytes 28
  15.2 10.4 %collective-permute-start.2 = (bf16[2,3,32,1024]{3,2,1,0:T(8,128)(2,1)S(1)}, bf16[2,3,32,1024]{3,2,1,0:T(8,128)(2,1)S(1)}, u32[]{:S(2)}, u32[]{:S(2)}) collective-permute-start(bf16[2,3,32,1024]{3,2,1,0:T(8,128)(2,1)S(1)} %pad_maximum_fusion.18), channel_id=1, source_target_pairs={{0,8},{1,9},{2,10},{3,11},{4,12},{5,13},{6,14},{7,15},{8,0},{9,1},... | collective-permute-start | bytes 1179656 | tf_op jit(solution)/shard_map/ppermute | solution.py:1337
  31.2 26.1 %collective-permute-start.8 = (bf16[1408,1024]{1,0:T(8,128)(2,1)}, bf16[1408,1024]{1,0:T(8,128)(2,1)}, u32[]{:S(2)}, u32[]{:S(2)}) collective-permute-start(bf16[1408,1024]{1,0:T(8,128)(2,1)} %get-tuple-element.682), channel_id=1, source_target_pairs={{0,1},{1,0},{2,3},{3,2},{4,5},{5,4},{6,7},{7,6},{8,9},{9,8},{10,11... | collective-permute-start | bytes 8650760 | tf_op jit(solution)/shard_map/ppermute | solution.py:1337
  33.0 12.2 %collective-permute-start.3 = (bf16[3,4,32,1024]{3,2,1,0:T(8,128)(2,1)S(1)}, bf16[3,4,32,1024]{3,2,1,0:T(8,128)(2,1)}, u32[]{:S(2)}, u32[]{:S(2)}) collective-permute-start(bf16[3,4,32,1024]{3,2,1,0:T(8,128)(2,1)S(1)} %put_in_line.4), channel_id=1, source_target_pairs={{0,2},{1,5},{2,0},{3,7},{4,6},{5,1},{6,4},{7,3},{8,10},{9,13},{10,... | collective-permute-start | bytes 2359304 | tf_op jit(solution)/shard_map/ppermute | solution.py:1337
  37.8 18.6 %collective-permute-start.4 = (bf16[5,32,1024]{2,1,0:T(8,128)(2,1)S(1)}, bf16[5,32,1024]{2,1,0:T(8,128)(2,1)S(1)}, u32[]{:S(2)}, u32[]{:S(2)}) collective-permute-start(bf16[5,32,1024]{2,1,0:T(8,128)(2,1)S(1)} %pad_maximum_fusion.21.shard), channel_id=1, source_target_pairs={{0,16},{1,17},{2,18},{3,19},{4,20},{5,21},{6,22},{7,23},{8,24},{9,... | collective-permute-start | bytes 983048 | tf_op jit(solution)/shard_map/ppermute | solution.py:1337
  46.5 26.4 %collective-permute-start.5 = (bf16[2,3,4,32,1024]{4,3,2,1,0:T(8,128)(2,1)S(1)}, bf16[2,3,4,32,1024]{4,3,2,1,0:T(8,128)(2,1)}, u32[]{:S(2)}, u32[]{:S(2)}) collective-permute-start(bf16[2,3,4,32,1024]{4,3,2,1,0:T(8,128)(2,1)S(1)} %pad_maximum_fusion.5.refs_0_), channel_id=1, source_target_pairs={{0,4},{1,3},{2,6},{3,1},{4,0},{5,7},{6,2},{7,5},{8,12},{9,11},{10,... | collective-permute-start | bytes 4718600 | tf_op jit(solution)/shard_map/ppermute | solution.py:1337
  56.4 16.5 %collective-permute-start.6 = (bf16[2,5,32,1024]{3,2,1,0:T(8,128)(2,1)S(1)}, bf16[2,5,32,1024]{3,2,1,0:T(8,128)(2,1)S(1)}, u32[]{:S(2)}, u32[]{:S(2)}) collective-permute-start(bf16[2,5,32,1024]{3,2,1,0:T(8,128)(2,1)S(1)} %pad_maximum_fusion.14), channel_id=1, source_target_pairs={{0,8},{1,9},{2,10},{3,11},{4,12},{5,13},{6,14},{7,15},{8,0},{9,1},... | collective-permute-start | bytes 1966088 | tf_op jit(solution)/shard_map/ppermute | solution.py:1337
  57.2 15.7 %collective-permute-start.7 = (bf16[2,3,4,32,1024]{4,3,2,1,0:T(8,128)(2,1)S(1)}, bf16[2,3,4,32,1024]{4,3,2,1,0:T(8,128)(2,1)S(1)}, u32[]{:S(2)}, u32[]{:S(2)}) collective-permute-start(bf16[2,3,4,32,1024]{4,3,2,1,0:T(8,128)(2,1)S(1)} %pad_maximum_fusion.5.refs_0_), channel_id=1, source_target_pairs={{0,1},{1,0},{2,3},{3,2},{4,5},{5,4},{6,7},{7,6},{8,9},{9,8},{10,11... | collective-permute-start | bytes 4718600 | tf_op jit(solution)/shard_map/ppermute | solution.py:1337
  72.9 6.6 collective-permute-start.9
  74.0 22.6 %collective-permute-start.10 = (bf16[5,4,32,1024]{3,2,1,0:T(8,128)(2,1)S(1)}, bf16[5,4,32,1024]{3,2,1,0:T(8,128)(2,1)}, u32[]{:S(2)}, u32[]{:S(2)}) collective-permute-start(bf16[5,4,32,1024]{3,2,1,0:T(8,128)(2,1)S(1)} %put_in_line.5), channel_id=1, source_target_pairs={{0,2},{1,5},{2,0},{3,7},{4,6},{5,1},{6,4},{7,3},{8,10},{9,13},{10,... | collective-permute-start | bytes 3932168 | tf_op jit(solution)/shard_map/ppermute | solution.py:1337
  75.2 21.4 %collective-permute-start.11 = (bf16[2,32,2816]{2,1,0:T(8,128)(2,1)S(1)}, bf16[2,32,2816]{2,1,0:T(8,128)(2,1)S(1)}, u32[]{:S(2)}, u32[]{:S(2)}) collective-permute-start(bf16[2,32,2816]{2,1,0:T(8,128)(2,1)S(1)} %convert_element_type.428.shard), channel_id=1, source_target_pairs={{0,16},{1,17},{2,18},{3,19},{4,20},{5,21},{6,22},{7,23},{8,24},{9,... | collective-permute-start | bytes 1081352 | tf_op jit(solution)/shard_map/ppermute | solution.py:1337
  99.7 32.0 %collective-permute-start.12 = (bf16[2,5,4,32,1024]{4,3,2,1,0:T(8,128)(2,1)}, bf16[2,5,4,32,1024]{4,3,2,1,0:T(8,128)(2,1)}, u32[]{:S(2)}, u32[]{:S(2)}) collective-permute-start(bf16[2,5,4,32,1024]{4,3,2,1,0:T(8,128)(2,1)} %pad_maximum_fusion.4.refs_0_), channel_id=1, source_target_pairs={{0,4},{1,3},{2,6},{3,1},{4,0},{5,7},{6,2},{7,5},{8,12},{9,11},{10,... | collective-permute-start | bytes 7864328 | tf_op jit(solution)/shard_map/ppermute | solution.py:1337
  100.4 31.3 %collective-permute-start.13 = (bf16[2,5,4,32,1024]{4,3,2,1,0:T(8,128)(2,1)}, bf16[2,5,4,32,1024]{4,3,2,1,0:T(8,128)(2,1)}, u32[]{:S(2)}, u32[]{:S(2)}) collective-permute-start(bf16[2,5,4,32,1024]{4,3,2,1,0:T(8,128)(2,1)} %pad_maximum_fusion.4.refs_0_), channel_id=1, source_target_pairs={{0,1},{1,0},{2,3},{3,2},{4,5},{5,4},{6,7},{7,6},{8,9},{9,8},{10,11... | collective-permute-start | bytes 7864328 | tf_op jit(solution)/shard_map/ppermute | solution.py:1337
  100.4 27.1 %collective-permute-start.14 = (bf16[2,2,32,2816]{3,2,1,0:T(8,128)(2,1)S(1)}, bf16[2,2,32,2816]{3,2,1,0:T(8,128)(2,1)S(1)}, u32[]{:S(2)}, u32[]{:S(2)}) collective-permute-start(bf16[2,2,32,2816]{3,2,1,0:T(8,128)(2,1)S(1)} %pad_maximum_fusion.12), channel_id=1, source_target_pairs={{0,8},{1,9},{2,10},{3,11},{4,12},{5,13},{6,14},{7,15},{8,0},{9,1},... | collective-permute-start | bytes 2162696 | tf_op jit(solution)/shard_map/ppermute | solution.py:1337
  102.2 25.2 %collective-permute-start.15 = (bf16[1,88,1024]{2,1,0:T(8,128)(2,1)S(1)}, bf16[1,88,1024]{2,1,0:T(8,128)(2,1)S(1)}, u32[]{:S(2)}, u32[]{:S(2)}) collective-permute-start(bf16[1,88,1024]{2,1,0:T(8,128)(2,1)S(1)} %convert_bitcast_fusion.shard), channel_id=1, source_target_pairs={{0,16},{1,17},{2,18},{3,19},{4,20},{5,21},{6,22},{7,23},{8,24},{9,... | collective-permute-start | bytes 540680 | tf_op jit(solution)/shard_map/ppermute | solution.py:1337
  131.6 28.9 %collective-permute-start.16 = (bf16[2,5,4,32,1024]{4,3,2,1,0:T(8,128)(2,1)}, bf16[2,5,4,32,1024]{4,3,2,1,0:T(8,128)(2,1)}, u32[]{:S(2)}, u32[]{:S(2)}) collective-permute-start(bf16[2,5,4,32,1024]{4,3,2,1,0:T(8,128)(2,1)} %collective-permute-done.12.refs_2_), channel_id=1, source_target_pairs={{0,1},{1,0},{2,3},{3,2},{4,5},{5,4},{6,7},{7,6},{8,9},{9,8},{10,11... | collective-permute-start | bytes 7864328 | tf_op jit(solution)/shard_map/ppermute | solution.py:1337
  132.0 27.7 %copy-start.1 = (bf16[2,4,32,2816]{3,2,1,0:T(8,128)(2,1)}, bf16[2,4,32,2816]{3,2,1,0:T(8,128)(2,1)S(1)}, u32[]{:S(2)}) copy-start(bf16[2,4,32,2816]{3,2,1,0:T(8,128)(2,1)S(1)} %put_in_line.6) | copy-start | bytes 4325380
  132.0 28.5 %collective-permute-start.17 = (bf16[2,4,32,2816]{3,2,1,0:T(8,128)(2,1)S(1)}, bf16[2,4,32,2816]{3,2,1,0:T(8,128)(2,1)S(1)}, u32[]{:S(2)}, u32[]{:S(2)}) collective-permute-start(bf16[2,4,32,2816]{3,2,1,0:T(8,128)(2,1)S(1)} %put_in_line.6), channel_id=1, source_target_pairs={{0,2},{1,5},{2,0},{3,7},{4,6},{5,1},{6,4},{7,3},{8,10},{9,13},{10,... | collective-permute-start | bytes 4325384 | tf_op jit(solution)/shard_map/ppermute | solution.py:1337
  132.9 26.9 %collective-permute-start.18 = (bf16[2,1,88,1024]{3,2,1,0:T(8,128)(2,1)S(1)}, bf16[2,1,88,1024]{3,2,1,0:T(8,128)(2,1)S(1)}, u32[]{:S(2)}, u32[]{:S(2)}) collective-permute-start(bf16[2,1,88,1024]{3,2,1,0:T(8,128)(2,1)S(1)} %pad_maximum_fusion.19), channel_id=1, source_target_pairs={{0,8},{1,9},{2,10},{3,11},{4,12},{5,13},{6,14},{7,15},{8,0},{9,1},... | collective-permute-start | bytes 1081352 | tf_op jit(solution)/shard_map/ppermute | solution.py:1337
  163.7 42.4 %collective-permute-start.19 = (bf16[2,2,4,32,2816]{4,3,2,1,0:T(8,128)(2,1)S(1)}, bf16[2,2,4,32,2816]{4,3,2,1,0:T(8,128)(2,1)}, u32[]{:S(2)}, u32[]{:S(2)}) collective-permute-start(bf16[2,2,4,32,2816]{4,3,2,1,0:T(8,128)(2,1)S(1)} %pad_maximum_fusion.1.refs_0_), channel_id=1, source_target_pairs={{0,4},{1,3},{2,6},{3,1},{4,0},{5,7},{6,2},{7,5},{8,12},{9,11},{10,... | collective-permute-start | bytes 8650760 | tf_op jit(solution)/shard_map/ppermute | solution.py:1337
  164.3 41.8 %collective-permute-start.21 = (bf16[2,2,4,32,2816]{4,3,2,1,0:T(8,128)(2,1)S(1)}, bf16[2,2,4,32,2816]{4,3,2,1,0:T(8,128)(2,1)}, u32[]{:S(2)}, u32[]{:S(2)}) collective-permute-start(bf16[2,2,4,32,2816]{4,3,2,1,0:T(8,128)(2,1)S(1)} %pad_maximum_fusion.1.refs_0_), channel_id=1, source_target_pairs={{0,1},{1,0},{2,3},{3,2},{4,5},{5,4},{6,7},{7,6},{8,9},{9,8},{10,11... | collective-permute-start | bytes 8650760 | tf_op jit(solution)/shard_map/ppermute | solution.py:1337
  165.2 34.8 %collective-permute-start.20 = (bf16[1,4,88,1024]{3,2,1,0:T(8,128)(2,1)S(1)}, bf16[1,4,88,1024]{3,2,1,0:T(8,128)(2,1)}, u32[]{:S(2)}, u32[]{:S(2)}) collective-permute-start(bf16[1,4,88,1024]{3,2,1,0:T(8,128)(2,1)S(1)} %put_in_line.7), channel_id=1, source_target_pairs={{0,2},{1,5},{2,0},{3,7},{4,6},{5,1},{6,4},{7,3},{8,10},{9,13},{10,... | collective-permute-start | bytes 2162696 | tf_op jit(solution)/shard_map/ppermute | solution.py:1337
  206.1 5.5 collective-permute-start.22
  207.3 19.1 %collective-permute-start.23 = (bf16[2,1,4,88,1024]{4,3,2,1,0:T(8,128)(2,1)S(1)}, bf16[2,1,4,88,1024]{4,3,2,1,0:T(8,128)(2,1)S(1)}, u32[]{:S(2)}, u32[]{:S(2)}) collective-permute-start(bf16[2,1,4,88,1024]{4,3,2,1,0:T(8,128)(2,1)S(1)} %pad_maximum_fusion.6.refs_0_), channel_id=1, source_target_pairs={{0,4},{1,3},{2,6},{3,1},{4,0},{5,7},{6,2},{7,5},{8,12},{9,11},{10,... | collective-permute-start | bytes 4325384 | tf_op jit(solution)/shard_map/ppermute | solution.py:1337
  207.9 18.5 %collective-permute-start.24 = (bf16[2,1,4,88,1024]{4,3,2,1,0:T(8,128)(2,1)S(1)}, bf16[2,1,4,88,1024]{4,3,2,1,0:T(8,128)(2,1)S(1)}, u32[]{:S(2)}, u32[]{:S(2)}) collective-permute-start(bf16[2,1,4,88,1024]{4,3,2,1,0:T(8,128)(2,1)S(1)} %pad_maximum_fusion.6.refs_0_), channel_id=1, source_target_pairs={{0,1},{1,0},{2,3},{3,2},{4,5},{5,4},{6,7},{7,6},{8,9},{9,8},{10,11... | collective-permute-start | bytes 4325384 | tf_op jit(solution)/shard_map/ppermute | solution.py:1337
  226.4 3.2 collective-permute-start.25
  325.0 18.1 %collective-permute-start.26 = (bf16[2,16,32,2816]{3,2,1,0:T(8,128)(2,1)}, bf16[2,16,32,2816]{3,2,1,0:T(8,128)(2,1)}, u32[]{:S(2)}, u32[]{:S(2)}) collective-permute-start(bf16[2,16,32,2816]{3,2,1,0:T(8,128)(2,1)} %get-tuple-element.324), channel_id=1, source_target_pairs={{0,1},{1,0},{2,3},{3,2},{4,5},{5,4},{6,7},{7,6},{8,9},{9,8},{10,11... | collective-permute-start | bytes 17301512 | tf_op jit(solution)/shard_map/ppermute | solution.py:1337
  325.2 17.9 %collective-permute-start.27 = (bf16[1,16,88,1024]{3,2,1,0:T(8,128)(2,1)}, bf16[1,16,88,1024]{3,2,1,0:T(8,128)(2,1)}, u32[]{:S(2)}, u32[]{:S(2)}) collective-permute-start(bf16[1,16,88,1024]{3,2,1,0:T(8,128)(2,1)} %bitcast.268), channel_id=1, source_target_pairs={{0,1},{1,0},{2,3},{3,2},{4,5},{5,4},{6,7},{7,6},{8,9},{9,8},{10,11... | collective-permute-start | bytes 8650760 | tf_op jit(solution)/shard_map/ppermute | solution.py:1337
  352.8 63.9 %collective-permute-start.29 = (bf16[2,4,2,32,2816]{4,3,2,1,0:T(8,128)(2,1)}, bf16[2,4,2,32,2816]{4,3,2,1,0:T(8,128)(2,1)}, u32[]{:S(2)}, u32[]{:S(2)}) collective-permute-start(bf16[2,4,2,32,2816]{4,3,2,1,0:T(8,128)(2,1)} %get-tuple-element.357), channel_id=1, source_target_pairs={{0,4},{1,3},{2,6},{3,1},{4,0},{5,7},{6,2},{7,5},{8,12},{9,11},{10,... | collective-permute-start | bytes 8650760 | tf_op jit(solution)/shard_map/ppermute | solution.py:1337
  360.8 55.8 %collective-permute-start.30 = (bf16[2,4,1,88,1024]{4,3,1,2,0:T(8,128)(2,1)}, bf16[2,4,1,88,1024]{4,3,1,2,0:T(8,128)(2,1)}, u32[]{:S(2)}, u32[]{:S(2)}) collective-permute-start(bf16[2,4,1,88,1024]{4,3,1,2,0:T(8,128)(2,1)} %bitcast.269), channel_id=1, source_target_pairs={{0,4},{1,3},{2,6},{3,1},{4,0},{5,7},{6,2},{7,5},{8,12},{9,11},{10,... | collective-permute-start | bytes 4325384 | tf_op jit(solution)/shard_map/ppermute | solution.py:1337
  363.6 53.0 %collective-permute-start.28 = (bf16[640,1024]{1,0:T(8,128)(2,1)}, bf16[640,1024]{1,0:T(8,128)(2,1)}, u32[]{:S(2)}, u32[]{:S(2)}) collective-permute-start(bf16[640,1024]{1,0:T(8,128)(2,1)} %pad_maximum_fusion.8), channel_id=1, source_target_pairs={{0,1},{1,0},{2,3},{3,2},{4,5},{5,4},{6,7},{7,6},{8,9},{9,8},{10,11... | collective-permute-start | bytes 3932168 | tf_op jit(solution)/shard_map/ppermute | solution.py:1337
  416.7 38.5 %collective-permute-start.31 = (bf16[5,16,32,1024]{3,2,1,0:T(8,128)(2,1)}, bf16[5,16,32,1024]{3,2,1,0:T(8,128)(2,1)}, u32[]{:S(2)}, u32[]{:S(2)}) collective-permute-start(bf16[5,16,32,1024]{3,2,1,0:T(8,128)(2,1)} %weight_part.6), channel_id=1, source_target_pairs={{0,1},{1,0},{2,3},{3,2},{4,5},{5,4},{6,7},{7,6},{8,9},{9,8},{10,11... | collective-permute-start | bytes 15728648 | tf_op jit(solution)/shard_map/ppermute | solution.py:1337
  419.3 35.9 %collective-permute-start.34 = (bf16[4,2,32,2816]{3,2,1,0:T(8,128)(2,1)S(1)}, bf16[4,2,32,2816]{3,2,1,0:T(8,128)(2,1)}, u32[]{:S(2)}, u32[]{:S(2)}) collective-permute-start(bf16[4,2,32,2816]{3,2,1,0:T(8,128)(2,1)S(1)} %fusion.3), channel_id=1, source_target_pairs={{0,2},{1,5},{2,0},{3,7},{4,6},{5,1},{6,4},{7,3},{8,10},{9,13},{10,... | collective-permute-start | bytes 4325384 | tf_op jit(solution)/shard_map/ppermute | solution.py:1337
  422.1 33.1 %collective-permute-start.33 = (bf16[4,1,88,1024]{3,2,1,0:T(8,128)(2,1)S(1)}, bf16[4,1,88,1024]{3,2,1,0:T(8,128)(2,1)}, u32[]{:S(2)}, u32[]{:S(2)}) collective-permute-start(bf16[4,1,88,1024]{3,2,1,0:T(8,128)(2,1)S(1)} %fusion.10), channel_id=1, source_target_pairs={{0,2},{1,5},{2,0},{3,7},{4,6},{5,1},{6,4},{7,3},{8,10},{9,13},{10,... | collective-permute-start | bytes 2162696 | tf_op jit(solution)/shard_map/ppermute | solution.py:1337
  423.9 31.3 %collective-permute-start.32 = (f32[128,1024]{1,0:T(8,128)}, f32[128,1024]{1,0:T(8,128)}, u32[]{:S(2)}, u32[]{:S(2)}) collective-permute-start(f32[128,1024]{1,0:T(8,128)} %get-tuple-element.671), channel_id=1, source_target_pairs={{0,1},{1,0},{2,3},{3,2},{4,5},{5,4},{6,7},{7,6},{8,9},{9,8},{10,11... | collective-permute-start | bytes 1572872 | tf_op jit(solution)/shard_map/ppermute | solution.py:1337
  470.4 39.3 %collective-permute-start.36 = (bf16[2,4,5,32,1024]{4,3,2,1,0:T(8,128)(2,1)}, bf16[2,4,5,32,1024]{4,3,2,1,0:T(8,128)(2,1)}, u32[]{:S(2)}, u32[]{:S(2)}) collective-permute-start(bf16[2,4,5,32,1024]{4,3,2,1,0:T(8,128)(2,1)} %get-tuple-element.393), channel_id=1, source_target_pairs={{0,4},{1,3},{2,6},{3,1},{4,0},{5,7},{6,2},{7,5},{8,12},{9,11},{10,... | collective-permute-start | bytes 7864328 | tf_op jit(solution)/shard_map/ppermute | solution.py:1337
  480.7 29.0 %collective-permute-start.35 = (bf16[3,16,32,512]{3,2,1,0:T(8,128)(2,1)}, bf16[3,16,32,512]{3,2,1,0:T(8,128)(2,1)}, u32[]{:S(2)}, u32[]{:S(2)}) collective-permute-start(bf16[3,16,32,512]{3,2,1,0:T(8,128)(2,1)} %weight_part.8), channel_id=1, source_target_pairs={{0,1},{1,0},{2,3},{3,2},{4,5},{5,4},{6,7},{7,6},{8,9},{9,8},{10,11... | collective-permute-start | bytes 4718600 | tf_op jit(solution)/shard_map/ppermute | solution.py:1337
  483.8 26.0 %collective-permute-start.37 = (bf16[2,2,32,2816]{3,2,1,0:T(8,128)(2,1)}, bf16[2,2,32,2816]{3,2,1,0:T(8,128)(2,1)}, u32[]{:S(2)}, u32[]{:S(2)}) collective-permute-start(bf16[2,2,32,2816]{3,2,1,0:T(8,128)(2,1)} %pad_maximum_fusion.13), channel_id=1, source_target_pairs={{0,8},{1,9},{2,10},{3,11},{4,12},{5,13},{6,14},{7,15},{8,0},{9,1},... | collective-permute-start | bytes 2162696 | tf_op jit(solution)/shard_map/ppermute | solution.py:1337
  485.5 24.2 %collective-permute-start.38 = (bf16[2,1,88,1024]{3,2,1,0:T(8,128)(2,1)}, bf16[2,1,88,1024]{3,2,1,0:T(8,128)(2,1)S(1)}, u32[]{:S(2)}, u32[]{:S(2)}) collective-permute-start(bf16[2,1,88,1024]{3,2,1,0:T(8,128)(2,1)} %pad_maximum_fusion.20), channel_id=1, source_target_pairs={{0,8},{1,9},{2,10},{3,11},{4,12},{5,13},{6,14},{7,15},{8,0},{9,1},... | collective-permute-start | bytes 1081352 | tf_op jit(solution)/shard_map/ppermute | solution.py:1337
  509.7 33.0 %copy-start.24 = (bf16[2,1,88,1024]{3,2,1,0:T(8,128)(2,1)}, bf16[2,1,88,1024]{3,2,1,0:T(8,128)(2,1)S(1)}, u32[]{:S(2)}) copy-start(bf16[2,1,88,1024]{3,2,1,0:T(8,128)(2,1)S(1)} %collective-permute-done.38) | copy-start | bytes 1081348
  513.2 22.1 %collective-permute-start.39 = (bf16[4,5,32,1024]{3,2,1,0:T(8,128)(2,1)}, bf16[4,5,32,1024]{3,2,1,0:T(8,128)(2,1)}, u32[]{:S(2)}, u32[]{:S(2)}) collective-permute-start(bf16[4,5,32,1024]{3,2,1,0:T(8,128)(2,1)} %fusion.6), channel_id=1, source_target_pairs={{0,2},{1,5},{2,0},{3,7},{4,6},{5,1},{6,4},{7,3},{8,10},{9,13},{10,... | collective-permute-start | bytes 3932168 | tf_op jit(solution)/shard_map/ppermute | solution.py:1337
  517.1 18.2 %collective-permute-start.40 = (bf16[2,32,2816]{2,1,0:T(8,128)(2,1)}, bf16[2,32,2816]{2,1,0:T(8,128)(2,1)S(1)}, u32[]{:S(2)}, u32[]{:S(2)}) collective-permute-start(bf16[2,32,2816]{2,1,0:T(8,128)(2,1)} %fusion.17), channel_id=1, source_target_pairs={{0,16},{1,17},{2,18},{3,19},{4,20},{5,21},{6,22},{7,23},{8,24},{9,... | collective-permute-start | bytes 1081352 | tf_op jit(solution)/shard_map/ppermute | solution.py:1337
  542.7 15.9 %collective-permute-start.41 = (bf16[3,16,32,512]{3,2,1,0:T(8,128)(2,1)}, bf16[3,16,32,512]{3,2,1,0:T(8,128)(2,1)}, u32[]{:S(2)}, u32[]{:S(2)}) collective-permute-start(bf16[3,16,32,512]{3,2,1,0:T(8,128)(2,1)} %weight_part.9), channel_id=1, source_target_pairs={{0,1},{1,0},{2,3},{3,2},{4,5},{5,4},{6,7},{7,6},{8,9},{9,8},{10,11... | collective-permute-start | bytes 4718600 | tf_op jit(solution)/shard_map/ppermute | solution.py:1337
  543.5 63.3 %collective-permute-start.49 = (bf16[1,88,1024]{2,1,0:T(8,128)(2,1)}, bf16[1,88,1024]{2,1,0:T(8,128)(2,1)}, u32[]{:S(2)}, u32[]{:S(2)}) collective-permute-start(bf16[1,88,1024]{2,1,0:T(8,128)(2,1)} %fusion.27), channel_id=1, source_target_pairs={{0,16},{1,17},{2,18},{3,19},{4,20},{5,21},{6,22},{7,23},{8,24},{9,... | collective-permute-start | bytes 540680 | tf_op jit(solution)/shard_map/ppermute | solution.py:1337
  556.8 18.1 %collective-permute-start.42 = (bf16[2,4,3,32,512]{4,3,2,1,0:T(8,128)(2,1)}, bf16[2,4,3,32,512]{4,3,2,1,0:T(8,128)(2,1)}, u32[]{:S(2)}, u32[]{:S(2)}) collective-permute-start(bf16[2,4,3,32,512]{4,3,2,1,0:T(8,128)(2,1)} %get-tuple-element.417), channel_id=1, source_target_pairs={{0,4},{1,3},{2,6},{3,1},{4,0},{5,7},{6,2},{7,5},{8,12},{9,11},{10,... | collective-permute-start | bytes 2359304 | tf_op jit(solution)/shard_map/ppermute | solution.py:1337
  558.2 16.7 %collective-permute-start.43 = (bf16[2,5,32,1024]{3,2,1,0:T(8,128)(2,1)}, bf16[2,5,32,1024]{3,2,1,0:T(8,128)(2,1)}, u32[]{:S(2)}, u32[]{:S(2)}) collective-permute-start(bf16[2,5,32,1024]{3,2,1,0:T(8,128)(2,1)} %pad_maximum_fusion.15), channel_id=1, source_target_pairs={{0,8},{1,9},{2,10},{3,11},{4,12},{5,13},{6,14},{7,15},{8,0},{9,1},... | collective-permute-start | bytes 1966088 | tf_op jit(solution)/shard_map/ppermute | solution.py:1337
  582.5 20.4 %collective-permute-start.44 = (bf16[2,4,3,32,512]{4,3,2,1,0:T(8,128)(2,1)}, bf16[2,4,3,32,512]{4,3,2,1,0:T(8,128)(2,1)}, u32[]{:S(2)}, u32[]{:S(2)}) collective-permute-start(bf16[2,4,3,32,512]{4,3,2,1,0:T(8,128)(2,1)} %get-tuple-element.427), channel_id=1, source_target_pairs={{0,4},{1,3},{2,6},{3,1},{4,0},{5,7},{6,2},{7,5},{8,12},{9,11},{10,... | collective-permute-start | bytes 2359304 | tf_op jit(solution)/shard_map/ppermute | solution.py:1337
  583.5 40.2 %collective-permute-start.52 = (f32[768,1024]{1,0:T(8,128)}, f32[768,1024]{1,0:T(8,128)}, u32[]{:S(2)}, u32[]{:S(2)}) collective-permute-start(f32[768,1024]{1,0:T(8,128)} %get-tuple-element.449), channel_id=1, source_target_pairs={{0,1},{1,0},{2,3},{3,2},{4,5},{5,4},{6,7},{7,6},{8,9},{9,8},{10,11... | collective-permute-start | bytes 9437192 | tf_op jit(solution)/shard_map/ppermute | solution.py:1337
  586.5 16.4 %collective-permute-start.45 = (bf16[4,3,32,512]{3,2,1,0:T(8,128)(2,1)}, bf16[4,3,32,512]{3,2,1,0:T(8,128)(2,1)}, u32[]{:S(2)}, u32[]{:S(2)}) collective-permute-start(bf16[4,3,32,512]{3,2,1,0:T(8,128)(2,1)} %fusion.13), channel_id=1, source_target_pairs={{0,2},{1,5},{2,0},{3,7},{4,6},{5,1},{6,4},{7,3},{8,10},{9,13},{10,... | collective-permute-start | bytes 1179656 | tf_op jit(solution)/shard_map/ppermute | solution.py:1337
  592.2 17.6 %collective-permute-start.48 = (bf16[5,32,1024]{2,1,0:T(8,128)(2,1)}, bf16[5,32,1024]{2,1,0:T(8,128)(2,1)}, u32[]{:S(2)}, u32[]{:S(2)}) collective-permute-start(bf16[5,32,1024]{2,1,0:T(8,128)(2,1)} %fusion.19), channel_id=1, source_target_pairs={{0,16},{1,17},{2,18},{3,19},{4,20},{5,21},{6,22},{7,23},{8,24},{9,... | collective-permute-start | bytes 983048 | tf_op jit(solution)/shard_map/ppermute | solution.py:1337
  604.1 9.7 %collective-permute-start.46 = (bf16[4,3,32,512]{3,2,1,0:T(8,128)(2,1)S(1)}, bf16[4,3,32,512]{3,2,1,0:T(8,128)(2,1)S(1)}, u32[]{:S(2)}, u32[]{:S(2)}) collective-permute-start(bf16[4,3,32,512]{3,2,1,0:T(8,128)(2,1)S(1)} %fusion.14), channel_id=1, source_target_pairs={{0,2},{1,5},{2,0},{3,7},{4,6},{5,1},{6,4},{7,3},{8,10},{9,13},{10,... | collective-permute-start | bytes 1179656 | tf_op jit(solution)/shard_map/ppermute | solution.py:1337
  606.4 7.4 %collective-permute-start.47 = (bf16[2,3,32,512]{3,2,1,0:T(8,128)(2,1)S(1)}, bf16[2,3,32,512]{3,2,1,0:T(8,128)(2,1)S(1)}, u32[]{:S(2)}, u32[]{:S(2)}) collective-permute-start(bf16[2,3,32,512]{3,2,1,0:T(8,128)(2,1)S(1)} %pad_maximum_fusion.23), channel_id=1, source_target_pairs={{0,8},{1,9},{2,10},{3,11},{4,12},{5,13},{6,14},{7,15},{8,0},{9,1},... | collective-permute-start | bytes 589832 | tf_op jit(solution)/shard_map/ppermute | solution.py:1337
  614.5 14.2 %collective-permute-start.51 = (bf16[3,32,512]{2,1,0:T(8,128)(2,1)}, bf16[3,32,512]{2,1,0:T(8,128)(2,1)}, u32[]{:S(2)}, u32[]{:S(2)}) collective-permute-start(bf16[3,32,512]{2,1,0:T(8,128)(2,1)} %fusion.28), channel_id=1, source_target_pairs={{0,16},{1,17},{2,18},{3,19},{4,20},{5,21},{6,22},{7,23},{8,24},{9,... | collective-permute-start | bytes 294920 | tf_op jit(solution)/shard_map/ppermute | solution.py:1337
  617.9 10.8 %collective-permute-start.50 = (bf16[2,3,32,512]{3,2,1,0:T(8,128)(2,1)}, bf16[2,3,32,512]{3,2,1,0:T(8,128)(2,1)}, u32[]{:S(2)}, u32[]{:S(2)}) collective-permute-start(bf16[2,3,32,512]{3,2,1,0:T(8,128)(2,1)} %pad_maximum_fusion.24), channel_id=1, source_target_pairs={{0,8},{1,9},{2,10},{3,11},{4,12},{5,13},{6,14},{7,15},{8,0},{9,1},... | collective-permute-start | bytes 589832 | tf_op jit(solution)/shard_map/ppermute | solution.py:1337
  629.6 6.5 collective-permute-start.53
  638.6 5.7 collective-permute-start.54
  640.7 4.6 collective-permute-start.55
  642.1 3.7 collective-permute-start.56
  645.9 4.3 collective-permute-start.57
  647.3 3.7 collective-permute-start.58
  648.4 4.6 collective-permute-start.59
  653.1 1.2 collective-permute-start.60
  (45 other events, 362.7 us)

commit v2 on v1

--- a/solution.py
+++ b/solution.py
@@ -515,6 +515,10 @@
     return jnp.where((lane >= HD) if half else (lane < HD), value, jnp.zeros_like(value))
 
 
+def both_halves(value):
+    return jnp.concatenate([lanes_of(value, 0), lanes_of(value, 1)], axis=0)
+
+
 def probs_width(prompt, size):
     blocks = prompt // TILE
     return TILE * blocks * (blocks + 1) // 2 + prompt + size
@@ -564,15 +568,14 @@
                 top = jnp.maximum(top, own)
             top = jnp.max(top, axis=1, keepdims=True)
             total = None
-            out = None
             for j, (keys, _) in enumerate(tiles):
                 e = jnp.exp(s_ref[:, j * TILE:(j + 1) * TILE] - top)
                 part = e[:, :PAIR] + e[:, PAIR:]
                 total = part if total is None else total + part
                 low = e.astype(BF)
                 e_ref[half, :, begins[i] + j * TILE:begins[i] + (j + 1) * TILE] = low
-                part = dot(low, v_ref[keys], (1, 0))
-                out = part if out is None else out + part
+            seen = len(tiles) * TILE
+            out = dot(e_ref[half, :, begins[i]:begins[i] + seen], v_ref[:seen], (1, 0))
             if i == blocks:
                 e = jnp.exp(own - top)
                 total = total + e
@@ -631,60 +634,73 @@
 
 
 def self_back_kernel(prompt, size, q_ref, k_ref, v_ref, do_ref, o_ref, e_ref, inv_ref, dq_ref, dk_ref, dv_ref,
-                     strip_ref, cross_ref, sums, far_sums, dk_acc, dv_acc):
+                     strip_ref, cross_ref, sums, far_sums, dk_acc, dv_acc, down_ref, low_ref, q_left, do_left):
     blocks = prompt // TILE
+    count = prompt + 2 * size
     begins = [TILE * i * (i + 1) // 2 for i in range(blocks + 1)]
     scale = BF(HD ** -0.5)
     lane = lax.broadcasted_iota(jnp.int32, (TILE, PAIR), 1)
-    dk_acc[...] = jnp.zeros_like(dk_acc)
-    dv_acc[...] = jnp.zeros_like(dv_acc)
-    for half in range(2):
-        sums[...] = jnp.zeros_like(sums)
-
-        def gather(left, grads, keys, acc):
-            acc[half * HD:(half + 1) * HD, keys] += dot(grads[half * HD:(half + 1) * HD], left, (1, 0))
-
-        for i in range(blocks + 1):
-            rows = slice(i * TILE, (i + 1) * TILE)
-            scaled = do_ref[rows].astype(F32) * inv_ref[rows]
-            do = lanes_of(scaled.astype(BF), half)
-            part = lanes_of(do.astype(F32) * o_ref[rows].astype(F32), half)
-            drop = jnp.sum(part, axis=1, keepdims=True)
-            do_left, q_left = do.T, (q_ref[rows] * scale).T
-            dq = None
-            for j in range(min(i + 1, blocks)):
-                keys = slice(j * TILE, (j + 1) * TILE)
+    parts = [slice(b * size, (b + 1) * size) for b in range(2)]
+    branches = [slice(prompt + b * size, prompt + (b + 1) * size) for b in range(2)]
+    for i in range(blocks + 1):
+        rows = slice(i * TILE, (i + 1) * TILE)
+        q_left[:, rows] = (q_ref[rows] * scale).T
+        do_left[:, rows] = (do_ref[rows].astype(F32) * inv_ref[rows]).astype(BF).T
+    sums[...] = jnp.zeros_like(sums)
+    for i in range(blocks + 1):
+        rows = slice(i * TILE, (i + 1) * TILE)
+        tiles = min(i + 1, blocks)
+        seen = tiles * TILE
+        scaled = (do_ref[rows].astype(F32) * inv_ref[rows]).astype(BF)
+        do = both_halves(scaled)
+        drops = scaled.astype(F32) * o_ref[rows].astype(F32)
+        drop = [jnp.sum(lanes_of(drops, half), axis=1, keepdims=True) for half in range(2)]
+        for j in range(tiles):
+            keys = slice(j * TILE, (j + 1) * TILE)
+            both = dot(do, v_ref[keys], (1, 1))
+            for half in range(2):
                 low = e_ref[half, :, begins[i] + j * TILE:begins[i] + (j + 1) * TILE]
-                ds = low.astype(F32) * (dot(do, v_ref[keys], (1, 1)) - drop)
+                ds = low.astype(F32) * (both[half * TILE:(half + 1) * TILE] - drop[half])
                 if i < blocks:
                     begin = TILE + prompt - (i + 1 - j) * TILE
-                    sums[:, begin:begin + TILE] += ds
+                    sums[half, :, begin:begin + TILE] += ds
                 else:
-                    far_sums[:, size + j * TILE:size + (j + 1) * TILE] = ds
+                    far_sums[half, :, size + j * TILE:size + (j + 1) * TILE] = ds
+                down_ref[half, rows, keys] = ds.astype(BF)
+                low_ref[half, rows, keys] = low
+        down = jnp.concatenate([down_ref[half, rows, :seen] for half in range(2)], axis=0)
+        dq = dot(down, k_ref[:seen], (1, 0))
+        if i == blocks:
+            more = []
+            for half in range(2):
+                lanes = slice(half * HD, (half + 1) * HD)
+                low = e_ref[half, :, begins[i] + prompt:]
+                own = jnp.concatenate(
+                    [
+                        dot(do[half * TILE + b * size:half * TILE + (b + 1) * size], v_ref[branches[b]], (1, 1))
+                        for b in range(2)
+                    ],
+                    axis=0,
+                )
+                ds = low.astype(F32) * (own - drop[half])
+                sums[half, :size, prompt:prompt + size] += ds[:size] + ds[size:]
                 down = ds.astype(BF)
-                part = dot(down, k_ref[keys], (1, 0))
-                dq = part if dq is None else dq + part
-                gather(down, q_left, keys, dk_acc)
-                gather(low, do_left, keys, dv_acc)
-            if i == blocks:
-                low = e_ref[half, :, begins[i] + prompt:]
-                parts = [slice(b * size, (b + 1) * size) for b in range(2)]
-                keys = [slice(prompt + b * size, prompt + (b + 1) * size) for b in range(2)]
-                own = jnp.concatenate([dot(do[parts[b]], v_ref[keys[b]], (1, 1)) for b in range(2)], axis=0)
-                ds = low.astype(F32) * (own - drop)
-                sums[:size, prompt:prompt + size] += ds[:size] + ds[size:]
-                down = ds.astype(BF)
-                dq = dq + jnp.concatenate(
-                    [dot(down[parts[b]], k_ref[keys[b]], (1, 0)) for b in range(2)], axis=0
-                )
+                more += [dot(down[parts[b]], k_ref[branches[b]], (1, 0)) for b in range(2)]
                 for b in range(2):
-                    gather(down[parts[b]], q_left[:, parts[b]], keys[b], dk_acc)
-                    gather(low[parts[b]], do_left[:, parts[b]], keys[b], dv_acc)
-            dq = (dq * (HD ** -0.5)).astype(BF)
-            dq_ref[rows] = dq if half == 0 else jnp.where(lane >= HD, dq, dq_ref[rows])
-        strip_ref[half] = fold(sums[...])
+                    dk_acc[lanes, branches[b]] = dot(q_left[lanes, branches[b]], down[parts[b]], (1, 0))
+                    dv_acc[lanes, branches[b]] = dot(do_left[lanes, branches[b]], low[parts[b]], (1, 0))
+            dq = dq + jnp.concatenate(more, axis=0)
+        dq_ref[rows] = (jnp.where(lane < HD, dq[:TILE], dq[TILE:]) * (HD ** -0.5)).astype(BF)
+    for half in range(2):
+        lanes = slice(half * HD, (half + 1) * HD)
+        for j in range(blocks):
+            keys = slice(j * TILE, (j + 1) * TILE)
+            rows = slice(j * TILE, count)
+            dk_acc[lanes, keys] = dot(q_left[lanes, rows], down_ref[half, rows, keys], (1, 0))
+            dv_acc[lanes, keys] = dot(do_left[lanes, rows], low_ref[half, rows, keys], (1, 0))
+        strip_ref[half] = fold(sums[half])
         for b in range(2):
-            wide = far_sums[b * size:(b + 1) * size]
+            wide = far_sums[half, b * size:(b + 1) * size]
             place = lax.broadcasted_iota(jnp.int32, wide.shape, 1)
             cross_ref[half, b] = fold(jnp.where(place < size, 0.0, wide))
     dk_ref[...] = dk_acc[...].T.astype(BF)
@@ -724,7 +740,16 @@
             jax.ShapeDtypeStruct((2 * pairs, 1, prompt + TILE), F32),
             jax.ShapeDtypeStruct((2 * pairs, 2, 1, prompt + size), F32),
         ],
-        scratch_shapes=[pltpu.VMEM((TILE, prompt + TILE), F32), pltpu.VMEM((2 * size, prompt + size), F32), acc, acc],
+        scratch_shapes=[
+            pltpu.VMEM((2, TILE, prompt + TILE), F32),
+            pltpu.VMEM((2, 2 * size, prompt + size), F32),
+            acc,
+            acc,
+            pltpu.VMEM((2, count, prompt), BF),
+            pltpu.VMEM((2, count, prompt), BF),
+            pltpu.VMEM((PAIR, count), BF),
+            pltpu.VMEM((PAIR, count), BF),
+        ],
         compiler_params=params(),
         cost_estimate=cost(8 * pairs),
         name="self_backward",
@@ -1063,17 +1088,16 @@
         columns = slice(pair * PAIR, (pair + 1) * PAIR)
         k = kv_ref[0, :, columns]
         v = kv_ref[1, :, columns]
-        mixed = []
+        s = dot(both_halves(q_ref[:, columns] * BF(HD ** -0.5)), k, (1, 1))
+        e = jnp.exp(s - jnp.max(s, axis=1, keepdims=True))
+        inverse = 1.0 / jnp.sum(e, axis=1, keepdims=True)
+        low = e.astype(BF)
+        mixed = dot(low, v, (1, 0)) * inverse
         for half in range(2):
-            q = lanes_of(q_ref[:, columns] * BF(HD ** -0.5), half)
-            s = dot(q, k, (1, 1))
-            e = jnp.exp(s - jnp.max(s, axis=1, keepdims=True))
-            inverse = 1.0 / jnp.sum(e, axis=1, keepdims=True)
-            low = e.astype(BF)
-            p_ref[2 * pair + half] = low
-            inverses = jnp.where(lane == 2 * pair + half, inverse, inverses)
-            mixed.append(dot(low, v, (1, 0)) * inverse)
-        o_scr[:, columns] = jnp.where(lane < HD, mixed[0], mixed[1]).astype(BF)
+            rows = slice(half * TILE, (half + 1) * TILE)
+            p_ref[2 * pair + half] = low[rows]
+            inverses = jnp.where(lane == 2 * pair + half, inverse[rows], inverses)
+        o_scr[:, columns] = jnp.where(lane < HD, mixed[:TILE], mixed[TILE:]).astype(BF)
     inv_ref[...] = inverses
     put_sides(o_ref, o_scr[...])
     x2 = x1_ref[...] + dot(o_scr[...], weight(4), (1, 0))
@@ -1162,17 +1186,17 @@
         do = (do_ref[:, columns].astype(F32) * inverse).astype(BF)
         drops = do.astype(F32) * o_ref[:, columns].astype(F32)
         q_left, do_left = (q_ref[:, columns] * BF(HD ** -0.5)).T, do.T
-        parts = []
+        drop = jnp.sum(both_halves(drops), axis=1, keepdims=True)
+        low = jnp.concatenate([p_ref[2 * pair], p_ref[2 * pair + 1]], axis=0)
+        down = (low.astype(F32) * (dot(both_halves(do), v, (1, 1)) - drop)).astype(BF)
+        dq = dot(down, k, (1, 0))
         for half in range(2):
             rows = slice(half * HD, (half + 1) * HD)
+            tile = slice(half * TILE, (half + 1) * TILE)
             places = slice(pair * PAIR + half * HD, pair * PAIR + (half + 1) * HD)
-            low = p_ref[2 * pair + half]
-            drop = jnp.sum(lanes_of(drops, half), axis=1, keepdims=True)
-            down = (low.astype(F32) * (dot(lanes_of(do, half), v, (1, 1)) - drop)).astype(BF)
-            parts.append(dot(down, k, (1, 0)))
-            dk_acc[places] += dot(q_left[rows], down, (1, 0))
-            dv_acc[places] += dot(do_left[rows], low, (1, 0))
-        dq_ref[:, columns] = (jnp.where(lane < HD, parts[0], parts[1]) * (HD ** -0.5)).astype(BF)
+            dk_acc[places] += dot(q_left[rows], down[tile], (1, 0))
+            dv_acc[places] += dot(do_left[rows], low[tile], (1, 0))
+        dq_ref[:, columns] = (jnp.where(lane < HD, dq[:TILE], dq[TILE:]) * (HD ** -0.5)).astype(BF)
     da2 = dot(dq_ref[...], wq_ref[...], (1, 1))
     back, terms = norm_back(x1_ref[...], gain_two_ref[...], da2)
     gains_ref[0] += terms
@@ -1465,7 +1489,7 @@
     here, near, far, across = spots(y, x, core)
     count, _, rows, columns = keep.shape
     grid = (count, LINE, SIDE * SIDE, rows, columns)
-    wide = columns // 2
+    wide = columns if columns <= D else columns // 2
     source = pl.BlockSpec((count, LINE, 1, rows, wide), lambda j, t, s: (0, 0, s[j], 0, t))
     out = jax.ShapeDtypeStruct((2, LINE, count, rows, columns), BF)
     block = (1, LINE, count, rows, wide)
@@ -1473,10 +1497,12 @@
         add_split_kernel,
         grid_spec=pltpu.PrefetchScalarGridSpec(
             num_scalar_prefetch=1,
-            grid=(4, 2),
+            grid=(4, columns // wide),
             in_specs=[source, source],
             out_specs=[
-                pl.BlockSpec(block, lambda j, t, s: (jnp.minimum(j, 1), 0, 0, 0, jnp.where(j < 2, t, 1))),
+                pl.BlockSpec(
+                    block, lambda j, t, s: (jnp.minimum(j, 1), 0, 0, 0, jnp.where(j < 2, t, columns // wide - 1))
+                ),
                 pl.BlockSpec(block, lambda j, t, s: (jnp.maximum(j - 2, 0), 0, 0, 0, jnp.where(j < 2, 0, t))),
             ],
         ),
@@ -1779,29 +1805,23 @@
     got_one = send(away_one, core_flip)
     grad_mixed_one, away_one = tie(grad_mixed_one, away_one)
 
-    part_two, grad_mixed_one, got_one, got_mid, got_line_exp, got_line_con = attend_back(
-        half, half // 2, got_one, got_mid, got_line_exp, got_line_con
+    part_two, grad_mixed_one, got_one, got_mid, got_line_exp, away_plan = attend_back(
+        half, half, got_one, got_mid, got_line_exp, away_plan
     )
     near_mid = plus(stay_mid[1], got_mid[1])
     got_near_mid = send(near_mid, first_flip)
+    away_plan, near_mid = tie(away_plan, near_mid)
+    away_two = weight_part(away_plan, [turned_one], jobs_of(part_two))
+    got_two = send(away_two, core_flip)
     last_exp = plus(line_exp[1], got_line_exp[1])
     got_last_exp = send(last_exp, line_far)
-    grad_mixed_one, near_mid, last_exp = tie(grad_mixed_one, near_mid, last_exp)
-
-    part_three, grad_mixed_one, got_near_mid, got_last_exp, away_plan = attend_back(
-        half + half // 2, half // 2, got_near_mid, got_last_exp, away_plan
-    )
-    away_two = weight_part(away_plan, [turned_one], jobs_of(part_two, part_three))
-    got_two = send(away_two, core_flip)
-    line_mid, away_mid = line_split(plus(plus(stay_mid[0], got_mid[0]), got_near_mid), place)
-    got_line_mid = send(away_mid, line_near)
-    keep_plan, away_two, away_mid = tie(keep_plan, away_two, away_mid)
+    keep_plan, away_two, last_exp = tie(keep_plan, away_two, last_exp)
     away_one, stay_one = weight_part(keep_plan, [turned_one], jobs_of(part_one), got_one)
     got_one = send(away_one, second_flip)
     leave_values = (
         stream_low,
         grad_after_one,
-        [part_one[:3], part_two[:3], part_three[:3]],
+        [part_one[:3], part_two[:3]],
         gain_rows[0],
         w_query,
         w_key,
@@ -1814,30 +1834,34 @@
 
     theirs_plan, away_one, got_two = tie(theirs_plan, away_one, got_two)
     theirs_grad, gain_one = leave(theirs_plan, blocks + 1, *leave_values)
-    theirs_grad, got_one, got_line_mid, keep_plan = tie(theirs_grad, got_one, got_line_mid, keep_plan)
-    away_two, stay_two = weight_part(keep_plan, [turned_one], jobs_of(part_two, part_three), got_two)
+    theirs_grad, got_one, got_near_mid, keep_plan, got_line_con = tie(
+        theirs_grad, got_one, got_near_mid, keep_plan, got_line_con
+    )
+    away_two, stay_two = weight_part(keep_plan, [turned_one], jobs_of(part_two), got_two)
     got_two = send(away_two, second_flip)
     away_two, stay_one, stay_mid, theirs_grad = tie(away_two, stay_one, stay_mid, theirs_grad)
     near_one = plus(stay_one[1], got_one[1])
     got_near_one = send(near_one, first_flip)
-    last_mid = plus(line_mid[1], got_line_mid[1])
-    got_last_mid = send(last_mid, line_far)
+    line_mid, away_mid = line_split(plus(plus(stay_mid[0], got_mid[0]), got_near_mid), place)
+    got_line_mid = send(away_mid, line_near)
     last_con = plus(line_con[1], got_line_con[1])
     got_last_con = send(last_con, line_far)
-    ours_plan, near_one, last_mid, last_con = tie(ours_plan, near_one, last_mid, last_con)
+    ours_plan, near_one, away_mid, last_con = tie(ours_plan, near_one, away_mid, last_con)
     ours_grad, gain_more = leave(ours_plan, blocks, *leave_values)
-    ours_grad, got_two, got_near_one = tie(ours_grad, got_two, got_near_one)
+    ours_grad, got_two, got_near_one, got_line_mid = tie(ours_grad, got_two, got_near_one, got_line_mid)
     near_two = plus(stay_two[1], got_two[1])
     got_near_two = send(near_two, first_flip)
     line_one, away_one = line_split(plus(plus(stay_one[0], got_one[0]), got_near_one), place)
     got_line_one = send(away_one, line_near)
+    last_mid = plus(line_mid[1], got_line_mid[1])
+    got_last_mid = send(last_mid, line_far)
     got_grad = send(theirs_grad, core_flip)
     half_rows = prompt // 2
     whole_output = both_groups(own_output, other_output, core)
     prompt_output, branch_output = whole_output[:, :half_rows], whole_output[:, half_rows:]
     encoder_out = both_groups(own_encoder, other_encoder, core)
-    got_near_two, got_line_one, got_last_mid, got_last_con, prompt_output, branch_output, encoder_out = tie(
-        got_near_two, got_line_one, got_last_mid, got_last_con, prompt_output, branch_output, encoder_out
+    got_near_two, got_line_one, got_last_con, got_last_exp, prompt_output, branch_output, encoder_out = tie(
+        got_near_two, got_line_one, got_last_con, got_last_exp, prompt_output, branch_output, encoder_out
     )
     line_two, away_two = line_split(plus(plus(stay_two[0], got_two[0]), got_near_two), place)
     got_line_two = send(away_two, line_near)
@@ -1853,14 +1877,16 @@
     owned_con = owned_part(line_con, got_line_con, got_last_con)[0]
     squares = square(owned_exp) + square(owned_con)
     prompt_grad = both_groups(ours_grad, got_grad[:half_rows], core)
-    squares, got_line_two, got_last_one, prompt_grad = tie(squares, got_line_two, got_last_one, prompt_grad)
+    squares, got_line_two, got_last_one, got_last_mid, prompt_grad = tie(
+        squares, got_line_two, got_last_one, got_last_mid, prompt_grad
+    )
     got_last_two = send(plus(line_two[1], got_line_two[1]), line_far)
     owned_mid = owned_part(line_mid, got_line_mid, got_last_mid)
     owned_one = owned_part(line_one, got_line_one, got_last_one)
     squares = squares + square(owned_mid) + square(owned_one)
     grad_bias = bias_gradient(
-        jnp.concatenate([part_one[3], part_two[3], part_three[3]]),
-        jnp.concatenate([part_one[4], part_two[4], part_three[4]]),
+        jnp.concatenate([part_one[3], part_two[3]]),
+        jnp.concatenate([part_one[4], part_two[4]]),
         buckets,
     )
     own_branch = lax.dynamic_slice_in_dim(theirs_grad, half_rows + core * size, size, 0)

time: 678 us -> 639 us (0.942)
  Pallas kernels: 414 us -> 378 us
    pallas_call x3 -> x2, Pallas kernels: 64.7 us -> 38.8 us  [self_backward(): pl.pallas_call(functools.partial(self_back_kernel, prompt, size), grid=(p...]
  transfers between devices with their start and end apart: 61 -> 61, of which waited for: 21 -> 19; matrix products, arithmetic and copies ran while one was open for 12% -> 13% of each run, Pallas kernels for 43% -> 41%
where the time goes in v2:
time: 639 us; the launch traced here: 627 us
  Pallas kernels  378 us (59%)
  other arithmetic  76.6 us (12%)
  waiting for transfers between devices  71.1 us (11%)
  starting transfers between devices  56.6 us (9%)
  local copies, waits for them, and re-layouts  27 us (4%)
  between operations  13.5 us (2%)
    pallas_call x1, Pallas kernels, mlp(): pl.pallas_call(mlp_kernel, grid_spec=pltpu.PrefetchScalarGridSpec(num_sca...  91.3 us
    ppermute x61, waiting for transfers between devices, send(): return lax.ppermute(value, AXES, moves(rule))  71.1 us
    ppermute x61, starting transfers between devices, send(): return lax.ppermute(value, AXES, moves(rule))  56.6 us
    pallas_call x2, Pallas kernels, self_forward(): pl.pallas_call(functools.partial(self_kernel, prompt, size, len(more)), g...  50.1 us
    pallas_call x6, Pallas kernels, weight_part(): pl.pallas_call(functools.partial(part_kernel, [left for left, _ in jobs],...  49 us
    pallas_call x2, Pallas kernels, middle_back(): pl.pallas_call(middle_back_kernel, grid=(blocks,), in_specs=[rows] * 6 +...  43 us
    pallas_call x2, Pallas kernels, self_backward(): pl.pallas_call(functools.partial(self_back_kernel, prompt, size), grid=(p...  38.8 us
    pallas_call x1, Pallas kernels, middle(): pl.pallas_call(functools.partial(middle_kernel, len(mixed)), grid=(count...  33.1 us
  transfers between devices with their start and end apart: 61, of which 19 were waited for; matrix products, arithmetic and copies ran while one was open for 13% of the time, Pallas kernels for 41%

profile of v2, /device:TPU:0, one launch (start us, length us, event | category | flops | bytes accessed | tf_op | source)
XLA Modules:
  0.0 627.4 jit_solution(16623150267990114041)
XLA Ops:
  2.0 4.1 collective-permute-start
  11.3 3.9 collective-permute-done.far
  16.1 9.5 %collective-permute-done.2.near = bf16[2,3,32,1024]{3,2,1,0:T(8,128)(2,1)S(1)} collective-permute-done((bf16[2,3,32,1024]{3,2,1,0:T(8,128)(2,1)S(1)}, bf16[2,3,32,1024]{3,2,1,0:T(8,128)(2,1)S(1)}, u32[]{:S(2)}, u32[]{:S(2)}) %collective-permute-start.2) | collective-permute-done | bytes 393248 | tf_op jit(solution)/shard_map/ppermute | solution.py:1361
  37.7 3.4 collective-permute-start.4
  42.1 3.1 collective-permute-done.3
  47.8 8.5 %collective-permute-done.4.far = bf16[5,32,1024]{2,1,0:T(8,128)(2,1)S(1)} collective-permute-done((bf16[5,32,1024]{2,1,0:T(8,128)(2,1)S(1)}, bf16[5,32,1024]{2,1,0:T(8,128)(2,1)S(1)}, u32[]{:S(2)}, u32[]{:S(2)}) %collective-permute-start.4) | collective-permute-done | bytes 327712 | tf_op jit(solution)/shard_map/ppermute | solution.py:1361
  57.2 3.1 broadcast_select_fusion.1
  61.7 1.7 pad_maximum_fusion.3.dy_ref
  65.1 7.7 %collective-permute-done.6.near = bf16[2,5,32,1024]{3,2,1,0:T(8,128)(2,1)S(1)} collective-permute-done((bf16[2,5,32,1024]{3,2,1,0:T(8,128)(2,1)S(1)}, bf16[2,5,32,1024]{3,2,1,0:T(8,128)(2,1)S(1)}, u32[]{:S(2)}, u32[]{:S(2)}) %collective-permute-start.6) | collective-permute-done | bytes 655392 | tf_op jit(solution)/shard_map/ppermute | solution.py:1361
  75.2 2.9 collective-permute-start.11
  79.5 17.0 %enter.1 = (bf16[2,512,1280]{2,1,0:T(8,128)(2,1)}, bf16[3,1280,1024]{2,1,0:T(8,128)(2,1)}, bf16[4,4,2,32,1024]{4,3,2,1,0:T(8,128)(2,1)}, bf16[4,4,2,32,1024]{4,3...) custom-call(s32[8,2]{1,0:T(8,128)} %stack.281.slots_ref, bf16[2,3,4,32,1024]{4,3,2,1,0:T(8,128)(2,1)} %copy-done.5, ...), custom_call_target="tpu_custom_call" | custom-call | flops 12 | bytes 1 | tf_op jit(solution)/shard_map/enter/pallas_call | solution.py:1040
  96.5 3.0 pad_maximum_fusion.4.refs_0_
  100.3 1.8 collective-permute-start.14
  102.4 25.0 %self_forward.2 = (bf16[1280,1024]{1,0:T(8,128)(2,1)}, bf16[16,256,3712]{2,1,0:T(8,128)(2,1)}, f32[1280,1024]{1,0:T(8,128)}) custom-call(s32[2]{0:T(128)} %copy-done.37, bf16[3,1280,1024]{2,1,0:T(8,128)(2,1)} %get-tuple-element.284.q_ref.k_ref.v_ref, bf16[3,1280,1024]{2,1,0:T(8,128)(2,1)} %get-tuple-element.284.q_ref.k_ref.v_ref, ...), custom_call_target="tpu_custom_call" | custom-call | flops 24 | bytes 1 | tf_op jit(solution)/shard_map/self_forward/pallas_call | solution.py:608
  127.4 4.1 collective-permute-done.12.refs_2_
  132.7 1.8 collective-permute-start.18
  134.5 25.1 %self_forward.3 = (bf16[1280,1024]{1,0:T(8,128)(2,1)}, bf16[16,256,3712]{2,1,0:T(8,128)(2,1)}, f32[1280,1024]{1,0:T(8,128)}) custom-call(s32[2]{0:T(128)} %copy-done.37, bf16[3,1280,1024]{2,1,0:T(8,128)(2,1)} %get-tuple-element.284.q_ref.k_ref.v_ref, ...), custom_call_target="tpu_custom_call", output_to_operand_aliasing={{0}: (6, {}), {1}: (7, {}), {2}: (8, {})} | custom-call | flops 24 | bytes 1 | tf_op jit(solution)/shard_map/self_forward/pallas_call | solution.py:608
  161.5 2.1 pad_maximum_fusion.1.refs_0_
  166.7 33.1 %middle.1 = (f32[1280,1024]{1,0:T(8,128)}, f32[1280,1024]{1,0:T(8,128)}, bf16[2,512,1280]{2,1,0:T(8,128)(2,1)}, bf16[1280,1024]{1,0:T(8,128)(2,1)}, bf16[1280,10...) custom-call(s32[8,2]{1,0:T(8,128)} %stack.281.slots_ref, ...), custom_call_target="tpu_custom_call" | custom-call | flops 30 | bytes 1 | tf_op jit(solution)/shard_map/middle/pallas_call | solution.py:1119
  199.8 6.2 collective-permute-done.19.refs_2_
  208.8 2.7 collective-permute-done.22.refs_3_
  211.5 8.0 %assemble.2 = (bf16[4,4,2,32,2816]{4,3,2,1,0:T(8,128)(2,1)}, bf16[4,4,2,32,2816]{4,3,2,1,0:T(8,128)(2,1)}) custom-call(s32[8,2]{1,0:T(8,128)S(1)} %copy-done.4, bf16[2,2,4,32,2816]{4,3,2,1,0:T(8,128)(2,1)S(1)} %pad_maximum_fusion.1.refs_0_, bf16[2,2,4,32,2816]{4,3,2,1,0:T(8,128)(2,1)} %collective-permute-done.21.refs_1_, ...), custom_call_target="tpu_custom_call" | custom-call | flops 4 | bytes 1 | tf_op jit(solution)/shard_map/assemble/pallas_call | solution.py:1446
  219.5 6.8 %collective-permute-done.23.refs_2_ = bf16[2,1,4,88,1024]{4,3,2,1,0:T(8,128)(2,1)S(1)} collective-permute-done((bf16[2,1,4,88,1024]{4,3,2,1,0:T(8,128)(2,1)S(1)}, bf16[2,1,4,88,1024]{4,3,2,1,0:T(8,128)(2,1)S(1)}, u32[]{:S(2)}, u32[]{:S(2)}) %collective-permute-start.23) | collective-permute-done | bytes 1441824 | tf_op jit(solution)/shard_map/ppermute | solution.py:1361
  226.3 3.2 collective-permute-done.25.refs_3_
  231.1 2.5 copy-done
  233.6 91.3 %mlp.1 = (bf16[1280,1024]{1,0:T(8,128)(2,1)}, f32[1280,1024]{1,0:T(8,128)}, bf16[2,16,32,2816]{3,2,1,0:T(8,128)(2,1)}, bf16[2,16,32,2816]{3,2,1,0:T(8,128)(2,1)}...) custom-call(s32[1]{0:T(128)} %bitcast.core_ref, f32[1280,1024]{1,0:T(8,128)} %get-tuple-element.303.x_ref.x2_ref, ...), custom_call_target="tpu_custom_call" | custom-call | flops 85 | bytes 1 | tf_op jit(solution)/shard_map/mlp/pallas_call | solution.py:836
  326.0 1.8 slice.227
  329.2 12.5 %middle_back.2 = (bf16[1280,1024]{1,0:T(8,128)(2,1)}, bf16[1280,1024]{1,0:T(8,128)(2,1)}, f32[1280,1024]{1,0:T(8,128)}, bf16[1280,1024]{1,0:T(8,128)(2,1)}, bf16...) custom-call(bf16[1280,1024]{1,0:T(8,128)(2,1)} %pad_maximum_fusion.3.dy, ...), custom_call_target="tpu_custom_call" | custom-call | flops 45 | bytes 1 | tf_op jit(solution)/shard_map/middle_back/pallas_call | solution.py:1228
  341.8 9.7 %add_split.2 = (bf16[2,4,2,32,2816]{4,3,2,1,0:T(8,128)(2,1)}, bf16[2,4,2,32,2816]{4,3,2,1,0:T(8,128)(2,1)}) custom-call(s32[4]{0:T(128)} %pad_add_fusion.2.spots_ref, bf16[2,4,4,32,2816]{4,3,2,1,0:T(8,128)(2,1)} %bitcast.250, bf16[2,4,4,32,2816]{4,3,2,1,0:T(8,128)(2,1)} %bitcast.64.two_ref), custom_call_target="tpu_custom_call" | custom-call | flops 1 | bytes 1 | tf_op jit(solution)/shard_map/add_split/pallas_call | solution.py:1496
  351.9 5.7 add_split.3
  361.0 30.5 %middle_back.3 = (bf16[1280,1024]{1,0:T(8,128)(2,1)}, bf16[1280,1024]{1,0:T(8,128)(2,1)}, f32[1280,1024]{1,0:T(8,128)}, bf16[1280,1024]{1,0:T(8,128)(2,1)}, bf16...) custom-call(bf16[1280,1024]{1,0:T(8,128)(2,1)} %pad_maximum_fusion.3, ...), custom_call_target="tpu_custom_call", output_to_operand_aliasing={{0}: (14, {}), {1}: (15, {}), {2}: (16, {}), {3}: (17, {}),... | custom-call | flops 45 | bytes 1 | tf_op jit(solution)/shard_map/middle_back/pallas_call | solution.py:1228
  391.5 2.2 slice_bitcast_fusion
  393.7 11.3 %weight_part.6 = bf16[5,16,32,1024]{3,2,1,0:T(8,128)(2,1)} custom-call(s32[5]{0:T(128)} %stack.310.plan_ref, bf16[2,512,1280]{2,1,0:T(8,128)(2,1)} %get-tuple-element.363.refs_0_, bf16[2,512,1280]{2,1,0:T(8,128)(2,1)} %get-tuple-element.364.refs_1_, bf16[2,512,256]{2,1,0:T(8,128)(2,1)} %get-tuple-element.365.refs_2_, ...), custom_call_target="tpu_custom_call" | custom-call | flops 2 | bytes 1 | tf_op jit(solution)/shard_map/weight_part/pallas_call | solution.py:909
  405.1 2.5 fusion.33
  409.4 1.7 fusion.3
  416.3 19.5 %self_backward.2 = (bf16[1280,512]{1,0:T(8,128)(2,1)}, bf16[1280,512]{1,0:T(8,128)(2,1)}, bf16[1280,512]{1,0:T(8,128)(2,1)}, f32[8,1,1280]{2,1,0:T(1,128)}, f32[8,2,1,1152]{3,2,1,0:T(1,128)}) custom-call(bf16[3,1280,1024]{2,1,0:T(8,128)(2,1)} %get-tuple-element.284.q_ref.k_ref.v_ref, bf16[3,1280,1024]{2,1,0:T(8,128)(2,1)} %get-tuple-element.284.q_ref.k_ref.v_ref, ...), custom_call_target="tpu_custom_call" | custom-call | flops 32 | bytes 1 | tf_op jit(solution)/shard_map/self_backward/pallas_call | solution.py:717
  435.8 2.2 collective-permute-done.33
  438.0 1.9 fusion.5
  440.0 2.3 fusion
  442.3 12.5 %weight_part.7 = (bf16[2,4,5,32,1024]{4,3,2,1,0:T(8,128)(2,1)}, bf16[2,4,5,32,1024]{4,3,2,1,0:T(8,128)(2,1)}) custom-call(s32[5]{0:T(128)} %stack.261.plan_ref, bf16[2,512,1280]{2,1,0:T(8,128)(2,1)} %get-tuple-element.363.refs_0_, bf16[2,512,1280]{2,1,0:T(8,128)(2,1)} %get-tuple-element.364.refs_1_, bf16[2,512,256]{2,1,0:T(8,128)(2,1)} %get-tuple-element.365.refs_2_, ...), custom_call_target="tpu_custom_call" | custom-call | flops 2 | bytes 1 | tf_op jit(solution)/shard_map/weight_part/pallas_call | solution.py:909
  457.0 6.1 weight_part.8
  468.9 1.8 collective-permute-start.41
  470.7 19.2 %self_backward.3 = (bf16[1280,512]{1,0:T(8,128)(2,1)}, bf16[1280,512]{1,0:T(8,128)(2,1)}, bf16[1280,512]{1,0:T(8,128)(2,1)}, f32[8,1,1280]{2,1,0:T(1,128)}, f32[8,2,1,1152]{3,2,1,0:T(1,128)}) custom-call(bf16[3,1280,1024]{2,1,0:T(8,128)(2,1)} %get-tuple-element.284.q_ref.k_ref.v_ref, bf16[3,1280,1024]{2,1,0:T(8,128)(2,1)} %get-tuple-element.284.q_ref.k_ref.v_ref, ...), custom_call_target="tpu_custom_call" | custom-call | flops 32 | bytes 1 | tf_op jit(solution)/shard_map/self_backward/pallas_call | solution.py:717
  490.9 3.6 fusion.6
  494.4 6.1 weight_part.9
  502.9 6.6 %weight_part.10 = (bf16[2,4,3,32,512]{4,3,2,1,0:T(8,128)(2,1)}, bf16[2,4,3,32,512]{4,3,2,1,0:T(8,128)(2,1)}) custom-call(s32[5]{0:T(128)} %stack.261.plan_ref, bf16[2,512,1280]{2,1,0:T(8,128)(2,1)} %get-tuple-element.389.refs_0_, bf16[1280,512]{1,0:T(8,128)(2,1)} %get-tuple-element.390.refs_1_.refs_0_, bf16[1280,512]{1,0:T(8,128)(2,1)} %get-tuple-element.391.refs_2_.refs_1_, ...), custom_call_target="tpu_custom_call" | custom-call | flops 2 | bytes 1 | tf_op jit(solution)/shard_map/weight_part/pallas_call | solution.py:909
  514.1 12.5 %leave.2 = (f32[768,1024]{1,0:T(8,128)}, f32[8,1024]{1,0:T(8,128)}) custom-call(s32[3]{0:T(128)} %pad_add_fusion.plan_ref, bf16[1280,1024]{1,0:T(8,128)(2,1)} %pad_maximum_fusion.2.refs_4_.x_ref, f32[1280,1024]{1,0:T(8,128)} %get-tuple-element.407.dx1_ref, bf16[1280,512]{1,0:T(8,128)(2,1)} %get-tuple-element.390.refs_1_.refs_0_, ...), custom_call_target="tpu_custom_call" | custom-call | flops 2 | bytes 1 | tf_op jit(solution)/shard_map/leave/pallas_call | solution.py:1281
  526.6 6.4 %weight_part.11 = (bf16[2,4,3,32,512]{4,3,2,1,0:T(8,128)(2,1)}, bf16[2,4,3,32,512]{4,3,2,1,0:T(8,128)(2,1)}) custom-call(s32[5]{0:T(128)} %stack.261.plan_ref, bf16[2,512,1280]{2,1,0:T(8,128)(2,1)} %get-tuple-element.389.refs_0_, bf16[1280,512]{1,0:T(8,128)(2,1)} %get-tuple-element.399.refs_1_.refs_3_, bf16[1280,512]{1,0:T(8,128)(2,1)} %get-tuple-element.400.refs_2_.refs_4_, ...), custom_call_target="tpu_custom_call" | custom-call | flops 2 | bytes 1 | tf_op jit(solution)/shard_map/weight_part/pallas_call | solution.py:909
  534.7 3.0 fusion.1
  539.0 1.9 fusion.13
  542.9 10.6 %leave.3 = (f32[512,1024]{1,0:T(8,128)}, f32[8,1024]{1,0:T(8,128)}) custom-call(s32[2]{0:T(128)} %iota_add_fusion.plan_ref, bf16[1280,1024]{1,0:T(8,128)(2,1)} %pad_maximum_fusion.2.refs_4_.x_ref, f32[1280,1024]{1,0:T(8,128)} %get-tuple-element.407.dx1_ref, bf16[1280,512]{1,0:T(8,128)(2,1)} %get-tuple-element.390.refs_1_.refs_0_, ...), custom_call_target="tpu_custom_call" | custom-call | flops 2 | bytes 1 | tf_op jit(solution)/shard_map/leave/pallas_call | solution.py:1281
  560.0 1.8 collective-permute-start.46
  561.8 1.8 fusion.19
  565.8 5.2 collective-permute-done.46
  573.7 2.3 collective-permute-start.49
  576.0 2.3 multiply_reduce_fusion.2
  578.4 2.7 multiply_reduce_fusion
  582.3 2.7 select_bitcast_fusion.1
  585.0 2.3 pad_maximum_fusion
  591.8 1.9 multiply_reduce_fusion.1
  599.8 2.5 collective-permute-start.54
  602.4 2.4 collective-permute-start.56
  611.4 2.4 collective-permute-done.59
  620.3 5.8 update.1
  (302 shorter events, 102.3 us)
Async XLA Ops:
  2.0 13.2 %collective-permute-start = (bf16[3,32,1024]{2,1,0:T(8,128)(2,1)S(1)}, bf16[3,32,1024]{2,1,0:T(8,128)(2,1)S(1)}, u32[]{:S(2)}, u32[]{:S(2)}) collective-permute-start(bf16[3,32,1024]{2,1,0:T(8,128)(2,1)S(1)} %get-tuple-element.681.shard), channel_id=1, source_target_pairs={{0,16},{1,17},{2,18},{3,19},{4,20},{5,21},{6,22},{7,23},{8,24},{9,... | collective-permute-start | bytes 589832 | tf_op jit(solution)/shard_map/ppermute | solution.py:1361
  7.4 1.2 collective-permute-start.1
  11.3 23.0 %copy-start.37 = (s32[2]{0:T(128)}, s32[2]{0:T(128)S(1)}, u32[]{:S(2)}) copy-start(s32[2]{0:T(128)S(1)} %pad_add_fusion.1.starts_ref) | copy-start | bytes 28
  15.2 10.4 %collective-permute-start.2 = (bf16[2,3,32,1024]{3,2,1,0:T(8,128)(2,1)S(1)}, bf16[2,3,32,1024]{3,2,1,0:T(8,128)(2,1)S(1)}, u32[]{:S(2)}, u32[]{:S(2)}) collective-permute-start(bf16[2,3,32,1024]{3,2,1,0:T(8,128)(2,1)S(1)} %pad_maximum_fusion.18), channel_id=1, source_target_pairs={{0,8},{1,9},{2,10},{3,11},{4,12},{5,13},{6,14},{7,15},{8,0},{9,1},... | collective-permute-start | bytes 1179656 | tf_op jit(solution)/shard_map/ppermute | solution.py:1361
  31.1 26.1 %collective-permute-start.8 = (bf16[1408,1024]{1,0:T(8,128)(2,1)}, bf16[1408,1024]{1,0:T(8,128)(2,1)}, u32[]{:S(2)}, u32[]{:S(2)}) collective-permute-start(bf16[1408,1024]{1,0:T(8,128)(2,1)} %get-tuple-element.670), channel_id=1, source_target_pairs={{0,1},{1,0},{2,3},{3,2},{4,5},{5,4},{6,7},{7,6},{8,9},{9,8},{10,11... | collective-permute-start | bytes 8650760 | tf_op jit(solution)/shard_map/ppermute | solution.py:1361
  33.0 12.2 %collective-permute-start.3 = (bf16[3,4,32,1024]{3,2,1,0:T(8,128)(2,1)S(1)}, bf16[3,4,32,1024]{3,2,1,0:T(8,128)(2,1)}, u32[]{:S(2)}, u32[]{:S(2)}) collective-permute-start(bf16[3,4,32,1024]{3,2,1,0:T(8,128)(2,1)S(1)} %put_in_line.4), channel_id=1, source_target_pairs={{0,2},{1,5},{2,0},{3,7},{4,6},{5,1},{6,4},{7,3},{8,10},{9,13},{10,... | collective-permute-start | bytes 2359304 | tf_op jit(solution)/shard_map/ppermute | solution.py:1361
  37.7 18.6 %collective-permute-start.4 = (bf16[5,32,1024]{2,1,0:T(8,128)(2,1)S(1)}, bf16[5,32,1024]{2,1,0:T(8,128)(2,1)S(1)}, u32[]{:S(2)}, u32[]{:S(2)}) collective-permute-start(bf16[5,32,1024]{2,1,0:T(8,128)(2,1)S(1)} %pad_maximum_fusion.21.shard), channel_id=1, source_target_pairs={{0,16},{1,17},{2,18},{3,19},{4,20},{5,21},{6,22},{7,23},{8,24},{9,... | collective-permute-start | bytes 983048 | tf_op jit(solution)/shard_map/ppermute | solution.py:1361
  46.4 26.4 %collective-permute-start.5 = (bf16[2,3,4,32,1024]{4,3,2,1,0:T(8,128)(2,1)S(1)}, bf16[2,3,4,32,1024]{4,3,2,1,0:T(8,128)(2,1)}, u32[]{:S(2)}, u32[]{:S(2)}) collective-permute-start(bf16[2,3,4,32,1024]{4,3,2,1,0:T(8,128)(2,1)S(1)} %pad_maximum_fusion.5.refs_0_), channel_id=1, source_target_pairs={{0,4},{1,3},{2,6},{3,1},{4,0},{5,7},{6,2},{7,5},{8,12},{9,11},{10,... | collective-permute-start | bytes 4718600 | tf_op jit(solution)/shard_map/ppermute | solution.py:1361
  56.4 16.5 %collective-permute-start.6 = (bf16[2,5,32,1024]{3,2,1,0:T(8,128)(2,1)S(1)}, bf16[2,5,32,1024]{3,2,1,0:T(8,128)(2,1)S(1)}, u32[]{:S(2)}, u32[]{:S(2)}) collective-permute-start(bf16[2,5,32,1024]{3,2,1,0:T(8,128)(2,1)S(1)} %pad_maximum_fusion.14), channel_id=1, source_target_pairs={{0,8},{1,9},{2,10},{3,11},{4,12},{5,13},{6,14},{7,15},{8,0},{9,1},... | collective-permute-start | bytes 1966088 | tf_op jit(solution)/shard_map/ppermute | solution.py:1361
  57.2 15.7 %collective-permute-start.7 = (bf16[2,3,4,32,1024]{4,3,2,1,0:T(8,128)(2,1)S(1)}, bf16[2,3,4,32,1024]{4,3,2,1,0:T(8,128)(2,1)S(1)}, u32[]{:S(2)}, u32[]{:S(2)}) collective-permute-start(bf16[2,3,4,32,1024]{4,3,2,1,0:T(8,128)(2,1)S(1)} %pad_maximum_fusion.5.refs_0_), channel_id=1, source_target_pairs={{0,1},{1,0},{2,3},{3,2},{4,5},{5,4},{6,7},{7,6},{8,9},{9,8},{10,11... | collective-permute-start | bytes 4718600 | tf_op jit(solution)/shard_map/ppermute | solution.py:1361
  72.8 6.6 %collective-permute-start.9 = (bf16[2,3,4,32,1024]{4,3,2,1,0:T(8,128)(2,1)}, bf16[2,3,4,32,1024]{4,3,2,1,0:T(8,128)(2,1)}, u32[]{:S(2)}, u32[]{:S(2)}) collective-permute-start(bf16[2,3,4,32,1024]{4,3,2,1,0:T(8,128)(2,1)} %collective-permute-done.5.refs_2_), channel_id=1, source_target_pairs={{0,1},{1,0},{2,3},{3,2},{4,5},{5,4},{6,7},{7,6},{8,9},{9,8},{10,11... | collective-permute-start | bytes 4718600 | tf_op jit(solution)/shard_map/ppermute | solution.py:1361
  74.0 22.5 %collective-permute-start.10 = (bf16[5,4,32,1024]{3,2,1,0:T(8,128)(2,1)S(1)}, bf16[5,4,32,1024]{3,2,1,0:T(8,128)(2,1)}, u32[]{:S(2)}, u32[]{:S(2)}) collective-permute-start(bf16[5,4,32,1024]{3,2,1,0:T(8,128)(2,1)S(1)} %put_in_line.5), channel_id=1, source_target_pairs={{0,2},{1,5},{2,0},{3,7},{4,6},{5,1},{6,4},{7,3},{8,10},{9,13},{10,... | collective-permute-start | bytes 3932168 | tf_op jit(solution)/shard_map/ppermute | solution.py:1361
  75.2 21.3 %collective-permute-start.11 = (bf16[2,32,2816]{2,1,0:T(8,128)(2,1)S(1)}, bf16[2,32,2816]{2,1,0:T(8,128)(2,1)S(1)}, u32[]{:S(2)}, u32[]{:S(2)}) collective-permute-start(bf16[2,32,2816]{2,1,0:T(8,128)(2,1)S(1)} %convert_element_type.428.shard), channel_id=1, source_target_pairs={{0,16},{1,17},{2,18},{3,19},{4,20},{5,21},{6,22},{7,23},{8,24},{9,... | collective-permute-start | bytes 1081352 | tf_op jit(solution)/shard_map/ppermute | solution.py:1361
  99.5 32.0 %collective-permute-start.12 = (bf16[2,5,4,32,1024]{4,3,2,1,0:T(8,128)(2,1)}, bf16[2,5,4,32,1024]{4,3,2,1,0:T(8,128)(2,1)}, u32[]{:S(2)}, u32[]{:S(2)}) collective-permute-start(bf16[2,5,4,32,1024]{4,3,2,1,0:T(8,128)(2,1)} %pad_maximum_fusion.4.refs_0_), channel_id=1, source_target_pairs={{0,4},{1,3},{2,6},{3,1},{4,0},{5,7},{6,2},{7,5},{8,12},{9,11},{10,... | collective-permute-start | bytes 7864328 | tf_op jit(solution)/shard_map/ppermute | solution.py:1361
  100.2 31.3 %collective-permute-start.13 = (bf16[2,5,4,32,1024]{4,3,2,1,0:T(8,128)(2,1)}, bf16[2,5,4,32,1024]{4,3,2,1,0:T(8,128)(2,1)}, u32[]{:S(2)}, u32[]{:S(2)}) collective-permute-start(bf16[2,5,4,32,1024]{4,3,2,1,0:T(8,128)(2,1)} %pad_maximum_fusion.4.refs_0_), channel_id=1, source_target_pairs={{0,1},{1,0},{2,3},{3,2},{4,5},{5,4},{6,7},{7,6},{8,9},{9,8},{10,11... | collective-permute-start | bytes 7864328 | tf_op jit(solution)/shard_map/ppermute | solution.py:1361
  100.3 27.1 %collective-permute-start.14 = (bf16[2,2,32,2816]{3,2,1,0:T(8,128)(2,1)S(1)}, bf16[2,2,32,2816]{3,2,1,0:T(8,128)(2,1)S(1)}, u32[]{:S(2)}, u32[]{:S(2)}) collective-permute-start(bf16[2,2,32,2816]{3,2,1,0:T(8,128)(2,1)S(1)} %pad_maximum_fusion.12), channel_id=1, source_target_pairs={{0,8},{1,9},{2,10},{3,11},{4,12},{5,13},{6,14},{7,15},{8,0},{9,1},... | collective-permute-start | bytes 2162696 | tf_op jit(solution)/shard_map/ppermute | solution.py:1361
  102.1 25.3 %collective-permute-start.15 = (bf16[1,88,1024]{2,1,0:T(8,128)(2,1)S(1)}, bf16[1,88,1024]{2,1,0:T(8,128)(2,1)S(1)}, u32[]{:S(2)}, u32[]{:S(2)}) collective-permute-start(bf16[1,88,1024]{2,1,0:T(8,128)(2,1)S(1)} %convert_bitcast_fusion.shard), channel_id=1, source_target_pairs={{0,16},{1,17},{2,18},{3,19},{4,20},{5,21},{6,22},{7,23},{8,24},{9,... | collective-permute-start | bytes 540680 | tf_op jit(solution)/shard_map/ppermute | solution.py:1361
  131.5 28.9 %collective-permute-start.16 = (bf16[2,5,4,32,1024]{4,3,2,1,0:T(8,128)(2,1)}, bf16[2,5,4,32,1024]{4,3,2,1,0:T(8,128)(2,1)}, u32[]{:S(2)}, u32[]{:S(2)}) collective-permute-start(bf16[2,5,4,32,1024]{4,3,2,1,0:T(8,128)(2,1)} %collective-permute-done.12.refs_2_), channel_id=1, source_target_pairs={{0,1},{1,0},{2,3},{3,2},{4,5},{5,4},{6,7},{7,6},{8,9},{9,8},{10,11... | collective-permute-start | bytes 7864328 | tf_op jit(solution)/shard_map/ppermute | solution.py:1361
  131.9 27.8 %copy-start.1 = (bf16[2,4,32,2816]{3,2,1,0:T(8,128)(2,1)}, bf16[2,4,32,2816]{3,2,1,0:T(8,128)(2,1)S(1)}, u32[]{:S(2)}) copy-start(bf16[2,4,32,2816]{3,2,1,0:T(8,128)(2,1)S(1)} %put_in_line.6) | copy-start | bytes 4325380
  131.9 28.5 %collective-permute-start.17 = (bf16[2,4,32,2816]{3,2,1,0:T(8,128)(2,1)S(1)}, bf16[2,4,32,2816]{3,2,1,0:T(8,128)(2,1)S(1)}, u32[]{:S(2)}, u32[]{:S(2)}) collective-permute-start(bf16[2,4,32,2816]{3,2,1,0:T(8,128)(2,1)S(1)} %put_in_line.6), channel_id=1, source_target_pairs={{0,2},{1,5},{2,0},{3,7},{4,6},{5,1},{6,4},{7,3},{8,10},{9,13},{10,... | collective-permute-start | bytes 4325384 | tf_op jit(solution)/shard_map/ppermute | solution.py:1361
  132.7 26.9 %collective-permute-start.18 = (bf16[2,1,88,1024]{3,2,1,0:T(8,128)(2,1)S(1)}, bf16[2,1,88,1024]{3,2,1,0:T(8,128)(2,1)S(1)}, u32[]{:S(2)}, u32[]{:S(2)}) collective-permute-start(bf16[2,1,88,1024]{3,2,1,0:T(8,128)(2,1)S(1)} %pad_maximum_fusion.19), channel_id=1, source_target_pairs={{0,8},{1,9},{2,10},{3,11},{4,12},{5,13},{6,14},{7,15},{8,0},{9,1},... | collective-permute-start | bytes 1081352 | tf_op jit(solution)/shard_map/ppermute | solution.py:1361
  163.6 42.4 %collective-permute-start.19 = (bf16[2,2,4,32,2816]{4,3,2,1,0:T(8,128)(2,1)S(1)}, bf16[2,2,4,32,2816]{4,3,2,1,0:T(8,128)(2,1)}, u32[]{:S(2)}, u32[]{:S(2)}) collective-permute-start(bf16[2,2,4,32,2816]{4,3,2,1,0:T(8,128)(2,1)S(1)} %pad_maximum_fusion.1.refs_0_), channel_id=1, source_target_pairs={{0,4},{1,3},{2,6},{3,1},{4,0},{5,7},{6,2},{7,5},{8,12},{9,11},{10,... | collective-permute-start | bytes 8650760 | tf_op jit(solution)/shard_map/ppermute | solution.py:1361
  164.2 41.8 %collective-permute-start.21 = (bf16[2,2,4,32,2816]{4,3,2,1,0:T(8,128)(2,1)S(1)}, bf16[2,2,4,32,2816]{4,3,2,1,0:T(8,128)(2,1)}, u32[]{:S(2)}, u32[]{:S(2)}) collective-permute-start(bf16[2,2,4,32,2816]{4,3,2,1,0:T(8,128)(2,1)S(1)} %pad_maximum_fusion.1.refs_0_), channel_id=1, source_target_pairs={{0,1},{1,0},{2,3},{3,2},{4,5},{5,4},{6,7},{7,6},{8,9},{9,8},{10,11... | collective-permute-start | bytes 8650760 | tf_op jit(solution)/shard_map/ppermute | solution.py:1361
  165.1 34.7 %collective-permute-start.20 = (bf16[1,4,88,1024]{3,2,1,0:T(8,128)(2,1)S(1)}, bf16[1,4,88,1024]{3,2,1,0:T(8,128)(2,1)}, u32[]{:S(2)}, u32[]{:S(2)}) collective-permute-start(bf16[1,4,88,1024]{3,2,1,0:T(8,128)(2,1)S(1)} %put_in_line.7), channel_id=1, source_target_pairs={{0,2},{1,5},{2,0},{3,7},{4,6},{5,1},{6,4},{7,3},{8,10},{9,13},{10,... | collective-permute-start | bytes 2162696 | tf_op jit(solution)/shard_map/ppermute | solution.py:1361
  206.0 5.5 collective-permute-start.22
  207.2 19.1 %collective-permute-start.23 = (bf16[2,1,4,88,1024]{4,3,2,1,0:T(8,128)(2,1)S(1)}, bf16[2,1,4,88,1024]{4,3,2,1,0:T(8,128)(2,1)S(1)}, u32[]{:S(2)}, u32[]{:S(2)}) collective-permute-start(bf16[2,1,4,88,1024]{4,3,2,1,0:T(8,128)(2,1)S(1)} %pad_maximum_fusion.6.refs_0_), channel_id=1, source_target_pairs={{0,4},{1,3},{2,6},{3,1},{4,0},{5,7},{6,2},{7,5},{8,12},{9,11},{10,... | collective-permute-start | bytes 4325384 | tf_op jit(solution)/shard_map/ppermute | solution.py:1361
  207.8 18.5 %collective-permute-start.24 = (bf16[2,1,4,88,1024]{4,3,2,1,0:T(8,128)(2,1)S(1)}, bf16[2,1,4,88,1024]{4,3,2,1,0:T(8,128)(2,1)S(1)}, u32[]{:S(2)}, u32[]{:S(2)}) collective-permute-start(bf16[2,1,4,88,1024]{4,3,2,1,0:T(8,128)(2,1)S(1)} %pad_maximum_fusion.6.refs_0_), channel_id=1, source_target_pairs={{0,1},{1,0},{2,3},{3,2},{4,5},{5,4},{6,7},{7,6},{8,9},{9,8},{10,11... | collective-permute-start | bytes 4325384 | tf_op jit(solution)/shard_map/ppermute | solution.py:1361
  226.3 3.2 collective-permute-start.25
  324.9 16.9 %collective-permute-start.26 = (bf16[2,16,32,2816]{3,2,1,0:T(8,128)(2,1)}, bf16[2,16,32,2816]{3,2,1,0:T(8,128)(2,1)}, u32[]{:S(2)}, u32[]{:S(2)}) collective-permute-start(bf16[2,16,32,2816]{3,2,1,0:T(8,128)(2,1)} %get-tuple-element.318), channel_id=1, source_target_pairs={{0,1},{1,0},{2,3},{3,2},{4,5},{5,4},{6,7},{7,6},{8,9},{9,8},{10,11... | collective-permute-start | bytes 17301512 | tf_op jit(solution)/shard_map/ppermute | solution.py:1361
  325.1 16.7 %collective-permute-start.27 = (bf16[1,16,88,1024]{3,2,1,0:T(8,128)(2,1)}, bf16[1,16,88,1024]{3,2,1,0:T(8,128)(2,1)}, u32[]{:S(2)}, u32[]{:S(2)}) collective-permute-start(bf16[1,16,88,1024]{3,2,1,0:T(8,128)(2,1)} %bitcast.268), channel_id=1, source_target_pairs={{0,1},{1,0},{2,3},{3,2},{4,5},{5,4},{6,7},{7,6},{8,9},{9,8},{10,11... | collective-permute-start | bytes 8650760 | tf_op jit(solution)/shard_map/ppermute | solution.py:1361
  351.5 57.0 %collective-permute-start.29 = (bf16[2,4,2,32,2816]{4,3,2,1,0:T(8,128)(2,1)}, bf16[2,4,2,32,2816]{4,3,2,1,0:T(8,128)(2,1)}, u32[]{:S(2)}, u32[]{:S(2)}) collective-permute-start(bf16[2,4,2,32,2816]{4,3,2,1,0:T(8,128)(2,1)} %get-tuple-element.351), channel_id=1, source_target_pairs={{0,4},{1,3},{2,6},{3,1},{4,0},{5,7},{6,2},{7,5},{8,12},{9,11},{10,... | collective-permute-start | bytes 8650760 | tf_op jit(solution)/shard_map/ppermute | solution.py:1361
  357.6 50.8 %collective-permute-start.30 = (bf16[2,4,1,88,1024]{4,3,1,2,0:T(8,128)(2,1)}, bf16[2,4,1,88,1024]{4,3,1,2,0:T(8,128)(2,1)}, u32[]{:S(2)}, u32[]{:S(2)}) collective-permute-start(bf16[2,4,1,88,1024]{4,3,1,2,0:T(8,128)(2,1)} %bitcast.269), channel_id=1, source_target_pairs={{0,4},{1,3},{2,6},{3,1},{4,0},{5,7},{6,2},{7,5},{8,12},{9,11},{10,... | collective-permute-start | bytes 4325384 | tf_op jit(solution)/shard_map/ppermute | solution.py:1361
  360.4 48.0 %collective-permute-start.28 = (bf16[640,1024]{1,0:T(8,128)(2,1)}, bf16[640,1024]{1,0:T(8,128)(2,1)}, u32[]{:S(2)}, u32[]{:S(2)}) collective-permute-start(bf16[640,1024]{1,0:T(8,128)(2,1)} %pad_maximum_fusion.8), channel_id=1, source_target_pairs={{0,1},{1,0},{2,3},{3,2},{4,5},{5,4},{6,7},{7,6},{8,9},{9,8},{10,11... | collective-permute-start | bytes 3932168 | tf_op jit(solution)/shard_map/ppermute | solution.py:1361
  408.4 29.6 %collective-permute-start.31 = (bf16[5,16,32,1024]{3,2,1,0:T(8,128)(2,1)}, bf16[5,16,32,1024]{3,2,1,0:T(8,128)(2,1)}, u32[]{:S(2)}, u32[]{:S(2)}) collective-permute-start(bf16[5,16,32,1024]{3,2,1,0:T(8,128)(2,1)} %weight_part.6), channel_id=1, source_target_pairs={{0,1},{1,0},{2,3},{3,2},{4,5},{5,4},{6,7},{7,6},{8,9},{9,8},{10,11... | collective-permute-start | bytes 15728648 | tf_op jit(solution)/shard_map/ppermute | solution.py:1361
  411.1 26.9 %collective-permute-start.34 = (bf16[4,2,32,2816]{3,2,1,0:T(8,128)(2,1)S(1)}, bf16[4,2,32,2816]{3,2,1,0:T(8,128)(2,1)}, u32[]{:S(2)}, u32[]{:S(2)}) collective-permute-start(bf16[4,2,32,2816]{3,2,1,0:T(8,128)(2,1)S(1)} %fusion.3), channel_id=1, source_target_pairs={{0,2},{1,5},{2,0},{3,7},{4,6},{5,1},{6,4},{7,3},{8,10},{9,13},{10,... | collective-permute-start | bytes 4325384 | tf_op jit(solution)/shard_map/ppermute | solution.py:1361
  413.8 24.2 %collective-permute-start.33 = (bf16[4,1,88,1024]{3,2,1,0:T(8,128)(2,1)S(1)}, bf16[4,1,88,1024]{3,2,1,0:T(8,128)(2,1)}, u32[]{:S(2)}, u32[]{:S(2)}) collective-permute-start(bf16[4,1,88,1024]{3,2,1,0:T(8,128)(2,1)S(1)} %fusion.10), channel_id=1, source_target_pairs={{0,2},{1,5},{2,0},{3,7},{4,6},{5,1},{6,4},{7,3},{8,10},{9,13},{10,... | collective-permute-start | bytes 2162696 | tf_op jit(solution)/shard_map/ppermute | solution.py:1361
  415.7 20.1 %collective-permute-start.32 = (f32[128,1024]{1,0:T(8,128)}, f32[128,1024]{1,0:T(8,128)}, u32[]{:S(2)}, u32[]{:S(2)}) collective-permute-start(f32[128,1024]{1,0:T(8,128)} %get-tuple-element.659), channel_id=1, source_target_pairs={{0,1},{1,0},{2,3},{3,2},{4,5},{5,4},{6,7},{7,6},{8,9},{9,8},{10,11... | collective-permute-start | bytes 1572872 | tf_op jit(solution)/shard_map/ppermute | solution.py:1361
  454.7 36.1 %collective-permute-start.36 = (bf16[2,4,5,32,1024]{4,3,2,1,0:T(8,128)(2,1)}, bf16[2,4,5,32,1024]{4,3,2,1,0:T(8,128)(2,1)}, u32[]{:S(2)}, u32[]{:S(2)}) collective-permute-start(bf16[2,4,5,32,1024]{4,3,2,1,0:T(8,128)(2,1)} %get-tuple-element.387), channel_id=1, source_target_pairs={{0,4},{1,3},{2,6},{3,1},{4,0},{5,7},{6,2},{7,5},{8,12},{9,11},{10,... | collective-permute-start | bytes 7864328 | tf_op jit(solution)/shard_map/ppermute | solution.py:1361
  463.1 27.7 %collective-permute-start.35 = (bf16[3,16,32,512]{3,2,1,0:T(8,128)(2,1)}, bf16[3,16,32,512]{3,2,1,0:T(8,128)(2,1)}, u32[]{:S(2)}, u32[]{:S(2)}) collective-permute-start(bf16[3,16,32,512]{3,2,1,0:T(8,128)(2,1)} %weight_part.8), channel_id=1, source_target_pairs={{0,1},{1,0},{2,3},{3,2},{4,5},{5,4},{6,7},{7,6},{8,9},{9,8},{10,11... | collective-permute-start | bytes 4718600 | tf_op jit(solution)/shard_map/ppermute | solution.py:1361
  466.2 24.7 %collective-permute-start.37 = (bf16[2,2,32,2816]{3,2,1,0:T(8,128)(2,1)}, bf16[2,2,32,2816]{3,2,1,0:T(8,128)(2,1)S(1)}, u32[]{:S(2)}, u32[]{:S(2)}) collective-permute-start(bf16[2,2,32,2816]{3,2,1,0:T(8,128)(2,1)} %pad_maximum_fusion.13), channel_id=1, source_target_pairs={{0,8},{1,9},{2,10},{3,11},{4,12},{5,13},{6,14},{7,15},{8,0},{9,1},... | collective-permute-start | bytes 2162696 | tf_op jit(solution)/shard_map/ppermute | solution.py:1361
  468.9 57.7 %collective-permute-start.41 = (bf16[2,1,88,1024]{3,2,1,0:T(8,128)(2,1)}, bf16[2,1,88,1024]{3,2,1,0:T(8,128)(2,1)}, u32[]{:S(2)}, u32[]{:S(2)}) collective-permute-start(bf16[2,1,88,1024]{3,2,1,0:T(8,128)(2,1)} %pad_maximum_fusion.20), channel_id=1, source_target_pairs={{0,8},{1,9},{2,10},{3,11},{4,12},{5,13},{6,14},{7,15},{8,0},{9,1},... | collective-permute-start | bytes 1081352 | tf_op jit(solution)/shard_map/ppermute | solution.py:1361
  500.5 13.6 %collective-permute-start.38 = (bf16[3,16,32,512]{3,2,1,0:T(8,128)(2,1)}, bf16[3,16,32,512]{3,2,1,0:T(8,128)(2,1)}, u32[]{:S(2)}, u32[]{:S(2)}) collective-permute-start(bf16[3,16,32,512]{3,2,1,0:T(8,128)(2,1)} %weight_part.9), channel_id=1, source_target_pairs={{0,1},{1,0},{2,3},{3,2},{4,5},{5,4},{6,7},{7,6},{8,9},{9,8},{10,11... | collective-permute-start | bytes 4718600 | tf_op jit(solution)/shard_map/ppermute | solution.py:1361
  500.5 26.0 %collective-permute-start.40 = (bf16[4,5,32,1024]{3,2,1,0:T(8,128)(2,1)}, bf16[4,5,32,1024]{3,2,1,0:T(8,128)(2,1)}, u32[]{:S(2)}, u32[]{:S(2)}) collective-permute-start(bf16[4,5,32,1024]{3,2,1,0:T(8,128)(2,1)} %fusion.6), channel_id=1, source_target_pairs={{0,2},{1,5},{2,0},{3,7},{4,6},{5,1},{6,4},{7,3},{8,10},{9,13},{10,... | collective-permute-start | bytes 3932168 | tf_op jit(solution)/shard_map/ppermute | solution.py:1361
  509.5 17.1 %collective-permute-start.39 = (bf16[2,4,3,32,512]{4,3,2,1,0:T(8,128)(2,1)}, bf16[2,4,3,32,512]{4,3,2,1,0:T(8,128)(2,1)}, u32[]{:S(2)}, u32[]{:S(2)}) collective-permute-start(bf16[2,4,3,32,512]{4,3,2,1,0:T(8,128)(2,1)} %get-tuple-element.405), channel_id=1, source_target_pairs={{0,4},{1,3},{2,6},{3,1},{4,0},{5,7},{6,2},{7,5},{8,12},{9,11},{10,... | collective-permute-start | bytes 2359304 | tf_op jit(solution)/shard_map/ppermute | solution.py:1361
  514.1 49.5 %collective-permute-start.48 = (bf16[2,32,2816]{2,1,0:T(8,128)(2,1)}, bf16[2,32,2816]{2,1,0:T(8,128)(2,1)}, u32[]{:S(2)}, u32[]{:S(2)}) collective-permute-start(bf16[2,32,2816]{2,1,0:T(8,128)(2,1)} %fusion.17), channel_id=1, source_target_pairs={{0,16},{1,17},{2,18},{3,19},{4,20},{5,21},{6,22},{7,23},{8,24},{9,... | collective-permute-start | bytes 1081352 | tf_op jit(solution)/shard_map/ppermute | solution.py:1361
  533.0 23.0 %collective-permute-start.42 = (bf16[2,4,3,32,512]{4,3,2,1,0:T(8,128)(2,1)}, bf16[2,4,3,32,512]{4,3,2,1,0:T(8,128)(2,1)}, u32[]{:S(2)}, u32[]{:S(2)}) collective-permute-start(bf16[2,4,3,32,512]{4,3,2,1,0:T(8,128)(2,1)} %get-tuple-element.415), channel_id=1, source_target_pairs={{0,4},{1,3},{2,6},{3,1},{4,0},{5,7},{6,2},{7,5},{8,12},{9,11},{10,... | collective-permute-start | bytes 2359304 | tf_op jit(solution)/shard_map/ppermute | solution.py:1361
  534.5 47.9 %collective-permute-start.52 = (f32[768,1024]{1,0:T(8,128)}, f32[768,1024]{1,0:T(8,128)}, u32[]{:S(2)}, u32[]{:S(2)}) collective-permute-start(f32[768,1024]{1,0:T(8,128)} %get-tuple-element.439), channel_id=1, source_target_pairs={{0,1},{1,0},{2,3},{3,2},{4,5},{5,4},{6,7},{7,6},{8,9},{9,8},{10,11... | collective-permute-start | bytes 9437192 | tf_op jit(solution)/shard_map/ppermute | solution.py:1361
  538.7 17.4 %collective-permute-start.44 = (bf16[2,5,32,1024]{3,2,1,0:T(8,128)(2,1)}, bf16[2,5,32,1024]{3,2,1,0:T(8,128)(2,1)}, u32[]{:S(2)}, u32[]{:S(2)}) collective-permute-start(bf16[2,5,32,1024]{3,2,1,0:T(8,128)(2,1)} %pad_maximum_fusion.15), channel_id=1, source_target_pairs={{0,8},{1,9},{2,10},{3,11},{4,12},{5,13},{6,14},{7,15},{8,0},{9,1},... | collective-permute-start | bytes 1966088 | tf_op jit(solution)/shard_map/ppermute | solution.py:1361
  540.9 13.5 %collective-permute-start.43 = (bf16[4,3,32,512]{3,2,1,0:T(8,128)(2,1)}, bf16[4,3,32,512]{3,2,1,0:T(8,128)(2,1)S(1)}, u32[]{:S(2)}, u32[]{:S(2)}) collective-permute-start(bf16[4,3,32,512]{3,2,1,0:T(8,128)(2,1)} %fusion.13), channel_id=1, source_target_pairs={{0,2},{1,5},{2,0},{3,7},{4,6},{5,1},{6,4},{7,3},{8,10},{9,13},{10,... | collective-permute-start | bytes 1179656 | tf_op jit(solution)/shard_map/ppermute | solution.py:1361
  554.4 11.4 %collective-permute-start.47 = (bf16[1,88,1024]{2,1,0:T(8,128)(2,1)S(1)}, bf16[1,88,1024]{2,1,0:T(8,128)(2,1)S(1)}, u32[]{:S(2)}, u32[]{:S(2)}) collective-permute-start(bf16[1,88,1024]{2,1,0:T(8,128)(2,1)S(1)} %fusion.27), channel_id=1, source_target_pairs={{0,16},{1,17},{2,18},{3,19},{4,20},{5,21},{6,22},{7,23},{8,24},{9,... | collective-permute-start | bytes 540680 | tf_op jit(solution)/shard_map/ppermute | solution.py:1361
  557.3 13.7 %collective-permute-start.45 = (bf16[4,3,32,512]{3,2,1,0:T(8,128)(2,1)S(1)}, bf16[4,3,32,512]{3,2,1,0:T(8,128)(2,1)S(1)}, u32[]{:S(2)}, u32[]{:S(2)}) collective-permute-start(bf16[4,3,32,512]{3,2,1,0:T(8,128)(2,1)S(1)} %fusion.14), channel_id=1, source_target_pairs={{0,2},{1,5},{2,0},{3,7},{4,6},{5,1},{6,4},{7,3},{8,10},{9,13},{10,... | collective-permute-start | bytes 1179656 | tf_op jit(solution)/shard_map/ppermute | solution.py:1361
  560.0 11.0 %collective-permute-start.46 = (bf16[2,3,32,512]{3,2,1,0:T(8,128)(2,1)S(1)}, bf16[2,3,32,512]{3,2,1,0:T(8,128)(2,1)S(1)}, u32[]{:S(2)}, u32[]{:S(2)}) collective-permute-start(bf16[2,3,32,512]{3,2,1,0:T(8,128)(2,1)S(1)} %pad_maximum_fusion.23), channel_id=1, source_target_pairs={{0,8},{1,9},{2,10},{3,11},{4,12},{5,13},{6,14},{7,15},{8,0},{9,1},... | collective-permute-start | bytes 589832 | tf_op jit(solution)/shard_map/ppermute | solution.py:1361
  563.6 23.8 %collective-permute-start.51 = (bf16[5,32,1024]{2,1,0:T(8,128)(2,1)}, bf16[5,32,1024]{2,1,0:T(8,128)(2,1)}, u32[]{:S(2)}, u32[]{:S(2)}) collective-permute-start(bf16[5,32,1024]{2,1,0:T(8,128)(2,1)} %fusion.19), channel_id=1, source_target_pairs={{0,16},{1,17},{2,18},{3,19},{4,20},{5,21},{6,22},{7,23},{8,24},{9,... | collective-permute-start | bytes 983048 | tf_op jit(solution)/shard_map/ppermute | solution.py:1361
  571.7 15.6 %collective-permute-start.50 = (bf16[3,32,512]{2,1,0:T(8,128)(2,1)}, bf16[3,32,512]{2,1,0:T(8,128)(2,1)}, u32[]{:S(2)}, u32[]{:S(2)}) collective-permute-start(bf16[3,32,512]{2,1,0:T(8,128)(2,1)} %fusion.28), channel_id=1, source_target_pairs={{0,16},{1,17},{2,18},{3,19},{4,20},{5,21},{6,22},{7,23},{8,24},{9,... | collective-permute-start | bytes 294920 | tf_op jit(solution)/shard_map/ppermute | solution.py:1361
  573.7 14.4 %collective-permute-start.49 = (bf16[2,3,32,512]{3,2,1,0:T(8,128)(2,1)}, bf16[2,3,32,512]{3,2,1,0:T(8,128)(2,1)}, u32[]{:S(2)}, u32[]{:S(2)}) collective-permute-start(bf16[2,3,32,512]{3,2,1,0:T(8,128)(2,1)} %pad_maximum_fusion.24), channel_id=1, source_target_pairs={{0,8},{1,9},{2,10},{3,11},{4,12},{5,13},{6,14},{7,15},{8,0},{9,1},... | collective-permute-start | bytes 589832 | tf_op jit(solution)/shard_map/ppermute | solution.py:1361
  589.0 8.3 %collective-permute-start.53 = (bf16[3,32,512]{2,1,0:T(8,128)(2,1)S(1)}, bf16[3,32,512]{2,1,0:T(8,128)(2,1)S(1)}, u32[]{:S(2)}, u32[]{:S(2)}) collective-permute-start(bf16[3,32,512]{2,1,0:T(8,128)(2,1)S(1)} %fusion.29), channel_id=1, source_target_pairs={{0,16},{1,17},{2,18},{3,19},{4,20},{5,21},{6,22},{7,23},{8,24},{9,... | collective-permute-start | bytes 294920 | tf_op jit(solution)/shard_map/ppermute | solution.py:1361
  597.4 22.3 %copy-start.41 = (f32[32,16]{0,1:T(8,128)S(1)}, f32[32,16]{0,1:T(8,128)}, u32[]{:S(2)}) copy-start(f32[32,16]{0,1:T(8,128)} %param.49) | copy-start | bytes 6148
  599.8 5.6 collective-permute-start.54
  602.3 4.6 collective-permute-start.55
  602.4 4.6 collective-permute-start.56
  607.0 4.3 collective-permute-start.57
  607.7 3.7 collective-permute-start.58
  609.1 4.6 collective-permute-start.59
  613.8 1.2 collective-permute-start.60
  (40 other events, 319.7 us)

commit v3 on v2

--- a/solution.py
+++ b/solution.py
@@ -770,8 +770,8 @@
     return jnp.dot(sums, buckets, precision=lax.Precision.HIGHEST).T
 
 
-def mlp_kernel(core_ref, x_ref, a_ref, a_t, dy_ref, wg_ref, wu_ref, wd_ref, out_ref, da_ref, away_ref, keep_ref,
-               away_con_ref, keep_con_ref, y_ref, hid, dgate, dup, dwd, sem):
+def mlp_kernel(branch_rows, core_ref, x_ref, a_ref, a_t, dy_ref, wg_ref, wu_ref, wd_ref, out_ref_own, out_ref_other, da_ref, away_ref, keep_ref,
+               away_con_ref, keep_con_ref, y_ref, hid, dboth, dwd, sem):
     count = a_ref.shape[0]
     step = pl.program_id(0)
 
@@ -783,10 +783,11 @@
         copy.wait()
 
     slope = 0.7978845608028654
+    w_both = jnp.concatenate([wg_ref[...], wu_ref[...]], axis=1)
     for i in range(0, count, TILE):
         rows = slice(i, i + TILE)
-        g = dot(a_ref[rows], wg_ref[...], (1, 0))
-        u = dot(a_ref[rows], wu_ref[...], (1, 0))
+        both = dot(a_ref[rows], w_both, (1, 0))
+        g, u = both[:, :TILE], both[:, TILE:]
         dh = dot(dy_ref[rows], wd_ref[...], (1, 1))
         square = g * g
         th = jnp.tanh(slope * g * (1.0 + 0.044715 * square))
@@ -797,21 +798,28 @@
         dg = (dh * u * slant).astype(BF)
         du = (dh * gelu).astype(BF)
         hid[rows] = low
-        dgate[rows] = dg
-        dup[rows] = du
+        dboth[rows, :TILE] = dg
+        dboth[rows, TILE:] = du
         y_ref[rows] += dot(low, wd_ref[...], (1, 0))
-        da_ref[rows] += dot(dg, wg_ref[...], (1, 1)) + dot(du, wu_ref[...], (1, 1))
+        da_ref[rows] += dot(dboth[rows], w_both, (1, 1))
     dwd[pl.ds(pl.multiple_of(step * TILE, TILE), TILE)] = dot(hid[...], dy_ref[...], (0, 0))
     core = core_ref[0]
-    for index, grad in enumerate((dgate, dup)):
-        blocks = dot(a_t[...], grad[...], (1, 0)).astype(BF).reshape(D // 64, 2, 32, TILE)
+    grads = dot(a_t[...], dboth[...], (1, 0)).astype(BF)
+    for index in range(2):
+        blocks = grads[:, index * TILE:(index + 1) * TILE].reshape(D // 64, 2, 32, TILE)
         away_ref[index] = jnp.where(core == 0, blocks[:, 1], blocks[:, 0])
         keep_ref[index] = jnp.where(core == 0, blocks[:, 0], blocks[:, 1])
 
     @pl.when(step == pl.num_programs(0) - 1)
     def _():
-        for i in range(0, count, TILE):
-            out_ref[i:i + TILE] = y_ref[i:i + TILE].astype(BF)
+        half = (count - branch_rows) // 2
+        part = branch_rows // 2
+        for out_ref, side in ((out_ref_own, core), (out_ref_other, 1 - core)):
+            for i in range(0, half, TILE):
+                begin = pl.multiple_of(side * half + i, TILE)
+                out_ref[i:i + TILE] = y_ref[pl.ds(begin, TILE)].astype(BF)
+            begin = pl.multiple_of(2 * half + side * part, part)
+            out_ref[half:] = y_ref[pl.ds(begin, part)].astype(BF)
         pairs, m, _ = keep_con_ref.shape
         for index in range(pairs):
             even = dwd[2 * index * m:(2 * index + 1) * m].astype(BF)
@@ -820,7 +828,7 @@
             keep_con_ref[index] = jnp.where(core == 0, even, odd)
 
 
-def mlp(core, after_two, inputs, turned, low_up, w_gate, w_up, w_con, owners):
+def mlp(core, after_two, inputs, turned, low_up, w_gate, w_up, w_con, owners, branch_rows):
     count = inputs.shape[0]
     hidden = w_gate.shape[1]
     m = hidden // owners
@@ -830,27 +838,28 @@
     row = pl.BlockSpec((TILE, D), lambda t, c: (t, 0))
     shared = pl.BlockSpec((2, D // 64, 32, TILE), lambda t, c: (0, 0, 0, t))
     part = jax.ShapeDtypeStruct((2, D // 64, 32, hidden), BF)
+    half_rows = pl.BlockSpec((count // 2, D), lambda t, c: (0, 0), pipeline_mode=once)
     con = pl.BlockSpec((owners // 2, m, D), lambda t, c: (0, 0, 0), pipeline_mode=once)
     con_part = jax.ShapeDtypeStruct((owners // 2, m, D), BF)
     tile = pltpu.VMEM((count, TILE), BF)
     return pl.pallas_call(
-        mlp_kernel,
+        functools.partial(mlp_kernel, branch_rows),
         grid_spec=pltpu.PrefetchScalarGridSpec(
             num_scalar_prefetch=1,
             grid=(hidden // TILE,),
             in_specs=[pl.BlockSpec(memory_space=pl.ANY), flat, whole_block(turned), flat, column, column, row],
-            out_specs=[flat, flat, shared, shared, con, con],
+            out_specs=[half_rows, half_rows, flat, shared, shared, con, con],
             scratch_shapes=[
                 pltpu.VMEM((count, D), F32),
                 tile,
-                tile,
-                tile,
+                pltpu.VMEM((count, 2 * TILE), BF),
                 pltpu.VMEM((hidden, D), F32),
                 pltpu.SemaphoreType.DMA,
             ],
         ),
         out_shape=[
-            jax.ShapeDtypeStruct((count, D), BF),
+            jax.ShapeDtypeStruct((count // 2, D), BF),
+            jax.ShapeDtypeStruct((count // 2, D), BF),
             jax.ShapeDtypeStruct((count, D), F32),
             part,
             part,
@@ -1722,14 +1731,13 @@
     w_con = assemble([close_con, close_con_two, far_con, far_con_two], slots)[0]
 
     owners = LINE * SIDE * SIDE * 2
-    output, grad_three, away_exp, keep_exp, away_con, keep_con = mlp(
-        core_ref, after_two, input_three, turned_three, low_up, w_gate, w_up, w_con, owners
+    own_output, output_to_give, grad_three, away_exp, keep_exp, away_con, keep_con = mlp(
+        core_ref, after_two, input_three, turned_three, low_up, w_gate, w_up, w_con, owners, 2 * size
     )
     got_exp = send(away_exp, core_flip)
     got_con = send(away_con[None], core_flip)
-    low_up, away_exp, away_con, grad_three, output = tie(low_up, away_exp, away_con, grad_three, output)
-    own_output, other_output = hand_over([output[:prompt], output[prompt:]], core)
-    low_up, own_output = tie(low_up, own_output)
+    other_output = send(output_to_give, core_flip)
+    low_up, away_exp, away_con, grad_three = tie(low_up, away_exp, away_con, grad_three)
 
     def middle_part(first, blocks, before=None):
         return middle_back(
@@ -1857,8 +1865,8 @@
     got_last_mid = send(last_mid, line_far)
     got_grad = send(theirs_grad, core_flip)
     half_rows = prompt // 2
-    whole_output = both_groups(own_output, other_output, core)
-    prompt_output, branch_output = whole_output[:, :half_rows], whole_output[:, half_rows:]
+    prompt_output = both_groups(own_output[:half_rows], other_output[:half_rows], core)
+    branch_output = both_groups(own_output[half_rows:], other_output[half_rows:], core)
     encoder_out = both_groups(own_encoder, other_encoder, core)
     got_near_two, got_line_one, got_last_con, got_last_exp, prompt_output, branch_output, encoder_out = tie(
         got_near_two, got_line_one, got_last_con, got_last_exp, prompt_output, branch_output, encoder_out

time: 639 us -> 634 us (level)
    another operation x9 -> x10, other arithmetic: 13.4 us -> 14.2 us  [both_groups(): jnp.stack([jnp.where(core == 0, mine, other), jnp.where(core == 0, other,...]
  transfers between devices with their start and end apart: 61 -> 61, of which waited for: 19 -> 22; matrix products, arithmetic and copies ran while one was open for 13% -> 12% of each run, Pallas kernels for 41% -> 41%
where the time goes in v3:
time: 634 us; the launch traced here: 624 us
  Pallas kernels  378 us (60%)
  other arithmetic  76.8 us (12%)
  waiting for transfers between devices  70.5 us (11%)
  starting transfers between devices  55.9 us (9%)
  local copies, waits for them, and re-layouts  24 us (4%)
  between operations  13.7 us (2%)
    pallas_call x1, Pallas kernels, mlp(): pl.pallas_call(functools.partial(mlp_kernel, branch_rows), grid_spec=pltp...  91.5 us
    ppermute x61, waiting for transfers between devices, send(): return lax.ppermute(value, AXES, moves(rule))  70.5 us
    ppermute x61, starting transfers between devices, send(): return lax.ppermute(value, AXES, moves(rule))  55.9 us
    pallas_call x2, Pallas kernels, self_forward(): pl.pallas_call(functools.partial(self_kernel, prompt, size, len(more)), g...  50 us
    pallas_call x6, Pallas kernels, weight_part(): pl.pallas_call(functools.partial(part_kernel, [left for left, _ in jobs],...  49.3 us
    pallas_call x2, Pallas kernels, middle_back(): pl.pallas_call(middle_back_kernel, grid=(blocks,), in_specs=[rows] * 6 +...  42.8 us
    pallas_call x2, Pallas kernels, self_backward(): pl.pallas_call(functools.partial(self_back_kernel, prompt, size), grid=(p...  38.4 us
    pallas_call x1, Pallas kernels, middle(): pl.pallas_call(functools.partial(middle_kernel, len(mixed)), grid=(count...  33.1 us
  transfers between devices with their start and end apart: 61, of which 22 were waited for; matrix products, arithmetic and copies ran while one was open for 12% of the time, Pallas kernels for 41%

profile of v3, /device:TPU:0, one launch (start us, length us, event | category | flops | bytes accessed | tf_op | source)
XLA Modules:
  0.0 623.6 jit_solution(18074737414926647244)
XLA Ops:
  2.0 4.1 collective-permute-start
  11.3 3.8 collective-permute-done.far
  16.1 9.5 %collective-permute-done.2.near = bf16[2,3,32,1024]{3,2,1,0:T(8,128)(2,1)S(1)} collective-permute-done((bf16[2,3,32,1024]{3,2,1,0:T(8,128)(2,1)S(1)}, bf16[2,3,32,1024]{3,2,1,0:T(8,128)(2,1)S(1)}, u32[]{:S(2)}, u32[]{:S(2)}) %collective-permute-start.2) | collective-permute-done | bytes 393248 | tf_op jit(solution)/shard_map/ppermute | solution.py:1370
  37.8 3.4 collective-permute-start.4
  42.1 3.1 collective-permute-done.3
  47.8 8.5 %collective-permute-done.4.far = bf16[5,32,1024]{2,1,0:T(8,128)(2,1)S(1)} collective-permute-done((bf16[5,32,1024]{2,1,0:T(8,128)(2,1)S(1)}, bf16[5,32,1024]{2,1,0:T(8,128)(2,1)S(1)}, u32[]{:S(2)}, u32[]{:S(2)}) %collective-permute-start.4) | collective-permute-done | bytes 327712 | tf_op jit(solution)/shard_map/ppermute | solution.py:1370
  57.2 3.1 broadcast_select_fusion.1
  61.7 1.7 pad_maximum_fusion.3.dy_ref
  65.1 7.7 %collective-permute-done.6.near = bf16[2,5,32,1024]{3,2,1,0:T(8,128)(2,1)S(1)} collective-permute-done((bf16[2,5,32,1024]{3,2,1,0:T(8,128)(2,1)S(1)}, bf16[2,5,32,1024]{3,2,1,0:T(8,128)(2,1)S(1)}, u32[]{:S(2)}, u32[]{:S(2)}) %collective-permute-start.6) | collective-permute-done | bytes 655392 | tf_op jit(solution)/shard_map/ppermute | solution.py:1370
  75.2 2.9 collective-permute-start.11
  79.5 17.0 %enter.1 = (bf16[2,512,1280]{2,1,0:T(8,128)(2,1)}, bf16[3,1280,1024]{2,1,0:T(8,128)(2,1)}, bf16[4,4,2,32,1024]{4,3,2,1,0:T(8,128)(2,1)}, bf16[4,4,2,32,1024]{4,3...) custom-call(s32[8,2]{1,0:T(8,128)} %stack.290.slots_ref, bf16[2,3,4,32,1024]{4,3,2,1,0:T(8,128)(2,1)} %copy-done.5, ...), custom_call_target="tpu_custom_call" | custom-call | flops 12 | bytes 1 | tf_op jit(solution)/shard_map/enter/pallas_call | solution.py:1049
  96.5 3.0 pad_maximum_fusion.4.refs_0_
  100.3 1.8 collective-permute-start.14
  102.4 25.0 %self_forward.2 = (bf16[1280,1024]{1,0:T(8,128)(2,1)}, bf16[16,256,3712]{2,1,0:T(8,128)(2,1)}, f32[1280,1024]{1,0:T(8,128)}) custom-call(s32[2]{0:T(128)} %copy-done.40, bf16[3,1280,1024]{2,1,0:T(8,128)(2,1)} %get-tuple-element.282.q_ref.k_ref.v_ref, bf16[3,1280,1024]{2,1,0:T(8,128)(2,1)} %get-tuple-element.282.q_ref.k_ref.v_ref, ...), custom_call_target="tpu_custom_call" | custom-call | flops 24 | bytes 1 | tf_op jit(solution)/shard_map/self_forward/pallas_call | solution.py:608
  127.4 4.1 collective-permute-done.12.refs_2_
  132.7 1.8 collective-permute-start.18
  134.6 25.1 %self_forward.3 = (bf16[1280,1024]{1,0:T(8,128)(2,1)}, bf16[16,256,3712]{2,1,0:T(8,128)(2,1)}, f32[1280,1024]{1,0:T(8,128)}) custom-call(s32[2]{0:T(128)} %copy-done.40, bf16[3,1280,1024]{2,1,0:T(8,128)(2,1)} %get-tuple-element.282.q_ref.k_ref.v_ref, ...), custom_call_target="tpu_custom_call", output_to_operand_aliasing={{0}: (6, {}), {1}: (7, {}), {2}: (8, {})} | custom-call | flops 24 | bytes 1 | tf_op jit(solution)/shard_map/self_forward/pallas_call | solution.py:608
  161.5 2.1 pad_maximum_fusion.1.refs_0_
  166.7 33.1 %middle.1 = (f32[1280,1024]{1,0:T(8,128)}, f32[1280,1024]{1,0:T(8,128)}, bf16[2,512,1280]{2,1,0:T(8,128)(2,1)}, bf16[1280,1024]{1,0:T(8,128)(2,1)}, bf16[1280,10...) custom-call(s32[8,2]{1,0:T(8,128)} %stack.290.slots_ref, ...), custom_call_target="tpu_custom_call" | custom-call | flops 30 | bytes 1 | tf_op jit(solution)/shard_map/middle/pallas_call | solution.py:1128
  199.8 6.1 collective-permute-done.19.refs_2_
  208.8 2.7 collective-permute-done.22.refs_3_
  211.5 8.0 %assemble.2 = (bf16[4,4,2,32,2816]{4,3,2,1,0:T(8,128)(2,1)}, bf16[4,4,2,32,2816]{4,3,2,1,0:T(8,128)(2,1)}) custom-call(s32[8,2]{1,0:T(8,128)S(1)} %copy-done.4, bf16[2,2,4,32,2816]{4,3,2,1,0:T(8,128)(2,1)S(1)} %pad_maximum_fusion.1.refs_0_, bf16[2,2,4,32,2816]{4,3,2,1,0:T(8,128)(2,1)} %collective-permute-done.21.refs_1_, ...), custom_call_target="tpu_custom_call" | custom-call | flops 4 | bytes 1 | tf_op jit(solution)/shard_map/assemble/pallas_call | solution.py:1455
  219.5 6.8 %collective-permute-done.23.refs_2_ = bf16[2,1,4,88,1024]{4,3,2,1,0:T(8,128)(2,1)S(1)} collective-permute-done((bf16[2,1,4,88,1024]{4,3,2,1,0:T(8,128)(2,1)S(1)}, bf16[2,1,4,88,1024]{4,3,2,1,0:T(8,128)(2,1)S(1)}, u32[]{:S(2)}, u32[]{:S(2)}) %collective-permute-start.23) | collective-permute-done | bytes 1441824 | tf_op jit(solution)/shard_map/ppermute | solution.py:1370
  226.3 3.2 collective-permute-done.25.refs_3_
  231.1 2.5 copy-done
  233.5 91.5 %mlp.1 = (bf16[640,1024]{1,0:T(8,128)(2,1)}, bf16[640,1024]{1,0:T(8,128)(2,1)}, f32[1280,1024]{1,0:T(8,128)}, bf16[2,16,32,2816]{3,2,1,0:T(8,128)(2,1)}, bf16[2,...) custom-call(s32[1]{0:T(128)} %bitcast.core_ref, ...), custom_call_target="tpu_custom_call" | custom-call | flops 85 | bytes 1 | tf_op jit(solution)/shard_map/mlp/pallas_call | solution.py:845
  326.2 12.5 %middle_back.2 = (bf16[1280,1024]{1,0:T(8,128)(2,1)}, bf16[1280,1024]{1,0:T(8,128)(2,1)}, f32[1280,1024]{1,0:T(8,128)}, bf16[1280,1024]{1,0:T(8,128)(2,1)}, bf16...) custom-call(bf16[1280,1024]{1,0:T(8,128)(2,1)} %pad_maximum_fusion.3.dy, ...), custom_call_target="tpu_custom_call" | custom-call | flops 45 | bytes 1 | tf_op jit(solution)/shard_map/middle_back/pallas_call | solution.py:1237
  339.0 9.7 %add_split.2 = (bf16[2,4,2,32,2816]{4,3,2,1,0:T(8,128)(2,1)}, bf16[2,4,2,32,2816]{4,3,2,1,0:T(8,128)(2,1)}) custom-call(s32[4]{0:T(128)} %pad_add_fusion.2.spots_ref, bf16[2,4,4,32,2816]{4,3,2,1,0:T(8,128)(2,1)} %bitcast.245, bf16[2,4,4,32,2816]{4,3,2,1,0:T(8,128)(2,1)} %bitcast.60.two_ref), custom_call_target="tpu_custom_call" | custom-call | flops 1 | bytes 1 | tf_op jit(solution)/shard_map/add_split/pallas_call | solution.py:1505
  349.2 5.7 add_split.3
  357.0 30.3 %middle_back.3 = (bf16[1280,1024]{1,0:T(8,128)(2,1)}, bf16[1280,1024]{1,0:T(8,128)(2,1)}, f32[1280,1024]{1,0:T(8,128)}, bf16[1280,1024]{1,0:T(8,128)(2,1)}, bf16...) custom-call(bf16[1280,1024]{1,0:T(8,128)(2,1)} %pad_maximum_fusion.3, ...), custom_call_target="tpu_custom_call", output_to_operand_aliasing={{0}: (14, {}), {1}: (15, {}), {2}: (16, {}), {3}: (17, {}),... | custom-call | flops 45 | bytes 1 | tf_op jit(solution)/shard_map/middle_back/pallas_call | solution.py:1237
  387.3 2.2 slice_bitcast_fusion
  389.6 11.5 %weight_part.6 = bf16[5,16,32,1024]{3,2,1,0:T(8,128)(2,1)} custom-call(s32[5]{0:T(128)} %stack.319.plan_ref, bf16[2,512,1280]{2,1,0:T(8,128)(2,1)} %get-tuple-element.358.refs_0_, bf16[2,512,1280]{2,1,0:T(8,128)(2,1)} %get-tuple-element.359.refs_1_, bf16[2,512,256]{2,1,0:T(8,128)(2,1)} %get-tuple-element.360.refs_2_, ...), custom_call_target="tpu_custom_call" | custom-call | flops 2 | bytes 1 | tf_op jit(solution)/shard_map/weight_part/pallas_call | solution.py:918
  401.1 2.5 fusion.32
  408.1 2.2 fusion.9
  413.2 19.1 %self_backward.2 = (bf16[1280,512]{1,0:T(8,128)(2,1)}, bf16[1280,512]{1,0:T(8,128)(2,1)}, bf16[1280,512]{1,0:T(8,128)(2,1)}, f32[8,1,1280]{2,1,0:T(1,128)}, f32[8,2,1,1152]{3,2,1,0:T(1,128)}) custom-call(bf16[3,1280,1024]{2,1,0:T(8,128)(2,1)} %get-tuple-element.282.q_ref.k_ref.v_ref, bf16[3,1280,1024]{2,1,0:T(8,128)(2,1)} %get-tuple-element.282.q_ref.k_ref.v_ref, ...), custom_call_target="tpu_custom_call" | custom-call | flops 32 | bytes 1 | tf_op jit(solution)/shard_map/self_backward/pallas_call | solution.py:717
  433.9 1.9 fusion.4
  435.8 2.3 fusion
  438.2 12.4 %weight_part.7 = (bf16[2,4,5,32,1024]{4,3,2,1,0:T(8,128)(2,1)}, bf16[2,4,5,32,1024]{4,3,2,1,0:T(8,128)(2,1)}) custom-call(s32[5]{0:T(128)} %stack.270.plan_ref, bf16[2,512,1280]{2,1,0:T(8,128)(2,1)} %get-tuple-element.358.refs_0_, bf16[2,512,1280]{2,1,0:T(8,128)(2,1)} %get-tuple-element.359.refs_1_, bf16[2,512,256]{2,1,0:T(8,128)(2,1)} %get-tuple-element.360.refs_2_, ...), custom_call_target="tpu_custom_call" | custom-call | flops 2 | bytes 1 | tf_op jit(solution)/shard_map/weight_part/pallas_call | solution.py:918
  452.8 6.3 %weight_part.8 = bf16[3,16,32,512]{3,2,1,0:T(8,128)(2,1)} custom-call(s32[5]{0:T(128)} %stack.319.plan_ref, bf16[2,512,1280]{2,1,0:T(8,128)(2,1)} %get-tuple-element.385.refs_0_, bf16[1280,512]{1,0:T(8,128)(2,1)} %get-tuple-element.386.refs_1_.refs_0_, bf16[1280,512]{1,0:T(8,128)(2,1)} %get-tuple-element.387.refs_2_.refs_1_, ...), custom_call_target="tpu_custom_call" | custom-call | flops 2 | bytes 1 | tf_op jit(solution)/shard_map/weight_part/pallas_call | solution.py:918
  465.5 1.8 collective-permute-start.41
  467.3 19.3 %self_backward.3 = (bf16[1280,512]{1,0:T(8,128)(2,1)}, bf16[1280,512]{1,0:T(8,128)(2,1)}, bf16[1280,512]{1,0:T(8,128)(2,1)}, f32[8,1,1280]{2,1,0:T(1,128)}, f32[8,2,1,1152]{3,2,1,0:T(1,128)}) custom-call(bf16[3,1280,1024]{2,1,0:T(8,128)(2,1)} %get-tuple-element.282.q_ref.k_ref.v_ref, bf16[3,1280,1024]{2,1,0:T(8,128)(2,1)} %get-tuple-element.282.q_ref.k_ref.v_ref, ...), custom_call_target="tpu_custom_call" | custom-call | flops 32 | bytes 1 | tf_op jit(solution)/shard_map/self_backward/pallas_call | solution.py:717
  487.5 3.6 fusion.5
  491.1 6.1 weight_part.9
  499.2 6.6 %weight_part.10 = (bf16[2,4,3,32,512]{4,3,2,1,0:T(8,128)(2,1)}, bf16[2,4,3,32,512]{4,3,2,1,0:T(8,128)(2,1)}) custom-call(s32[5]{0:T(128)} %stack.270.plan_ref, bf16[2,512,1280]{2,1,0:T(8,128)(2,1)} %get-tuple-element.385.refs_0_, bf16[1280,512]{1,0:T(8,128)(2,1)} %get-tuple-element.386.refs_1_.refs_0_, bf16[1280,512]{1,0:T(8,128)(2,1)} %get-tuple-element.387.refs_2_.refs_1_, ...), custom_call_target="tpu_custom_call" | custom-call | flops 2 | bytes 1 | tf_op jit(solution)/shard_map/weight_part/pallas_call | solution.py:918
  510.4 12.5 %leave.2 = (f32[768,1024]{1,0:T(8,128)}, f32[8,1024]{1,0:T(8,128)}) custom-call(s32[3]{0:T(128)} %pad_add_fusion.plan_ref, bf16[1280,1024]{1,0:T(8,128)(2,1)} %pad_maximum_fusion.2.refs_4_.x_ref, f32[1280,1024]{1,0:T(8,128)} %get-tuple-element.403.dx1_ref, bf16[1280,512]{1,0:T(8,128)(2,1)} %get-tuple-element.386.refs_1_.refs_0_, ...), custom_call_target="tpu_custom_call" | custom-call | flops 2 | bytes 1 | tf_op jit(solution)/shard_map/leave/pallas_call | solution.py:1290
  523.2 6.4 %weight_part.11 = (bf16[2,4,3,32,512]{4,3,2,1,0:T(8,128)(2,1)}, bf16[2,4,3,32,512]{4,3,2,1,0:T(8,128)(2,1)}) custom-call(s32[5]{0:T(128)} %stack.270.plan_ref, bf16[2,512,1280]{2,1,0:T(8,128)(2,1)} %get-tuple-element.385.refs_0_, bf16[1280,512]{1,0:T(8,128)(2,1)} %get-tuple-element.395.refs_1_.refs_3_, bf16[1280,512]{1,0:T(8,128)(2,1)} %get-tuple-element.396.refs_2_.refs_4_, ...), custom_call_target="tpu_custom_call" | custom-call | flops 2 | bytes 1 | tf_op jit(solution)/shard_map/weight_part/pallas_call | solution.py:918
  531.0 3.0 fusion.1
  535.3 1.9 fusion.12
  539.2 10.6 %leave.3 = (f32[512,1024]{1,0:T(8,128)}, f32[8,1024]{1,0:T(8,128)}) custom-call(s32[2]{0:T(128)} %iota_add_fusion.plan_ref, bf16[1280,1024]{1,0:T(8,128)(2,1)} %pad_maximum_fusion.2.refs_4_.x_ref, f32[1280,1024]{1,0:T(8,128)} %get-tuple-element.403.dx1_ref, bf16[1280,512]{1,0:T(8,128)(2,1)} %get-tuple-element.386.refs_1_.refs_0_, ...), custom_call_target="tpu_custom_call" | custom-call | flops 2 | bytes 1 | tf_op jit(solution)/shard_map/leave/pallas_call | solution.py:1290
  550.8 1.9 collective-permute-start.47
  556.4 1.8 collective-permute-start.46
  558.1 1.8 fusion.18
  562.2 5.1 collective-permute-done.46
  570.0 2.3 collective-permute-start.49
  572.4 2.4 multiply_reduce_fusion.2
  574.7 2.7 multiply_reduce_fusion
  578.7 2.7 select_bitcast_fusion.1
  581.4 2.3 pad_maximum_fusion
  588.1 1.9 multiply_reduce_fusion.1
  596.1 2.5 collective-permute-start.54
  598.7 2.4 collective-permute-start.56
  605.2 1.7 collective-permute-start.59
  607.9 1.8 collective-permute-done.59
  616.3 5.8 update.1
  (303 shorter events, 98.7 us)
Async XLA Ops:
  2.0 13.2 %collective-permute-start = (bf16[3,32,1024]{2,1,0:T(8,128)(2,1)S(1)}, bf16[3,32,1024]{2,1,0:T(8,128)(2,1)S(1)}, u32[]{:S(2)}, u32[]{:S(2)}) collective-permute-start(bf16[3,32,1024]{2,1,0:T(8,128)(2,1)S(1)} %get-tuple-element.675.shard), channel_id=1, source_target_pairs={{0,16},{1,17},{2,18},{3,19},{4,20},{5,21},{6,22},{7,23},{8,24},{9,... | collective-permute-start | bytes 589832 | tf_op jit(solution)/shard_map/ppermute | solution.py:1370
  7.4 1.2 collective-permute-start.1
  11.3 23.0 %copy-start.40 = (s32[2]{0:T(128)}, s32[2]{0:T(128)S(1)}, u32[]{:S(2)}) copy-start(s32[2]{0:T(128)S(1)} %pad_add_fusion.1.starts_ref) | copy-start | bytes 28
  15.2 10.4 %collective-permute-start.2 = (bf16[2,3,32,1024]{3,2,1,0:T(8,128)(2,1)S(1)}, bf16[2,3,32,1024]{3,2,1,0:T(8,128)(2,1)S(1)}, u32[]{:S(2)}, u32[]{:S(2)}) collective-permute-start(bf16[2,3,32,1024]{3,2,1,0:T(8,128)(2,1)S(1)} %pad_maximum_fusion.17), channel_id=1, source_target_pairs={{0,8},{1,9},{2,10},{3,11},{4,12},{5,13},{6,14},{7,15},{8,0},{9,1},... | collective-permute-start | bytes 1179656 | tf_op jit(solution)/shard_map/ppermute | solution.py:1370
  31.1 26.1 %collective-permute-start.8 = (bf16[1408,1024]{1,0:T(8,128)(2,1)}, bf16[1408,1024]{1,0:T(8,128)(2,1)}, u32[]{:S(2)}, u32[]{:S(2)}) collective-permute-start(bf16[1408,1024]{1,0:T(8,128)(2,1)} %get-tuple-element.664), channel_id=1, source_target_pairs={{0,1},{1,0},{2,3},{3,2},{4,5},{5,4},{6,7},{7,6},{8,9},{9,8},{10,11... | collective-permute-start | bytes 8650760 | tf_op jit(solution)/shard_map/ppermute | solution.py:1370
  33.0 12.2 %collective-permute-start.3 = (bf16[3,4,32,1024]{3,2,1,0:T(8,128)(2,1)S(1)}, bf16[3,4,32,1024]{3,2,1,0:T(8,128)(2,1)}, u32[]{:S(2)}, u32[]{:S(2)}) collective-permute-start(bf16[3,4,32,1024]{3,2,1,0:T(8,128)(2,1)S(1)} %put_in_line.4), channel_id=1, source_target_pairs={{0,2},{1,5},{2,0},{3,7},{4,6},{5,1},{6,4},{7,3},{8,10},{9,13},{10,... | collective-permute-start | bytes 2359304 | tf_op jit(solution)/shard_map/ppermute | solution.py:1370
  37.8 18.6 %collective-permute-start.4 = (bf16[5,32,1024]{2,1,0:T(8,128)(2,1)S(1)}, bf16[5,32,1024]{2,1,0:T(8,128)(2,1)S(1)}, u32[]{:S(2)}, u32[]{:S(2)}) collective-permute-start(bf16[5,32,1024]{2,1,0:T(8,128)(2,1)S(1)} %pad_maximum_fusion.20.shard), channel_id=1, source_target_pairs={{0,16},{1,17},{2,18},{3,19},{4,20},{5,21},{6,22},{7,23},{8,24},{9,... | collective-permute-start | bytes 983048 | tf_op jit(solution)/shard_map/ppermute | solution.py:1370
  46.4 26.4 %collective-permute-start.5 = (bf16[2,3,4,32,1024]{4,3,2,1,0:T(8,128)(2,1)S(1)}, bf16[2,3,4,32,1024]{4,3,2,1,0:T(8,128)(2,1)}, u32[]{:S(2)}, u32[]{:S(2)}) collective-permute-start(bf16[2,3,4,32,1024]{4,3,2,1,0:T(8,128)(2,1)S(1)} %pad_maximum_fusion.6.refs_0_), channel_id=1, source_target_pairs={{0,4},{1,3},{2,6},{3,1},{4,0},{5,7},{6,2},{7,5},{8,12},{9,11},{10,... | collective-permute-start | bytes 4718600 | tf_op jit(solution)/shard_map/ppermute | solution.py:1370
  56.4 16.5 %collective-permute-start.6 = (bf16[2,5,32,1024]{3,2,1,0:T(8,128)(2,1)S(1)}, bf16[2,5,32,1024]{3,2,1,0:T(8,128)(2,1)S(1)}, u32[]{:S(2)}, u32[]{:S(2)}) collective-permute-start(bf16[2,5,32,1024]{3,2,1,0:T(8,128)(2,1)S(1)} %pad_maximum_fusion.13), channel_id=1, source_target_pairs={{0,8},{1,9},{2,10},{3,11},{4,12},{5,13},{6,14},{7,15},{8,0},{9,1},... | collective-permute-start | bytes 1966088 | tf_op jit(solution)/shard_map/ppermute | solution.py:1370
  57.2 15.7 %collective-permute-start.7 = (bf16[2,3,4,32,1024]{4,3,2,1,0:T(8,128)(2,1)S(1)}, bf16[2,3,4,32,1024]{4,3,2,1,0:T(8,128)(2,1)S(1)}, u32[]{:S(2)}, u32[]{:S(2)}) collective-permute-start(bf16[2,3,4,32,1024]{4,3,2,1,0:T(8,128)(2,1)S(1)} %pad_maximum_fusion.6.refs_0_), channel_id=1, source_target_pairs={{0,1},{1,0},{2,3},{3,2},{4,5},{5,4},{6,7},{7,6},{8,9},{9,8},{10,11... | collective-permute-start | bytes 4718600 | tf_op jit(solution)/shard_map/ppermute | solution.py:1370
  72.9 6.6 %collective-permute-start.9 = (bf16[2,3,4,32,1024]{4,3,2,1,0:T(8,128)(2,1)}, bf16[2,3,4,32,1024]{4,3,2,1,0:T(8,128)(2,1)}, u32[]{:S(2)}, u32[]{:S(2)}) collective-permute-start(bf16[2,3,4,32,1024]{4,3,2,1,0:T(8,128)(2,1)} %collective-permute-done.5.refs_2_), channel_id=1, source_target_pairs={{0,1},{1,0},{2,3},{3,2},{4,5},{5,4},{6,7},{7,6},{8,9},{9,8},{10,11... | collective-permute-start | bytes 4718600 | tf_op jit(solution)/shard_map/ppermute | solution.py:1370
  74.0 22.5 %collective-permute-start.10 = (bf16[5,4,32,1024]{3,2,1,0:T(8,128)(2,1)S(1)}, bf16[5,4,32,1024]{3,2,1,0:T(8,128)(2,1)}, u32[]{:S(2)}, u32[]{:S(2)}) collective-permute-start(bf16[5,4,32,1024]{3,2,1,0:T(8,128)(2,1)S(1)} %put_in_line.5), channel_id=1, source_target_pairs={{0,2},{1,5},{2,0},{3,7},{4,6},{5,1},{6,4},{7,3},{8,10},{9,13},{10,... | collective-permute-start | bytes 3932168 | tf_op jit(solution)/shard_map/ppermute | solution.py:1370
  75.2 21.3 %collective-permute-start.11 = (bf16[2,32,2816]{2,1,0:T(8,128)(2,1)S(1)}, bf16[2,32,2816]{2,1,0:T(8,128)(2,1)S(1)}, u32[]{:S(2)}, u32[]{:S(2)}) collective-permute-start(bf16[2,32,2816]{2,1,0:T(8,128)(2,1)S(1)} %convert_element_type.428.shard), channel_id=1, source_target_pairs={{0,16},{1,17},{2,18},{3,19},{4,20},{5,21},{6,22},{7,23},{8,24},{9,... | collective-permute-start | bytes 1081352 | tf_op jit(solution)/shard_map/ppermute | solution.py:1370
  99.6 32.0 %collective-permute-start.12 = (bf16[2,5,4,32,1024]{4,3,2,1,0:T(8,128)(2,1)}, bf16[2,5,4,32,1024]{4,3,2,1,0:T(8,128)(2,1)}, u32[]{:S(2)}, u32[]{:S(2)}) collective-permute-start(bf16[2,5,4,32,1024]{4,3,2,1,0:T(8,128)(2,1)} %pad_maximum_fusion.4.refs_0_), channel_id=1, source_target_pairs={{0,4},{1,3},{2,6},{3,1},{4,0},{5,7},{6,2},{7,5},{8,12},{9,11},{10,... | collective-permute-start | bytes 7864328 | tf_op jit(solution)/shard_map/ppermute | solution.py:1370
  100.2 31.3 %collective-permute-start.13 = (bf16[2,5,4,32,1024]{4,3,2,1,0:T(8,128)(2,1)}, bf16[2,5,4,32,1024]{4,3,2,1,0:T(8,128)(2,1)}, u32[]{:S(2)}, u32[]{:S(2)}) collective-permute-start(bf16[2,5,4,32,1024]{4,3,2,1,0:T(8,128)(2,1)} %pad_maximum_fusion.4.refs_0_), channel_id=1, source_target_pairs={{0,1},{1,0},{2,3},{3,2},{4,5},{5,4},{6,7},{7,6},{8,9},{9,8},{10,11... | collective-permute-start | bytes 7864328 | tf_op jit(solution)/shard_map/ppermute | solution.py:1370
  100.3 27.1 %collective-permute-start.14 = (bf16[2,2,32,2816]{3,2,1,0:T(8,128)(2,1)S(1)}, bf16[2,2,32,2816]{3,2,1,0:T(8,128)(2,1)S(1)}, u32[]{:S(2)}, u32[]{:S(2)}) collective-permute-start(bf16[2,2,32,2816]{3,2,1,0:T(8,128)(2,1)S(1)} %pad_maximum_fusion.11), channel_id=1, source_target_pairs={{0,8},{1,9},{2,10},{3,11},{4,12},{5,13},{6,14},{7,15},{8,0},{9,1},... | collective-permute-start | bytes 2162696 | tf_op jit(solution)/shard_map/ppermute | solution.py:1370
  102.1 25.3 %collective-permute-start.15 = (bf16[1,88,1024]{2,1,0:T(8,128)(2,1)S(1)}, bf16[1,88,1024]{2,1,0:T(8,128)(2,1)S(1)}, u32[]{:S(2)}, u32[]{:S(2)}) collective-permute-start(bf16[1,88,1024]{2,1,0:T(8,128)(2,1)S(1)} %convert_bitcast_fusion.shard), channel_id=1, source_target_pairs={{0,16},{1,17},{2,18},{3,19},{4,20},{5,21},{6,22},{7,23},{8,24},{9,... | collective-permute-start | bytes 540680 | tf_op jit(solution)/shard_map/ppermute | solution.py:1370
  131.5 28.9 %collective-permute-start.16 = (bf16[2,5,4,32,1024]{4,3,2,1,0:T(8,128)(2,1)}, bf16[2,5,4,32,1024]{4,3,2,1,0:T(8,128)(2,1)}, u32[]{:S(2)}, u32[]{:S(2)}) collective-permute-start(bf16[2,5,4,32,1024]{4,3,2,1,0:T(8,128)(2,1)} %collective-permute-done.12.refs_2_), channel_id=1, source_target_pairs={{0,1},{1,0},{2,3},{3,2},{4,5},{5,4},{6,7},{7,6},{8,9},{9,8},{10,11... | collective-permute-start | bytes 7864328 | tf_op jit(solution)/shard_map/ppermute | solution.py:1370
  131.9 27.7 %copy-start.1 = (bf16[2,4,32,2816]{3,2,1,0:T(8,128)(2,1)}, bf16[2,4,32,2816]{3,2,1,0:T(8,128)(2,1)S(1)}, u32[]{:S(2)}) copy-start(bf16[2,4,32,2816]{3,2,1,0:T(8,128)(2,1)S(1)} %put_in_line.6) | copy-start | bytes 4325380
  131.9 28.5 %collective-permute-start.17 = (bf16[2,4,32,2816]{3,2,1,0:T(8,128)(2,1)S(1)}, bf16[2,4,32,2816]{3,2,1,0:T(8,128)(2,1)S(1)}, u32[]{:S(2)}, u32[]{:S(2)}) collective-permute-start(bf16[2,4,32,2816]{3,2,1,0:T(8,128)(2,1)S(1)} %put_in_line.6), channel_id=1, source_target_pairs={{0,2},{1,5},{2,0},{3,7},{4,6},{5,1},{6,4},{7,3},{8,10},{9,13},{10,... | collective-permute-start | bytes 4325384 | tf_op jit(solution)/shard_map/ppermute | solution.py:1370
  132.7 26.9 %collective-permute-start.18 = (bf16[2,1,88,1024]{3,2,1,0:T(8,128)(2,1)S(1)}, bf16[2,1,88,1024]{3,2,1,0:T(8,128)(2,1)S(1)}, u32[]{:S(2)}, u32[]{:S(2)}) collective-permute-start(bf16[2,1,88,1024]{3,2,1,0:T(8,128)(2,1)S(1)} %pad_maximum_fusion.18), channel_id=1, source_target_pairs={{0,8},{1,9},{2,10},{3,11},{4,12},{5,13},{6,14},{7,15},{8,0},{9,1},... | collective-permute-start | bytes 1081352 | tf_op jit(solution)/shard_map/ppermute | solution.py:1370
  163.6 42.4 %collective-permute-start.19 = (bf16[2,2,4,32,2816]{4,3,2,1,0:T(8,128)(2,1)S(1)}, bf16[2,2,4,32,2816]{4,3,2,1,0:T(8,128)(2,1)}, u32[]{:S(2)}, u32[]{:S(2)}) collective-permute-start(bf16[2,2,4,32,2816]{4,3,2,1,0:T(8,128)(2,1)S(1)} %pad_maximum_fusion.1.refs_0_), channel_id=1, source_target_pairs={{0,4},{1,3},{2,6},{3,1},{4,0},{5,7},{6,2},{7,5},{8,12},{9,11},{10,... | collective-permute-start | bytes 8650760 | tf_op jit(solution)/shard_map/ppermute | solution.py:1370
  164.2 41.8 %collective-permute-start.21 = (bf16[2,2,4,32,2816]{4,3,2,1,0:T(8,128)(2,1)S(1)}, bf16[2,2,4,32,2816]{4,3,2,1,0:T(8,128)(2,1)}, u32[]{:S(2)}, u32[]{:S(2)}) collective-permute-start(bf16[2,2,4,32,2816]{4,3,2,1,0:T(8,128)(2,1)S(1)} %pad_maximum_fusion.1.refs_0_), channel_id=1, source_target_pairs={{0,1},{1,0},{2,3},{3,2},{4,5},{5,4},{6,7},{7,6},{8,9},{9,8},{10,11... | collective-permute-start | bytes 8650760 | tf_op jit(solution)/shard_map/ppermute | solution.py:1370
  165.1 34.7 %collective-permute-start.20 = (bf16[1,4,88,1024]{3,2,1,0:T(8,128)(2,1)S(1)}, bf16[1,4,88,1024]{3,2,1,0:T(8,128)(2,1)}, u32[]{:S(2)}, u32[]{:S(2)}) collective-permute-start(bf16[1,4,88,1024]{3,2,1,0:T(8,128)(2,1)S(1)} %put_in_line.7), channel_id=1, source_target_pairs={{0,2},{1,5},{2,0},{3,7},{4,6},{5,1},{6,4},{7,3},{8,10},{9,13},{10,... | collective-permute-start | bytes 2162696 | tf_op jit(solution)/shard_map/ppermute | solution.py:1370
  206.0 5.5 collective-permute-start.22
  207.2 19.1 %collective-permute-start.23 = (bf16[2,1,4,88,1024]{4,3,2,1,0:T(8,128)(2,1)S(1)}, bf16[2,1,4,88,1024]{4,3,2,1,0:T(8,128)(2,1)S(1)}, u32[]{:S(2)}, u32[]{:S(2)}) collective-permute-start(bf16[2,1,4,88,1024]{4,3,2,1,0:T(8,128)(2,1)S(1)} %pad_maximum_fusion.7.refs_0_), channel_id=1, source_target_pairs={{0,4},{1,3},{2,6},{3,1},{4,0},{5,7},{6,2},{7,5},{8,12},{9,11},{10,... | collective-permute-start | bytes 4325384 | tf_op jit(solution)/shard_map/ppermute | solution.py:1370
  207.8 18.5 %collective-permute-start.24 = (bf16[2,1,4,88,1024]{4,3,2,1,0:T(8,128)(2,1)S(1)}, bf16[2,1,4,88,1024]{4,3,2,1,0:T(8,128)(2,1)S(1)}, u32[]{:S(2)}, u32[]{:S(2)}) collective-permute-start(bf16[2,1,4,88,1024]{4,3,2,1,0:T(8,128)(2,1)S(1)} %pad_maximum_fusion.7.refs_0_), channel_id=1, source_target_pairs={{0,1},{1,0},{2,3},{3,2},{4,5},{5,4},{6,7},{7,6},{8,9},{9,8},{10,11... | collective-permute-start | bytes 4325384 | tf_op jit(solution)/shard_map/ppermute | solution.py:1370
  226.3 3.2 collective-permute-start.25
  325.0 13.9 %collective-permute-start.26 = (bf16[2,16,32,2816]{3,2,1,0:T(8,128)(2,1)}, bf16[2,16,32,2816]{3,2,1,0:T(8,128)(2,1)}, u32[]{:S(2)}, u32[]{:S(2)}) collective-permute-start(bf16[2,16,32,2816]{3,2,1,0:T(8,128)(2,1)} %get-tuple-element.316), channel_id=1, source_target_pairs={{0,1},{1,0},{2,3},{3,2},{4,5},{5,4},{6,7},{7,6},{8,9},{9,8},{10,11... | collective-permute-start | bytes 17301512 | tf_op jit(solution)/shard_map/ppermute | solution.py:1370
  325.2 13.5 %collective-permute-start.27 = (bf16[1,16,88,1024]{3,2,1,0:T(8,128)(2,1)}, bf16[1,16,88,1024]{3,2,1,0:T(8,128)(2,1)S(1)}, u32[]{:S(2)}, u32[]{:S(2)}) collective-permute-start(bf16[1,16,88,1024]{3,2,1,0:T(8,128)(2,1)} %bitcast.263), channel_id=1, source_target_pairs={{0,1},{1,0},{2,3},{3,2},{4,5},{5,4},{6,7},{7,6},{8,9},{9,8},{10,11... | collective-permute-start | bytes 8650760 | tf_op jit(solution)/shard_map/ppermute | solution.py:1370
  348.7 55.7 %collective-permute-start.29 = (bf16[2,4,2,32,2816]{4,3,2,1,0:T(8,128)(2,1)}, bf16[2,4,2,32,2816]{4,3,2,1,0:T(8,128)(2,1)S(1)}, u32[]{:S(2)}, u32[]{:S(2)}) collective-permute-start(bf16[2,4,2,32,2816]{4,3,2,1,0:T(8,128)(2,1)} %get-tuple-element.346), channel_id=1, source_target_pairs={{0,4},{1,3},{2,6},{3,1},{4,0},{5,7},{6,2},{7,5},{8,12},{9,11},{10,... | collective-permute-start | bytes 8650760 | tf_op jit(solution)/shard_map/ppermute | solution.py:1370
  354.9 49.5 %collective-permute-start.30 = (bf16[2,4,1,88,1024]{4,3,1,2,0:T(8,128)(2,1)}, bf16[2,4,1,88,1024]{4,3,1,2,0:T(8,128)(2,1)}, u32[]{:S(2)}, u32[]{:S(2)}) collective-permute-start(bf16[2,4,1,88,1024]{4,3,1,2,0:T(8,128)(2,1)} %bitcast.264), channel_id=1, source_target_pairs={{0,4},{1,3},{2,6},{3,1},{4,0},{5,7},{6,2},{7,5},{8,12},{9,11},{10,... | collective-permute-start | bytes 4325384 | tf_op jit(solution)/shard_map/ppermute | solution.py:1370
  356.4 48.0 %collective-permute-start.28 = (bf16[640,1024]{1,0:T(8,128)(2,1)}, bf16[640,1024]{1,0:T(8,128)(2,1)}, u32[]{:S(2)}, u32[]{:S(2)}) collective-permute-start(bf16[640,1024]{1,0:T(8,128)(2,1)} %get-tuple-element.368), channel_id=1, source_target_pairs={{0,1},{1,0},{2,3},{3,2},{4,5},{5,4},{6,7},{7,6},{8,9},{9,8},{10,11... | collective-permute-start | bytes 3932168 | tf_op jit(solution)/shard_map/ppermute | solution.py:1370
  404.4 28.0 %copy-start.10 = (bf16[2,4,2,32,2816]{4,3,2,1,0:T(8,128)(2,1)}, bf16[2,4,2,32,2816]{4,3,2,1,0:T(8,128)(2,1)S(1)}, u32[]{:S(2)}) copy-start(bf16[2,4,2,32,2816]{4,3,2,1,0:T(8,128)(2,1)S(1)} %collective-permute-done.29) | copy-start | bytes 8650756
  404.4 29.4 %collective-permute-start.31 = (bf16[5,16,32,1024]{3,2,1,0:T(8,128)(2,1)}, bf16[5,16,32,1024]{3,2,1,0:T(8,128)(2,1)}, u32[]{:S(2)}, u32[]{:S(2)}) collective-permute-start(bf16[5,16,32,1024]{3,2,1,0:T(8,128)(2,1)} %weight_part.6), channel_id=1, source_target_pairs={{0,1},{1,0},{2,3},{3,2},{4,5},{5,4},{6,7},{7,6},{8,9},{9,8},{10,11... | collective-permute-start | bytes 15728648 | tf_op jit(solution)/shard_map/ppermute | solution.py:1370
  406.8 27.1 %collective-permute-start.34 = (bf16[4,2,32,2816]{3,2,1,0:T(8,128)(2,1)}, bf16[4,2,32,2816]{3,2,1,0:T(8,128)(2,1)}, u32[]{:S(2)}, u32[]{:S(2)}) collective-permute-start(bf16[4,2,32,2816]{3,2,1,0:T(8,128)(2,1)} %fusion.2), channel_id=1, source_target_pairs={{0,2},{1,5},{2,0},{3,7},{4,6},{5,1},{6,4},{7,3},{8,10},{9,13},{10,... | collective-permute-start | bytes 4325384 | tf_op jit(solution)/shard_map/ppermute | solution.py:1370
  410.4 23.5 %collective-permute-start.33 = (bf16[4,1,88,1024]{3,2,1,0:T(8,128)(2,1)}, bf16[4,1,88,1024]{3,2,1,0:T(8,128)(2,1)}, u32[]{:S(2)}, u32[]{:S(2)}) collective-permute-start(bf16[4,1,88,1024]{3,2,1,0:T(8,128)(2,1)} %fusion.9), channel_id=1, source_target_pairs={{0,2},{1,5},{2,0},{3,7},{4,6},{5,1},{6,4},{7,3},{8,10},{9,13},{10,... | collective-permute-start | bytes 2162696 | tf_op jit(solution)/shard_map/ppermute | solution.py:1370
  412.1 20.3 %collective-permute-start.32 = (f32[128,1024]{1,0:T(8,128)}, f32[128,1024]{1,0:T(8,128)}, u32[]{:S(2)}, u32[]{:S(2)}) collective-permute-start(f32[128,1024]{1,0:T(8,128)} %get-tuple-element.655), channel_id=1, source_target_pairs={{0,1},{1,0},{2,3},{3,2},{4,5},{5,4},{6,7},{7,6},{8,9},{9,8},{10,11... | collective-permute-start | bytes 1572872 | tf_op jit(solution)/shard_map/ppermute | solution.py:1370
  450.6 36.9 %collective-permute-start.36 = (bf16[2,4,5,32,1024]{4,3,2,1,0:T(8,128)(2,1)}, bf16[2,4,5,32,1024]{4,3,2,1,0:T(8,128)(2,1)}, u32[]{:S(2)}, u32[]{:S(2)}) collective-permute-start(bf16[2,4,5,32,1024]{4,3,2,1,0:T(8,128)(2,1)} %get-tuple-element.383), channel_id=1, source_target_pairs={{0,4},{1,3},{2,6},{3,1},{4,0},{5,7},{6,2},{7,5},{8,12},{9,11},{10,... | collective-permute-start | bytes 7864328 | tf_op jit(solution)/shard_map/ppermute | solution.py:1370
  459.1 28.4 %collective-permute-start.35 = (bf16[3,16,32,512]{3,2,1,0:T(8,128)(2,1)}, bf16[3,16,32,512]{3,2,1,0:T(8,128)(2,1)}, u32[]{:S(2)}, u32[]{:S(2)}) collective-permute-start(bf16[3,16,32,512]{3,2,1,0:T(8,128)(2,1)} %weight_part.8), channel_id=1, source_target_pairs={{0,1},{1,0},{2,3},{3,2},{4,5},{5,4},{6,7},{7,6},{8,9},{9,8},{10,11... | collective-permute-start | bytes 4718600 | tf_op jit(solution)/shard_map/ppermute | solution.py:1370
  462.8 24.7 %collective-permute-start.37 = (bf16[2,2,32,2816]{3,2,1,0:T(8,128)(2,1)}, bf16[2,2,32,2816]{3,2,1,0:T(8,128)(2,1)S(1)}, u32[]{:S(2)}, u32[]{:S(2)}) collective-permute-start(bf16[2,2,32,2816]{3,2,1,0:T(8,128)(2,1)} %pad_maximum_fusion.12), channel_id=1, source_target_pairs={{0,8},{1,9},{2,10},{3,11},{4,12},{5,13},{6,14},{7,15},{8,0},{9,1},... | collective-permute-start | bytes 2162696 | tf_op jit(solution)/shard_map/ppermute | solution.py:1370
  465.5 57.4 %collective-permute-start.41 = (bf16[2,1,88,1024]{3,2,1,0:T(8,128)(2,1)}, bf16[2,1,88,1024]{3,2,1,0:T(8,128)(2,1)}, u32[]{:S(2)}, u32[]{:S(2)}) collective-permute-start(bf16[2,1,88,1024]{3,2,1,0:T(8,128)(2,1)} %pad_maximum_fusion.19), channel_id=1, source_target_pairs={{0,8},{1,9},{2,10},{3,11},{4,12},{5,13},{6,14},{7,15},{8,0},{9,1},... | collective-permute-start | bytes 1081352 | tf_op jit(solution)/shard_map/ppermute | solution.py:1370
  497.2 13.2 %collective-permute-start.38 = (bf16[3,16,32,512]{3,2,1,0:T(8,128)(2,1)}, bf16[3,16,32,512]{3,2,1,0:T(8,128)(2,1)}, u32[]{:S(2)}, u32[]{:S(2)}) collective-permute-start(bf16[3,16,32,512]{3,2,1,0:T(8,128)(2,1)} %weight_part.9), channel_id=1, source_target_pairs={{0,1},{1,0},{2,3},{3,2},{4,5},{5,4},{6,7},{7,6},{8,9},{9,8},{10,11... | collective-permute-start | bytes 4718600 | tf_op jit(solution)/shard_map/ppermute | solution.py:1370
  497.2 26.0 %collective-permute-start.40 = (bf16[4,5,32,1024]{3,2,1,0:T(8,128)(2,1)}, bf16[4,5,32,1024]{3,2,1,0:T(8,128)(2,1)}, u32[]{:S(2)}, u32[]{:S(2)}) collective-permute-start(bf16[4,5,32,1024]{3,2,1,0:T(8,128)(2,1)} %fusion.5), channel_id=1, source_target_pairs={{0,2},{1,5},{2,0},{3,7},{4,6},{5,1},{6,4},{7,3},{8,10},{9,13},{10,... | collective-permute-start | bytes 3932168 | tf_op jit(solution)/shard_map/ppermute | solution.py:1370
  505.8 17.4 %collective-permute-start.39 = (bf16[2,4,3,32,512]{4,3,2,1,0:T(8,128)(2,1)}, bf16[2,4,3,32,512]{4,3,2,1,0:T(8,128)(2,1)}, u32[]{:S(2)}, u32[]{:S(2)}) collective-permute-start(bf16[2,4,3,32,512]{4,3,2,1,0:T(8,128)(2,1)} %get-tuple-element.401), channel_id=1, source_target_pairs={{0,4},{1,3},{2,6},{3,1},{4,0},{5,7},{6,2},{7,5},{8,12},{9,11},{10,... | collective-permute-start | bytes 2359304 | tf_op jit(solution)/shard_map/ppermute | solution.py:1370
  510.4 49.6 %collective-permute-start.48 = (bf16[2,32,2816]{2,1,0:T(8,128)(2,1)}, bf16[2,32,2816]{2,1,0:T(8,128)(2,1)}, u32[]{:S(2)}, u32[]{:S(2)}) collective-permute-start(bf16[2,32,2816]{2,1,0:T(8,128)(2,1)} %fusion.16), channel_id=1, source_target_pairs={{0,16},{1,17},{2,18},{3,19},{4,20},{5,21},{6,22},{7,23},{8,24},{9,... | collective-permute-start | bytes 1081352 | tf_op jit(solution)/shard_map/ppermute | solution.py:1370
  529.6 23.0 %collective-permute-start.42 = (bf16[2,4,3,32,512]{4,3,2,1,0:T(8,128)(2,1)}, bf16[2,4,3,32,512]{4,3,2,1,0:T(8,128)(2,1)}, u32[]{:S(2)}, u32[]{:S(2)}) collective-permute-start(bf16[2,4,3,32,512]{4,3,2,1,0:T(8,128)(2,1)} %get-tuple-element.411), channel_id=1, source_target_pairs={{0,4},{1,3},{2,6},{3,1},{4,0},{5,7},{6,2},{7,5},{8,12},{9,11},{10,... | collective-permute-start | bytes 2359304 | tf_op jit(solution)/shard_map/ppermute | solution.py:1370
  530.8 47.9 %collective-permute-start.52 = (f32[768,1024]{1,0:T(8,128)}, f32[768,1024]{1,0:T(8,128)}, u32[]{:S(2)}, u32[]{:S(2)}) collective-permute-start(f32[768,1024]{1,0:T(8,128)} %get-tuple-element.435), channel_id=1, source_target_pairs={{0,1},{1,0},{2,3},{3,2},{4,5},{5,4},{6,7},{7,6},{8,9},{9,8},{10,11... | collective-permute-start | bytes 9437192 | tf_op jit(solution)/shard_map/ppermute | solution.py:1370
  535.0 17.6 %collective-permute-start.44 = (bf16[2,5,32,1024]{3,2,1,0:T(8,128)(2,1)}, bf16[2,5,32,1024]{3,2,1,0:T(8,128)(2,1)}, u32[]{:S(2)}, u32[]{:S(2)}) collective-permute-start(bf16[2,5,32,1024]{3,2,1,0:T(8,128)(2,1)} %pad_maximum_fusion.14), channel_id=1, source_target_pairs={{0,8},{1,9},{2,10},{3,11},{4,12},{5,13},{6,14},{7,15},{8,0},{9,1},... | collective-permute-start | bytes 1966088 | tf_op jit(solution)/shard_map/ppermute | solution.py:1370
  537.2 13.6 %collective-permute-start.43 = (bf16[4,3,32,512]{3,2,1,0:T(8,128)(2,1)}, bf16[4,3,32,512]{3,2,1,0:T(8,128)(2,1)S(1)}, u32[]{:S(2)}, u32[]{:S(2)}) collective-permute-start(bf16[4,3,32,512]{3,2,1,0:T(8,128)(2,1)} %fusion.12), channel_id=1, source_target_pairs={{0,2},{1,5},{2,0},{3,7},{4,6},{5,1},{6,4},{7,3},{8,10},{9,13},{10,... | collective-permute-start | bytes 1179656 | tf_op jit(solution)/shard_map/ppermute | solution.py:1370
  550.8 11.4 %collective-permute-start.47 = (bf16[1,88,1024]{2,1,0:T(8,128)(2,1)S(1)}, bf16[1,88,1024]{2,1,0:T(8,128)(2,1)S(1)}, u32[]{:S(2)}, u32[]{:S(2)}) collective-permute-start(bf16[1,88,1024]{2,1,0:T(8,128)(2,1)S(1)} %fusion.26), channel_id=1, source_target_pairs={{0,16},{1,17},{2,18},{3,19},{4,20},{5,21},{6,22},{7,23},{8,24},{9,... | collective-permute-start | bytes 540680 | tf_op jit(solution)/shard_map/ppermute | solution.py:1370
  553.9 13.5 %collective-permute-start.45 = (bf16[4,3,32,512]{3,2,1,0:T(8,128)(2,1)S(1)}, bf16[4,3,32,512]{3,2,1,0:T(8,128)(2,1)S(1)}, u32[]{:S(2)}, u32[]{:S(2)}) collective-permute-start(bf16[4,3,32,512]{3,2,1,0:T(8,128)(2,1)S(1)} %fusion.13), channel_id=1, source_target_pairs={{0,2},{1,5},{2,0},{3,7},{4,6},{5,1},{6,4},{7,3},{8,10},{9,13},{10,... | collective-permute-start | bytes 1179656 | tf_op jit(solution)/shard_map/ppermute | solution.py:1370
  556.4 10.9 %collective-permute-start.46 = (bf16[2,3,32,512]{3,2,1,0:T(8,128)(2,1)S(1)}, bf16[2,3,32,512]{3,2,1,0:T(8,128)(2,1)S(1)}, u32[]{:S(2)}, u32[]{:S(2)}) collective-permute-start(bf16[2,3,32,512]{3,2,1,0:T(8,128)(2,1)S(1)} %pad_maximum_fusion.22), channel_id=1, source_target_pairs={{0,8},{1,9},{2,10},{3,11},{4,12},{5,13},{6,14},{7,15},{8,0},{9,1},... | collective-permute-start | bytes 589832 | tf_op jit(solution)/shard_map/ppermute | solution.py:1370
  559.9 23.8 %collective-permute-start.51 = (bf16[5,32,1024]{2,1,0:T(8,128)(2,1)}, bf16[5,32,1024]{2,1,0:T(8,128)(2,1)}, u32[]{:S(2)}, u32[]{:S(2)}) collective-permute-start(bf16[5,32,1024]{2,1,0:T(8,128)(2,1)} %fusion.18), channel_id=1, source_target_pairs={{0,16},{1,17},{2,18},{3,19},{4,20},{5,21},{6,22},{7,23},{8,24},{9,... | collective-permute-start | bytes 983048 | tf_op jit(solution)/shard_map/ppermute | solution.py:1370
  568.0 15.7 %collective-permute-start.50 = (bf16[3,32,512]{2,1,0:T(8,128)(2,1)}, bf16[3,32,512]{2,1,0:T(8,128)(2,1)}, u32[]{:S(2)}, u32[]{:S(2)}) collective-permute-start(bf16[3,32,512]{2,1,0:T(8,128)(2,1)} %fusion.27), channel_id=1, source_target_pairs={{0,16},{1,17},{2,18},{3,19},{4,20},{5,21},{6,22},{7,23},{8,24},{9,... | collective-permute-start | bytes 294920 | tf_op jit(solution)/shard_map/ppermute | solution.py:1370
  570.0 14.4 %collective-permute-start.49 = (bf16[2,3,32,512]{3,2,1,0:T(8,128)(2,1)}, bf16[2,3,32,512]{3,2,1,0:T(8,128)(2,1)}, u32[]{:S(2)}, u32[]{:S(2)}) collective-permute-start(bf16[2,3,32,512]{3,2,1,0:T(8,128)(2,1)} %pad_maximum_fusion.23), channel_id=1, source_target_pairs={{0,8},{1,9},{2,10},{3,11},{4,12},{5,13},{6,14},{7,15},{8,0},{9,1},... | collective-permute-start | bytes 589832 | tf_op jit(solution)/shard_map/ppermute | solution.py:1370
  585.4 8.3 %collective-permute-start.53 = (bf16[3,32,512]{2,1,0:T(8,128)(2,1)S(1)}, bf16[3,32,512]{2,1,0:T(8,128)(2,1)S(1)}, u32[]{:S(2)}, u32[]{:S(2)}) collective-permute-start(bf16[3,32,512]{2,1,0:T(8,128)(2,1)S(1)} %fusion.28), channel_id=1, source_target_pairs={{0,16},{1,17},{2,18},{3,19},{4,20},{5,21},{6,22},{7,23},{8,24},{9,... | collective-permute-start | bytes 294920 | tf_op jit(solution)/shard_map/ppermute | solution.py:1370
  596.1 5.6 collective-permute-start.54
  598.6 4.6 collective-permute-start.55
  598.7 4.6 collective-permute-start.56
  603.3 4.3 collective-permute-start.57
  604.2 3.7 collective-permute-start.58
  605.2 4.6 collective-permute-start.59
  609.8 1.2 collective-permute-start.60
  (43 other events, 358.2 us)

commit v4 on v3

--- a/solution.py
+++ b/solution.py
@@ -909,6 +909,8 @@
         return pl.BlockSpec((None,) + left.shape[1:], lambda t, p: (p[0], 0, 0), pipeline_mode=pl.Buffered(1))
 
     def tile(right):
+        if isinstance(right, tuple):
+            return pl.BlockSpec((None, right[0].shape[1], TILE), lambda t, p: (right[1], 0, t))
         return pl.BlockSpec((right.shape[0], TILE), lambda t, p: (0, t) if right.shape[1] > TILE else (0, 0))
 
     shared = pl.BlockSpec((len(jobs), D // 64, m, TILE), lambda t, p: (0, 0, 0, t))
@@ -930,7 +932,7 @@
         compiler_params=params(),
         cost_estimate=cost(2),
         name="weight_part",
-    )(plan, *lefts, *(value for right in rights for value in right), *([] if got is None else [got]))
+    )(plan, *lefts, *(value[0] if isinstance(value, tuple) else value for right in rights for value in right), *([] if got is None else [got]))
 
 
 def root(value):
@@ -1775,7 +1777,7 @@
     keep_plan = jnp.stack([core, far, across, here, near])
     away_plan = jnp.stack([1 - core, far, across, here, near])
     lefts_mid = [turned_mixed_one, turned_two, turned_encoder, turned_mixed_two]
-    jobs_mid = [(0, self_low), (1, query_two_low), (2, kv_two_low[0]), (2, kv_two_low[1]), (3, cross_low)]
+    jobs_mid = [(0, self_low), (1, query_two_low), (2, (kv_two_low, 0)), (2, (kv_two_low, 1)), (3, cross_low)]
     away_mid = weight_part(away_plan, lefts_mid, jobs_mid)
     encoder_grad = matmul_t(kv_two_low[0], w_key_two) + matmul_t(kv_two_low[1], w_value_two)
     away_mid, encoder_grad, other_output, got_exp, got_con = tie(away_mid, encoder_grad, other_output, got_exp, got_con)

time: 634 us -> 633 us (level)
  transfers between devices with their start and end apart: 61 -> 61, of which waited for: 22 -> 20; matrix products, arithmetic and copies ran while one was open for 12% -> 12% of each run, Pallas kernels for 41% -> 41%
where the time goes in v4:
time: 633 us; the launch traced here: 623 us
  Pallas kernels  378 us (60%)
  other arithmetic  78.4 us (12%)
  waiting for transfers between devices  71.4 us (11%)
  starting transfers between devices  55.5 us (9%)
  local copies, waits for them, and re-layouts  22.7 us (4%)
  between operations  13.7 us (2%)
    pallas_call x1, Pallas kernels, mlp(): pl.pallas_call(functools.partial(mlp_kernel, branch_rows), grid_spec=pltp...  91.5 us
    ppermute x61, waiting for transfers between devices, send(): return lax.ppermute(value, AXES, moves(rule))  71.4 us
    ppermute x61, starting transfers between devices, send(): return lax.ppermute(value, AXES, moves(rule))  55.5 us
    pallas_call x2, Pallas kernels, self_forward(): pl.pallas_call(functools.partial(self_kernel, prompt, size, len(more)), g...  50.1 us
    pallas_call x6, Pallas kernels, weight_part(): pl.pallas_call(functools.partial(part_kernel, [left for left, _ in jobs],...  49.2 us
    pallas_call x2, Pallas kernels, middle_back(): pl.pallas_call(middle_back_kernel, grid=(blocks,), in_specs=[rows] * 6 +...  42.8 us
    pallas_call x2, Pallas kernels, self_backward(): pl.pallas_call(functools.partial(self_back_kernel, prompt, size), grid=(p...  38.4 us
    pallas_call x1, Pallas kernels, middle(): pl.pallas_call(functools.partial(middle_kernel, len(mixed)), grid=(count...  33.1 us
  transfers between devices with their start and end apart: 61, of which 20 were waited for; matrix products, arithmetic and copies ran while one was open for 12% of the time, Pallas kernels for 41%

profile of v4, /device:TPU:0, one launch (start us, length us, event | category | flops | bytes accessed | tf_op | source)
XLA Modules:
  0.0 622.6 jit_solution(5254762298538724287)
XLA Ops:
  2.0 4.1 collective-permute-start
  11.4 3.8 collective-permute-done.far
  16.1 9.5 %collective-permute-done.2.near = bf16[2,3,32,1024]{3,2,1,0:T(8,128)(2,1)S(1)} collective-permute-done((bf16[2,3,32,1024]{3,2,1,0:T(8,128)(2,1)S(1)}, bf16[2,3,32,1024]{3,2,1,0:T(8,128)(2,1)S(1)}, u32[]{:S(2)}, u32[]{:S(2)}) %collective-permute-start.2) | collective-permute-done | bytes 393248 | tf_op jit(solution)/shard_map/ppermute | solution.py:1372
  37.7 3.4 collective-permute-start.4
  42.0 3.1 collective-permute-done.3
  47.7 8.5 %collective-permute-done.4.far = bf16[5,32,1024]{2,1,0:T(8,128)(2,1)S(1)} collective-permute-done((bf16[5,32,1024]{2,1,0:T(8,128)(2,1)S(1)}, bf16[5,32,1024]{2,1,0:T(8,128)(2,1)S(1)}, u32[]{:S(2)}, u32[]{:S(2)}) %collective-permute-start.4) | collective-permute-done | bytes 327712 | tf_op jit(solution)/shard_map/ppermute | solution.py:1372
  57.1 3.1 broadcast_select_fusion.1
  65.1 7.7 %collective-permute-done.6.near = bf16[2,5,32,1024]{3,2,1,0:T(8,128)(2,1)S(1)} collective-permute-done((bf16[2,5,32,1024]{3,2,1,0:T(8,128)(2,1)S(1)}, bf16[2,5,32,1024]{3,2,1,0:T(8,128)(2,1)S(1)}, u32[]{:S(2)}, u32[]{:S(2)}) %collective-permute-start.6) | collective-permute-done | bytes 655392 | tf_op jit(solution)/shard_map/ppermute | solution.py:1372
  75.1 2.9 collective-permute-start.11
  79.4 17.0 %enter.1 = (bf16[2,512,1280]{2,1,0:T(8,128)(2,1)}, bf16[3,1280,1024]{2,1,0:T(8,128)(2,1)}, bf16[4,4,2,32,1024]{4,3,2,1,0:T(8,128)(2,1)}, bf16[4,4,2,32,1024]{4,3...) custom-call(s32[8,2]{1,0:T(8,128)} %stack.290.slots_ref, bf16[2,3,4,32,1024]{4,3,2,1,0:T(8,128)(2,1)} %copy-done.6, ...), custom_call_target="tpu_custom_call" | custom-call | flops 12 | bytes 1 | tf_op jit(solution)/shard_map/enter/pallas_call | solution.py:1051
  96.5 3.0 pad_maximum_fusion.4.refs_0_
  100.3 1.8 collective-permute-start.14
  102.4 25.0 %self_forward.2 = (bf16[1280,1024]{1,0:T(8,128)(2,1)}, bf16[16,256,3712]{2,1,0:T(8,128)(2,1)}, f32[1280,1024]{1,0:T(8,128)}) custom-call(s32[2]{0:T(128)} %copy-done.38, bf16[3,1280,1024]{2,1,0:T(8,128)(2,1)} %get-tuple-element.282.q_ref.k_ref.v_ref, bf16[3,1280,1024]{2,1,0:T(8,128)(2,1)} %get-tuple-element.282.q_ref.k_ref.v_ref, ...), custom_call_target="tpu_custom_call" | custom-call | flops 24 | bytes 1 | tf_op jit(solution)/shard_map/self_forward/pallas_call | solution.py:608
  127.4 4.1 collective-permute-done.12.refs_2_
  132.7 1.8 collective-permute-start.18
  134.5 25.2 %self_forward.3 = (bf16[1280,1024]{1,0:T(8,128)(2,1)}, bf16[16,256,3712]{2,1,0:T(8,128)(2,1)}, f32[1280,1024]{1,0:T(8,128)}) custom-call(s32[2]{0:T(128)} %copy-done.38, bf16[3,1280,1024]{2,1,0:T(8,128)(2,1)} %get-tuple-element.282.q_ref.k_ref.v_ref, ...), custom_call_target="tpu_custom_call", output_to_operand_aliasing={{0}: (6, {}), {1}: (7, {}), {2}: (8, {})} | custom-call | flops 24 | bytes 1 | tf_op jit(solution)/shard_map/self_forward/pallas_call | solution.py:608
  161.6 2.1 pad_maximum_fusion.1.refs_0_
  166.8 33.1 %middle.1 = (f32[1280,1024]{1,0:T(8,128)}, f32[1280,1024]{1,0:T(8,128)}, bf16[2,512,1280]{2,1,0:T(8,128)(2,1)}, bf16[1280,1024]{1,0:T(8,128)(2,1)}, bf16[1280,10...) custom-call(s32[8,2]{1,0:T(8,128)} %stack.290.slots_ref, ...), custom_call_target="tpu_custom_call" | custom-call | flops 30 | bytes 1 | tf_op jit(solution)/shard_map/middle/pallas_call | solution.py:1130
  199.9 6.2 collective-permute-done.19.refs_2_
  208.9 2.7 collective-permute-done.22.refs_3_
  211.5 8.0 %assemble.2 = (bf16[4,4,2,32,2816]{4,3,2,1,0:T(8,128)(2,1)}, bf16[4,4,2,32,2816]{4,3,2,1,0:T(8,128)(2,1)}) custom-call(s32[8,2]{1,0:T(8,128)S(1)} %copy-done.4, bf16[2,2,4,32,2816]{4,3,2,1,0:T(8,128)(2,1)S(1)} %pad_maximum_fusion.1.refs_0_, bf16[2,2,4,32,2816]{4,3,2,1,0:T(8,128)(2,1)} %collective-permute-done.21.refs_1_, ...), custom_call_target="tpu_custom_call" | custom-call | flops 4 | bytes 1 | tf_op jit(solution)/shard_map/assemble/pallas_call | solution.py:1457
  219.5 6.8 %collective-permute-done.23.refs_2_ = bf16[2,1,4,88,1024]{4,3,2,1,0:T(8,128)(2,1)S(1)} collective-permute-done((bf16[2,1,4,88,1024]{4,3,2,1,0:T(8,128)(2,1)S(1)}, bf16[2,1,4,88,1024]{4,3,2,1,0:T(8,128)(2,1)S(1)}, u32[]{:S(2)}, u32[]{:S(2)}) %collective-permute-start.23) | collective-permute-done | bytes 1441824 | tf_op jit(solution)/shard_map/ppermute | solution.py:1372
  226.4 3.2 collective-permute-done.25.refs_3_
  231.1 2.5 copy-done
  233.6 91.5 %mlp.1 = (bf16[640,1024]{1,0:T(8,128)(2,1)}, bf16[640,1024]{1,0:T(8,128)(2,1)}, f32[1280,1024]{1,0:T(8,128)}, bf16[2,16,32,2816]{3,2,1,0:T(8,128)(2,1)}, bf16[2,...) custom-call(s32[1]{0:T(128)} %bitcast.core_ref, ...), custom_call_target="tpu_custom_call" | custom-call | flops 85 | bytes 1 | tf_op jit(solution)/shard_map/mlp/pallas_call | solution.py:845
  326.2 12.5 %middle_back.2 = (bf16[1280,1024]{1,0:T(8,128)(2,1)}, bf16[1280,1024]{1,0:T(8,128)(2,1)}, f32[1280,1024]{1,0:T(8,128)}, bf16[1280,1024]{1,0:T(8,128)(2,1)}, bf16...) custom-call(bf16[1280,1024]{1,0:T(8,128)(2,1)} %pad_maximum_fusion.3.dy, ...), custom_call_target="tpu_custom_call" | custom-call | flops 45 | bytes 1 | tf_op jit(solution)/shard_map/middle_back/pallas_call | solution.py:1239
  339.0 9.7 %add_split.2 = (bf16[2,4,2,32,2816]{4,3,2,1,0:T(8,128)(2,1)}, bf16[2,4,2,32,2816]{4,3,2,1,0:T(8,128)(2,1)}) custom-call(s32[4]{0:T(128)} %pad_add_fusion.2.spots_ref, bf16[2,4,4,32,2816]{4,3,2,1,0:T(8,128)(2,1)} %bitcast.245, bf16[2,4,4,32,2816]{4,3,2,1,0:T(8,128)(2,1)} %bitcast.60.two_ref), custom_call_target="tpu_custom_call" | custom-call | flops 1 | bytes 1 | tf_op jit(solution)/shard_map/add_split/pallas_call | solution.py:1507
  349.2 5.7 add_split.3
  357.0 30.3 %middle_back.3 = (bf16[1280,1024]{1,0:T(8,128)(2,1)}, bf16[1280,1024]{1,0:T(8,128)(2,1)}, f32[1280,1024]{1,0:T(8,128)}, bf16[1280,1024]{1,0:T(8,128)(2,1)}, bf16...) custom-call(bf16[1280,1024]{1,0:T(8,128)(2,1)} %pad_maximum_fusion.3, ...), custom_call_target="tpu_custom_call", output_to_operand_aliasing={{0}: (14, {}), {1}: (15, {}), {2}: (16, {}), {3}: (17, {}),... | custom-call | flops 45 | bytes 1 | tf_op jit(solution)/shard_map/middle_back/pallas_call | solution.py:1239
  387.3 11.5 %weight_part.6 = bf16[5,16,32,1024]{3,2,1,0:T(8,128)(2,1)} custom-call(s32[5]{0:T(128)} %stack.319.plan_ref, bf16[2,512,1280]{2,1,0:T(8,128)(2,1)} %get-tuple-element.358.refs_0_, bf16[2,512,1280]{2,1,0:T(8,128)(2,1)} %get-tuple-element.359.refs_1_, bf16[2,512,256]{2,1,0:T(8,128)(2,1)} %get-tuple-element.360.refs_2_, ...), custom_call_target="tpu_custom_call" | custom-call | flops 2 | bytes 1 | tf_op jit(solution)/shard_map/weight_part/pallas_call | solution.py:920
  401.9 1.7 fusion.2
  404.9 2.2 fusion.9
  409.9 19.1 %self_backward.2 = (bf16[1280,512]{1,0:T(8,128)(2,1)}, bf16[1280,512]{1,0:T(8,128)(2,1)}, bf16[1280,512]{1,0:T(8,128)(2,1)}, f32[8,1,1280]{2,1,0:T(1,128)}, f32[8,2,1,1152]{3,2,1,0:T(1,128)}) custom-call(bf16[3,1280,1024]{2,1,0:T(8,128)(2,1)} %get-tuple-element.282.q_ref.k_ref.v_ref, bf16[3,1280,1024]{2,1,0:T(8,128)(2,1)} %get-tuple-element.282.q_ref.k_ref.v_ref, ...), custom_call_target="tpu_custom_call" | custom-call | flops 32 | bytes 1 | tf_op jit(solution)/shard_map/self_backward/pallas_call | solution.py:717
  431.6 1.9 fusion.4
  433.5 2.3 fusion
  435.9 12.5 %weight_part.7 = (bf16[2,4,5,32,1024]{4,3,2,1,0:T(8,128)(2,1)}, bf16[2,4,5,32,1024]{4,3,2,1,0:T(8,128)(2,1)}) custom-call(s32[5]{0:T(128)} %stack.270.plan_ref, bf16[2,512,1280]{2,1,0:T(8,128)(2,1)} %get-tuple-element.358.refs_0_, bf16[2,512,1280]{2,1,0:T(8,128)(2,1)} %get-tuple-element.359.refs_1_, bf16[2,512,256]{2,1,0:T(8,128)(2,1)} %get-tuple-element.360.refs_2_, ...), custom_call_target="tpu_custom_call" | custom-call | flops 2 | bytes 1 | tf_op jit(solution)/shard_map/weight_part/pallas_call | solution.py:920
  450.6 6.1 weight_part.8
  463.0 1.8 collective-permute-start.41
  464.9 19.3 %self_backward.3 = (bf16[1280,512]{1,0:T(8,128)(2,1)}, bf16[1280,512]{1,0:T(8,128)(2,1)}, bf16[1280,512]{1,0:T(8,128)(2,1)}, f32[8,1,1280]{2,1,0:T(1,128)}, f32[8,2,1,1152]{3,2,1,0:T(1,128)}) custom-call(bf16[3,1280,1024]{2,1,0:T(8,128)(2,1)} %get-tuple-element.282.q_ref.k_ref.v_ref, bf16[3,1280,1024]{2,1,0:T(8,128)(2,1)} %get-tuple-element.282.q_ref.k_ref.v_ref, ...), custom_call_target="tpu_custom_call" | custom-call | flops 32 | bytes 1 | tf_op jit(solution)/shard_map/self_backward/pallas_call | solution.py:717
  485.1 3.4 fusion.5
  488.5 6.1 weight_part.9
  496.2 1.8 fusion.21
  498.0 6.6 %weight_part.10 = (bf16[2,4,3,32,512]{4,3,2,1,0:T(8,128)(2,1)}, bf16[2,4,3,32,512]{4,3,2,1,0:T(8,128)(2,1)}) custom-call(s32[5]{0:T(128)} %stack.270.plan_ref, bf16[2,512,1280]{2,1,0:T(8,128)(2,1)} %get-tuple-element.385.refs_0_, bf16[1280,512]{1,0:T(8,128)(2,1)} %get-tuple-element.386.refs_1_.refs_0_, bf16[1280,512]{1,0:T(8,128)(2,1)} %get-tuple-element.387.refs_2_.refs_1_, ...), custom_call_target="tpu_custom_call" | custom-call | flops 2 | bytes 1 | tf_op jit(solution)/shard_map/weight_part/pallas_call | solution.py:920
  509.2 12.5 %leave.2 = (f32[768,1024]{1,0:T(8,128)}, f32[8,1024]{1,0:T(8,128)}) custom-call(s32[3]{0:T(128)} %pad_add_fusion.plan_ref, bf16[1280,1024]{1,0:T(8,128)(2,1)} %pad_maximum_fusion.2.refs_4_.x_ref, f32[1280,1024]{1,0:T(8,128)} %get-tuple-element.403.dx1_ref, bf16[1280,512]{1,0:T(8,128)(2,1)} %get-tuple-element.386.refs_1_.refs_0_, ...), custom_call_target="tpu_custom_call" | custom-call | flops 2 | bytes 1 | tf_op jit(solution)/shard_map/leave/pallas_call | solution.py:1292
  521.7 6.4 %weight_part.11 = (bf16[2,4,3,32,512]{4,3,2,1,0:T(8,128)(2,1)}, bf16[2,4,3,32,512]{4,3,2,1,0:T(8,128)(2,1)}) custom-call(s32[5]{0:T(128)} %stack.270.plan_ref, bf16[2,512,1280]{2,1,0:T(8,128)(2,1)} %get-tuple-element.385.refs_0_, bf16[1280,512]{1,0:T(8,128)(2,1)} %get-tuple-element.395.refs_1_.refs_3_, bf16[1280,512]{1,0:T(8,128)(2,1)} %get-tuple-element.396.refs_2_.refs_4_, ...), custom_call_target="tpu_custom_call" | custom-call | flops 2 | bytes 1 | tf_op jit(solution)/shard_map/weight_part/pallas_call | solution.py:920
  528.8 3.0 fusion.1
  533.3 1.9 fusion.17
  537.1 10.6 %leave.3 = (f32[512,1024]{1,0:T(8,128)}, f32[8,1024]{1,0:T(8,128)}) custom-call(s32[2]{0:T(128)} %iota_add_fusion.plan_ref, bf16[1280,1024]{1,0:T(8,128)(2,1)} %pad_maximum_fusion.2.refs_4_.x_ref, f32[1280,1024]{1,0:T(8,128)} %get-tuple-element.403.dx1_ref, bf16[1280,512]{1,0:T(8,128)(2,1)} %get-tuple-element.386.refs_1_.refs_0_, ...), custom_call_target="tpu_custom_call" | custom-call | flops 2 | bytes 1 | tf_op jit(solution)/shard_map/leave/pallas_call | solution.py:1292
  548.7 2.6 collective-permute-start.47
  555.2 1.8 collective-permute-start.46
  556.9 1.8 fusion.23
  558.8 2.0 collective-permute-done.47
  560.8 5.4 collective-permute-done.46
  568.8 2.2 collective-permute-start.49
  571.1 2.3 multiply_reduce_fusion.2
  573.4 2.7 multiply_reduce_fusion
  577.5 2.7 select_bitcast_fusion.1
  580.2 2.3 pad_maximum_fusion
  587.2 1.9 multiply_reduce_fusion.1
  595.2 2.5 collective-permute-start.54
  597.8 2.4 collective-permute-start.56
  604.1 1.9 collective-permute-start.59
  606.8 2.0 collective-permute-done.59
  615.2 5.8 update.1
  (298 shorter events, 97.7 us)
Async XLA Ops:
  2.0 13.2 %collective-permute-start = (bf16[3,32,1024]{2,1,0:T(8,128)(2,1)S(1)}, bf16[3,32,1024]{2,1,0:T(8,128)(2,1)S(1)}, u32[]{:S(2)}, u32[]{:S(2)}) collective-permute-start(bf16[3,32,1024]{2,1,0:T(8,128)(2,1)S(1)} %get-tuple-element.673.shard), channel_id=1, source_target_pairs={{0,16},{1,17},{2,18},{3,19},{4,20},{5,21},{6,22},{7,23},{8,24},{9,... | collective-permute-start | bytes 589832 | tf_op jit(solution)/shard_map/ppermute | solution.py:1372
  7.4 1.2 collective-permute-start.1
  11.4 22.9 %copy-start.38 = (s32[2]{0:T(128)}, s32[2]{0:T(128)S(1)}, u32[]{:S(2)}) copy-start(s32[2]{0:T(128)S(1)} %pad_add_fusion.1.starts_ref) | copy-start | bytes 28
  15.2 10.4 %collective-permute-start.2 = (bf16[2,3,32,1024]{3,2,1,0:T(8,128)(2,1)S(1)}, bf16[2,3,32,1024]{3,2,1,0:T(8,128)(2,1)S(1)}, u32[]{:S(2)}, u32[]{:S(2)}) collective-permute-start(bf16[2,3,32,1024]{3,2,1,0:T(8,128)(2,1)S(1)} %pad_maximum_fusion.17), channel_id=1, source_target_pairs={{0,8},{1,9},{2,10},{3,11},{4,12},{5,13},{6,14},{7,15},{8,0},{9,1},... | collective-permute-start | bytes 1179656 | tf_op jit(solution)/shard_map/ppermute | solution.py:1372
  31.1 26.1 %collective-permute-start.8 = (bf16[1408,1024]{1,0:T(8,128)(2,1)}, bf16[1408,1024]{1,0:T(8,128)(2,1)}, u32[]{:S(2)}, u32[]{:S(2)}) collective-permute-start(bf16[1408,1024]{1,0:T(8,128)(2,1)} %get-tuple-element.662), channel_id=1, source_target_pairs={{0,1},{1,0},{2,3},{3,2},{4,5},{5,4},{6,7},{7,6},{8,9},{9,8},{10,11... | collective-permute-start | bytes 8650760 | tf_op jit(solution)/shard_map/ppermute | solution.py:1372
  32.9 12.2 %collective-permute-start.3 = (bf16[3,4,32,1024]{3,2,1,0:T(8,128)(2,1)S(1)}, bf16[3,4,32,1024]{3,2,1,0:T(8,128)(2,1)}, u32[]{:S(2)}, u32[]{:S(2)}) collective-permute-start(bf16[3,4,32,1024]{3,2,1,0:T(8,128)(2,1)S(1)} %put_in_line.4), channel_id=1, source_target_pairs={{0,2},{1,5},{2,0},{3,7},{4,6},{5,1},{6,4},{7,3},{8,10},{9,13},{10,... | collective-permute-start | bytes 2359304 | tf_op jit(solution)/shard_map/ppermute | solution.py:1372
  37.7 18.6 %collective-permute-start.4 = (bf16[5,32,1024]{2,1,0:T(8,128)(2,1)S(1)}, bf16[5,32,1024]{2,1,0:T(8,128)(2,1)S(1)}, u32[]{:S(2)}, u32[]{:S(2)}) collective-permute-start(bf16[5,32,1024]{2,1,0:T(8,128)(2,1)S(1)} %pad_maximum_fusion.20.shard), channel_id=1, source_target_pairs={{0,16},{1,17},{2,18},{3,19},{4,20},{5,21},{6,22},{7,23},{8,24},{9,... | collective-permute-start | bytes 983048 | tf_op jit(solution)/shard_map/ppermute | solution.py:1372
  46.4 26.4 %collective-permute-start.5 = (bf16[2,3,4,32,1024]{4,3,2,1,0:T(8,128)(2,1)S(1)}, bf16[2,3,4,32,1024]{4,3,2,1,0:T(8,128)(2,1)}, u32[]{:S(2)}, u32[]{:S(2)}) collective-permute-start(bf16[2,3,4,32,1024]{4,3,2,1,0:T(8,128)(2,1)S(1)} %pad_maximum_fusion.6.refs_0_), channel_id=1, source_target_pairs={{0,4},{1,3},{2,6},{3,1},{4,0},{5,7},{6,2},{7,5},{8,12},{9,11},{10,... | collective-permute-start | bytes 4718600 | tf_op jit(solution)/shard_map/ppermute | solution.py:1372
  56.3 16.5 %collective-permute-start.6 = (bf16[2,5,32,1024]{3,2,1,0:T(8,128)(2,1)S(1)}, bf16[2,5,32,1024]{3,2,1,0:T(8,128)(2,1)S(1)}, u32[]{:S(2)}, u32[]{:S(2)}) collective-permute-start(bf16[2,5,32,1024]{3,2,1,0:T(8,128)(2,1)S(1)} %pad_maximum_fusion.13), channel_id=1, source_target_pairs={{0,8},{1,9},{2,10},{3,11},{4,12},{5,13},{6,14},{7,15},{8,0},{9,1},... | collective-permute-start | bytes 1966088 | tf_op jit(solution)/shard_map/ppermute | solution.py:1372
  57.1 15.7 %collective-permute-start.7 = (bf16[2,3,4,32,1024]{4,3,2,1,0:T(8,128)(2,1)S(1)}, bf16[2,3,4,32,1024]{4,3,2,1,0:T(8,128)(2,1)S(1)}, u32[]{:S(2)}, u32[]{:S(2)}) collective-permute-start(bf16[2,3,4,32,1024]{4,3,2,1,0:T(8,128)(2,1)S(1)} %pad_maximum_fusion.6.refs_0_), channel_id=1, source_target_pairs={{0,1},{1,0},{2,3},{3,2},{4,5},{5,4},{6,7},{7,6},{8,9},{9,8},{10,11... | collective-permute-start | bytes 4718600 | tf_op jit(solution)/shard_map/ppermute | solution.py:1372
  72.8 6.6 %collective-permute-start.9 = (bf16[2,3,4,32,1024]{4,3,2,1,0:T(8,128)(2,1)}, bf16[2,3,4,32,1024]{4,3,2,1,0:T(8,128)(2,1)}, u32[]{:S(2)}, u32[]{:S(2)}) collective-permute-start(bf16[2,3,4,32,1024]{4,3,2,1,0:T(8,128)(2,1)} %collective-permute-done.5.refs_2_), channel_id=1, source_target_pairs={{0,1},{1,0},{2,3},{3,2},{4,5},{5,4},{6,7},{7,6},{8,9},{9,8},{10,11... | collective-permute-start | bytes 4718600 | tf_op jit(solution)/shard_map/ppermute | solution.py:1372
  74.0 22.5 %collective-permute-start.10 = (bf16[5,4,32,1024]{3,2,1,0:T(8,128)(2,1)S(1)}, bf16[5,4,32,1024]{3,2,1,0:T(8,128)(2,1)}, u32[]{:S(2)}, u32[]{:S(2)}) collective-permute-start(bf16[5,4,32,1024]{3,2,1,0:T(8,128)(2,1)S(1)} %put_in_line.5), channel_id=1, source_target_pairs={{0,2},{1,5},{2,0},{3,7},{4,6},{5,1},{6,4},{7,3},{8,10},{9,13},{10,... | collective-permute-start | bytes 3932168 | tf_op jit(solution)/shard_map/ppermute | solution.py:1372
  75.1 21.3 %collective-permute-start.11 = (bf16[2,32,2816]{2,1,0:T(8,128)(2,1)S(1)}, bf16[2,32,2816]{2,1,0:T(8,128)(2,1)S(1)}, u32[]{:S(2)}, u32[]{:S(2)}) collective-permute-start(bf16[2,32,2816]{2,1,0:T(8,128)(2,1)S(1)} %convert_element_type.428.shard), channel_id=1, source_target_pairs={{0,16},{1,17},{2,18},{3,19},{4,20},{5,21},{6,22},{7,23},{8,24},{9,... | collective-permute-start | bytes 1081352 | tf_op jit(solution)/shard_map/ppermute | solution.py:1372
  99.5 32.0 %collective-permute-start.12 = (bf16[2,5,4,32,1024]{4,3,2,1,0:T(8,128)(2,1)}, bf16[2,5,4,32,1024]{4,3,2,1,0:T(8,128)(2,1)}, u32[]{:S(2)}, u32[]{:S(2)}) collective-permute-start(bf16[2,5,4,32,1024]{4,3,2,1,0:T(8,128)(2,1)} %pad_maximum_fusion.4.refs_0_), channel_id=1, source_target_pairs={{0,4},{1,3},{2,6},{3,1},{4,0},{5,7},{6,2},{7,5},{8,12},{9,11},{10,... | collective-permute-start | bytes 7864328 | tf_op jit(solution)/shard_map/ppermute | solution.py:1372
  100.2 31.3 %collective-permute-start.13 = (bf16[2,5,4,32,1024]{4,3,2,1,0:T(8,128)(2,1)}, bf16[2,5,4,32,1024]{4,3,2,1,0:T(8,128)(2,1)}, u32[]{:S(2)}, u32[]{:S(2)}) collective-permute-start(bf16[2,5,4,32,1024]{4,3,2,1,0:T(8,128)(2,1)} %pad_maximum_fusion.4.refs_0_), channel_id=1, source_target_pairs={{0,1},{1,0},{2,3},{3,2},{4,5},{5,4},{6,7},{7,6},{8,9},{9,8},{10,11... | collective-permute-start | bytes 7864328 | tf_op jit(solution)/shard_map/ppermute | solution.py:1372
  100.3 27.1 %collective-permute-start.14 = (bf16[2,2,32,2816]{3,2,1,0:T(8,128)(2,1)S(1)}, bf16[2,2,32,2816]{3,2,1,0:T(8,128)(2,1)S(1)}, u32[]{:S(2)}, u32[]{:S(2)}) collective-permute-start(bf16[2,2,32,2816]{3,2,1,0:T(8,128)(2,1)S(1)} %pad_maximum_fusion.11), channel_id=1, source_target_pairs={{0,8},{1,9},{2,10},{3,11},{4,12},{5,13},{6,14},{7,15},{8,0},{9,1},... | collective-permute-start | bytes 2162696 | tf_op jit(solution)/shard_map/ppermute | solution.py:1372
  102.1 25.3 %collective-permute-start.15 = (bf16[1,88,1024]{2,1,0:T(8,128)(2,1)S(1)}, bf16[1,88,1024]{2,1,0:T(8,128)(2,1)S(1)}, u32[]{:S(2)}, u32[]{:S(2)}) collective-permute-start(bf16[1,88,1024]{2,1,0:T(8,128)(2,1)S(1)} %convert_bitcast_fusion.shard), channel_id=1, source_target_pairs={{0,16},{1,17},{2,18},{3,19},{4,20},{5,21},{6,22},{7,23},{8,24},{9,... | collective-permute-start | bytes 540680 | tf_op jit(solution)/shard_map/ppermute | solution.py:1372
  131.5 29.0 %collective-permute-start.16 = (bf16[2,5,4,32,1024]{4,3,2,1,0:T(8,128)(2,1)}, bf16[2,5,4,32,1024]{4,3,2,1,0:T(8,128)(2,1)}, u32[]{:S(2)}, u32[]{:S(2)}) collective-permute-start(bf16[2,5,4,32,1024]{4,3,2,1,0:T(8,128)(2,1)} %collective-permute-done.12.refs_2_), channel_id=1, source_target_pairs={{0,1},{1,0},{2,3},{3,2},{4,5},{5,4},{6,7},{7,6},{8,9},{9,8},{10,11... | collective-permute-start | bytes 7864328 | tf_op jit(solution)/shard_map/ppermute | solution.py:1372
  131.9 27.8 %copy-start.1 = (bf16[2,4,32,2816]{3,2,1,0:T(8,128)(2,1)}, bf16[2,4,32,2816]{3,2,1,0:T(8,128)(2,1)S(1)}, u32[]{:S(2)}) copy-start(bf16[2,4,32,2816]{3,2,1,0:T(8,128)(2,1)S(1)} %put_in_line.6) | copy-start | bytes 4325380
  131.9 28.6 %collective-permute-start.17 = (bf16[2,4,32,2816]{3,2,1,0:T(8,128)(2,1)S(1)}, bf16[2,4,32,2816]{3,2,1,0:T(8,128)(2,1)S(1)}, u32[]{:S(2)}, u32[]{:S(2)}) collective-permute-start(bf16[2,4,32,2816]{3,2,1,0:T(8,128)(2,1)S(1)} %put_in_line.6), channel_id=1, source_target_pairs={{0,2},{1,5},{2,0},{3,7},{4,6},{5,1},{6,4},{7,3},{8,10},{9,13},{10,... | collective-permute-start | bytes 4325384 | tf_op jit(solution)/shard_map/ppermute | solution.py:1372
  132.7 27.0 %collective-permute-start.18 = (bf16[2,1,88,1024]{3,2,1,0:T(8,128)(2,1)S(1)}, bf16[2,1,88,1024]{3,2,1,0:T(8,128)(2,1)S(1)}, u32[]{:S(2)}, u32[]{:S(2)}) collective-permute-start(bf16[2,1,88,1024]{3,2,1,0:T(8,128)(2,1)S(1)} %pad_maximum_fusion.18), channel_id=1, source_target_pairs={{0,8},{1,9},{2,10},{3,11},{4,12},{5,13},{6,14},{7,15},{8,0},{9,1},... | collective-permute-start | bytes 1081352 | tf_op jit(solution)/shard_map/ppermute | solution.py:1372
  163.7 42.4 %collective-permute-start.19 = (bf16[2,2,4,32,2816]{4,3,2,1,0:T(8,128)(2,1)S(1)}, bf16[2,2,4,32,2816]{4,3,2,1,0:T(8,128)(2,1)}, u32[]{:S(2)}, u32[]{:S(2)}) collective-permute-start(bf16[2,2,4,32,2816]{4,3,2,1,0:T(8,128)(2,1)S(1)} %pad_maximum_fusion.1.refs_0_), channel_id=1, source_target_pairs={{0,4},{1,3},{2,6},{3,1},{4,0},{5,7},{6,2},{7,5},{8,12},{9,11},{10,... | collective-permute-start | bytes 8650760 | tf_op jit(solution)/shard_map/ppermute | solution.py:1372
  164.2 41.8 %collective-permute-start.21 = (bf16[2,2,4,32,2816]{4,3,2,1,0:T(8,128)(2,1)S(1)}, bf16[2,2,4,32,2816]{4,3,2,1,0:T(8,128)(2,1)}, u32[]{:S(2)}, u32[]{:S(2)}) collective-permute-start(bf16[2,2,4,32,2816]{4,3,2,1,0:T(8,128)(2,1)S(1)} %pad_maximum_fusion.1.refs_0_), channel_id=1, source_target_pairs={{0,1},{1,0},{2,3},{3,2},{4,5},{5,4},{6,7},{7,6},{8,9},{9,8},{10,11... | collective-permute-start | bytes 8650760 | tf_op jit(solution)/shard_map/ppermute | solution.py:1372
  165.2 34.7 %collective-permute-start.20 = (bf16[1,4,88,1024]{3,2,1,0:T(8,128)(2,1)S(1)}, bf16[1,4,88,1024]{3,2,1,0:T(8,128)(2,1)}, u32[]{:S(2)}, u32[]{:S(2)}) collective-permute-start(bf16[1,4,88,1024]{3,2,1,0:T(8,128)(2,1)S(1)} %put_in_line.7), channel_id=1, source_target_pairs={{0,2},{1,5},{2,0},{3,7},{4,6},{5,1},{6,4},{7,3},{8,10},{9,13},{10,... | collective-permute-start | bytes 2162696 | tf_op jit(solution)/shard_map/ppermute | solution.py:1372
  206.0 5.5 collective-permute-start.22
  207.3 19.1 %collective-permute-start.23 = (bf16[2,1,4,88,1024]{4,3,2,1,0:T(8,128)(2,1)S(1)}, bf16[2,1,4,88,1024]{4,3,2,1,0:T(8,128)(2,1)S(1)}, u32[]{:S(2)}, u32[]{:S(2)}) collective-permute-start(bf16[2,1,4,88,1024]{4,3,2,1,0:T(8,128)(2,1)S(1)} %pad_maximum_fusion.7.refs_0_), channel_id=1, source_target_pairs={{0,4},{1,3},{2,6},{3,1},{4,0},{5,7},{6,2},{7,5},{8,12},{9,11},{10,... | collective-permute-start | bytes 4325384 | tf_op jit(solution)/shard_map/ppermute | solution.py:1372
  207.8 18.5 %collective-permute-start.24 = (bf16[2,1,4,88,1024]{4,3,2,1,0:T(8,128)(2,1)S(1)}, bf16[2,1,4,88,1024]{4,3,2,1,0:T(8,128)(2,1)S(1)}, u32[]{:S(2)}, u32[]{:S(2)}) collective-permute-start(bf16[2,1,4,88,1024]{4,3,2,1,0:T(8,128)(2,1)S(1)} %pad_maximum_fusion.7.refs_0_), channel_id=1, source_target_pairs={{0,1},{1,0},{2,3},{3,2},{4,5},{5,4},{6,7},{7,6},{8,9},{9,8},{10,11... | collective-permute-start | bytes 4325384 | tf_op jit(solution)/shard_map/ppermute | solution.py:1372
  226.4 3.2 collective-permute-start.25
  325.1 13.9 %collective-permute-start.26 = (bf16[2,16,32,2816]{3,2,1,0:T(8,128)(2,1)}, bf16[2,16,32,2816]{3,2,1,0:T(8,128)(2,1)}, u32[]{:S(2)}, u32[]{:S(2)}) collective-permute-start(bf16[2,16,32,2816]{3,2,1,0:T(8,128)(2,1)} %get-tuple-element.316), channel_id=1, source_target_pairs={{0,1},{1,0},{2,3},{3,2},{4,5},{5,4},{6,7},{7,6},{8,9},{9,8},{10,11... | collective-permute-start | bytes 17301512 | tf_op jit(solution)/shard_map/ppermute | solution.py:1372
  325.3 13.5 %collective-permute-start.27 = (bf16[1,16,88,1024]{3,2,1,0:T(8,128)(2,1)}, bf16[1,16,88,1024]{3,2,1,0:T(8,128)(2,1)S(1)}, u32[]{:S(2)}, u32[]{:S(2)}) collective-permute-start(bf16[1,16,88,1024]{3,2,1,0:T(8,128)(2,1)} %bitcast.263), channel_id=1, source_target_pairs={{0,1},{1,0},{2,3},{3,2},{4,5},{5,4},{6,7},{7,6},{8,9},{9,8},{10,11... | collective-permute-start | bytes 8650760 | tf_op jit(solution)/shard_map/ppermute | solution.py:1372
  348.7 52.6 %collective-permute-start.29 = (bf16[2,4,2,32,2816]{4,3,2,1,0:T(8,128)(2,1)}, bf16[2,4,2,32,2816]{4,3,2,1,0:T(8,128)(2,1)}, u32[]{:S(2)}, u32[]{:S(2)}) collective-permute-start(bf16[2,4,2,32,2816]{4,3,2,1,0:T(8,128)(2,1)} %get-tuple-element.346), channel_id=1, source_target_pairs={{0,4},{1,3},{2,6},{3,1},{4,0},{5,7},{6,2},{7,5},{8,12},{9,11},{10,... | collective-permute-start | bytes 8650760 | tf_op jit(solution)/shard_map/ppermute | solution.py:1372
  354.9 46.4 %collective-permute-start.30 = (bf16[2,4,1,88,1024]{4,3,1,2,0:T(8,128)(2,1)}, bf16[2,4,1,88,1024]{4,3,1,2,0:T(8,128)(2,1)}, u32[]{:S(2)}, u32[]{:S(2)}) collective-permute-start(bf16[2,4,1,88,1024]{4,3,1,2,0:T(8,128)(2,1)} %bitcast.264), channel_id=1, source_target_pairs={{0,4},{1,3},{2,6},{3,1},{4,0},{5,7},{6,2},{7,5},{8,12},{9,11},{10,... | collective-permute-start | bytes 4325384 | tf_op jit(solution)/shard_map/ppermute | solution.py:1372
  356.4 44.8 %collective-permute-start.28 = (bf16[640,1024]{1,0:T(8,128)(2,1)}, bf16[640,1024]{1,0:T(8,128)(2,1)}, u32[]{:S(2)}, u32[]{:S(2)}) collective-permute-start(bf16[640,1024]{1,0:T(8,128)(2,1)} %get-tuple-element.368), channel_id=1, source_target_pairs={{0,1},{1,0},{2,3},{3,2},{4,5},{5,4},{6,7},{7,6},{8,9},{9,8},{10,11... | collective-permute-start | bytes 3932168 | tf_op jit(solution)/shard_map/ppermute | solution.py:1372
  401.3 29.2 %collective-permute-start.31 = (bf16[5,16,32,1024]{3,2,1,0:T(8,128)(2,1)}, bf16[5,16,32,1024]{3,2,1,0:T(8,128)(2,1)}, u32[]{:S(2)}, u32[]{:S(2)}) collective-permute-start(bf16[5,16,32,1024]{3,2,1,0:T(8,128)(2,1)} %weight_part.6), channel_id=1, source_target_pairs={{0,1},{1,0},{2,3},{3,2},{4,5},{5,4},{6,7},{7,6},{8,9},{9,8},{10,11... | collective-permute-start | bytes 15728648 | tf_op jit(solution)/shard_map/ppermute | solution.py:1372
  403.6 26.9 %collective-permute-start.34 = (bf16[4,2,32,2816]{3,2,1,0:T(8,128)(2,1)S(1)}, bf16[4,2,32,2816]{3,2,1,0:T(8,128)(2,1)S(1)}, u32[]{:S(2)}, u32[]{:S(2)}) collective-permute-start(bf16[4,2,32,2816]{3,2,1,0:T(8,128)(2,1)S(1)} %fusion.2), channel_id=1, source_target_pairs={{0,2},{1,5},{2,0},{3,7},{4,6},{5,1},{6,4},{7,3},{8,10},{9,13},{10,... | collective-permute-start | bytes 4325384 | tf_op jit(solution)/shard_map/ppermute | solution.py:1372
  407.2 23.3 %collective-permute-start.33 = (bf16[4,1,88,1024]{3,2,1,0:T(8,128)(2,1)}, bf16[4,1,88,1024]{3,2,1,0:T(8,128)(2,1)}, u32[]{:S(2)}, u32[]{:S(2)}) collective-permute-start(bf16[4,1,88,1024]{3,2,1,0:T(8,128)(2,1)} %fusion.9), channel_id=1, source_target_pairs={{0,2},{1,5},{2,0},{3,7},{4,6},{5,1},{6,4},{7,3},{8,10},{9,13},{10,... | collective-permute-start | bytes 2162696 | tf_op jit(solution)/shard_map/ppermute | solution.py:1372
  408.8 20.3 %collective-permute-start.32 = (f32[128,1024]{1,0:T(8,128)}, f32[128,1024]{1,0:T(8,128)}, u32[]{:S(2)}, u32[]{:S(2)}) collective-permute-start(f32[128,1024]{1,0:T(8,128)} %get-tuple-element.655), channel_id=1, source_target_pairs={{0,1},{1,0},{2,3},{3,2},{4,5},{5,4},{6,7},{7,6},{8,9},{9,8},{10,11... | collective-permute-start | bytes 1572872 | tf_op jit(solution)/shard_map/ppermute | solution.py:1372
  448.3 36.8 %collective-permute-start.36 = (bf16[2,4,5,32,1024]{4,3,2,1,0:T(8,128)(2,1)}, bf16[2,4,5,32,1024]{4,3,2,1,0:T(8,128)(2,1)}, u32[]{:S(2)}, u32[]{:S(2)}) collective-permute-start(bf16[2,4,5,32,1024]{4,3,2,1,0:T(8,128)(2,1)} %get-tuple-element.383), channel_id=1, source_target_pairs={{0,4},{1,3},{2,6},{3,1},{4,0},{5,7},{6,2},{7,5},{8,12},{9,11},{10,... | collective-permute-start | bytes 7864328 | tf_op jit(solution)/shard_map/ppermute | solution.py:1372
  456.7 28.4 %collective-permute-start.35 = (bf16[3,16,32,512]{3,2,1,0:T(8,128)(2,1)}, bf16[3,16,32,512]{3,2,1,0:T(8,128)(2,1)}, u32[]{:S(2)}, u32[]{:S(2)}) collective-permute-start(bf16[3,16,32,512]{3,2,1,0:T(8,128)(2,1)} %weight_part.8), channel_id=1, source_target_pairs={{0,1},{1,0},{2,3},{3,2},{4,5},{5,4},{6,7},{7,6},{8,9},{9,8},{10,11... | collective-permute-start | bytes 4718600 | tf_op jit(solution)/shard_map/ppermute | solution.py:1372
  460.3 24.7 %collective-permute-start.37 = (bf16[2,2,32,2816]{3,2,1,0:T(8,128)(2,1)}, bf16[2,2,32,2816]{3,2,1,0:T(8,128)(2,1)}, u32[]{:S(2)}, u32[]{:S(2)}) collective-permute-start(bf16[2,2,32,2816]{3,2,1,0:T(8,128)(2,1)} %pad_maximum_fusion.12), channel_id=1, source_target_pairs={{0,8},{1,9},{2,10},{3,11},{4,12},{5,13},{6,14},{7,15},{8,0},{9,1},... | collective-permute-start | bytes 2162696 | tf_op jit(solution)/shard_map/ppermute | solution.py:1372
  463.0 58.6 %collective-permute-start.41 = (bf16[2,1,88,1024]{3,2,1,0:T(8,128)(2,1)S(1)}, bf16[2,1,88,1024]{3,2,1,0:T(8,128)(2,1)}, u32[]{:S(2)}, u32[]{:S(2)}) collective-permute-start(bf16[2,1,88,1024]{3,2,1,0:T(8,128)(2,1)S(1)} %copy-done.29), channel_id=1, source_target_pairs={{0,8},{1,9},{2,10},{3,11},{4,12},{5,13},{6,14},{7,15},{8,0},{9,1},... | collective-permute-start | bytes 1081352 | tf_op jit(solution)/shard_map/ppermute | solution.py:1372
  494.6 14.6 %collective-permute-start.38 = (bf16[3,16,32,512]{3,2,1,0:T(8,128)(2,1)}, bf16[3,16,32,512]{3,2,1,0:T(8,128)(2,1)}, u32[]{:S(2)}, u32[]{:S(2)}) collective-permute-start(bf16[3,16,32,512]{3,2,1,0:T(8,128)(2,1)} %weight_part.9), channel_id=1, source_target_pairs={{0,1},{1,0},{2,3},{3,2},{4,5},{5,4},{6,7},{7,6},{8,9},{9,8},{10,11... | collective-permute-start | bytes 4718600 | tf_op jit(solution)/shard_map/ppermute | solution.py:1372
  494.6 27.1 %collective-permute-start.40 = (bf16[4,5,32,1024]{3,2,1,0:T(8,128)(2,1)}, bf16[4,5,32,1024]{3,2,1,0:T(8,128)(2,1)}, u32[]{:S(2)}, u32[]{:S(2)}) collective-permute-start(bf16[4,5,32,1024]{3,2,1,0:T(8,128)(2,1)} %fusion.5), channel_id=1, source_target_pairs={{0,2},{1,5},{2,0},{3,7},{4,6},{5,1},{6,4},{7,3},{8,10},{9,13},{10,... | collective-permute-start | bytes 3932168 | tf_op jit(solution)/shard_map/ppermute | solution.py:1372
  504.6 17.1 %collective-permute-start.39 = (bf16[2,4,3,32,512]{4,3,2,1,0:T(8,128)(2,1)}, bf16[2,4,3,32,512]{4,3,2,1,0:T(8,128)(2,1)}, u32[]{:S(2)}, u32[]{:S(2)}) collective-permute-start(bf16[2,4,3,32,512]{4,3,2,1,0:T(8,128)(2,1)} %get-tuple-element.401), channel_id=1, source_target_pairs={{0,4},{1,3},{2,6},{3,1},{4,0},{5,7},{6,2},{7,5},{8,12},{9,11},{10,... | collective-permute-start | bytes 2359304 | tf_op jit(solution)/shard_map/ppermute | solution.py:1372
  509.2 49.6 %collective-permute-start.48 = (bf16[2,32,2816]{2,1,0:T(8,128)(2,1)}, bf16[2,32,2816]{2,1,0:T(8,128)(2,1)}, u32[]{:S(2)}, u32[]{:S(2)}) collective-permute-start(bf16[2,32,2816]{2,1,0:T(8,128)(2,1)} %fusion.21), channel_id=1, source_target_pairs={{0,16},{1,17},{2,18},{3,19},{4,20},{5,21},{6,22},{7,23},{8,24},{9,... | collective-permute-start | bytes 1081352 | tf_op jit(solution)/shard_map/ppermute | solution.py:1372
  528.1 23.1 %collective-permute-start.42 = (bf16[2,4,3,32,512]{4,3,2,1,0:T(8,128)(2,1)}, bf16[2,4,3,32,512]{4,3,2,1,0:T(8,128)(2,1)}, u32[]{:S(2)}, u32[]{:S(2)}) collective-permute-start(bf16[2,4,3,32,512]{4,3,2,1,0:T(8,128)(2,1)} %get-tuple-element.411), channel_id=1, source_target_pairs={{0,4},{1,3},{2,6},{3,1},{4,0},{5,7},{6,2},{7,5},{8,12},{9,11},{10,... | collective-permute-start | bytes 2359304 | tf_op jit(solution)/shard_map/ppermute | solution.py:1372
  528.8 48.6 %collective-permute-start.52 = (f32[768,1024]{1,0:T(8,128)}, f32[768,1024]{1,0:T(8,128)}, u32[]{:S(2)}, u32[]{:S(2)}) collective-permute-start(f32[768,1024]{1,0:T(8,128)} %get-tuple-element.435), channel_id=1, source_target_pairs={{0,1},{1,0},{2,3},{3,2},{4,5},{5,4},{6,7},{7,6},{8,9},{9,8},{10,11... | collective-permute-start | bytes 9437192 | tf_op jit(solution)/shard_map/ppermute | solution.py:1372
  532.8 18.4 %collective-permute-start.44 = (bf16[2,5,32,1024]{3,2,1,0:T(8,128)(2,1)}, bf16[2,5,32,1024]{3,2,1,0:T(8,128)(2,1)}, u32[]{:S(2)}, u32[]{:S(2)}) collective-permute-start(bf16[2,5,32,1024]{3,2,1,0:T(8,128)(2,1)} %pad_maximum_fusion.14), channel_id=1, source_target_pairs={{0,8},{1,9},{2,10},{3,11},{4,12},{5,13},{6,14},{7,15},{8,0},{9,1},... | collective-permute-start | bytes 1966088 | tf_op jit(solution)/shard_map/ppermute | solution.py:1372
  535.2 13.5 %collective-permute-start.43 = (bf16[4,3,32,512]{3,2,1,0:T(8,128)(2,1)}, bf16[4,3,32,512]{3,2,1,0:T(8,128)(2,1)S(1)}, u32[]{:S(2)}, u32[]{:S(2)}) collective-permute-start(bf16[4,3,32,512]{3,2,1,0:T(8,128)(2,1)} %fusion.17), channel_id=1, source_target_pairs={{0,2},{1,5},{2,0},{3,7},{4,6},{5,1},{6,4},{7,3},{8,10},{9,13},{10,... | collective-permute-start | bytes 1179656 | tf_op jit(solution)/shard_map/ppermute | solution.py:1372
  548.7 12.1 %collective-permute-start.47 = (bf16[1,88,1024]{2,1,0:T(8,128)(2,1)S(1)}, bf16[1,88,1024]{2,1,0:T(8,128)(2,1)S(1)}, u32[]{:S(2)}, u32[]{:S(2)}) collective-permute-start(bf16[1,88,1024]{2,1,0:T(8,128)(2,1)S(1)} %fusion.31), channel_id=1, source_target_pairs={{0,16},{1,17},{2,18},{3,19},{4,20},{5,21},{6,22},{7,23},{8,24},{9,... | collective-permute-start | bytes 540680 | tf_op jit(solution)/shard_map/ppermute | solution.py:1372
  552.5 13.7 %collective-permute-start.45 = (bf16[4,3,32,512]{3,2,1,0:T(8,128)(2,1)S(1)}, bf16[4,3,32,512]{3,2,1,0:T(8,128)(2,1)S(1)}, u32[]{:S(2)}, u32[]{:S(2)}) collective-permute-start(bf16[4,3,32,512]{3,2,1,0:T(8,128)(2,1)S(1)} %fusion.18), channel_id=1, source_target_pairs={{0,2},{1,5},{2,0},{3,7},{4,6},{5,1},{6,4},{7,3},{8,10},{9,13},{10,... | collective-permute-start | bytes 1179656 | tf_op jit(solution)/shard_map/ppermute | solution.py:1372
  555.2 10.9 %collective-permute-start.46 = (bf16[2,3,32,512]{3,2,1,0:T(8,128)(2,1)S(1)}, bf16[2,3,32,512]{3,2,1,0:T(8,128)(2,1)S(1)}, u32[]{:S(2)}, u32[]{:S(2)}) collective-permute-start(bf16[2,3,32,512]{3,2,1,0:T(8,128)(2,1)S(1)} %pad_maximum_fusion.22), channel_id=1, source_target_pairs={{0,8},{1,9},{2,10},{3,11},{4,12},{5,13},{6,14},{7,15},{8,0},{9,1},... | collective-permute-start | bytes 589832 | tf_op jit(solution)/shard_map/ppermute | solution.py:1372
  558.7 23.7 %collective-permute-start.51 = (bf16[5,32,1024]{2,1,0:T(8,128)(2,1)}, bf16[5,32,1024]{2,1,0:T(8,128)(2,1)}, u32[]{:S(2)}, u32[]{:S(2)}) collective-permute-start(bf16[5,32,1024]{2,1,0:T(8,128)(2,1)} %fusion.23), channel_id=1, source_target_pairs={{0,16},{1,17},{2,18},{3,19},{4,20},{5,21},{6,22},{7,23},{8,24},{9,... | collective-permute-start | bytes 983048 | tf_op jit(solution)/shard_map/ppermute | solution.py:1372
  566.8 15.7 %collective-permute-start.50 = (bf16[3,32,512]{2,1,0:T(8,128)(2,1)}, bf16[3,32,512]{2,1,0:T(8,128)(2,1)}, u32[]{:S(2)}, u32[]{:S(2)}) collective-permute-start(bf16[3,32,512]{2,1,0:T(8,128)(2,1)} %fusion.32), channel_id=1, source_target_pairs={{0,16},{1,17},{2,18},{3,19},{4,20},{5,21},{6,22},{7,23},{8,24},{9,... | collective-permute-start | bytes 294920 | tf_op jit(solution)/shard_map/ppermute | solution.py:1372
  568.8 14.7 %collective-permute-start.49 = (bf16[2,3,32,512]{3,2,1,0:T(8,128)(2,1)}, bf16[2,3,32,512]{3,2,1,0:T(8,128)(2,1)}, u32[]{:S(2)}, u32[]{:S(2)}) collective-permute-start(bf16[2,3,32,512]{3,2,1,0:T(8,128)(2,1)} %pad_maximum_fusion.23), channel_id=1, source_target_pairs={{0,8},{1,9},{2,10},{3,11},{4,12},{5,13},{6,14},{7,15},{8,0},{9,1},... | collective-permute-start | bytes 589832 | tf_op jit(solution)/shard_map/ppermute | solution.py:1372
  584.5 8.3 %collective-permute-start.53 = (bf16[3,32,512]{2,1,0:T(8,128)(2,1)S(1)}, bf16[3,32,512]{2,1,0:T(8,128)(2,1)S(1)}, u32[]{:S(2)}, u32[]{:S(2)}) collective-permute-start(bf16[3,32,512]{2,1,0:T(8,128)(2,1)S(1)} %fusion.33), channel_id=1, source_target_pairs={{0,16},{1,17},{2,18},{3,19},{4,20},{5,21},{6,22},{7,23},{8,24},{9,... | collective-permute-start | bytes 294920 | tf_op jit(solution)/shard_map/ppermute | solution.py:1372
  592.8 21.8 %copy-start.42 = (f32[32,16]{0,1:T(8,128)S(1)}, f32[32,16]{0,1:T(8,128)}, u32[]{:S(2)}) copy-start(f32[32,16]{0,1:T(8,128)} %param.49) | copy-start | bytes 6148
  595.2 5.7 collective-permute-start.54
  597.7 4.6 collective-permute-start.55
  597.8 4.6 collective-permute-start.56
  602.4 4.3 collective-permute-start.57
  603.0 3.8 collective-permute-start.58
  604.1 4.6 collective-permute-start.59
  608.8 1.2 collective-permute-start.60
  (41 other events, 308.0 us)
